TPU v7x, 256 devices: a whole 4x4x8 slice. The times are simulated.
256 devices in a mesh: vocab: 8 (over x, core), tok: 32 (over y, z).
Axes of the slice: x: 4, y: 4, z: 8, core: 2. Of those that a mesh axis runs over, the one named last changes fastest.
Arguments:
- student_hidden: bfloat16 [512, 4096], P('tok'), may hold values from -40 to 40
- teacher_hidden: bfloat16 [512, 4096], P('tok'), may hold values from -40 to 40
- student_weight: bfloat16 [4096, 131072], P(None, ('vocab', 'tok')), may hold values from -0.1 to 0.1
- teacher_weight: bfloat16 [4096, 131072], P(None, ('vocab', 'tok')), may hold values from -0.1 to 0.1
- source_rows: int32 [512], P('tok'), may hold values from 0 to 511, each once
Outputs:
- loss: float32 [], replicated
- hidden_grad: bfloat16 [512, 4096], P('tok', 'vocab')
Inputs may be any that keep to these rules, and one draw needn't show every extreme that they name: source_rows is a permutation of the 512 teacher rows.
All inputs are finite; a program needn't handle non-finite values.
Results may differ from a plain program's by a relative error of at most 0.025.
Values may be sent and summed in bfloat16 or wider, within the bound.
No kernel may reach another device: no remote copies, remote signals or barrier semaphores. Data moves between devices by JAX's collectives and lax.ppermute only.
A program may use at most 64 MiB of HBM per device.

v0:
```python
import jax
import jax.numpy as jnp
from jax import lax
from jax.sharding import PartitionSpec as P


def per_device(student_hidden, teacher_hidden, student_weight, teacher_weight, source_rows):
    student_logits = jnp.dot(
        lax.all_gather(student_hidden, "tok", axis=0, tiled=True),
        student_weight,
        preferred_element_type=jnp.float32,
    )
    all_teacher, all_sources = (
        lax.all_gather(teacher_hidden, "tok", axis=0, tiled=True),
        lax.all_gather(source_rows, "tok", axis=0, tiled=True),
    )
    teacher_rows = jnp.take(all_teacher, all_sources, axis=0)
    teacher_logits = jnp.dot(teacher_rows, teacher_weight, preferred_element_type=jnp.float32)
    student_top, teacher_top = lax.pmax(
        (jnp.max(student_logits, axis=1), jnp.max(teacher_logits, axis=1)), ("vocab", "tok")
    )
    student_exp = jnp.exp(student_logits - student_top[:, None])
    teacher_exp = jnp.exp(teacher_logits - teacher_top[:, None])
    student_total, teacher_total = lax.psum(
        (jnp.sum(student_exp, axis=1), jnp.sum(teacher_exp, axis=1)), ("vocab", "tok")
    )
    student_norm = student_top + jnp.log(student_total)
    teacher_norm = teacher_top + jnp.log(teacher_total)
    log_student = student_logits - student_norm[:, None]
    log_teacher = teacher_logits - teacher_norm[:, None]
    student_prob = jnp.exp(log_student)
    divergence = lax.psum(
        jnp.sum(student_prob * (log_student - log_teacher), axis=1), ("vocab", "tok")
    )
    logit_grad = (student_prob * (log_student - log_teacher - divergence[:, None])).astype(
        jnp.bfloat16
    )
    token_total = logit_grad.shape[0]
    partial_rows = lax.psum_scatter(
        lax.dot_general(
            logit_grad, student_weight, (((1,), (1,)), ((), ())), preferred_element_type=jnp.float32
        ),
        "tok",
        scatter_dimension=0,
        tiled=True,
    )
    hidden_grad = lax.psum_scatter(partial_rows, "vocab", scatter_dimension=1, tiled=True).astype(
        jnp.bfloat16
    )
    loss = jnp.sum(divergence) / token_total
    return (loss, hidden_grad)


def solution(mesh):
    in_specs = (
        P("tok", None),
        P("tok", None),
        P(None, ("vocab", "tok")),
        P(None, ("vocab", "tok")),
        P("tok"),
    )
    out_specs = (P(), P("tok", "vocab"))
    return jax.shard_map(
        per_device, mesh=mesh, in_specs=in_specs, out_specs=out_specs, check_vma=False
    )
```

profile of v0, /device:TPU:6, one launch (start us, length us, event | category | flops | bytes accessed | tf_op | source)
XLA Modules:
  0.0 677.8 jit_solution(208653667176869686)
XLA Ops:
  7.2 0.0 all-gather.5.cloned.1.call-start
  7.2 0.7 all-gather.5.cloned.1.call-update
  7.9 0.0 all-gather.3.cloned.1.call-start
  7.9 0.7 all-gather.3.cloned.1.call-update
  8.6 0.0 reduce-scatter.3.cloned.1.call-start
  8.7 1.3 dynamic-slice
  10.6 0.9 dynamic-update-slice
  11.5 23.8 %all-reduce = s32[512]{0:T(512)S(1)} all-reduce(s32[512]{0:T(512)S(1)} %dynamic-update-slice), channel_id=1, replica_groups=mesh['vocab'=8,'tok'=32] {'tok'}, use_global_device_ids=true, to_apply=%add | all-reduce | flops 512 | bytes 4096
  35.3 60.0 %all-gather.5.cloned.1.call-done = bf16[512,4096]{1,0:T(8,128)(2,1)} async-done(((bf16[16,4096]{1,0:T(8,128)(2,1)}), bf16[512,4096]{1,0:T(8,128)(2,1)}) %all-gather.5.cloned.1.call-update) | async-done | bytes 4194320 | tf_op jit(solution)/shard_map/all_gather | solution.py:14
  95.3 11.3 %gather_fusion = bf16[512,4096]{1,0:T(8,128)(2,1)} fusion(bf16[512,4096]{1,0:T(8,128)(2,1)} %all-gather.5.cloned.1.call-done, s32[1024]{0:T(1024)S(1)} %pad_clamp_fusion), kind=kCustom, calls=%fused_computation | custom fusion | bytes 8390656 | tf_op jit(solution)/shard_map/jit(_take)/gather | solution.py:17
  106.6 6.0 fusion.9
  112.7 64.4 %all-gather.3.cloned.1.call-done = bf16[512,4096]{1,0:T(8,128)(2,1)} async-done(((bf16[16,4096]{1,0:T(8,128)(2,1)}), bf16[512,4096]{1,0:T(8,128)(2,1)}) %all-gather.3.cloned.1.call-update) | async-done | bytes 4194320 | tf_op jit(solution)/shard_map/all_gather | solution.py:9
  177.0 5.8 fusion.10
  182.9 72.9 %all-reduce.2 = (f32[512]{0:T(512)S(1)}, f32[512]{0:T(512)S(1)}) all-reduce(f32[512]{0:T(512)S(1)} %get-tuple-element.6, f32[512]{0:T(512)S(1)} %get-tuple-element.8), channel_id=1, replica_groups=mesh['vocab'=8,'tok'=32] {'vocab','tok'}, use_global_device_ids=true, to_apply=%region_5.6 | all-reduce | flops 1024 | bytes 8192 | tf_op jit(solution)/shard_map/pmax | solution.py:19
  255.8 0.3 exponential_reduce_fusion
  256.1 74.1 %all-reduce.1 = (f32[512]{0:T(512)S(1)}, f32[512]{0:T(512)S(1)}) all-reduce(f32[512]{0:T(512)S(1)} %get-tuple-element.10, f32[512]{0:T(512)S(1)} %get-tuple-element.11), channel_id=1, replica_groups=mesh['vocab'=8,'tok'=32] {'vocab','tok'}, use_global_device_ids=true, to_apply=%region_7.8 | all-reduce | flops 1024 | bytes 8192 | tf_op jit(solution)/shard_map/psum | solution.py:24
  330.2 0.3 multiply_reduce_fusion
  330.5 74.2 %psum.23 = f32[512]{0:T(512)S(1)} all-reduce(f32[512]{0:T(512)S(1)} %multiply_reduce_fusion), channel_id=1, replica_groups=mesh['vocab'=8,'tok'=32] {'vocab','tok'}, use_global_device_ids=true, to_apply=%region_9.10 | all-reduce | flops 512 | bytes 4096 | tf_op jit(solution)/shard_map/psum | solution.py:32
  404.7 7.9 %fusion.4 = f32[512,4096]{1,0:T(8,128)} fusion(bf16[4096,512]{1,0:T(8,128)(2,1)} %param.7, f32[512,512]{0,1:T(8,128)S(1)} %get-tuple-element.9, f32[512,512]{0,1:T(8,128)S(1)} %get-tuple-element.7, f32[512]{0:T(512)S(1)} %psum.23, f32[512]{0:T(512)S(1)} %log_add_fusion, f32[512]{0:T(512)S(1)} %log_add_fusion.1), kind=kOutput, calls=%fused_computation.10 | convolution fusion | flops 2149056512 | bytes 14686208 | tf_op jit(solution)/shard_map/dot_general | solution.py:40
  412.6 0.0 reduce-scatter.3.cloned.1.call-update
  412.6 0.0 reduce-scatter.5.cloned.1.call-start
  412.7 225.2 %reduce-scatter.3.cloned.1.call-done = f32[16,4096]{1,0:T(8,128)} async-done(((f32[512,4096]{1,0:T(8,128)}), f32[16,4096]{1,0:T(8,128)}) %reduce-scatter.3.cloned.1.call-update) | async-done | bytes 262160 | tf_op jit(solution)/shard_map/reduce_scatter | solution.py:39
  637.9 0.0 reduce-scatter.5.cloned.1.call-update
  637.9 0.6 reduce_sum.39
  639.2 29.6 %reduce-scatter.5.cloned.1.call-done = f32[16,512]{1,0:T(8,128)} async-done(((f32[16,4096]{1,0:T(8,128)}), f32[16,512]{1,0:T(8,128)}) %reduce-scatter.5.cloned.1.call-update) | async-done | bytes 32784 | tf_op jit(solution)/shard_map/reduce_scatter | solution.py:47
  668.8 1.4 convert_element_type.7
  (6 shorter events, 0.0 us)
Async XLA Ops:
  7.2 88.2 %all-gather.5.cloned.1.call-start = ((), (), s32[]{:S(2)}) async-start(), calls=%async_computation.3 | async-start | bytes 4325376 | tf_op jit(solution)/shard_map/all_gather | solution.py:14
  7.9 169.1 %all-gather.3.cloned.1.call-start = ((), (), s32[]{:S(2)}) async-start(), calls=%async_computation.2 | async-start | bytes 4325376 | tf_op jit(solution)/shard_map/all_gather | solution.py:9
  8.6 629.3 %reduce-scatter.3.cloned.1.call-start = ((), (), s32[]{:S(2)}) async-start(), calls=%async_computation.4 | async-start | bytes 8650752 | tf_op jit(solution)/shard_map/reduce_scatter | solution.py:39
  412.6 256.2 %reduce-scatter.5.cloned.1.call-start = ((), (), s32[]{:S(2)}) async-start(), calls=%async_computation.5 | async-start | bytes 294912 | tf_op jit(solution)/shard_map/reduce_scatter | solution.py:47
Sparse Core Ops, SparseCore 0:
  10.6 84.6 all-gather.4
  97.9 79.0 all-gather.2
  412.7 225.1 reduce-scatter.2
  640.4 28.3 reduce-scatter.4
where the time goes:
time: 682 us; the launch traced here: 678 us
  waiting for transfers between devices  381 us (56%)
  blocking collectives  245 us (36%)
  matrix products  19.8 us (3%)
  between operations  16.2 us (2%)
  local copies, waits for them, and re-layouts  13.4 us (2%)
    reduce_scatter x1, waiting for transfers between devices, per_device(): lax.psum_scatter(lax.dot_general(logit_grad, student_weight, (((1,), (1,)...  225 us
    psum x1, blocking collectives, per_device(): lax.psum(jnp.sum(student_prob * (log_student - log_teacher), axis=1), ('v...  74.2 us
    psum x1, blocking collectives, per_device(): lax.psum((jnp.sum(student_exp, axis=1), jnp.sum(teacher_exp, axis=1)), ('...  74.1 us
    pmax x1, blocking collectives, per_device(): lax.pmax((jnp.max(student_logits, axis=1), jnp.max(teacher_logits, axis=1...  72.9 us
    all_gather x1, waiting for transfers between devices, per_device(): lax.all_gather(student_hidden, 'tok', axis=0, tiled=True)  64.4 us
    all_gather x1, waiting for transfers between devices, per_device(): lax.all_gather(teacher_hidden, 'tok', axis=0, tiled=True)  60 us
    reduce_scatter x1, waiting for transfers between devices, per_device(): lax.psum_scatter(partial_rows, 'vocab', scatter_dimension=1, tiled=True)  29.6 us
    unnamed x1, blocking collectives  23.8 us
  transfers between devices with their start and end apart: 4, of which 4 were waited for; matrix products, arithmetic and copies ran while one was open for 3% of the time, Pallas kernels for 0%

commit v1 on v0

v1 whole, which is shorter than its diff:
```python
import functools

import jax
import jax.numpy as jnp
from jax import lax
from jax.experimental import pallas as pl
from jax.experimental.pallas import tpu as pltpu
from jax.sharding import PartitionSpec as P

BF = jnp.bfloat16
F32 = jnp.float32
TOK, VOC = 32, 8
NY, NZ = 4, 8
N = 512
D = 4096
C = 512
SA = 512
TA = 256
TB = 1024
MIB = 1 << 20

Y_GROUPS = [[y * NZ + z for y in range(NY)] for z in range(NZ)]
Z_GROUPS = [[y * NZ + z for z in range(NZ)] for y in range(NY)]


def dot(a, b, dims=((1,), (0,))):
    return lax.dot_general(a, b, (dims, ((), ())), preferred_element_type=F32)


def params(limit):
    return pltpu.CompilerParams(vmem_limit_bytes=limit * MIB)


def pack_kernel(where_ref, a_ref, b_ref, out_ref):
    x = jnp.concatenate([a_ref[...], b_ref[...]], axis=1)
    out_ref[...] = jnp.broadcast_to(x[None], out_ref.shape)


def pack(where, a, a_width, b, b_width):
    rows = a.shape[0]
    width = a_width + b_width
    return pl.pallas_call(
        pack_kernel,
        grid_spec=pltpu.PrefetchScalarGridSpec(
            num_scalar_prefetch=1,
            grid=(1,),
            in_specs=[
                pl.BlockSpec((rows, a_width), lambda i, w: (0, w[0])),
                pl.BlockSpec((rows, b_width), lambda i, w: (0, w[1])),
            ],
            out_specs=pl.BlockSpec((TOK, rows, width), lambda i, w: (0, 0, 0)),
        ),
        out_shape=jax.ShapeDtypeStruct((TOK, rows, width), BF),
        compiler_params=params(16),
    )(where, a, b)


def first_kernel(core_ref, own_ref, other_ref, w_own_ref, w_other_ref, out_ref):
    out_ref[...] = dot(own_ref[...], w_own_ref[...]) + dot(other_ref[...], w_other_ref[...])


def first(core, own, other, teacher_weight):
    base = VOC * TA // TB
    return pl.pallas_call(
        first_kernel,
        grid_spec=pltpu.PrefetchScalarGridSpec(
            num_scalar_prefetch=1,
            grid=(1,),
            in_specs=[
                pl.BlockSpec((N, TB), lambda i, c: (0, 0)),
                pl.BlockSpec((N, TB), lambda i, c: (0, 0)),
                pl.BlockSpec((TB, C), lambda i, c: (base + c[0], 0)),
                pl.BlockSpec((TB, C), lambda i, c: (base + 1 - c[0], 0)),
            ],
            out_specs=pl.BlockSpec((N, C), lambda i, c: (0, 0)),
        ),
        out_shape=jax.ShapeDtypeStruct((N, C), F32),
        compiler_params=params(24),
        cost_estimate=pl.CostEstimate(
            flops=4 * N * TB * C, bytes_accessed=5 * MIB, transcendentals=0
        ),
    )(core, own, other, teacher_weight, teacher_weight)


def logits_kernel(rows_ref, sw_ref, tw_ref, part_ref, index_ref, s_ref, d_ref, stat_ref, t_ref):
    step = pl.program_id(0)
    rows = rows_ref[0]
    s_part = dot(rows[:, :SA], sw_ref[...])
    t_part = dot(rows[:, SA:], tw_ref[...])

    @pl.when(step == 0)
    def _():
        s_ref[...] = s_part
        t_ref[...] = part_ref[...] + t_part

    @pl.when(step > 0)
    def _():
        s_ref[...] += s_part
        t_ref[...] += t_part

    @pl.when(step == VOC - 1)
    def _():
        digits = index_ref[...].astype(F32)
        index = (digits[:, 0:1] * 32.0 + digits[:, 1:2]).astype(jnp.int32)
        column = lax.broadcasted_iota(jnp.int32, (N, N), 1)
        select = (index == column).astype(F32).astype(BF)
        t = t_ref[...]
        high = t.astype(BF)
        rest = t - high.astype(F32)
        middle = rest.astype(BF)
        low = (rest - middle.astype(F32)).astype(BF)
        t = dot(select, high) + dot(select, middle) + dot(select, low)
        s = s_ref[...]
        d = s - t
        d_ref[...] = d
        s_top = jnp.max(s, axis=1, keepdims=True)
        t_top = jnp.max(t, axis=1, keepdims=True)
        e = jnp.exp(s - s_top)
        s_sum = jnp.sum(e, axis=1, keepdims=True)
        mix = jnp.sum(e * d, axis=1, keepdims=True)
        t_sum = jnp.sum(jnp.exp(t - t_top), axis=1, keepdims=True)
        lane = lax.broadcasted_iota(jnp.int32, (N, 128), 1)
        table = jnp.zeros((N, 128), F32)
        for k, value in enumerate((s_top, s_sum, mix, t_top, t_sum)):
            table = jnp.where(lane == k, value, table)
        stat = jnp.transpose(table)[:8]
        stat_ref[...] = jnp.broadcast_to(stat[None], stat_ref.shape)


def logits(rows, student_weight, teacher_weight, part, packed):
    return pl.pallas_call(
        logits_kernel,
        grid=(VOC,),
        in_specs=[
            pl.BlockSpec((1, N, SA + TA), lambda i: (i, 0, 0)),
            pl.BlockSpec((SA, C), lambda i: (i, 0)),
            pl.BlockSpec((TA, C), lambda i: (i, 0)),
            pl.BlockSpec((N, C), lambda i: (0, 0)),
            pl.BlockSpec((N, 128), lambda i: (0, TB // 128)),
        ],
        out_specs=[
            pl.BlockSpec((N, C), lambda i: (0, 0)),
            pl.BlockSpec((N, C), lambda i: (0, 0)),
            pl.BlockSpec((VOC, 8, N), lambda i: (0, 0, 0)),
        ],
        out_shape=[
            jax.ShapeDtypeStruct((N, C), F32),
            jax.ShapeDtypeStruct((N, C), F32),
            jax.ShapeDtypeStruct((VOC, 8, N), F32),
        ],
        scratch_shapes=[pltpu.VMEM((N, C), F32)],
        compiler_params=params(32),
        cost_estimate=pl.CostEstimate(
            flops=2 * N * C * (D + VOC * TA), bytes_accessed=16 * MIB, transcendentals=2 * N * C
        ),
    )(rows, student_weight, teacher_weight, part, packed)


def merge(stats):
    s_top = jnp.max(stats[:, 0:1], axis=0)
    t_top = jnp.max(stats[:, 3:4], axis=0)
    s_scale = jnp.exp(stats[:, 0:1] - s_top[None])
    t_scale = jnp.exp(stats[:, 3:4] - t_top[None])
    s_sum = jnp.sum(stats[:, 1:2] * s_scale, axis=0)
    mix = jnp.sum(stats[:, 2:3] * s_scale, axis=0)
    t_sum = jnp.sum(stats[:, 4:5] * t_scale, axis=0)
    return s_top, s_sum, mix, t_top, t_sum


def merge_kernel(in_ref, out_ref):
    values = merge(in_ref[...])
    row = lax.broadcasted_iota(jnp.int32, (8, N), 0)
    stat = jnp.zeros((8, N), F32)
    for k, value in enumerate(values):
        stat = jnp.where(row == k, value, stat)
    out_ref[...] = jnp.broadcast_to(stat[None], out_ref.shape)


def merged(stats, copies):
    return pl.pallas_call(
        merge_kernel,
        out_shape=jax.ShapeDtypeStruct((copies, 8, N), F32),
        compiler_params=params(16),
    )(stats)


def exchange(x, axis, groups=None):
    n = x.shape[0]
    flat = x.reshape((n * x.shape[1],) + x.shape[2:])
    out = lax.all_to_all(flat, axis, 0, 0, axis_index_groups=groups, tiled=True)
    return out.reshape(x.shape)


def grad_kernel(stat_ref, s_ref, d_ref, sw_ref, out_ref, loss_ref, g_ref):
    @pl.when(pl.program_id(0) == 0)
    def _():
        s_top, s_sum, mix, t_top, t_sum = merge(stat_ref[...])
        mean = mix / s_sum
        divergence = mean - (s_top + jnp.log(s_sum)) + (t_top + jnp.log(t_sum))
        loss_ref[...] = jnp.sum(divergence, axis=1, keepdims=True) / N
        row = lax.broadcasted_iota(jnp.int32, (128, N), 0)
        table = jnp.zeros((128, N), F32)
        for k, value in enumerate((s_top, 1.0 / s_sum, mean)):
            table = jnp.where(row == k, value, table)
        table = jnp.transpose(table)
        prob = jnp.exp(s_ref[...] - table[:, 0:1]) * table[:, 1:2]
        g_ref[...] = (prob * (d_ref[...] - table[:, 2:3])).astype(BF)

    out_ref[0] = dot(g_ref[...], sw_ref[...], ((1,), (1,))).astype(BF)


def gradient(stats, s, d, student_weight):
    width = D // VOC
    return pl.pallas_call(
        grad_kernel,
        grid=(VOC,),
        in_specs=[
            pl.BlockSpec((NZ, 8, N), lambda i: (0, 0, 0)),
            pl.BlockSpec((N, C), lambda i: (0, 0)),
            pl.BlockSpec((N, C), lambda i: (0, 0)),
            pl.BlockSpec((width, C), lambda i: (i, 0)),
        ],
        out_specs=[
            pl.BlockSpec((1, N, width), lambda i: (i, 0, 0)),
            pl.BlockSpec((1, 1), lambda i: (0, 0)),
        ],
        out_shape=[
            jax.ShapeDtypeStruct((VOC, N, width), BF),
            jax.ShapeDtypeStruct((1, 1), F32),
        ],
        scratch_shapes=[pltpu.VMEM((N, C), BF)],
        compiler_params=params(32),
        cost_estimate=pl.CostEstimate(
            flops=2 * N * C * D, bytes_accessed=10 * MIB, transcendentals=N * C
        ),
    )(stats, s, d, student_weight)


def per_device(student_hidden, teacher_hidden, student_weight, teacher_weight, source_rows):
    v = lax.axis_index("vocab").astype(jnp.int32)
    core = v % 2
    slices = exchange(
        pack(jnp.stack([v, v]), student_hidden, SA, teacher_hidden, TA), "tok"
    ).reshape(N, SA + TA)
    rows = lax.all_gather(slices, "vocab", axis=0)
    digits = jnp.stack([source_rows // 32, source_rows % 32], axis=1).astype(BF)
    digits = jnp.pad(digits, ((0, 0), (0, 126)))
    packed = pack(
        jnp.stack([VOC * TA // TB + core, 0 * core]), teacher_hidden, TB, digits, 128
    )
    packed, _ = lax.optimization_barrier((packed, slices))
    packed = exchange(packed, "tok").reshape(N, TB + 128)
    other = lax.ppermute(packed, "vocab", [(k, k ^ 1) for k in range(VOC)])
    part = first(core[None], packed, other, teacher_weight)
    s, d, stats = logits(rows, student_weight, teacher_weight, part, packed)
    stats = merged(exchange(stats, "vocab"), NY)
    stats = merged(exchange(stats, "tok", Y_GROUPS), NZ)
    stats = exchange(stats, "tok", Z_GROUPS)
    partial, loss = gradient(stats, s, d, student_weight)
    partial = lax.psum_scatter(partial, "vocab", scatter_dimension=0)
    parts = exchange(partial.reshape(TOK, N // TOK, D // VOC), "tok")
    hidden_grad = jnp.sum(parts.astype(F32), axis=0).astype(BF)
    return loss[0, 0], hidden_grad


def solution(mesh):
    in_specs = (
        P("tok", None),
        P("tok", None),
        P(None, ("vocab", "tok")),
        P(None, ("vocab", "tok")),
        P("tok"),
    )
    out_specs = (P(), P("tok", "vocab"))
    return jax.shard_map(
        per_device, mesh=mesh, in_specs=in_specs, out_specs=out_specs, check_vma=False
    )
```

time: 682 us -> 208 us (0.30)
  waiting for transfers between devices: 381 us -> 33.9 us
  blocking collectives: 245 us -> 126 us
  matrix products: 19.8 us -> 0 us
  Pallas kernels: 0 us -> 14.9 us
    reduce_scatter x2 -> x1, waiting for transfers between devices: 255 us -> 31 us  [per_device(): partial = lax.psum_scatter(partial, 'vocab', scatter_dimension=0)]
    psum x2 -> x0, blocking collectives: 148 us -> none  [the longest x1 74.2 us: per_device(): lax.psum(jnp.sum(student_prob * (log_student - log_teacher), axis=1), ('v...]
    all_to_all x0 -> x6, blocking collectives: none -> 126 us  [exchange(): out = lax.all_to_all(flat, axis, 0, 0, axis_index_groups=groups, tiled=True)]
    all_gather x2 -> x1, waiting for transfers between devices: 124 us -> 0.02 us  [per_device(): rows = lax.all_gather(slices, 'vocab', axis=0)]
    pmax x1 -> x0, blocking collectives: 72.9 us -> none  [per_device(): lax.pmax((jnp.max(student_logits, axis=1), jnp.max(teacher_logits, axis=1...]
    unnamed x1 -> x0, blocking collectives: 23.8 us -> none
    dot_general x3 -> x0, matrix products: 19.8 us -> none  [the longest x1 7.89 us: per_device(): lax.dot_general(logit_grad, student_weight, (((1,), (1,)), ((), ())), pre...]
    pallas_call x0 -> x7, Pallas kernels: none -> 14.9 us  [the longest x1 7.78 us: logits(): pl.pallas_call(logits_kernel, grid=(VOC,), in_specs=[pl.BlockSpec((1, N,...]
  transfers between devices with their start and end apart: 4 -> 3, of which waited for: 4 -> 2; matrix products, arithmetic and copies ran while one was open for 3% -> 0% of each run, Pallas kernels for 0% -> 1%
where the time goes in v1:
time: 208 us; the launch traced here: 205 us
  blocking collectives  126 us (61%)
  waiting for transfers between devices  33.9 us (16%)
  Pallas kernels  14.9 us (7%)
  local copies, waits for them, and re-layouts  14.1 us (7%)
  between operations  14.1 us (7%)
    all_to_all x6, blocking collectives, exchange(): out = lax.all_to_all(flat, axis, 0, 0, axis_index_groups=groups, tiled=True)  126 us
    reduce_scatter x1, waiting for transfers between devices, per_device(): partial = lax.psum_scatter(partial, 'vocab', scatter_dimension=0)  31 us
    unnamed x18, local copies, waits for them, and re-layouts  14 us
    pallas_call x1, Pallas kernels, logits(): pl.pallas_call(logits_kernel, grid=(VOC,), in_specs=[pl.BlockSpec((1, N,...  7.78 us
    pallas_call x1, Pallas kernels, gradient(): pl.pallas_call(grad_kernel, grid=(VOC,), in_specs=[pl.BlockSpec((NZ, 8, N...  4.52 us
  transfers between devices with their start and end apart: 3, of which 2 were waited for; matrix products, arithmetic and copies ran while one was open for 0% of the time, Pallas kernels for 1%

profile of v1, /device:TPU:6, one launch (start us, length us, event | category | flops | bytes accessed | tf_op | source)
XLA Modules:
  0.0 204.7 jit_solution(2791754506028729141)
XLA Ops:
  7.2 0.0 all-gather.2.cloned.1.call-start
  7.2 0.1 pad_add_fusion.where_ref
  7.3 0.0 copy-start.6
  7.3 0.9 copy-done.6
  8.2 0.0 copy-start.8
  8.2 0.9 copy-done.8
  9.1 0.6 shard_map.68
  9.7 34.8 %all_to_all.41 = bf16[32,16,768]{2,1,0:T(8,128)(2,1)} all-to-all(bf16[32,16,768]{2,1,0:T(8,128)(2,1)S(1)} %shard_map.68), channel_id=1, replica_groups=mesh['vocab'=8,'tok'=32] {'tok'}, dimensions={0} | all-to-all | bytes 1572864 | tf_op jit(solution)/shard_map/all_to_all | solution.py:190
  44.5 0.0 all-gather.2.cloned.1.call-update
  44.5 0.0 reduce-scatter.2.cloned.1.call-start
  44.6 0.7 convert_bitcast_fusion
  45.2 0.1 copy.9
  45.3 0.1 pad_add_fusion.1.where_ref
  45.4 0.0 copy-start.7
  45.4 0.9 copy-done.7
  46.3 0.6 shard_map.69
  47.0 36.9 %all_to_all.42 = bf16[32,16,1152]{2,1,0:T(8,128)(2,1)S(1)} all-to-all(bf16[32,16,1152]{2,1,0:T(8,128)(2,1)S(1)} %shard_map.69), channel_id=1, replica_groups=mesh['vocab'=8,'tok'=32] {'tok'}, dimensions={0} | all-to-all | bytes 2359296 | tf_op jit(solution)/shard_map/all_to_all | solution.py:190
  83.8 0.0 collective-permute-start
  83.9 2.8 %collective-permute-done.other_ref = bf16[512,1152]{1,0:T(8,128)(2,1)S(1)} collective-permute-done((bf16[512,1152]{1,0:T(8,128)(2,1)S(1)}, bf16[512,1152]{1,0:T(8,128)(2,1)S(1)}, u32[]{:S(2)}, u32[]{:S(2)}) %collective-permute-start) | collective-permute-done | bytes 1179680 | tf_op jit(solution)/shard_map/ppermute | solution.py:253
  86.7 0.0 copy-start
  86.7 2.2 %copy-done = bf16[4096,512]{1,0:T(8,128)(2,1)S(1)} copy-done((bf16[4096,512]{1,0:T(8,128)(2,1)S(1)}, bf16[4096,512]{1,0:T(8,128)(2,1)}, u32[]{:S(2)}) %copy-start) | copy-done | bytes 4194328
  88.9 1.2 shard_map.70.part_ref
  90.1 0.0 all-gather.2.cloned.1.call-done.rows_ref
  90.2 0.0 copy-start.1
  90.2 2.2 %copy-done.1 = bf16[4096,512]{1,0:T(8,128)(2,1)S(1)} copy-done((bf16[4096,512]{1,0:T(8,128)(2,1)S(1)}, bf16[4096,512]{1,0:T(8,128)(2,1)}, u32[]{:S(2)}) %copy-start.1) | copy-done | bytes 4194328
  92.3 0.0 copy-start.2
  92.4 2.8 %copy-done.2 = bf16[8,512,768]{2,1,0:T(8,128)(2,1)S(1)} copy-done((bf16[8,512,768]{2,1,0:T(8,128)(2,1)S(1)}, bf16[8,512,768]{2,1,0:T(8,128)(2,1)}, u32[]{:S(2)}) %copy-start.2) | copy-done | bytes 6291480
  95.1 0.0 copy-start.4
  95.1 2.2 %copy-done.4 = bf16[4096,512]{1,0:T(8,128)(2,1)S(1)} copy-done((bf16[4096,512]{1,0:T(8,128)(2,1)S(1)}, bf16[4096,512]{1,0:T(8,128)(2,1)}, u32[]{:S(2)}) %copy-start.4) | copy-done | bytes 4194328
  97.3 0.0 copy-start.5
  97.3 7.8 %shard_map.71 = (f32[512,512]{1,0:T(8,128)S(1)}, f32[512,512]{1,0:T(8,128)S(1)}, f32[8,8,512]{2,1,0:T(8,128)S(1)}) custom-call(bf16[8,512,768]{2,1,0:T(8,128)(2,1)S(1)} %copy-done.2, bf16[4096,512]{1,0:T(8,128)(2,1)S(1)} %copy-done.4, bf16[4096,512]{1,0:T(8,128)(2,1)S(1)} %copy-done.1, f32[512,512]{1,0:T(8,128)S(1)} %shard_map.70.part_ref, ...), custom_call_target="tpu_custom_call" | custom-call | flops 3221225472 | bytes 16777216 | tf_op jit(solution)/shard_map/pallas_call | solution.py:131
  105.1 8.7 %all_to_all.43.in_ref = f32[8,8,512]{2,1,0:T(8,128)S(1)} all-to-all(f32[8,8,512]{2,1,0:T(8,128)S(1)} %get-tuple-element.7), channel_id=1, replica_groups=mesh['vocab'=8,'tok'=32] {'vocab'}, dimensions={0} | all-to-all | bytes 262144 | tf_op jit(solution)/shard_map/all_to_all | solution.py:190
  113.8 0.1 shard_map.72
  113.9 8.3 %all_to_all.44.in_ref = f32[4,8,512]{2,1,0:T(8,128)S(1)} all-to-all(f32[4,8,512]{2,1,0:T(8,128)S(1)} %shard_map.72), channel_id=1, replica_groups={{0,8,16,24},{1,9,17,25},{2,10,18,26},{3,11,19,27},{4,12,20,28},{5,13,21..., dimensions={0} | all-to-all | bytes 131072 | tf_op jit(solution)/shard_map/all_to_all | solution.py:190
  122.1 0.1 shard_map.73
  122.2 11.5 %all_to_all.45.stat_ref = f32[8,8,512]{2,1,0:T(8,128)S(1)} all-to-all(f32[8,8,512]{2,1,0:T(8,128)S(1)} %shard_map.73), channel_id=1, replica_groups={{0,1,2,3,4,5,6,7},{8,9,10,11,12,13,14,15},{16,17,18,19,20,21,22,23},{24..., dimensions={0} | all-to-all | bytes 262144 | tf_op jit(solution)/shard_map/all_to_all | solution.py:190
  133.7 0.0 copy-done.5
  133.7 4.5 %shard_map.74 = (bf16[8,512,512]{2,1,0:T(8,128)(2,1)S(1)}, f32[1,1]{1,0:T(1,128)}) custom-call(f32[8,8,512]{2,1,0:T(8,128)S(1)} %all_to_all.45.stat_ref, f32[512,512]{1,0:T(8,128)S(1)} %get-tuple-element.8.s_ref, f32[512,512]{1,0:T(8,128)S(1)} %get-tuple-element.9.d_ref, bf16[4096,512]{1,0:T(8,128)(2,1)S(1)} %copy-done.5), custom_call_target="tpu_custom_call" | custom-call | flops 2147483648 | bytes 10485760 | tf_op jit(solution)/shard_map/pallas_call | solution.py:214
  138.2 0.0 copy-start.3
  138.2 1.9 copy-done.3
  140.1 0.0 reduce-scatter.2.cloned.1.call-update
  140.1 31.0 %reduce-scatter.2.cloned.1.call-done = bf16[1,512,512]{2,1,0:T(8,128)(2,1)} async-done(((bf16[8,512,512]{2,1,0:T(8,128)(2,1)}), bf16[1,512,512]{2,1,0:T(8,128)(2,1)}) %reduce-scatter.2.cloned.1.call-update) | async-done | bytes 524304 | tf_op jit(solution)/shard_map/reduce_scatter | solution.py:260
  171.2 26.0 %all_to_all.46 = bf16[32,16,512]{2,1,0:T(8,128)(2,1)S(1)} all-to-all(bf16[32,16,512]{2,1,0:T(8,128)(2,1)} %bitcast.15), channel_id=1, replica_groups=mesh['vocab'=8,'tok'=32] {'tok'}, dimensions={0} | all-to-all | bytes 1048576 | tf_op jit(solution)/shard_map/all_to_all | solution.py:190
  197.2 0.7 reduce_sum.12
  (2 shorter events, 0.0 us)
Async XLA Ops:
  7.2 83.0 %all-gather.2.cloned.1.call-start = ((), (), s32[]{:S(2)}) async-start(), calls=%async_computation.7 | async-start | bytes 7077888 | tf_op jit(solution)/shard_map/all_gather | solution.py:245
  7.3 0.9 copy-start.6
  8.2 0.9 copy-start.8
  44.5 126.7 %reduce-scatter.2.cloned.1.call-start = ((), (), s32[]{:S(2)}) async-start(), calls=%async_computation.8 | async-start | bytes 4718592 | tf_op jit(solution)/shard_map/reduce_scatter | solution.py:260
  45.4 0.9 copy-start.7
  83.8 2.8 %collective-permute-start = (bf16[512,1152]{1,0:T(8,128)(2,1)S(1)}, bf16[512,1152]{1,0:T(8,128)(2,1)S(1)}, u32[]{:S(2)}, u32[]{:S(2)}) collective-permute-start(bf16[512,1152]{1,0:T(8,128)(2,1)S(1)} %bitcast.11), channel_id=1, source_target_pairs={{0,32},{32,0},{64,96},{96,64},{128,160},{160,128},{192,224},{224,1... | collective-permute-start | bytes 3538952 | tf_op jit(solution)/shard_map/ppermute | solution.py:253
  86.7 2.2 %copy-start = (bf16[4096,512]{1,0:T(8,128)(2,1)S(1)}, bf16[4096,512]{1,0:T(8,128)(2,1)}, u32[]{:S(2)}) copy-start(bf16[4096,512]{1,0:T(8,128)(2,1)} %tw_ref.1) | copy-start | bytes 12582916
  90.2 2.2 %copy-start.1 = (bf16[4096,512]{1,0:T(8,128)(2,1)S(1)}, bf16[4096,512]{1,0:T(8,128)(2,1)}, u32[]{:S(2)}) copy-start(bf16[4096,512]{1,0:T(8,128)(2,1)} %tw_ref.1) | copy-start | bytes 12582916
  92.3 2.8 %copy-start.2 = (bf16[8,512,768]{2,1,0:T(8,128)(2,1)S(1)}, bf16[8,512,768]{2,1,0:T(8,128)(2,1)}, u32[]{:S(2)}) copy-start(bf16[8,512,768]{2,1,0:T(8,128)(2,1)} %all-gather.2.cloned.1.call-done.rows_ref) | copy-start | bytes 18874372
  95.1 2.2 %copy-start.4 = (bf16[4096,512]{1,0:T(8,128)(2,1)S(1)}, bf16[4096,512]{1,0:T(8,128)(2,1)}, u32[]{:S(2)}) copy-start(bf16[4096,512]{1,0:T(8,128)(2,1)} %sw_ref.3) | copy-start | bytes 12582916
  97.3 36.3 %copy-start.5 = (bf16[4096,512]{1,0:T(8,128)(2,1)S(1)}, bf16[4096,512]{1,0:T(8,128)(2,1)}, u32[]{:S(2)}) copy-start(bf16[4096,512]{1,0:T(8,128)(2,1)} %sw_ref.3) | copy-start | bytes 12582916
  138.2 1.9 copy-start.3
Sparse Core Ops, SparseCore 0:
  44.6 37.7 all-gather.1
  140.3 30.8 reduce-scatter.1

commit v2 on v0

v2 whole, which is shorter than its diff:
```python
import functools

import jax
import jax.numpy as jnp
from jax import lax
from jax.experimental import pallas as pl
from jax.experimental.pallas import tpu as pltpu
from jax.sharding import PartitionSpec as P

BF = jnp.bfloat16
F32 = jnp.float32
TOK, VOC = 32, 8
NX = 4
N = 512
D = 4096
C = 512
SA = 512
TA = 256
TB = 1024
MIB = 1 << 20

X_GROUPS = [[2 * x + core for x in range(NX)] for core in range(2)]


def dot(a, b, dims=((1,), (0,))):
    return lax.dot_general(a, b, (dims, ((), ())), preferred_element_type=F32)


PARAMS = pltpu.CompilerParams(vmem_limit_bytes=56 * MIB)


def pack_kernel(where_ref, a_ref, b_ref, out_ref):
    x = jnp.concatenate([a_ref[...], b_ref[...]], axis=1)
    out_ref[...] = jnp.broadcast_to(x[None], out_ref.shape)


def pack(where, a, a_width, b, b_width):
    rows = a.shape[0]
    width = a_width + b_width
    return pl.pallas_call(
        pack_kernel,
        grid_spec=pltpu.PrefetchScalarGridSpec(
            num_scalar_prefetch=1,
            grid=(1,),
            in_specs=[
                pl.BlockSpec((rows, a_width), lambda i, w: (0, w[0])),
                pl.BlockSpec((rows, b_width), lambda i, w: (0, w[1])),
            ],
            out_specs=pl.BlockSpec((TOK, rows, width), lambda i, w: (0, 0, 0)),
        ),
        out_shape=jax.ShapeDtypeStruct((TOK, rows, width), BF),
        compiler_params=PARAMS,
    )(where, a, b)


def pieces_kernel(where_ref, *refs):
    count = (len(refs) - 2) // 3
    s_ref, t_ref = refs[-2:]
    s = t = None
    for k in range(count):
        rows, sw, tw = refs[3 * k : 3 * k + 3]
        s_part = dot(rows[:, :SA], sw[...])
        t_part = dot(rows[:, SA:], tw[...])
        s = s_part if s is None else s + s_part
        t = t_part if t is None else t + t_part
    s_ref[...] = s
    t_ref[...] = t


def piece_specs(k):
    return [
        pl.BlockSpec((N, SA + TA), lambda i, w: (0, 0)),
        pl.BlockSpec((SA, C), lambda i, w: (w[k], 0)),
        pl.BlockSpec((TA, C), lambda i, w: (w[k], 0)),
    ]


def pieces(where, rows, student_weight, teacher_weight):
    count = len(rows)
    whole = pl.BlockSpec((N, C), lambda i, w: (0, 0))
    return pl.pallas_call(
        pieces_kernel,
        grid_spec=pltpu.PrefetchScalarGridSpec(
            num_scalar_prefetch=1,
            grid=(1,),
            in_specs=[spec for k in range(count) for spec in piece_specs(k)],
            out_specs=[whole, whole],
        ),
        out_shape=[jax.ShapeDtypeStruct((N, C), F32)] * 2,
        compiler_params=PARAMS,
        cost_estimate=pl.CostEstimate(
            flops=2 * N * C * (SA + TA) * count, bytes_accessed=2 * MIB * count, transcendentals=0
        ),
    )(where, *(x for r in rows for x in (r, student_weight, teacher_weight)))


def pack_stats(lse_s, mean, lse_t):
    half = N // 2
    row = lax.broadcasted_iota(jnp.int32, (8, half), 0)
    out = jnp.zeros((8, half), F32)
    for k, value in enumerate((lse_s, mean, lse_t)):
        out = jnp.where(row == k, value[:, :half], out)
        out = jnp.where(row == k + 4, value[:, half:], out)
    return out


def merge(stats):
    def rows(k):
        return jnp.concatenate([stats[:, k : k + 1], stats[:, k + 4 : k + 5]], axis=2)

    def lse(x):
        top = jnp.max(x, axis=0)
        return top + jnp.log(jnp.sum(jnp.exp(x - top[None]), axis=0))

    each_s, each_mean, each_t = rows(0), rows(1), rows(2)
    lse_s = lse(each_s)
    mean = jnp.sum(jnp.exp(each_s - lse_s[None]) * each_mean, axis=0)
    return lse_s, mean, lse(each_t)


def logits_kernel(
    where_ref, c_ref, d_ref, c2_ref, d2_ref, sw1_ref, tw1_ref, sw2_ref, tw2_ref,
    own_ref, other_ref, w_own_ref, w_other_ref, s0_ref, t0_ref, s_ref, diff_ref, stat_ref,
):
    half = N // 2

    def far(x_ref, y_ref, a, b):
        return jnp.concatenate([x_ref[:, a:b], y_ref[:, a:b]], axis=0)

    s = s0_ref[...] + (
        dot(far(c_ref, d_ref, 0, SA), sw1_ref[...]) + dot(far(c2_ref, d2_ref, 0, SA), sw2_ref[...])
    )
    t = t0_ref[...] + (
        dot(far(c_ref, d_ref, SA, SA + TA), tw1_ref[...])
        + dot(far(c2_ref, d2_ref, SA, SA + TA), tw2_ref[...])
        + dot(own_ref[:, :TB], w_own_ref[...])
        + dot(other_ref[:, :TB], w_other_ref[...])
    )
    digits = own_ref[:, TB:].astype(F32)
    index = (digits[:, 0:1] * 32.0 + digits[:, 1:2]).astype(jnp.int32)
    column = lax.broadcasted_iota(jnp.int32, (N, N), 1)
    select = (index == column).astype(F32).astype(BF)
    high = t.astype(BF)
    rest = t - high.astype(F32)
    middle = rest.astype(BF)
    low = (rest - middle.astype(F32)).astype(BF)
    t = dot(select, high) + dot(select, middle) + dot(select, low)
    diff = s - t
    s_ref[...] = s
    diff_ref[...] = diff
    s_top = jnp.max(s, axis=1, keepdims=True)
    t_top = jnp.max(t, axis=1, keepdims=True)
    e = jnp.exp(s - s_top)
    s_sum = jnp.sum(e, axis=1, keepdims=True)
    mix = jnp.sum(e * diff, axis=1, keepdims=True)
    t_sum = jnp.sum(jnp.exp(t - t_top), axis=1, keepdims=True)
    lane = lax.broadcasted_iota(jnp.int32, (N, 128), 1)
    table = jnp.zeros((N, 128), F32)
    for k, value in enumerate((s_top, s_sum, mix, t_top, t_sum)):
        table = jnp.where(lane == k, value, table)
    table = jnp.transpose(table)
    s_top, s_sum, mix, t_top, t_sum = (table[k : k + 1] for k in range(5))
    stat = pack_stats(s_top + jnp.log(s_sum), mix / s_sum, t_top + jnp.log(t_sum))
    stat_ref[...] = jnp.broadcast_to(stat[None], stat_ref.shape)


def logits(where, far, student_weight, teacher_weight, own, other, s0, t0):
    base = VOC * TA // TB
    half = N // 2
    whole = pl.BlockSpec((N, C), lambda i, w: (0, 0))
    piece = pl.BlockSpec((half, SA + TA), lambda i, w: (0, 0))
    packed = pl.BlockSpec((N, TB + 128), lambda i, w: (0, 0))
    return pl.pallas_call(
        logits_kernel,
        grid_spec=pltpu.PrefetchScalarGridSpec(
            num_scalar_prefetch=1,
            grid=(1,),
            in_specs=[piece] * 4
            + [
                pl.BlockSpec((SA, C), lambda i, w: (w[0], 0)),
                pl.BlockSpec((TA, C), lambda i, w: (w[0], 0)),
                pl.BlockSpec((SA, C), lambda i, w: (w[1], 0)),
                pl.BlockSpec((TA, C), lambda i, w: (w[1], 0)),
                packed,
                packed,
                pl.BlockSpec((TB, C), lambda i, w: (base + w[2], 0)),
                pl.BlockSpec((TB, C), lambda i, w: (base + 1 - w[2], 0)),
                whole,
                whole,
            ],
            out_specs=[
                whole,
                whole,
                pl.BlockSpec((VOC, 8, half), lambda i, w: (0, 0, 0)),
            ],
        ),
        out_shape=[
            jax.ShapeDtypeStruct((N, C), F32),
            jax.ShapeDtypeStruct((N, C), F32),
            jax.ShapeDtypeStruct((VOC, 8, half), F32),
        ],
        compiler_params=PARAMS,
        cost_estimate=pl.CostEstimate(
            flops=2 * N * C * (2 * (SA + TA) + 2 * TB + 3 * N),
            bytes_accessed=14 * MIB,
            transcendentals=2 * N * C,
        ),
    )(
        where, *far, student_weight, teacher_weight, student_weight, teacher_weight,
        own, other, teacher_weight, teacher_weight, s0, t0,
    )


def merge_kernel(in_ref, out_ref):
    out_ref[...] = jnp.broadcast_to(pack_stats(*merge(in_ref[...]))[None], out_ref.shape)


def merged(stats, copies):
    return pl.pallas_call(
        merge_kernel,
        out_shape=jax.ShapeDtypeStruct((copies,) + stats.shape[1:], F32),
        compiler_params=PARAMS,
    )(stats)


def exchange(x, axis, groups=None):
    n = x.shape[0]
    flat = x.reshape((n * x.shape[1],) + x.shape[2:])
    out = lax.all_to_all(flat, axis, 0, 0, axis_index_groups=groups, tiled=True)
    return out.reshape(x.shape)


def grad_first_kernel(core_ref, stat_ref, s_ref, d_ref, sw_ref, out_ref, g_ref, loss_ref):
    @pl.when(pl.program_id(0) == 0)
    def _():
        lse_s, mean, lse_t = merge(stat_ref[...])
        loss_ref[...] = jnp.sum(mean - lse_s + lse_t, axis=1, keepdims=True) / N
        row = lax.broadcasted_iota(jnp.int32, (128, N), 0)
        table = jnp.where(row == 0, lse_s, jnp.where(row == 1, mean, 0.0))
        table = jnp.transpose(table)
        prob = jnp.exp(s_ref[...] - table[:, 0:1])
        g_ref[...] = (prob * (d_ref[...] - table[:, 1:2])).astype(BF)

    out_ref[0] = dot(g_ref[...], sw_ref[...], ((1,), (1,))).astype(BF)


def grad_second_kernel(core_ref, g_ref, in_ref, sw_ref, out_ref):
    out_ref[0] = (dot(g_ref[...], sw_ref[...], ((1,), (1,))) + in_ref[0].astype(F32)).astype(BF)


WIDTH = D // VOC
GRAD_COST = pl.CostEstimate(flops=N * C * D, bytes_accessed=8 * MIB, transcendentals=N * C)


def grad_first(core, stats, s, d, student_weight):
    whole = pl.BlockSpec((N, C), lambda i, c: (0, 0))
    return pl.pallas_call(
        grad_first_kernel,
        grid_spec=pltpu.PrefetchScalarGridSpec(
            num_scalar_prefetch=1,
            grid=(NX,),
            in_specs=[
                pl.BlockSpec(stats.shape, lambda i, c: (0, 0, 0)),
                whole,
                whole,
                pl.BlockSpec((WIDTH, C), lambda i, c: (2 * i + 1 - c[0], 0)),
            ],
            out_specs=[
                pl.BlockSpec((1, N, WIDTH), lambda i, c: (i, 0, 0)),
                whole,
                pl.BlockSpec((1, 1), lambda i, c: (0, 0)),
            ],
        ),
        out_shape=[
            jax.ShapeDtypeStruct((NX, N, WIDTH), BF),
            jax.ShapeDtypeStruct((N, C), BF),
            jax.ShapeDtypeStruct((1, 1), F32),
        ],
        compiler_params=PARAMS,
        cost_estimate=GRAD_COST,
    )(core, stats, s, d, student_weight)


def grad_second(core, g, received, student_weight):
    return pl.pallas_call(
        grad_second_kernel,
        grid_spec=pltpu.PrefetchScalarGridSpec(
            num_scalar_prefetch=1,
            grid=(NX,),
            in_specs=[
                pl.BlockSpec((N, C), lambda i, c: (0, 0)),
                pl.BlockSpec((1, N, WIDTH), lambda i, c: (i, 0, 0)),
                pl.BlockSpec((WIDTH, C), lambda i, c: (2 * i + c[0], 0)),
            ],
            out_specs=pl.BlockSpec((1, N, WIDTH), lambda i, c: (i, 0, 0)),
        ),
        out_shape=jax.ShapeDtypeStruct((NX, N, WIDTH), BF),
        compiler_params=PARAMS,
        cost_estimate=GRAD_COST,
    )(core, g, received, student_weight)


def sum_kernel(in_ref, out_ref):
    out_ref[...] = jnp.sum(in_ref[...].astype(F32), axis=0).astype(BF)


def summed(x, blocks):
    n, rows, width = x.shape
    rows //= blocks
    return pl.pallas_call(
        sum_kernel,
        grid=(blocks,),
        in_specs=[pl.BlockSpec((n, rows, width), lambda i: (0, i, 0))],
        out_specs=pl.BlockSpec((rows, width), lambda i: (i, 0)),
        out_shape=jax.ShapeDtypeStruct((rows * blocks, width), BF),
        compiler_params=PARAMS,
    )(x)


def along_x(a, step):
    pairs = [(k, (k // 2 + step) % NX * 2 + k % 2) for k in range(VOC)]
    return lax.ppermute(a, "vocab", pairs)


def to_other_core(a):
    return lax.ppermute(a, "vocab", [(k, k ^ 1) for k in range(VOC)])


def per_device(student_hidden, teacher_hidden, student_weight, teacher_weight, source_rows):
    v = lax.axis_index("vocab").astype(jnp.int32)
    x, core = v // 2, v % 2

    def slice_of(step, other):
        return (x + step) % NX * 2 + (core + other) % 2

    own = exchange(pack(jnp.stack([v, v]), student_hidden, SA, teacher_hidden, TA), "tok")
    own = own.reshape(N, SA + TA)
    left, right = along_x(own, 1), along_x(own, -1)
    own2 = to_other_core(own)
    digits = jnp.stack([source_rows // 32, source_rows % 32], axis=1).astype(BF)
    digits = jnp.pad(digits, ((0, 0), (0, 126)))
    packed = pack(
        jnp.stack([VOC * TA // TB + core, 0 * core]), teacher_hidden, TB, digits, 128
    )
    packed, _ = lax.optimization_barrier((packed, own))
    packed = exchange(packed, "tok").reshape(N, TB + 128)
    packed2 = to_other_core(packed)
    half = N // 2
    far1, far2 = along_x(left[:half], 1), along_x(right[half:], -1)
    left2, right2 = to_other_core(left), to_other_core(right)
    far = (far1, far2, to_other_core(far1), to_other_core(far2))
    where = jnp.stack([slice_of(k, o) for k in (0, -1, 1) for o in (0, 1)])
    s0, t0 = pieces(
        where, (own, own2, left, left2, right, right2), student_weight, teacher_weight
    )
    where = jnp.stack([slice_of(2, 0), slice_of(2, 1), core])
    s, d, stats = logits(
        where, far, student_weight, teacher_weight, packed, packed2, s0, t0
    )
    stats = merged(exchange(stats, "vocab"), TOK)
    stats = exchange(stats, "tok")
    partial, g, loss = grad_first(core[None], stats, s, d, student_weight)
    partial = grad_second(core[None], g, to_other_core(partial), student_weight)
    partial = summed(exchange(partial, "vocab", X_GROUPS), 4)
    hidden_grad = summed(exchange(partial.reshape(TOK, N // TOK, WIDTH), "tok"), 1)
    return loss[0, 0], hidden_grad


def solution(mesh):
    in_specs = (
        P("tok", None),
        P("tok", None),
        P(None, ("vocab", "tok")),
        P(None, ("vocab", "tok")),
        P("tok"),
    )
    out_specs = (P(), P("tok", "vocab"))
    return jax.shard_map(
        per_device, mesh=mesh, in_specs=in_specs, out_specs=out_specs, check_vma=False
    )
```

time: 682 us -> 212 us (0.31)
  waiting for transfers between devices: 381 us -> 63.7 us
  blocking collectives: 245 us -> 78.6 us
  Pallas kernels: 0 us -> 39.9 us
  starting transfers between devices: 0.16 us -> 21.1 us
  matrix products: 19.8 us -> 0 us
  between operations: 16.2 us -> 0.78 us
  local copies, waits for them, and re-layouts: 13.4 us -> 2.71 us
    reduce_scatter x2 -> x0, waiting for transfers between devices: 255 us -> none  [the longest x1 225 us: per_device(): lax.psum_scatter(lax.dot_general(logit_grad, student_weight, (((1,), (1,)...]
    psum x2 -> x0, blocking collectives: 148 us -> none  [the longest x1 74.2 us: per_device(): lax.psum(jnp.sum(student_prob * (log_student - log_teacher), axis=1), ('v...]
    all_gather x2 -> x0, waiting for transfers between devices: 124 us -> none  [the longest x1 64.4 us: per_device(): lax.all_gather(student_hidden, 'tok', axis=0, tiled=True)]
    all_to_all x0 -> x4, blocking collectives: none -> 78.6 us  [exchange(): out = lax.all_to_all(flat, axis, 0, 0, axis_index_groups=groups, tiled=True)]
    pmax x1 -> x0, blocking collectives: 72.9 us -> none  [per_device(): lax.pmax((jnp.max(student_logits, axis=1), jnp.max(teacher_logits, axis=1...]
    all_to_all x0 -> x2, waiting for transfers between devices: none -> 48.4 us  [exchange(): out = lax.all_to_all(flat, axis, 0, 0, axis_index_groups=groups, tiled=True)]
    pallas_call x0 -> x9, Pallas kernels: none -> 39.9 us  [the longest x1 8.57 us: logits(): pl.pallas_call(logits_kernel, grid_spec=pltpu.PrefetchScalarGridSpec(num_...]
    unnamed x1 -> x0, blocking collectives: 23.8 us -> none
  transfers between devices with their start and end apart: 4 -> 13, of which waited for: 4 -> 5; matrix products, arithmetic and copies ran while one was open for 3% -> 1% of each run, Pallas kernels for 0% -> 5%
where the time goes in v2:
time: 212 us; the launch traced here: 209 us
  blocking collectives  78.6 us (37%)
  waiting for transfers between devices  63.7 us (30%)
  Pallas kernels  39.9 us (19%)
  starting transfers between devices  21.1 us (10%)
  local copies, waits for them, and re-layouts  2.71 us (1%)
    all_to_all x4, blocking collectives, exchange(): out = lax.all_to_all(flat, axis, 0, 0, axis_index_groups=groups, tiled=True)  78.6 us
    all_to_all x2, waiting for transfers between devices, exchange(): out = lax.all_to_all(flat, axis, 0, 0, axis_index_groups=groups, tiled=True)  48.4 us
    all_to_all x2, starting transfers between devices, exchange(): out = lax.all_to_all(flat, axis, 0, 0, axis_index_groups=groups, tiled=True)  16.2 us
    ppermute x4, waiting for transfers between devices, along_x(): return lax.ppermute(a, 'vocab', pairs)  10.9 us
    pallas_call x1, Pallas kernels, logits(): pl.pallas_call(logits_kernel, grid_spec=pltpu.PrefetchScalarGridSpec(num_...  8.57 us
    pallas_call x1, Pallas kernels, pieces(): pl.pallas_call(pieces_kernel, grid_spec=pltpu.PrefetchScalarGridSpec(num_...  8.19 us
    pallas_call x1, Pallas kernels, grad_first(): pl.pallas_call(grad_first_kernel, grid_spec=pltpu.PrefetchScalarGridSpec(...  6.15 us
    pallas_call x2, Pallas kernels, summed(): pl.pallas_call(sum_kernel, grid=(blocks,), in_specs=[pl.BlockSpec((n, row...  5.29 us
  transfers between devices with their start and end apart: 13, of which 5 were waited for; matrix products, arithmetic and copies ran while one was open for 1% of the time, Pallas kernels for 5%

profile of v2, /device:TPU:6, one launch (start us, length us, event | category | flops | bytes accessed | tf_op | source)
XLA Modules:
  0.0 208.6 jit_solution(1046859621148724145)
XLA Ops:
  0.6 0.0 copy-start.5
  0.6 0.6 pad_add_fusion.1.where_ref
  1.2 2.3 %shard_map.68 = bf16[32,16,768]{2,1,0:T(8,128)(2,1)} custom-call(s32[2]{0:T(128)} %pad_add_fusion.1.where_ref, bf16[16,4096]{1,0:T(8,128)(2,1)} %a_ref.2, bf16[16,4096]{1,0:T(8,128)(2,1)} %a_ref.3), custom_call_target="tpu_custom_call" | custom-call | tf_op jit(solution)/shard_map/pallas_call | solution.py:40
  3.6 11.5 %all-to-all-start = ((bf16[32,16,768]{2,1,0:T(8,128)(2,1)}), bf16[32,16,768]{2,1,0:T(8,128)(2,1)S(1)}, u32[]{:S(2)}, u32[]{:S(2)}) async-start(bf16[32,16,768]{2,1,0:T(8,128)(2,1)} %shard_map.68), calls=%async_computation | async-start | bytes 1572864 | tf_op jit(solution)/shard_map/all_to_all | solution.py:229
  15.1 0.0 copy-done.5
  15.1 0.1 copy.9
  15.2 0.6 pad.4.b_ref
  15.8 0.6 pad_add_fusion.2.where_ref
  16.4 2.5 %shard_map.69 = bf16[32,16,1152]{2,1,0:T(8,128)(2,1)} custom-call(s32[2]{0:T(128)} %pad_add_fusion.2.where_ref, bf16[16,4096]{1,0:T(8,128)(2,1)} %a_ref.3, bf16[16,128]{1,0:T(8,128)(2,1)} %pad.4.b_ref), custom_call_target="tpu_custom_call" | custom-call | tf_op jit(solution)/shard_map/pallas_call | solution.py:40
  18.9 19.5 %all-to-all-done = bf16[32,16,768]{2,1,0:T(8,128)(2,1)S(1)} async-done(((bf16[32,16,768]{2,1,0:T(8,128)(2,1)}), bf16[32,16,768]{2,1,0:T(8,128)(2,1)S(1)}, u32[]{:S(2)}, u32[]{:S(2)}) %all-to-all-start) | async-done | bytes 786464 | tf_op jit(solution)/shard_map/all_to_all | solution.py:229
  38.4 0.0 copy-start.1
  38.4 4.7 %all-to-all-start.1 = ((bf16[32,16,1152]{2,1,0:T(8,128)(2,1)}), bf16[32,16,1152]{2,1,0:T(8,128)(2,1)S(1)}, u32[]{:S(2)}, u32[]{:S(2)}) async-start(bf16[32,16,1152]{2,1,0:T(8,128)(2,1)} %shard_map.69), calls=%async_computation.1 | async-start | bytes 2359296 | tf_op jit(solution)/shard_map/all_to_all | solution.py:229
  43.2 0.6 collective-permute-start
  43.7 1.5 collective-permute-start.2
  45.3 0.0 collective-permute-start.7
  45.3 28.9 %all-to-all-done.1 = bf16[32,16,1152]{2,1,0:T(8,128)(2,1)S(1)} async-done(((bf16[32,16,1152]{2,1,0:T(8,128)(2,1)}), bf16[32,16,1152]{2,1,0:T(8,128)(2,1)S(1)}, u32[]{:S(2)}, u32[]{:S(2)}) %all-to-all-start.1) | async-done | bytes 1179680 | tf_op jit(solution)/shard_map/all_to_all | solution.py:229
  74.2 0.0 copy-start
  74.2 0.0 collective-permute-start.6
  74.2 0.0 collective-permute-done.refs_6_
  74.2 0.0 copy-start.3
  74.2 0.5 collective-permute-start.8
  74.7 0.0 collective-permute-done.2.refs_12_
  74.7 0.0 copy-start.4
  74.7 0.1 collective-permute-start.9
  74.9 0.6 collective-permute-start.1
  75.4 0.0 collective-permute-done.7.refs_3_
  75.5 1.6 collective-permute-start.3
  77.1 9.4 %collective-permute-done.1.c_ref = bf16[256,768]{1,0:T(8,128)(2,1)} collective-permute-done((bf16[256,768]{1,0:T(8,128)(2,1)S(1)}, bf16[256,768]{1,0:T(8,128)(2,1)}, u32[]{:S(2)}, u32[]{:S(2)}) %collective-permute-start.1) | collective-permute-done | bytes 393248 | tf_op jit(solution)/shard_map/ppermute | solution.py:322
  86.5 0.0 collective-permute-start.4
  86.5 1.5 collective-permute-done.3.d_ref
  88.0 0.0 collective-permute-start.5
  88.0 0.6 stack.72.where_ref
  88.6 0.6 pad_add_fusion.where_ref
  89.2 0.0 collective-permute-done.8.refs_9_
  89.2 0.0 collective-permute-done.9.refs_15_
  89.2 0.0 copy-done.1
  89.2 0.0 copy-done.3
  89.3 0.0 copy-done.4
  89.3 8.2 %shard_map.70 = (f32[512,512]{1,0:T(8,128)}, f32[512,512]{1,0:T(8,128)}) custom-call(s32[6]{0:T(128)} %stack.72.where_ref, bf16[512,768]{1,0:T(8,128)(2,1)} %bitcast.24, bf16[4096,512]{1,0:T(8,128)(2,1)} %sw_ref.3, bf16[4096,512]{1,0:T(8,128)(2,1)} %w_other_ref.1, bf16[512,768]{1,0:T(8,128)(2,1)} %collective-permute-done.7.refs_3_, ...), custom_call_target="tpu_custom_call" | custom-call | flops 2415919104 | bytes 12582912 | tf_op jit(solution)/shard_map/pallas_call | solution.py:81
  97.5 0.0 copy-done
  97.5 0.0 collective-permute-done.4.c2_ref
  97.5 0.0 collective-permute-done.5.d2_ref
  97.5 0.0 collective-permute-done.6.other_ref
  97.5 8.6 %shard_map.71 = (f32[512,512]{1,0:T(8,128)}, f32[512,512]{1,0:T(8,128)}, f32[8,8,256]{2,1,0:T(8,128)}) custom-call(s32[3]{0:T(128)} %pad_add_fusion.where_ref, bf16[256,768]{1,0:T(8,128)(2,1)} %collective-permute-done.1.c_ref, bf16[256,768]{1,0:T(8,128)(2,1)} %collective-permute-done.3.d_ref, bf16[256,768]{1,0:T(8,128)(2,1)} %collective-permute-done.4.c2_ref, ...), custom_call_target="tpu_custom_call" | custom-call | flops 2684354560 | bytes 14680064 | tf_op jit(solution)/shard_map/pallas_call | solution.py:173
  106.1 8.3 %all_to_all.43.in_ref = f32[8,8,256]{2,1,0:T(8,128)} all-to-all(f32[8,8,256]{2,1,0:T(8,128)} %get-tuple-element.14), channel_id=1, replica_groups=mesh['vocab'=8,'tok'=32] {'vocab'}, dimensions={0} | all-to-all | bytes 131072 | tf_op jit(solution)/shard_map/all_to_all | solution.py:229
  114.3 1.7 shard_map.72
  116.0 17.4 %all_to_all.44.stat_ref = f32[32,8,256]{2,1,0:T(8,128)} all-to-all(f32[32,8,256]{2,1,0:T(8,128)} %shard_map.72), channel_id=1, replica_groups=mesh['vocab'=8,'tok'=32] {'tok'}, dimensions={0} | all-to-all | bytes 524288 | tf_op jit(solution)/shard_map/all_to_all | solution.py:229
  133.4 6.2 %shard_map.73 = (bf16[4,512,512]{2,1,0:T(8,128)(2,1)}, bf16[512,512]{1,0:T(8,128)(2,1)}, f32[1,1]{1,0:T(1,128)}) custom-call(s32[1]{0:T(128)} %bitcast.core_ref, f32[32,8,256]{2,1,0:T(8,128)} %all_to_all.44.stat_ref, f32[512,512]{1,0:T(8,128)} %get-tuple-element.15.s_ref, f32[512,512]{1,0:T(8,128)} %get-tuple-element.16.d_ref, bf16[4096,512]{1,0:T(8,128)(2,1)} %sw_ref.3), custom_call_target="tpu_custom_call" | custom-call | flops 1073741824 | bytes 8388608 | tf_op jit(solution)/shard_map/pallas_call | solution.py:257
  139.5 0.0 collective-permute-start.10
  139.6 4.4 %collective-permute-done.10.in_ref = bf16[4,512,512]{2,1,0:T(8,128)(2,1)S(1)} collective-permute-done((bf16[4,512,512]{2,1,0:T(8,128)(2,1)}, bf16[4,512,512]{2,1,0:T(8,128)(2,1)S(1)}, u32[]{:S(2)}, u32[]{:S(2)}) %collective-permute-start.10) | collective-permute-done | bytes 2097184 | tf_op jit(solution)/shard_map/ppermute | solution.py:326
  143.9 0.0 copy-start.2
  143.9 1.3 copy-done.2
  145.2 5.2 %shard_map.74 = bf16[4,512,512]{2,1,0:T(8,128)(2,1)} custom-call(s32[1]{0:T(128)} %bitcast.core_ref, bf16[512,512]{1,0:T(8,128)(2,1)} %get-tuple-element.18.g_ref, bf16[4,512,512]{2,1,0:T(8,128)(2,1)} %copy-done.2, bf16[4096,512]{1,0:T(8,128)(2,1)} %sw_ref.3), custom_call_target="tpu_custom_call" | custom-call | flops 1073741824 | bytes 8388608 | tf_op jit(solution)/shard_map/pallas_call | solution.py:285
  150.4 31.4 %all_to_all.45.in_ref = bf16[4,512,512]{2,1,0:T(8,128)(2,1)} all-to-all(bf16[4,512,512]{2,1,0:T(8,128)(2,1)} %shard_map.74), channel_id=1, replica_groups={{0,64,128,192},{32,96,160,224},{1,65,129,193},{33,97,161,225},{2,66,130..., dimensions={0} | all-to-all | bytes 4194304 | tf_op jit(solution)/shard_map/all_to_all | solution.py:229
  181.8 3.6 %shard_map.75 = bf16[512,512]{1,0:T(8,128)(2,1)} custom-call(bf16[4,512,512]{2,1,0:T(8,128)(2,1)} %all_to_all.45.in_ref), custom_call_target="tpu_custom_call" | custom-call | tf_op jit(solution)/shard_map/pallas_call | solution.py:310
  185.3 21.5 %all_to_all.46.in_ref = bf16[32,16,512]{2,1,0:T(8,128)(2,1)} all-to-all(bf16[32,16,512]{2,1,0:T(8,128)(2,1)} %bitcast.25), channel_id=1, replica_groups=mesh['vocab'=8,'tok'=32] {'tok'}, dimensions={0} | all-to-all | bytes 1048576 | tf_op jit(solution)/shard_map/all_to_all | solution.py:229
  206.9 1.7 shard_map.76
  (4 shorter events, 0.1 us)
Async XLA Ops:
  0.6 14.4 %copy-start.5 = (s32[16]{0:T(128)S(1)}, s32[16]{0:T(128)}, u32[]{:S(2)}) copy-start(s32[16]{0:T(128)} %param.9) | copy-start | bytes 196
  3.6 34.9 %all-to-all-start = ((bf16[32,16,768]{2,1,0:T(8,128)(2,1)}), bf16[32,16,768]{2,1,0:T(8,128)(2,1)S(1)}, u32[]{:S(2)}, u32[]{:S(2)}) async-start(bf16[32,16,768]{2,1,0:T(8,128)(2,1)} %shard_map.68), calls=%async_computation | async-start | bytes 1572864 | tf_op jit(solution)/shard_map/all_to_all | solution.py:229
  38.4 50.8 %copy-start.1 = (bf16[32,16,768]{2,1,0:T(8,128)(2,1)}, bf16[32,16,768]{2,1,0:T(8,128)(2,1)S(1)}, u32[]{:S(2)}) copy-start(bf16[32,16,768]{2,1,0:T(8,128)(2,1)S(1)} %all-to-all-done) | copy-start | bytes 2359300
  38.4 35.8 %all-to-all-start.1 = ((bf16[32,16,1152]{2,1,0:T(8,128)(2,1)}), bf16[32,16,1152]{2,1,0:T(8,128)(2,1)S(1)}, u32[]{:S(2)}, u32[]{:S(2)}) async-start(bf16[32,16,1152]{2,1,0:T(8,128)(2,1)} %shard_map.69), calls=%async_computation.1 | async-start | bytes 2359296 | tf_op jit(solution)/shard_map/all_to_all | solution.py:229
  43.2 31.0 %collective-permute-start = (bf16[512,768]{1,0:T(8,128)(2,1)S(1)}, bf16[512,768]{1,0:T(8,128)(2,1)S(1)}, u32[]{:S(2)}, u32[]{:S(2)}) collective-permute-start(bf16[512,768]{1,0:T(8,128)(2,1)S(1)} %bitcast.21), channel_id=1, source_target_pairs={{0,64},{32,96},{64,128},{96,160},{128,192},{160,224},{192,0},{224,... | collective-permute-start | bytes 2359304 | tf_op jit(solution)/shard_map/ppermute | solution.py:322
  43.7 31.0 %collective-permute-start.2 = (bf16[512,768]{1,0:T(8,128)(2,1)S(1)}, bf16[512,768]{1,0:T(8,128)(2,1)S(1)}, u32[]{:S(2)}, u32[]{:S(2)}) collective-permute-start(bf16[512,768]{1,0:T(8,128)(2,1)S(1)} %bitcast.22), channel_id=1, source_target_pairs={{0,192},{32,224},{64,0},{96,32},{128,64},{160,96},{192,128},{224,1... | collective-permute-start | bytes 2359304 | tf_op jit(solution)/shard_map/ppermute | solution.py:322
  45.3 30.2 %collective-permute-start.7 = (bf16[512,768]{1,0:T(8,128)(2,1)S(1)}, bf16[512,768]{1,0:T(8,128)(2,1)}, u32[]{:S(2)}, u32[]{:S(2)}) collective-permute-start(bf16[512,768]{1,0:T(8,128)(2,1)S(1)} %bitcast.23), channel_id=1, source_target_pairs={{0,32},{32,0},{64,96},{96,64},{128,160},{160,128},{192,224},{224,1... | collective-permute-start | bytes 2359304 | tf_op jit(solution)/shard_map/ppermute | solution.py:326
  74.2 23.3 %copy-start = (bf16[32,16,1152]{2,1,0:T(8,128)(2,1)}, bf16[32,16,1152]{2,1,0:T(8,128)(2,1)S(1)}, u32[]{:S(2)}) copy-start(bf16[32,16,1152]{2,1,0:T(8,128)(2,1)S(1)} %all-to-all-done.1) | copy-start | bytes 3538948
  74.2 23.3 %collective-permute-start.6 = (bf16[512,1152]{1,0:T(8,128)(2,1)S(1)}, bf16[512,1152]{1,0:T(8,128)(2,1)}, u32[]{:S(2)}, u32[]{:S(2)}) collective-permute-start(bf16[512,1152]{1,0:T(8,128)(2,1)S(1)} %bitcast.19), channel_id=1, source_target_pairs={{0,32},{32,0},{64,96},{96,64},{128,160},{160,128},{192,224},{224,1... | collective-permute-start | bytes 3538952 | tf_op jit(solution)/shard_map/ppermute | solution.py:326
  74.2 15.0 %copy-start.3 = (bf16[512,768]{1,0:T(8,128)(2,1)}, bf16[512,768]{1,0:T(8,128)(2,1)S(1)}, u32[]{:S(2)}) copy-start(bf16[512,768]{1,0:T(8,128)(2,1)S(1)} %collective-permute-done.refs_6_) | copy-start | bytes 2359300
  74.2 15.0 %collective-permute-start.8 = (bf16[512,768]{1,0:T(8,128)(2,1)S(1)}, bf16[512,768]{1,0:T(8,128)(2,1)}, u32[]{:S(2)}, u32[]{:S(2)}) collective-permute-start(bf16[512,768]{1,0:T(8,128)(2,1)S(1)} %collective-permute-done.refs_6_), channel_id=1, source_target_pairs={{0,32},{32,0},{64,96},{96,64},{128,160},{160,128},{192,224},{224,1... | collective-permute-start | bytes 2359304 | tf_op jit(solution)/shard_map/ppermute | solution.py:326
  74.7 14.5 %copy-start.4 = (bf16[512,768]{1,0:T(8,128)(2,1)}, bf16[512,768]{1,0:T(8,128)(2,1)S(1)}, u32[]{:S(2)}) copy-start(bf16[512,768]{1,0:T(8,128)(2,1)S(1)} %collective-permute-done.2.refs_12_) | copy-start | bytes 2359300
  74.7 14.5 %collective-permute-start.9 = (bf16[512,768]{1,0:T(8,128)(2,1)S(1)}, bf16[512,768]{1,0:T(8,128)(2,1)}, u32[]{:S(2)}, u32[]{:S(2)}) collective-permute-start(bf16[512,768]{1,0:T(8,128)(2,1)S(1)} %collective-permute-done.2.refs_12_), channel_id=1, source_target_pairs={{0,32},{32,0},{64,96},{96,64},{128,160},{160,128},{192,224},{224,1... | collective-permute-start | bytes 2359304 | tf_op jit(solution)/shard_map/ppermute | solution.py:326
  74.9 11.6 %collective-permute-start.1 = (bf16[256,768]{1,0:T(8,128)(2,1)S(1)}, bf16[256,768]{1,0:T(8,128)(2,1)}, u32[]{:S(2)}, u32[]{:S(2)}) collective-permute-start(bf16[256,768]{1,0:T(8,128)(2,1)S(1)} %slice.8), channel_id=1, source_target_pairs={{0,64},{32,96},{64,128},{96,160},{128,192},{160,224},{192,0},{224,... | collective-permute-start | bytes 1179656 | tf_op jit(solution)/shard_map/ppermute | solution.py:322
  75.5 12.6 %collective-permute-start.3 = (bf16[256,768]{1,0:T(8,128)(2,1)S(1)}, bf16[256,768]{1,0:T(8,128)(2,1)}, u32[]{:S(2)}, u32[]{:S(2)}) collective-permute-start(bf16[256,768]{1,0:T(8,128)(2,1)S(1)} %slice.9), channel_id=1, source_target_pairs={{0,192},{32,224},{64,0},{96,32},{128,64},{160,96},{192,128},{224,1... | collective-permute-start | bytes 1179656 | tf_op jit(solution)/shard_map/ppermute | solution.py:322
  86.5 11.0 %collective-permute-start.4 = (bf16[256,768]{1,0:T(8,128)(2,1)}, bf16[256,768]{1,0:T(8,128)(2,1)}, u32[]{:S(2)}, u32[]{:S(2)}) collective-permute-start(bf16[256,768]{1,0:T(8,128)(2,1)} %collective-permute-done.1.c_ref), channel_id=1, source_target_pairs={{0,32},{32,0},{64,96},{96,64},{128,160},{160,128},{192,224},{224,1... | collective-permute-start | bytes 1179656 | tf_op jit(solution)/shard_map/ppermute | solution.py:326
  88.0 9.5 %collective-permute-start.5 = (bf16[256,768]{1,0:T(8,128)(2,1)}, bf16[256,768]{1,0:T(8,128)(2,1)}, u32[]{:S(2)}, u32[]{:S(2)}) collective-permute-start(bf16[256,768]{1,0:T(8,128)(2,1)} %collective-permute-done.3.d_ref), channel_id=1, source_target_pairs={{0,32},{32,0},{64,96},{96,64},{128,160},{160,128},{192,224},{224,1... | collective-permute-start | bytes 1179656 | tf_op jit(solution)/shard_map/ppermute | solution.py:326
  139.5 4.4 %collective-permute-start.10 = (bf16[4,512,512]{2,1,0:T(8,128)(2,1)}, bf16[4,512,512]{2,1,0:T(8,128)(2,1)S(1)}, u32[]{:S(2)}, u32[]{:S(2)}) collective-permute-start(bf16[4,512,512]{2,1,0:T(8,128)(2,1)} %get-tuple-element.19), channel_id=1, source_target_pairs={{0,32},{32,0},{64,96},{96,64},{128,160},{160,128},{192,224},{224,1... | collective-permute-start | bytes 6291464 | tf_op jit(solution)/shard_map/ppermute | solution.py:326
  143.9 1.3 copy-start.2

commit v3 on v0

v3 whole, which is shorter than its diff:
```python
import functools

import jax
import jax.numpy as jnp
from jax import lax
from jax.experimental import pallas as pl
from jax.experimental.pallas import tpu as pltpu
from jax.sharding import PartitionSpec as P

BF = jnp.bfloat16
F32 = jnp.float32
TOK, VOC = 32, 8
NX, NY, NZ = 4, 4, 8
N = 512
D = 4096
C = 512
W = 512
ROWS = N // TOK
NEAR = N // NY
HALF = NX * W
MIB = 1 << 20
STEPS = (0, -1, 1, 2)

X_GROUPS = [[2 * x + core for x in range(NX)] for core in range(2)]
Z_GROUPS = [[y * NZ + z for z in range(NZ)] for y in range(NY)]


def dot(a, b, dims=((1,), (0,))):
    return lax.dot_general(a, b, (dims, ((), ())), preferred_element_type=F32)


PARAMS = pltpu.CompilerParams(vmem_limit_bytes=20 * MIB)
VM = pl.BlockSpec(memory_space=pltpu.VMEM)
SM = pl.BlockSpec(memory_space=pltpu.SMEM)
HBM = pl.BlockSpec(memory_space=pltpu.HBM)


def out(shape, dtype):
    return pltpu.VMEM(shape, dtype)


def in_hbm(x):
    return pltpu.with_memory_space_constraint(x, pltpu.HBM)


def cost(flops, mib=0):
    return pl.CostEstimate(flops=flops, bytes_accessed=mib * MIB, transcendentals=0)


def call(kernel, in_specs, outs, *args, scratch=(), flops=0):
    return pl.pallas_call(
        kernel,
        in_specs=in_specs,
        out_specs=[VM] * len(outs),
        out_shape=[out(*o) for o in outs],
        scratch_shapes=list(scratch),
        compiler_params=PARAMS,
        cost_estimate=cost(flops),
    )(*args)


def at_block(index, size):
    return pl.ds(pl.multiple_of(index * size, size), size)


def started(src, dst, sem):
    copy = pltpu.make_async_copy(src, dst, sem)
    copy.start()
    return copy


def pack_kernel(place_ref, source_ref, s_ref, t_ref, out_ref, s_buf, t_buf, sem):
    columns = at_block(place_ref[1] * NX + place_ref[0], W)
    copies = [
        started(s_ref.at[:, columns], s_buf, sem.at[0]),
        started(t_ref.at[:, columns], t_buf, sem.at[1]),
    ]
    row = lax.broadcasted_iota(jnp.int32, (ROWS, 128), 0)
    lane = lax.broadcasted_iota(jnp.int32, (ROWS, 128), 1)
    digits = jnp.zeros((ROWS, 128), jnp.int32)
    for r in range(ROWS):
        source = source_ref[r]
        value = jnp.where(lane == 0, source >> 5, jnp.where(lane == 1, source & 31, 0))
        digits = jnp.where(row == r, value, digits)
    digits = digits.astype(F32).astype(BF)
    out_ref[:, :, 2 * W :] = jnp.broadcast_to(digits[None], (NZ, ROWS, 128))
    for k, (copy, buf) in enumerate(zip(copies, (s_buf, t_buf))):
        copy.wait()
        out_ref[:, :, k * W : (k + 1) * W] = jnp.broadcast_to(buf[...][None], (NZ, ROWS, W))


def split_kernel(in_ref, s_ref, t_ref, digits_ref):
    s_ref[...] = in_ref[:, :W]
    t_ref[...] = in_ref[:, W : 2 * W]
    digits_ref[...] = in_ref[:, 2 * W :]


def join_kernel(place_ref, s0, s1, s2, s3, t0, t1, t2, t3, digits_ref, s_out, t_out):
    for step, ref in zip(STEPS, (s0, s1, s2, s3)):
        s_out[at_block((place_ref[2] + step) % NY, NEAR)] = ref[...]
    for k, ref in enumerate((t0, t1, t2, t3)):
        t_out[:, k * W : (k + 1) * W] = ref[...]
    t_out[:, HALF:] = digits_ref[...]


def hold_kernel(place_ref, sw_ref, tw_ref, sw2_ref, tw2_ref, sw_out, tw_out, sw2_out, tw2_out, sem):
    half = at_block(place_ref[1], HALF)
    copies = [
        started(sw_ref, sw_out, sem.at[0]),
        started(tw_ref.at[half], tw_out, sem.at[1]),
        started(sw2_ref.at[half], sw2_out, sem.at[2]),
        started(tw2_ref.at[half], tw2_out, sem.at[3]),
    ]
    for copy in copies:
        copy.wait()


def partial_logits(place_ref, sw_ref, tw_ref, s_refs, t_ref, out_ref, first):
    s0, s1, s2, s3, s4 = s_refs
    blocks = [s0[...], s1[...], s2[...], jnp.concatenate([s3[...], s4[...]], axis=0)]
    s_total = t_total = None
    for k, (step, block) in enumerate(zip(STEPS, blocks)):
        at = (place_ref[0] + step) % NX
        s_part = dot(block, sw_ref[at_block(first + at, W)])
        t_part = dot(t_ref[:, k * W : (k + 1) * W], tw_ref[at_block(at, W)])
        s_total = s_part if s_total is None else s_total + s_part
        t_total = t_part if t_total is None else t_total + t_part
    out_ref[0] = s_total
    out_ref[1] = t_total


def other_kernel(
    place_ref, sw_ref, tw_ref, s0, s1, s2, s3, s4, t0, t1, t2, t3, t4, out_ref, t_all
):
    for step, ref in zip(STEPS, (t0, t1, t2)):
        t_all[at_block((place_ref[2] + step) % NY, NEAR)] = ref[...]
    far = (place_ref[2] + STEPS[3]) % NY * 2
    for k, ref in enumerate((t3, t4)):
        t_all[at_block(far + k, NEAR // 2)] = ref[...]
    partial_logits(place_ref, sw_ref, tw_ref, (s0, s1, s2, s3, s4), t_all, out_ref, 0)


def own_kernel(place_ref, sw_ref, tw_ref, s0, s1, s2, s3, s4, t_all, out_ref):
    first = place_ref[1] * NX
    partial_logits(place_ref, sw_ref, tw_ref, (s0, s1, s2, s3, s4), t_all, out_ref, first)


def pack_stats(lse_s, mean, lse_t):
    half = N // 2
    row = lax.broadcasted_iota(jnp.int32, (8, half), 0)
    out = jnp.zeros((8, half), F32)
    for k, value in enumerate((lse_s, mean, lse_t)):
        out = jnp.where(row == k, value[:, :half], out)
        out = jnp.where(row == k + 4, value[:, half:], out)
    return out


def merge(stats):
    def rows(k):
        return jnp.concatenate([stats[:, k : k + 1], stats[:, k + 4 : k + 5]], axis=2)

    def lse(x):
        top = jnp.max(x, axis=0)
        return top + jnp.log(jnp.sum(jnp.exp(x - top[None]), axis=0))

    each_s, each_mean, each_t = rows(0), rows(1), rows(2)
    lse_s = lse(each_s)
    mean = jnp.sum(jnp.exp(each_s - lse_s[None]) * each_mean, axis=0)
    return lse_s, mean, lse(each_t)


def logits_kernel(own_ref, other_ref, digits_ref, s_ref, diff_ref, stat_ref):
    digits = digits_ref[:, HALF:].astype(F32)
    index = (digits[:, 0:1] * 32.0 + digits[:, 1:2]).astype(jnp.int32)
    column = lax.broadcasted_iota(jnp.int32, (N, N), 1)
    select = (index == column).astype(F32).astype(BF)
    t = own_ref[1] + other_ref[1]
    high = t.astype(BF)
    rest = t - high.astype(F32)
    middle = rest.astype(BF)
    low = (rest - middle.astype(F32)).astype(BF)
    t = dot(select, high) + dot(select, middle) + dot(select, low)
    s = own_ref[0] + other_ref[0]
    s_ref[...] = s
    diff = s - t
    diff_ref[...] = diff
    s_top = jnp.max(s, axis=1, keepdims=True)
    t_top = jnp.max(t, axis=1, keepdims=True)
    e = jnp.exp(s - s_top)
    s_sum = jnp.sum(e, axis=1, keepdims=True)
    mix = jnp.sum(e * diff, axis=1, keepdims=True)
    t_sum = jnp.sum(jnp.exp(t - t_top), axis=1, keepdims=True)
    lane = lax.broadcasted_iota(jnp.int32, (N, 128), 1)
    table = jnp.zeros((N, 128), F32)
    for k, value in enumerate((s_top, s_sum, mix, t_top, t_sum)):
        table = jnp.where(lane == k, value, table)
    table = jnp.transpose(table)
    s_top, s_sum, mix, t_top, t_sum = (table[k : k + 1] for k in range(5))
    stat = pack_stats(s_top + jnp.log(s_sum), mix / s_sum, t_top + jnp.log(t_sum))
    stat_ref[...] = jnp.broadcast_to(stat[None], stat_ref.shape)


def merge_kernel(in_ref, out_ref):
    out_ref[...] = jnp.broadcast_to(pack_stats(*merge(in_ref[...]))[None], out_ref.shape)


def exchange(x, axis, groups=None):
    n = x.shape[0]
    flat = x.reshape((n * x.shape[1],) + x.shape[2:])
    out = lax.all_to_all(flat, axis, 0, 0, axis_index_groups=groups, tiled=True)
    return out.reshape(x.shape)


def grad_first_kernel(place_ref, stat_ref, s_ref, d_ref, sw_ref, out_ref, g_ref, loss_ref):
    lse_s, mean, lse_t = merge(stat_ref[...])
    loss_ref[...] = jnp.sum(mean - lse_s + lse_t, axis=1, keepdims=True) / N
    row = lax.broadcasted_iota(jnp.int32, (128, N), 0)
    table = jnp.where(row == 0, lse_s, jnp.where(row == 1, mean, 0.0))
    table = jnp.transpose(table)
    prob = jnp.exp(s_ref[...] - table[:, 0:1])
    g = (prob * (d_ref[...] - table[:, 1:2])).astype(BF)
    g_ref[...] = g
    for x in range(NX):
        columns = sw_ref[at_block(2 * x + 1 - place_ref[1], W)]
        out_ref[x] = dot(g, columns, ((1,), (1,))).astype(BF)


def grad_second_kernel(place_ref, g_ref, in_ref, sw_ref, out_ref):
    for x in range(NX):
        columns = sw_ref[at_block(2 * x + place_ref[1], W)]
        part = dot(g_ref[...], columns, ((1,), (1,)))
        out_ref[x] = (part + in_ref[x].astype(F32)).astype(BF)


def sum_kernel(in_ref, out_ref):
    out_ref[...] = jnp.sum(in_ref[...].astype(F32), axis=0).astype(BF)


def summed(x):
    return call(sum_kernel, [VM], [(x.shape[1:], BF)], x)[0]


def along_x(a, step):
    pairs = [(k, (k // 2 + step) % NX * 2 + k % 2) for k in range(VOC)]
    return lax.ppermute(a, "vocab", pairs)


def along_y(a, step):
    pairs = [(k, (k // NZ + step) % NY * NZ + k % NZ) for k in range(TOK)]
    return lax.ppermute(a, "tok", pairs)


def to_other_core(a):
    return lax.ppermute(a, "vocab", [(k, k ^ 1) for k in range(VOC)])


def ring(a, along):
    return [a] + [along(a, -step) for step in STEPS[1:3]] + [along(a, 2)]


def per_device(student_hidden, teacher_hidden, student_weight, teacher_weight, source_rows):
    v = lax.axis_index("vocab").astype(jnp.int32)
    y = lax.axis_index("tok").astype(jnp.int32) // NZ
    place = jnp.stack([v // 2, v % 2, y])
    packed = call(
        pack_kernel,
        [SM, SM, HBM, HBM],
        [((NZ, ROWS, 2 * W + 128), BF)],
        place, source_rows, in_hbm(student_hidden), in_hbm(teacher_hidden),
        scratch=[pltpu.VMEM((ROWS, W), BF)] * 2 + [pltpu.SemaphoreType.DMA((2,))],
    )[0]
    sw2, tw2 = to_other_core(student_weight), to_other_core(teacher_weight)
    near = exchange(packed, "tok", Z_GROUPS).reshape(NEAR, 2 * W + 128)
    near, sw2, tw2 = lax.optimization_barrier((near, sw2, tw2))
    s_near, t_near, digits = call(
        split_kernel, [VM], [((NEAR, W), BF), ((NEAR, W), BF), ((NEAR, 128), BF)], near
    )
    s_near, t_near = ring(s_near, along_y), ring(t_near, along_x)
    s_near, t_near = lax.optimization_barrier((s_near, t_near))
    s_mine, t_mine = call(
        join_kernel,
        [SM] + [VM] * 9,
        [((N, W), BF), ((NEAR, HALF + 128), BF)],
        place, *s_near, *t_near, digits,
    )
    s_left, s_right = along_x(s_mine, 1), along_x(s_mine, -1)
    t_left, t_right = along_y(t_mine, 1), along_y(t_mine, -1)
    held = call(
        hold_kernel,
        [SM] + [HBM] * 4,
        [((D, C), BF)] + [((HALF, C), BF)] * 3,
        place, *(in_hbm(x) for x in (student_weight, teacher_weight, sw2, tw2)),
        scratch=[pltpu.SemaphoreType.DMA((4,))],
    )
    s_left, s_right, t_left, t_right, held = lax.optimization_barrier(
        (s_left, s_right, t_left, t_right, held)
    )
    sw, tw, sw2, tw2 = held
    s_rows = (
        s_mine, s_left, s_right,
        along_x(s_left[: N // 2], 1), along_x(s_right[N // 2 :], -1),
    )
    t_rows = (
        t_mine, t_left, t_right,
        along_y(t_left[: NEAR // 2], 1), along_y(t_right[NEAR // 2 :], -1),
    )
    s_rows, t_rows = lax.optimization_barrier((s_rows, t_rows))
    flops = 4 * N * HALF * C
    for_other, t_all = call(
        other_kernel,
        [SM] + [VM] * 12,
        [((2, N, C), F32), ((N, HALF + 128), BF)],
        place, sw2, tw2, *s_rows, *t_rows,
        flops=flops,
    )
    own = call(
        own_kernel,
        [SM] + [VM] * 8,
        [((2, N, C), F32)],
        place, sw, tw, *s_rows, t_all,
        flops=flops,
    )[0]
    other, own = lax.optimization_barrier((to_other_core(for_other), own))
    s, d, stats = call(
        logits_kernel,
        [VM] * 3,
        [((N, C), F32), ((N, C), F32), ((VOC, 8, N // 2), F32)],
        own, other, t_all,
        flops=6 * N * N * C,
    )
    stats = exchange(stats, "vocab")
    stats = call(merge_kernel, [VM], [((TOK, 8, N // 2), F32)], stats)[0]
    stats = exchange(stats, "tok")
    for_other, g, loss = call(
        grad_first_kernel,
        [SM] + [VM] * 4,
        [((NX, N, W), BF), ((N, C), BF), ((1, 1), F32)],
        place, stats, s, d, sw,
        flops=N * C * D,
    )
    partial = call(
        grad_second_kernel,
        [SM] + [VM] * 3,
        [((NX, N, W), BF)],
        place, g, to_other_core(for_other), sw,
        flops=N * C * D,
    )[0]
    partial = summed(exchange(partial, "vocab", X_GROUPS))
    hidden_grad = summed(exchange(partial.reshape(TOK, ROWS, W), "tok"))
    return loss[0, 0], hidden_grad


def solution(mesh):
    in_specs = (
        P("tok", None),
        P("tok", None),
        P(None, ("vocab", "tok")),
        P(None, ("vocab", "tok")),
        P("tok"),
    )
    out_specs = (P(), P("tok", "vocab"))
    return jax.shard_map(
        per_device, mesh=mesh, in_specs=in_specs, out_specs=out_specs, check_vma=False
    )
```

time: 682 us -> 164 us (0.24)
  waiting for transfers between devices: 381 us -> 39.5 us
  blocking collectives: 245 us -> 73.9 us
  starting transfers between devices: 0.16 us -> 25.1 us
  matrix products: 19.8 us -> 0 us
  Pallas kernels: 0 us -> 19.6 us
  between operations: 16.2 us -> 1.94 us
  local copies, waits for them, and re-layouts: 13.4 us -> 1.34 us
    reduce_scatter x2 -> x0, waiting for transfers between devices: 255 us -> none  [the longest x1 225 us: per_device(): lax.psum_scatter(lax.dot_general(logit_grad, student_weight, (((1,), (1,)...]
    psum x2 -> x0, blocking collectives: 148 us -> none  [the longest x1 74.2 us: per_device(): lax.psum(jnp.sum(student_prob * (log_student - log_teacher), axis=1), ('v...]
    all_gather x2 -> x0, waiting for transfers between devices: 124 us -> none  [the longest x1 64.4 us: per_device(): lax.all_gather(student_hidden, 'tok', axis=0, tiled=True)]
    all_to_all x0 -> x4, blocking collectives: none -> 73.9 us  [exchange(): out = lax.all_to_all(flat, axis, 0, 0, axis_index_groups=groups, tiled=True)]
    pmax x1 -> x0, blocking collectives: 72.9 us -> none  [per_device(): lax.pmax((jnp.max(student_logits, axis=1), jnp.max(teacher_logits, axis=1...]
    unnamed x1 -> x0, blocking collectives: 23.8 us -> none
    ppermute x0 -> x18, waiting for transfers between devices: none -> 22.7 us  [the longest x7 15.8 us: along_x(): return lax.ppermute(a, 'vocab', pairs)]
    ppermute x0 -> x18, starting transfers between devices: none -> 20.6 us  [the longest x7 12 us: along_y(): return lax.ppermute(a, 'tok', pairs)]
  transfers between devices with their start and end apart: 4 -> 19, of which waited for: 4 -> 11; matrix products, arithmetic and copies ran while one was open for 3% -> 0% of each run, Pallas kernels for 0% -> 5%
where the time goes in v3:
time: 164 us; the launch traced here: 161 us
  blocking collectives  73.9 us (45%)
  waiting for transfers between devices  39.5 us (24%)
  starting transfers between devices  25.1 us (15%)
  Pallas kernels  19.6 us (12%)
  between operations  1.94 us (1%)
    all_to_all x4, blocking collectives, exchange(): out = lax.all_to_all(flat, axis, 0, 0, axis_index_groups=groups, tiled=True)  73.9 us
    pallas_call x12, Pallas kernels, call(): pl.pallas_call(kernel, in_specs=in_specs, out_specs=[VM] * len(outs), out...  19.6 us
    all_to_all x1, waiting for transfers between devices, exchange(): out = lax.all_to_all(flat, axis, 0, 0, axis_index_groups=groups, tiled=True)  16.8 us
    ppermute x7, waiting for transfers between devices, along_x(): return lax.ppermute(a, 'vocab', pairs)  15.8 us
    ppermute x7, starting transfers between devices, along_y(): return lax.ppermute(a, 'tok', pairs)  12 us
    ppermute x7, starting transfers between devices, along_x(): return lax.ppermute(a, 'vocab', pairs)  7.82 us
    ppermute x4, waiting for transfers between devices, to_other_core(): return lax.ppermute(a, 'vocab', [(k, k ^ 1) for k in range(VOC)])  5.42 us
    all_to_all x1, starting transfers between devices, exchange(): out = lax.all_to_all(flat, axis, 0, 0, axis_index_groups=groups, tiled=True)  4.49 us
  transfers between devices with their start and end apart: 19, of which 11 were waited for; matrix products, arithmetic and copies ran while one was open for 0% of the time, Pallas kernels for 5%

profile of v3, /device:TPU:6, one launch (start us, length us, event | category | flops | bytes accessed | tf_op | source)
XLA Modules:
  0.0 161.4 jit_solution(1442897178864703974)
XLA Ops:
  0.6 0.1 collective-permute-start
  0.7 0.5 collective-permute-start.1
  1.2 0.1 pad_add_fusion.place_ref
  1.3 0.0 copy-start
  1.3 0.7 copy-done
  2.0 1.3 shard_map.68
  3.3 21.1 %all_to_all.36 = bf16[8,16,1152]{2,1,0:T(8,128)(2,1)S(1)} all-to-all(bf16[8,16,1152]{2,1,0:T(8,128)(2,1)S(1)} %shard_map.68), channel_id=1, replica_groups={{0,1,2,3,4,5,6,7},{8,9,10,11,12,13,14,15},{16,17,18,19,20,21,22,23},{24..., dimensions={0} | all-to-all | bytes 589824 | tf_op jit(solution)/shard_map/all_to_all | solution.py:210
  24.4 0.0 collective-permute-done.sw2_ref
  24.4 0.0 collective-permute-done.1.tw2_ref
  24.4 1.7 %collective-permute-start.2 = (bf16[128,512]{1,0:T(8,128)(2,1)S(1)}, bf16[128,512]{1,0:T(8,128)(2,1)S(1)}, u32[]{:S(2)}, u32[]{:S(2)}) collective-permute-start(bf16[128,512]{1,0:T(8,128)(2,1)S(1)} %get-tuple-element.53.s0), channel_id=1, source_target_pairs={{0,8},{1,9},{2,10},{3,11},{4,12},{5,13},{6,14},{7,15},{8,16},{9,17... | collective-permute-start | bytes 393224 | tf_op jit(solution)/shard_map/ppermute | solution.py:250
  26.1 1.7 %collective-permute-start.3 = (bf16[128,512]{1,0:T(8,128)(2,1)S(1)}, bf16[128,512]{1,0:T(8,128)(2,1)S(1)}, u32[]{:S(2)}, u32[]{:S(2)}) collective-permute-start(bf16[128,512]{1,0:T(8,128)(2,1)S(1)} %get-tuple-element.53.s0), channel_id=1, source_target_pairs={{0,24},{1,25},{2,26},{3,27},{4,28},{5,29},{6,30},{7,31},{8,0},{9,1... | collective-permute-start | bytes 393224 | tf_op jit(solution)/shard_map/ppermute | solution.py:250
  27.7 2.0 %collective-permute-start.4 = (bf16[128,512]{1,0:T(8,128)(2,1)S(1)}, bf16[128,512]{1,0:T(8,128)(2,1)S(1)}, u32[]{:S(2)}, u32[]{:S(2)}) collective-permute-start(bf16[128,512]{1,0:T(8,128)(2,1)S(1)} %get-tuple-element.53.s0), channel_id=1, source_target_pairs={{0,16},{1,17},{2,18},{3,19},{4,20},{5,21},{6,22},{7,23},{8,24},{9,... | collective-permute-start | bytes 393224 | tf_op jit(solution)/shard_map/ppermute | solution.py:250
  29.7 0.5 collective-permute-start.5
  30.2 1.5 collective-permute-start.6
  31.7 0.0 collective-permute-done.2.s1
  31.8 1.4 collective-permute-start.7
  33.2 0.0 collective-permute-done.3.s2
  33.2 1.5 collective-permute-done.4.s3
  34.7 0.6 collective-permute-done.5.t1
  35.3 1.1 collective-permute-done.6.t2
  36.4 1.8 %collective-permute-done.7.t3 = bf16[128,512]{1,0:T(8,128)(2,1)S(1)} collective-permute-done((bf16[128,512]{1,0:T(8,128)(2,1)S(1)}, bf16[128,512]{1,0:T(8,128)(2,1)S(1)}, u32[]{:S(2)}, u32[]{:S(2)}) %collective-permute-start.7) | collective-permute-done | bytes 131104 | tf_op jit(solution)/shard_map/ppermute | solution.py:245
  38.2 0.6 shard_map.70
  38.9 0.8 collective-permute-start.10
  39.6 2.6 %collective-permute-start.11 = (bf16[128,2176]{1,0:T(8,128)(2,1)S(1)}, bf16[128,2176]{1,0:T(8,128)(2,1)S(1)}, u32[]{:S(2)}, u32[]{:S(2)}) collective-permute-start(bf16[128,2176]{1,0:T(8,128)(2,1)S(1)} %get-tuple-element.81.t0), channel_id=1, source_target_pairs={{0,24},{1,25},{2,26},{3,27},{4,28},{5,29},{6,30},{7,31},{8,0},{9,1... | collective-permute-start | bytes 1671176 | tf_op jit(solution)/shard_map/ppermute | solution.py:250
  42.2 1.7 %collective-permute-start.8 = (bf16[512,512]{1,0:T(8,128)(2,1)S(1)}, bf16[512,512]{1,0:T(8,128)(2,1)S(1)}, u32[]{:S(2)}, u32[]{:S(2)}) collective-permute-start(bf16[512,512]{1,0:T(8,128)(2,1)S(1)} %get-tuple-element.76.s0), channel_id=1, source_target_pairs={{0,64},{32,96},{64,128},{96,160},{128,192},{160,224},{192,0},{224,... | collective-permute-start | bytes 1572872 | tf_op jit(solution)/shard_map/ppermute | solution.py:245
  43.9 0.3 collective-permute-start.9
  44.2 4.6 %shard_map.71 = (bf16[4096,512]{1,0:T(8,128)(2,1)S(1)}, bf16[2048,512]{1,0:T(8,128)(2,1)S(1)}, bf16[2048,512]{1,0:T(8,128)(2,1)S(1)}, bf16[2048,512]{1,0:T(8,128)(2,1)S(1)}) custom-call(s32[3]{0:T(128)S(1)} %pad_add_fusion.place_ref, bf16[4096,512]{1,0:T(8,128)(2,1)} %sw_ref.1, bf16[4096,512]{1,0:T(8,128)(2,1)} %tw_ref.1, ...), custom_call_target="tpu_custom_call" | custom-call | tf_op jit(solution)/shard_map/pallas_call | solution.py:51
  48.8 3.4 %collective-permute-done.8.s1 = bf16[512,512]{1,0:T(8,128)(2,1)S(1)} collective-permute-done((bf16[512,512]{1,0:T(8,128)(2,1)S(1)}, bf16[512,512]{1,0:T(8,128)(2,1)S(1)}, u32[]{:S(2)}, u32[]{:S(2)}) %collective-permute-start.8) | collective-permute-done | bytes 524320 | tf_op jit(solution)/shard_map/ppermute | solution.py:245
  52.2 3.0 %collective-permute-done.9.s2 = bf16[512,512]{1,0:T(8,128)(2,1)S(1)} collective-permute-done((bf16[512,512]{1,0:T(8,128)(2,1)S(1)}, bf16[512,512]{1,0:T(8,128)(2,1)S(1)}, u32[]{:S(2)}, u32[]{:S(2)}) %collective-permute-start.9) | collective-permute-done | bytes 524320 | tf_op jit(solution)/shard_map/ppermute | solution.py:245
  55.2 0.0 collective-permute-done.10.t1
  55.2 0.0 collective-permute-done.11.t2
  55.3 0.1 collective-permute-start.14
  55.4 3.3 %collective-permute-start.15 = (bf16[64,2176]{1,0:T(8,128)(2,1)S(1)}, bf16[64,2176]{1,0:T(8,128)(2,1)S(1)}, u32[]{:S(2)}, u32[]{:S(2)}) collective-permute-start(bf16[64,2176]{1,0:T(8,128)(2,1)S(1)} %slice.15), channel_id=1, source_target_pairs={{0,24},{1,25},{2,26},{3,27},{4,28},{5,29},{6,30},{7,31},{8,0},{9,1... | collective-permute-start | bytes 835592 | tf_op jit(solution)/shard_map/ppermute | solution.py:250
  58.7 0.4 collective-permute-start.12
  59.1 2.0 %collective-permute-start.13 = (bf16[256,512]{1,0:T(8,128)(2,1)S(1)}, bf16[256,512]{1,0:T(8,128)(2,1)S(1)}, u32[]{:S(2)}, u32[]{:S(2)}) collective-permute-start(bf16[256,512]{1,0:T(8,128)(2,1)S(1)} %slice.13), channel_id=1, source_target_pairs={{0,192},{32,224},{64,0},{96,32},{128,64},{160,96},{192,128},{224,1... | collective-permute-start | bytes 786440 | tf_op jit(solution)/shard_map/ppermute | solution.py:245
  61.1 4.1 %collective-permute-done.12.s3 = bf16[256,512]{1,0:T(8,128)(2,1)S(1)} collective-permute-done((bf16[256,512]{1,0:T(8,128)(2,1)S(1)}, bf16[256,512]{1,0:T(8,128)(2,1)S(1)}, u32[]{:S(2)}, u32[]{:S(2)}) %collective-permute-start.12) | collective-permute-done | bytes 262176 | tf_op jit(solution)/shard_map/ppermute | solution.py:245
  65.1 1.8 %collective-permute-done.13.s4 = bf16[256,512]{1,0:T(8,128)(2,1)S(1)} collective-permute-done((bf16[256,512]{1,0:T(8,128)(2,1)S(1)}, bf16[256,512]{1,0:T(8,128)(2,1)S(1)}, u32[]{:S(2)}, u32[]{:S(2)}) %collective-permute-start.13) | collective-permute-done | bytes 262176 | tf_op jit(solution)/shard_map/ppermute | solution.py:245
  66.9 0.0 collective-permute-done.14.t3
  66.9 0.0 collective-permute-done.15.t4
  66.9 3.0 %shard_map.72 = (f32[2,512,512]{2,1,0:T(8,128)S(1)}, bf16[512,2176]{1,0:T(8,128)(2,1)S(1)}) custom-call(s32[3]{0:T(128)S(1)} %pad_add_fusion.place_ref, bf16[2048,512]{1,0:T(8,128)(2,1)S(1)} %get-tuple-element.70.sw_ref, bf16[2048,512]{1,0:T(8,128)(2,1)S(1)} %get-tuple-element.71.tw_ref, bf16[512,512]{1,0:T(8,128)(2,1)S(1)} %get-tuple-element.76.s0, ...), custom_call_target="tpu_custom_call" | custom-call | flops 2147483648 | tf_op jit(solution)/shard_map/pallas_call | solution.py:51
  69.9 0.1 collective-permute-start.16
  70.0 2.9 %shard_map.73.own_ref = f32[2,512,512]{2,1,0:T(8,128)S(1)} custom-call(s32[3]{0:T(128)S(1)} %pad_add_fusion.place_ref, bf16[4096,512]{1,0:T(8,128)(2,1)S(1)} %get-tuple-element.87.sw_ref, bf16[2048,512]{1,0:T(8,128)(2,1)S(1)} %get-tuple-element.88.tw_ref, bf16[512,512]{1,0:T(8,128)(2,1)S(1)} %get-tuple-element.76.s0, ...), custom_call_target="tpu_custom_call" | custom-call | flops 2147483648 | tf_op jit(solution)/shard_map/pallas_call | solution.py:51
  72.9 1.3 collective-permute-done.16.other_ref
  74.1 1.7 %shard_map.74 = (f32[512,512]{1,0:T(8,128)S(1)}, f32[512,512]{1,0:T(8,128)S(1)}, f32[8,8,256]{2,1,0:T(8,128)S(1)}) custom-call(f32[2,512,512]{2,1,0:T(8,128)S(1)} %shard_map.73.own_ref, f32[2,512,512]{2,1,0:T(8,128)S(1)} %collective-permute-done.16.other_ref, bf16[512,2176]{1,0:T(8,128)(2,1)S(1)} %get-tuple-element.89.t_all.digits_ref), custom_call_target="tpu_custom_call" | custom-call | flops 805306368 | tf_op jit(solution)/shard_map/pallas_call | solution.py:51
  75.9 7.9 %all_to_all.37.in_ref = f32[8,8,256]{2,1,0:T(8,128)S(1)} all-to-all(f32[8,8,256]{2,1,0:T(8,128)S(1)} %get-tuple-element.92), channel_id=1, replica_groups=mesh['vocab'=8,'tok'=32] {'vocab'}, dimensions={0} | all-to-all | bytes 131072 | tf_op jit(solution)/shard_map/all_to_all | solution.py:210
  83.7 0.1 shard_map.75
  83.9 15.5 %all_to_all.38.stat_ref = f32[32,8,256]{2,1,0:T(8,128)S(1)} all-to-all(f32[32,8,256]{2,1,0:T(8,128)S(1)} %shard_map.75), channel_id=1, replica_groups=mesh['vocab'=8,'tok'=32] {'tok'}, dimensions={0} | all-to-all | bytes 524288 | tf_op jit(solution)/shard_map/all_to_all | solution.py:210
  99.4 2.4 %shard_map.76 = (bf16[4,512,512]{2,1,0:T(8,128)(2,1)S(1)}, bf16[512,512]{1,0:T(8,128)(2,1)S(1)}, f32[1,1]{1,0:T(1,128)S(1)}) custom-call(s32[3]{0:T(128)S(1)} %pad_add_fusion.place_ref, f32[32,8,256]{2,1,0:T(8,128)S(1)} %all_to_all.38.stat_ref, f32[512,512]{1,0:T(8,128)S(1)} %get-tuple-element.93.s_ref, f32[512,512]{1,0:T(8,128)S(1)} %get-tuple-element.94.d_ref, ...), custom_call_target="tpu_custom_call" | custom-call | flops 1073741824 | tf_op jit(solution)/shard_map/pallas_call | solution.py:51
  101.8 0.1 collective-permute-start.17
  101.9 4.1 %collective-permute-done.17.in_ref = bf16[4,512,512]{2,1,0:T(8,128)(2,1)S(1)} collective-permute-done((bf16[4,512,512]{2,1,0:T(8,128)(2,1)S(1)}, bf16[4,512,512]{2,1,0:T(8,128)(2,1)S(1)}, u32[]{:S(2)}, u32[]{:S(2)}) %collective-permute-start.17) | collective-permute-done | bytes 2097184 | tf_op jit(solution)/shard_map/ppermute | solution.py:254
  106.0 1.8 %shard_map.77 = bf16[4,512,512]{2,1,0:T(8,128)(2,1)S(1)} custom-call(s32[3]{0:T(128)S(1)} %pad_add_fusion.place_ref, bf16[512,512]{1,0:T(8,128)(2,1)S(1)} %get-tuple-element.96.g_ref, bf16[4,512,512]{2,1,0:T(8,128)(2,1)S(1)} %collective-permute-done.17.in_ref, bf16[4096,512]{1,0:T(8,128)(2,1)S(1)} %get-tuple-element.87.sw_ref), custom_call_target="tpu_custom_call" | custom-call | flops 1073741824 | tf_op jit(solution)/shard_map/pallas_call | solution.py:51
  107.8 29.4 %all_to_all.39.in_ref = bf16[4,512,512]{2,1,0:T(8,128)(2,1)S(1)} all-to-all(bf16[4,512,512]{2,1,0:T(8,128)(2,1)S(1)} %shard_map.77), channel_id=1, replica_groups={{0,64,128,192},{32,96,160,224},{1,65,129,193},{33,97,161,225},{2,66,130..., dimensions={0} | all-to-all | bytes 4194304 | tf_op jit(solution)/shard_map/all_to_all | solution.py:210
  137.2 1.1 shard_map.78
  138.3 4.5 %all-to-all-start.4 = ((bf16[32,16,512]{2,1,0:T(8,128)(2,1)}), bf16[32,16,512]{2,1,0:T(8,128)(2,1)S(1)}, u32[]{:S(2)}, u32[]{:S(2)}) async-start(bf16[32,16,512]{2,1,0:T(8,128)(2,1)} %bitcast.5), calls=%async_computation.4 | async-start | bytes 1048576 | tf_op jit(solution)/shard_map/all_to_all | solution.py:210
  142.8 16.8 %all-to-all-done.4.in_ref = bf16[32,16,512]{2,1,0:T(8,128)(2,1)S(1)} async-done(((bf16[32,16,512]{2,1,0:T(8,128)(2,1)}), bf16[32,16,512]{2,1,0:T(8,128)(2,1)S(1)}, u32[]{:S(2)}, u32[]{:S(2)}) %all-to-all-start.4) | async-done | bytes 524320 | tf_op jit(solution)/shard_map/all_to_all | solution.py:210
  159.6 0.1 shard_map.79
  159.6 0.6 copy.8
  (5 shorter events, 0.1 us)
Async XLA Ops:
  0.6 23.8 %collective-permute-start = (bf16[4096,512]{1,0:T(8,128)(2,1)}, bf16[4096,512]{1,0:T(8,128)(2,1)}, u32[]{:S(2)}, u32[]{:S(2)}) collective-permute-start(bf16[4096,512]{1,0:T(8,128)(2,1)} %sw_ref.1), channel_id=1, source_target_pairs={{0,32},{32,0},{64,96},{96,64},{128,160},{160,128},{192,224},{224,1... | collective-permute-start | bytes 12582920 | tf_op jit(solution)/shard_map/ppermute | solution.py:254
  0.7 23.7 %collective-permute-start.1 = (bf16[4096,512]{1,0:T(8,128)(2,1)}, bf16[4096,512]{1,0:T(8,128)(2,1)}, u32[]{:S(2)}, u32[]{:S(2)}) collective-permute-start(bf16[4096,512]{1,0:T(8,128)(2,1)} %tw_ref.1), channel_id=1, source_target_pairs={{0,32},{32,0},{64,96},{96,64},{128,160},{160,128},{192,224},{224,1... | collective-permute-start | bytes 12582920 | tf_op jit(solution)/shard_map/ppermute | solution.py:254
  1.3 0.7 copy-start
  24.4 7.3 %collective-permute-start.2 = (bf16[128,512]{1,0:T(8,128)(2,1)S(1)}, bf16[128,512]{1,0:T(8,128)(2,1)S(1)}, u32[]{:S(2)}, u32[]{:S(2)}) collective-permute-start(bf16[128,512]{1,0:T(8,128)(2,1)S(1)} %get-tuple-element.53.s0), channel_id=1, source_target_pairs={{0,8},{1,9},{2,10},{3,11},{4,12},{5,13},{6,14},{7,15},{8,16},{9,17... | collective-permute-start | bytes 393224 | tf_op jit(solution)/shard_map/ppermute | solution.py:250
  26.1 7.1 %collective-permute-start.3 = (bf16[128,512]{1,0:T(8,128)(2,1)S(1)}, bf16[128,512]{1,0:T(8,128)(2,1)S(1)}, u32[]{:S(2)}, u32[]{:S(2)}) collective-permute-start(bf16[128,512]{1,0:T(8,128)(2,1)S(1)} %get-tuple-element.53.s0), channel_id=1, source_target_pairs={{0,24},{1,25},{2,26},{3,27},{4,28},{5,29},{6,30},{7,31},{8,0},{9,1... | collective-permute-start | bytes 393224 | tf_op jit(solution)/shard_map/ppermute | solution.py:250
  27.7 7.0 %collective-permute-start.4 = (bf16[128,512]{1,0:T(8,128)(2,1)S(1)}, bf16[128,512]{1,0:T(8,128)(2,1)S(1)}, u32[]{:S(2)}, u32[]{:S(2)}) collective-permute-start(bf16[128,512]{1,0:T(8,128)(2,1)S(1)} %get-tuple-element.53.s0), channel_id=1, source_target_pairs={{0,16},{1,17},{2,18},{3,19},{4,20},{5,21},{6,22},{7,23},{8,24},{9,... | collective-permute-start | bytes 393224 | tf_op jit(solution)/shard_map/ppermute | solution.py:250
  29.7 5.6 %collective-permute-start.5 = (bf16[128,512]{1,0:T(8,128)(2,1)S(1)}, bf16[128,512]{1,0:T(8,128)(2,1)S(1)}, u32[]{:S(2)}, u32[]{:S(2)}) collective-permute-start(bf16[128,512]{1,0:T(8,128)(2,1)S(1)} %get-tuple-element.57.t0), channel_id=1, source_target_pairs={{0,64},{32,96},{64,128},{96,160},{128,192},{160,224},{192,0},{224,... | collective-permute-start | bytes 393224 | tf_op jit(solution)/shard_map/ppermute | solution.py:245
  30.2 6.2 %collective-permute-start.6 = (bf16[128,512]{1,0:T(8,128)(2,1)S(1)}, bf16[128,512]{1,0:T(8,128)(2,1)S(1)}, u32[]{:S(2)}, u32[]{:S(2)}) collective-permute-start(bf16[128,512]{1,0:T(8,128)(2,1)S(1)} %get-tuple-element.57.t0), channel_id=1, source_target_pairs={{0,192},{32,224},{64,0},{96,32},{128,64},{160,96},{192,128},{224,1... | collective-permute-start | bytes 393224 | tf_op jit(solution)/shard_map/ppermute | solution.py:245
  31.8 6.5 %collective-permute-start.7 = (bf16[128,512]{1,0:T(8,128)(2,1)S(1)}, bf16[128,512]{1,0:T(8,128)(2,1)S(1)}, u32[]{:S(2)}, u32[]{:S(2)}) collective-permute-start(bf16[128,512]{1,0:T(8,128)(2,1)S(1)} %get-tuple-element.57.t0), channel_id=1, source_target_pairs={{0,128},{32,160},{64,192},{96,224},{128,0},{160,32},{192,64},{224,... | collective-permute-start | bytes 393224 | tf_op jit(solution)/shard_map/ppermute | solution.py:245
  38.9 16.4 %collective-permute-start.10 = (bf16[128,2176]{1,0:T(8,128)(2,1)S(1)}, bf16[128,2176]{1,0:T(8,128)(2,1)S(1)}, u32[]{:S(2)}, u32[]{:S(2)}) collective-permute-start(bf16[128,2176]{1,0:T(8,128)(2,1)S(1)} %get-tuple-element.81.t0), channel_id=1, source_target_pairs={{0,8},{1,9},{2,10},{3,11},{4,12},{5,13},{6,14},{7,15},{8,16},{9,17... | collective-permute-start | bytes 1671176 | tf_op jit(solution)/shard_map/ppermute | solution.py:250
  39.6 15.6 %collective-permute-start.11 = (bf16[128,2176]{1,0:T(8,128)(2,1)S(1)}, bf16[128,2176]{1,0:T(8,128)(2,1)S(1)}, u32[]{:S(2)}, u32[]{:S(2)}) collective-permute-start(bf16[128,2176]{1,0:T(8,128)(2,1)S(1)} %get-tuple-element.81.t0), channel_id=1, source_target_pairs={{0,24},{1,25},{2,26},{3,27},{4,28},{5,29},{6,30},{7,31},{8,0},{9,1... | collective-permute-start | bytes 1671176 | tf_op jit(solution)/shard_map/ppermute | solution.py:250
  42.2 10.0 %collective-permute-start.8 = (bf16[512,512]{1,0:T(8,128)(2,1)S(1)}, bf16[512,512]{1,0:T(8,128)(2,1)S(1)}, u32[]{:S(2)}, u32[]{:S(2)}) collective-permute-start(bf16[512,512]{1,0:T(8,128)(2,1)S(1)} %get-tuple-element.76.s0), channel_id=1, source_target_pairs={{0,64},{32,96},{64,128},{96,160},{128,192},{160,224},{192,0},{224,... | collective-permute-start | bytes 1572872 | tf_op jit(solution)/shard_map/ppermute | solution.py:245
  43.9 11.4 %collective-permute-start.9 = (bf16[512,512]{1,0:T(8,128)(2,1)S(1)}, bf16[512,512]{1,0:T(8,128)(2,1)S(1)}, u32[]{:S(2)}, u32[]{:S(2)}) collective-permute-start(bf16[512,512]{1,0:T(8,128)(2,1)S(1)} %get-tuple-element.76.s0), channel_id=1, source_target_pairs={{0,192},{32,224},{64,0},{96,32},{128,64},{160,96},{192,128},{224,1... | collective-permute-start | bytes 1572872 | tf_op jit(solution)/shard_map/ppermute | solution.py:245
  55.3 11.7 %collective-permute-start.14 = (bf16[64,2176]{1,0:T(8,128)(2,1)S(1)}, bf16[64,2176]{1,0:T(8,128)(2,1)S(1)}, u32[]{:S(2)}, u32[]{:S(2)}) collective-permute-start(bf16[64,2176]{1,0:T(8,128)(2,1)S(1)} %slice.14), channel_id=1, source_target_pairs={{0,8},{1,9},{2,10},{3,11},{4,12},{5,13},{6,14},{7,15},{8,16},{9,17... | collective-permute-start | bytes 835592 | tf_op jit(solution)/shard_map/ppermute | solution.py:250
  55.4 11.6 %collective-permute-start.15 = (bf16[64,2176]{1,0:T(8,128)(2,1)S(1)}, bf16[64,2176]{1,0:T(8,128)(2,1)S(1)}, u32[]{:S(2)}, u32[]{:S(2)}) collective-permute-start(bf16[64,2176]{1,0:T(8,128)(2,1)S(1)} %slice.15), channel_id=1, source_target_pairs={{0,24},{1,25},{2,26},{3,27},{4,28},{5,29},{6,30},{7,31},{8,0},{9,1... | collective-permute-start | bytes 835592 | tf_op jit(solution)/shard_map/ppermute | solution.py:250
  58.7 6.4 %collective-permute-start.12 = (bf16[256,512]{1,0:T(8,128)(2,1)S(1)}, bf16[256,512]{1,0:T(8,128)(2,1)S(1)}, u32[]{:S(2)}, u32[]{:S(2)}) collective-permute-start(bf16[256,512]{1,0:T(8,128)(2,1)S(1)} %slice.12), channel_id=1, source_target_pairs={{0,64},{32,96},{64,128},{96,160},{128,192},{160,224},{192,0},{224,... | collective-permute-start | bytes 786440 | tf_op jit(solution)/shard_map/ppermute | solution.py:245
  59.1 7.8 %collective-permute-start.13 = (bf16[256,512]{1,0:T(8,128)(2,1)S(1)}, bf16[256,512]{1,0:T(8,128)(2,1)S(1)}, u32[]{:S(2)}, u32[]{:S(2)}) collective-permute-start(bf16[256,512]{1,0:T(8,128)(2,1)S(1)} %slice.13), channel_id=1, source_target_pairs={{0,192},{32,224},{64,0},{96,32},{128,64},{160,96},{192,128},{224,1... | collective-permute-start | bytes 786440 | tf_op jit(solution)/shard_map/ppermute | solution.py:245
  69.9 4.2 %collective-permute-start.16 = (f32[2,512,512]{2,1,0:T(8,128)S(1)}, f32[2,512,512]{2,1,0:T(8,128)S(1)}, u32[]{:S(2)}, u32[]{:S(2)}) collective-permute-start(f32[2,512,512]{2,1,0:T(8,128)S(1)} %get-tuple-element.86), channel_id=1, source_target_pairs={{0,32},{32,0},{64,96},{96,64},{128,160},{160,128},{192,224},{224,1... | collective-permute-start | bytes 6291464 | tf_op jit(solution)/shard_map/ppermute | solution.py:254
  101.8 4.2 %collective-permute-start.17 = (bf16[4,512,512]{2,1,0:T(8,128)(2,1)S(1)}, bf16[4,512,512]{2,1,0:T(8,128)(2,1)S(1)}, u32[]{:S(2)}, u32[]{:S(2)}) collective-permute-start(bf16[4,512,512]{2,1,0:T(8,128)(2,1)S(1)} %get-tuple-element.97), channel_id=1, source_target_pairs={{0,32},{32,0},{64,96},{96,64},{128,160},{160,128},{192,224},{224,1... | collective-permute-start | bytes 6291464 | tf_op jit(solution)/shard_map/ppermute | solution.py:254
  138.3 21.3 %all-to-all-start.4 = ((bf16[32,16,512]{2,1,0:T(8,128)(2,1)}), bf16[32,16,512]{2,1,0:T(8,128)(2,1)S(1)}, u32[]{:S(2)}, u32[]{:S(2)}) async-start(bf16[32,16,512]{2,1,0:T(8,128)(2,1)} %bitcast.5), calls=%async_computation.4 | async-start | bytes 1048576 | tf_op jit(solution)/shard_map/all_to_all | solution.py:210

commit v4 on v3

--- a/solution.py
+++ b/solution.py
@@ -211,7 +211,18 @@
     return out.reshape(x.shape)
 
 
-def grad_first_kernel(place_ref, stat_ref, s_ref, d_ref, sw_ref, out_ref, g_ref, loss_ref):
+H = W // 2
+
+
+def terms(place_ref, g, sw_ref, core, second):
+    for step in STEPS:
+        block = ((place_ref[0] + step) % NX * 2 + core) * 2 + second
+        yield dot(g, sw_ref[at_block(block, H)], ((1,), (1,)))
+
+
+def first_for_other_kernel(
+    place_ref, stat_ref, s_ref, d_ref, sw_ref, out_ref, g_ref, turned_ref, loss_ref
+):
     lse_s, mean, lse_t = merge(stat_ref[...])
     loss_ref[...] = jnp.sum(mean - lse_s + lse_t, axis=1, keepdims=True) / N
     row = lax.broadcasted_iota(jnp.int32, (128, N), 0)
@@ -220,16 +231,55 @@
     prob = jnp.exp(s_ref[...] - table[:, 0:1])
     g = (prob * (d_ref[...] - table[:, 1:2])).astype(BF)
     g_ref[...] = g
-    for x in range(NX):
-        columns = sw_ref[at_block(2 * x + 1 - place_ref[1], W)]
-        out_ref[x] = dot(g, columns, ((1,), (1,))).astype(BF)
-
-
-def grad_second_kernel(place_ref, g_ref, in_ref, sw_ref, out_ref):
-    for x in range(NX):
-        columns = sw_ref[at_block(2 * x + place_ref[1], W)]
-        part = dot(g_ref[...], columns, ((1,), (1,)))
-        out_ref[x] = (part + in_ref[x].astype(F32)).astype(BF)
+    for k, part in enumerate(terms(place_ref, g, sw_ref, 1 - place_ref[1], 0)):
+        out_ref[:, k * H : (k + 1) * H] = part.astype(BF)
+    for k, step in enumerate(STEPS):
+        turned_ref[k * NEAR : (k + 1) * NEAR] = g_ref[at_block((place_ref[2] + step) % NY, NEAR)]
+
+
+def second_for_other_kernel(place_ref, g_ref, sw_ref, out_ref):
+    for k, part in enumerate(terms(place_ref, g_ref[...], sw_ref, 1 - place_ref[1], 1)):
+        out_ref[:, k * H : (k + 1) * H] = part.astype(BF)
+
+
+def first_own_kernel(place_ref, g_ref, in_ref, sw_ref, *out_refs):
+    for k, part in enumerate(terms(place_ref, g_ref[...], sw_ref, place_ref[1], 0)):
+        received = in_ref[:, k * H : (k + 1) * H].astype(F32)
+        out_refs[k][...] = (part + received).astype(BF)
+
+
+def second_own_kernel(place_ref, g_ref, in_ref, sw_ref, *out_refs):
+    for k, part in enumerate(terms(place_ref, g_ref[...], sw_ref, place_ref[1], 1)):
+        columns = slice(k * H, (k + 1) * H)
+        total = (part + in_ref[:, columns].astype(F32)).astype(BF)
+        for j, ref in enumerate(out_refs):
+            ref[:, columns] = total[j * NEAR : (j + 1) * NEAR]
+
+
+def total_of(refs):
+    total = refs[0][...].astype(F32)
+    for ref in refs[1:]:
+        total = total + ref[...].astype(F32)
+    return total
+
+
+def sum_first_kernel(place_ref, *refs):
+    buf = refs[-1]
+    buf[...] = total_of(refs[:4])
+    for step, ref in zip(STEPS, refs[4:8]):
+        ref[...] = buf[at_block((place_ref[2] + step) % NY, NEAR)].astype(BF)
+
+
+def sum_second_kernel(*refs):
+    total = total_of(refs[:4]).astype(BF)
+    for k, ref in enumerate(refs[4:]):
+        ref[...] = total[:, k * H : (k + 1) * H]
+
+
+def sum_both_kernel(*refs):
+    out_ref = refs[-1]
+    out_ref[:, :H] = total_of(refs[:4]).astype(BF)
+    out_ref[:, H:] = total_of(refs[4:8]).astype(BF)
 
 
 def sum_kernel(in_ref, out_ref):
@@ -256,6 +306,10 @@
 
 def ring(a, along):
     return [a] + [along(a, -step) for step in STEPS[1:3]] + [along(a, 2)]
+
+
+def to_ring(blocks, along):
+    return [along(a, step) if step else a for step, a in zip(STEPS, blocks)]
 
 
 def per_device(student_hidden, teacher_hidden, student_weight, teacher_weight, source_rows):
@@ -331,22 +385,44 @@
     stats = exchange(stats, "vocab")
     stats = call(merge_kernel, [VM], [((TOK, 8, N // 2), F32)], stats)[0]
     stats = exchange(stats, "tok")
-    for_other, g, loss = call(
-        grad_first_kernel,
+    flops = N * C * D // 2
+    half = ((N, NX * H), BF)
+    first, g, turned, loss = call(
+        first_for_other_kernel,
         [SM] + [VM] * 4,
-        [((NX, N, W), BF), ((N, C), BF), ((1, 1), F32)],
+        [half, ((N, C), BF), ((N, C), BF), ((1, 1), F32)],
         place, stats, s, d, sw,
-        flops=N * C * D,
-    )
-    partial = call(
-        grad_second_kernel,
+        flops=flops,
+    )
+    second = call(
+        second_for_other_kernel, [SM, VM, VM], [half], place, turned, sw, flops=flops
+    )[0]
+    first = call(
+        first_own_kernel,
         [SM] + [VM] * 3,
-        [((NX, N, W), BF)],
-        place, g, to_other_core(for_other), sw,
-        flops=N * C * D,
-    )[0]
-    partial = summed(exchange(partial, "vocab", X_GROUPS))
-    hidden_grad = summed(exchange(partial.reshape(TOK, ROWS, W), "tok"))
+        [((N, H), BF)] * 4,
+        place, g, to_other_core(first), sw,
+        flops=flops,
+    )
+    first = to_ring(first, along_x)
+    second = call(
+        second_own_kernel,
+        [SM] + [VM] * 3,
+        [((NEAR, NX * H), BF)] * 4,
+        place, turned, to_other_core(second), sw,
+        flops=flops,
+    )
+    second = to_ring(second, along_y)
+    blocks = [((NEAR, H), BF)] * 4
+    first = call(
+        sum_first_kernel, [SM] + [VM] * 4, blocks, place, *first,
+        scratch=[pltpu.VMEM((N, H), F32)],
+    )
+    first = to_ring(first, along_y)
+    second = call(sum_second_kernel, [VM] * 4, blocks, *second)
+    second = to_ring(second, along_x)
+    partial = call(sum_both_kernel, [VM] * 8, [((NEAR, W), BF)], *first, *second)[0]
+    hidden_grad = summed(exchange(partial.reshape(NZ, ROWS, W), "tok", Z_GROUPS))
     return loss[0, 0], hidden_grad
 
 

time: 164 us -> 154 us (0.939)
  blocking collectives: 73.9 us -> 44.5 us
  starting transfers between devices: 25.1 us -> 44 us
  Pallas kernels: 19.6 us -> 21.6 us
    all_to_all x4 -> x3, blocking collectives: 73.9 us -> 44.5 us  [exchange(): out = lax.all_to_all(flat, axis, 0, 0, axis_index_groups=groups, tiled=True)]
    ppermute x7 -> x13, starting transfers between devices: 7.82 us -> 17.4 us  [along_x(): return lax.ppermute(a, 'vocab', pairs)]
    ppermute x7 -> x13, waiting for transfers between devices: 1.54 us -> 11 us  [along_y(): return lax.ppermute(a, 'tok', pairs)]
    ppermute x7 -> x13, starting transfers between devices: 12 us -> 20.1 us  [along_y(): return lax.ppermute(a, 'tok', pairs)]
    all_to_all x1, waiting for transfers between devices: 16.8 us -> 9.04 us  [exchange(): out = lax.all_to_all(flat, axis, 0, 0, axis_index_groups=groups, tiled=True)]
    pallas_call x12 -> x16, Pallas kernels: 19.6 us -> 21.6 us  [call(): pl.pallas_call(kernel, in_specs=in_specs, out_specs=[VM] * len(outs), out...]
    ppermute x4 -> x5, waiting for transfers between devices: 5.42 us -> 3.42 us  [to_other_core(): return lax.ppermute(a, 'vocab', [(k, k ^ 1) for k in range(VOC)])]
    ppermute x7 -> x13, waiting for transfers between devices: 15.8 us -> 15.8 us  [along_x(): return lax.ppermute(a, 'vocab', pairs)]
  transfers between devices with their start and end apart: 19 -> 32, of which waited for: 11 -> 16; matrix products, arithmetic and copies ran while one was open for 0% -> 0% of each run, Pallas kernels for 5% -> 8%
where the time goes in v4:
time: 154 us; the launch traced here: 153 us
  blocking collectives  44.5 us (29%)
  starting transfers between devices  44 us (29%)
  waiting for transfers between devices  39.3 us (26%)
  Pallas kernels  21.6 us (14%)
  between operations  1.97 us (1%)
    all_to_all x3, blocking collectives, exchange(): out = lax.all_to_all(flat, axis, 0, 0, axis_index_groups=groups, tiled=True)  44.5 us
    pallas_call x16, Pallas kernels, call(): pl.pallas_call(kernel, in_specs=in_specs, out_specs=[VM] * len(outs), out...  21.6 us
    ppermute x13, starting transfers between devices, along_y(): return lax.ppermute(a, 'tok', pairs)  20.1 us
    ppermute x13, starting transfers between devices, along_x(): return lax.ppermute(a, 'vocab', pairs)  17.4 us
    ppermute x13, waiting for transfers between devices, along_x(): return lax.ppermute(a, 'vocab', pairs)  15.8 us
    ppermute x13, waiting for transfers between devices, along_y(): return lax.ppermute(a, 'tok', pairs)  11 us
    all_to_all x1, waiting for transfers between devices, exchange(): out = lax.all_to_all(flat, axis, 0, 0, axis_index_groups=groups, tiled=True)  9.04 us
    all_to_all x1, starting transfers between devices, exchange(): out = lax.all_to_all(flat, axis, 0, 0, axis_index_groups=groups, tiled=True)  5.23 us
  transfers between devices with their start and end apart: 32, of which 16 were waited for; matrix products, arithmetic and copies ran while one was open for 0% of the time, Pallas kernels for 8%

profile of v4, /device:TPU:6, one launch (start us, length us, event | category | flops | bytes accessed | tf_op | source)
XLA Modules:
  0.0 152.7 jit_solution(13494476837152836972)
XLA Ops:
  0.6 0.1 collective-permute-start
  0.7 0.5 collective-permute-start.1
  1.3 0.7 copy-done
  2.0 1.3 shard_map.68
  3.3 21.1 %all_to_all.30 = bf16[8,16,1152]{2,1,0:T(8,128)(2,1)S(1)} all-to-all(bf16[8,16,1152]{2,1,0:T(8,128)(2,1)S(1)} %shard_map.68), channel_id=1, replica_groups={{0,1,2,3,4,5,6,7},{8,9,10,11,12,13,14,15},{16,17,18,19,20,21,22,23},{24..., dimensions={0} | all-to-all | bytes 589824 | tf_op jit(solution)/shard_map/all_to_all | solution.py:210
  24.4 1.7 %collective-permute-start.2 = (bf16[128,512]{1,0:T(8,128)(2,1)S(1)}, bf16[128,512]{1,0:T(8,128)(2,1)S(1)}, u32[]{:S(2)}, u32[]{:S(2)}) collective-permute-start(bf16[128,512]{1,0:T(8,128)(2,1)S(1)} %get-tuple-element.70.s0), channel_id=1, source_target_pairs={{0,8},{1,9},{2,10},{3,11},{4,12},{5,13},{6,14},{7,15},{8,16},{9,17... | collective-permute-start | bytes 393224 | tf_op jit(solution)/shard_map/ppermute | solution.py:300
  26.1 1.7 %collective-permute-start.3 = (bf16[128,512]{1,0:T(8,128)(2,1)S(1)}, bf16[128,512]{1,0:T(8,128)(2,1)S(1)}, u32[]{:S(2)}, u32[]{:S(2)}) collective-permute-start(bf16[128,512]{1,0:T(8,128)(2,1)S(1)} %get-tuple-element.70.s0), channel_id=1, source_target_pairs={{0,24},{1,25},{2,26},{3,27},{4,28},{5,29},{6,30},{7,31},{8,0},{9,1... | collective-permute-start | bytes 393224 | tf_op jit(solution)/shard_map/ppermute | solution.py:300
  27.7 2.0 %collective-permute-start.4 = (bf16[128,512]{1,0:T(8,128)(2,1)S(1)}, bf16[128,512]{1,0:T(8,128)(2,1)S(1)}, u32[]{:S(2)}, u32[]{:S(2)}) collective-permute-start(bf16[128,512]{1,0:T(8,128)(2,1)S(1)} %get-tuple-element.70.s0), channel_id=1, source_target_pairs={{0,16},{1,17},{2,18},{3,19},{4,20},{5,21},{6,22},{7,23},{8,24},{9,... | collective-permute-start | bytes 393224 | tf_op jit(solution)/shard_map/ppermute | solution.py:300
  29.7 0.5 collective-permute-start.5
  30.2 1.5 %collective-permute-start.6 = (bf16[128,512]{1,0:T(8,128)(2,1)S(1)}, bf16[128,512]{1,0:T(8,128)(2,1)S(1)}, u32[]{:S(2)}, u32[]{:S(2)}) collective-permute-start(bf16[128,512]{1,0:T(8,128)(2,1)S(1)} %get-tuple-element.74.t0), channel_id=1, source_target_pairs={{0,192},{32,224},{64,0},{96,32},{128,64},{160,96},{192,128},{224,1... | collective-permute-start | bytes 393224 | tf_op jit(solution)/shard_map/ppermute | solution.py:295
  31.8 1.4 collective-permute-start.7
  33.2 1.5 collective-permute-done.4.s3
  34.7 0.6 collective-permute-done.5.t1
  35.3 1.1 collective-permute-done.6.t2
  36.4 1.8 %collective-permute-done.7.t3 = bf16[128,512]{1,0:T(8,128)(2,1)S(1)} collective-permute-done((bf16[128,512]{1,0:T(8,128)(2,1)S(1)}, bf16[128,512]{1,0:T(8,128)(2,1)S(1)}, u32[]{:S(2)}, u32[]{:S(2)}) %collective-permute-start.7) | collective-permute-done | bytes 131104 | tf_op jit(solution)/shard_map/ppermute | solution.py:295
  38.2 0.6 shard_map.70
  38.9 0.8 collective-permute-start.10
  39.6 2.6 %collective-permute-start.11 = (bf16[128,2176]{1,0:T(8,128)(2,1)S(1)}, bf16[128,2176]{1,0:T(8,128)(2,1)S(1)}, u32[]{:S(2)}, u32[]{:S(2)}) collective-permute-start(bf16[128,2176]{1,0:T(8,128)(2,1)S(1)} %get-tuple-element.98.t0), channel_id=1, source_target_pairs={{0,24},{1,25},{2,26},{3,27},{4,28},{5,29},{6,30},{7,31},{8,0},{9,1... | collective-permute-start | bytes 1671176 | tf_op jit(solution)/shard_map/ppermute | solution.py:300
  42.2 1.7 %collective-permute-start.8 = (bf16[512,512]{1,0:T(8,128)(2,1)S(1)}, bf16[512,512]{1,0:T(8,128)(2,1)S(1)}, u32[]{:S(2)}, u32[]{:S(2)}) collective-permute-start(bf16[512,512]{1,0:T(8,128)(2,1)S(1)} %get-tuple-element.93.s0), channel_id=1, source_target_pairs={{0,64},{32,96},{64,128},{96,160},{128,192},{160,224},{192,0},{224,... | collective-permute-start | bytes 1572872 | tf_op jit(solution)/shard_map/ppermute | solution.py:295
  43.9 0.3 collective-permute-start.9
  44.2 4.6 %shard_map.71 = (bf16[4096,512]{1,0:T(8,128)(2,1)S(1)}, bf16[2048,512]{1,0:T(8,128)(2,1)S(1)}, bf16[2048,512]{1,0:T(8,128)(2,1)S(1)}, bf16[2048,512]{1,0:T(8,128)(2,1)S(1)}) custom-call(s32[3]{0:T(128)S(1)} %pad_add_fusion.place_ref, bf16[4096,512]{1,0:T(8,128)(2,1)} %sw_ref.1, bf16[4096,512]{1,0:T(8,128)(2,1)} %tw_ref.1, ...), custom_call_target="tpu_custom_call" | custom-call | tf_op jit(solution)/shard_map/pallas_call | solution.py:51
  48.8 3.4 %collective-permute-done.8.s1 = bf16[512,512]{1,0:T(8,128)(2,1)S(1)} collective-permute-done((bf16[512,512]{1,0:T(8,128)(2,1)S(1)}, bf16[512,512]{1,0:T(8,128)(2,1)S(1)}, u32[]{:S(2)}, u32[]{:S(2)}) %collective-permute-start.8) | collective-permute-done | bytes 524320 | tf_op jit(solution)/shard_map/ppermute | solution.py:295
  52.2 3.0 %collective-permute-done.9.s2 = bf16[512,512]{1,0:T(8,128)(2,1)S(1)} collective-permute-done((bf16[512,512]{1,0:T(8,128)(2,1)S(1)}, bf16[512,512]{1,0:T(8,128)(2,1)S(1)}, u32[]{:S(2)}, u32[]{:S(2)}) %collective-permute-start.9) | collective-permute-done | bytes 524320 | tf_op jit(solution)/shard_map/ppermute | solution.py:295
  55.4 3.3 %collective-permute-start.15 = (bf16[64,2176]{1,0:T(8,128)(2,1)S(1)}, bf16[64,2176]{1,0:T(8,128)(2,1)S(1)}, u32[]{:S(2)}, u32[]{:S(2)}) collective-permute-start(bf16[64,2176]{1,0:T(8,128)(2,1)S(1)} %slice.15), channel_id=1, source_target_pairs={{0,24},{1,25},{2,26},{3,27},{4,28},{5,29},{6,30},{7,31},{8,0},{9,1... | collective-permute-start | bytes 835592 | tf_op jit(solution)/shard_map/ppermute | solution.py:300
  58.7 0.4 collective-permute-start.12
  59.1 2.0 %collective-permute-start.13 = (bf16[256,512]{1,0:T(8,128)(2,1)S(1)}, bf16[256,512]{1,0:T(8,128)(2,1)S(1)}, u32[]{:S(2)}, u32[]{:S(2)}) collective-permute-start(bf16[256,512]{1,0:T(8,128)(2,1)S(1)} %slice.13), channel_id=1, source_target_pairs={{0,192},{32,224},{64,0},{96,32},{128,64},{160,96},{192,128},{224,1... | collective-permute-start | bytes 786440 | tf_op jit(solution)/shard_map/ppermute | solution.py:295
  61.1 4.1 %collective-permute-done.12.s3 = bf16[256,512]{1,0:T(8,128)(2,1)S(1)} collective-permute-done((bf16[256,512]{1,0:T(8,128)(2,1)S(1)}, bf16[256,512]{1,0:T(8,128)(2,1)S(1)}, u32[]{:S(2)}, u32[]{:S(2)}) %collective-permute-start.12) | collective-permute-done | bytes 262176 | tf_op jit(solution)/shard_map/ppermute | solution.py:295
  65.1 1.8 %collective-permute-done.13.s4 = bf16[256,512]{1,0:T(8,128)(2,1)S(1)} collective-permute-done((bf16[256,512]{1,0:T(8,128)(2,1)S(1)}, bf16[256,512]{1,0:T(8,128)(2,1)S(1)}, u32[]{:S(2)}, u32[]{:S(2)}) %collective-permute-start.13) | collective-permute-done | bytes 262176 | tf_op jit(solution)/shard_map/ppermute | solution.py:295
  66.9 3.0 %shard_map.72 = (f32[2,512,512]{2,1,0:T(8,128)S(1)}, bf16[512,2176]{1,0:T(8,128)(2,1)S(1)}) custom-call(s32[3]{0:T(128)S(1)} %pad_add_fusion.place_ref, bf16[2048,512]{1,0:T(8,128)(2,1)S(1)} %get-tuple-element.87.sw_ref, bf16[2048,512]{1,0:T(8,128)(2,1)S(1)} %get-tuple-element.88.tw_ref, bf16[512,512]{1,0:T(8,128)(2,1)S(1)} %get-tuple-element.93.s0, ...), custom_call_target="tpu_custom_call" | custom-call | flops 2147483648 | tf_op jit(solution)/shard_map/pallas_call | solution.py:51
  70.0 2.9 %shard_map.73.own_ref = f32[2,512,512]{2,1,0:T(8,128)S(1)} custom-call(s32[3]{0:T(128)S(1)} %pad_add_fusion.place_ref, bf16[4096,512]{1,0:T(8,128)(2,1)S(1)} %get-tuple-element.104.sw_ref, bf16[2048,512]{1,0:T(8,128)(2,1)S(1)} %get-tuple-element.105.tw_ref, bf16[512,512]{1,0:T(8,128)(2,1)S(1)} %get-tuple-element.93.s0, ...), custom_call_target="tpu_custom_call" | custom-call | flops 2147483648 | tf_op jit(solution)/shard_map/pallas_call | solution.py:51
  72.9 1.3 collective-permute-done.16.other_ref
  74.1 1.7 %shard_map.74 = (f32[512,512]{1,0:T(8,128)S(1)}, f32[512,512]{1,0:T(8,128)S(1)}, f32[8,8,256]{2,1,0:T(8,128)S(1)}) custom-call(f32[2,512,512]{2,1,0:T(8,128)S(1)} %shard_map.73.own_ref, f32[2,512,512]{2,1,0:T(8,128)S(1)} %collective-permute-done.16.other_ref, bf16[512,2176]{1,0:T(8,128)(2,1)S(1)} %get-tuple-element.106.t_all.digits_ref), custom_call_target="tpu_custom_call" | custom-call | flops 805306368 | tf_op jit(solution)/shard_map/pallas_call | solution.py:51
  75.9 7.9 %all_to_all.31.in_ref = f32[8,8,256]{2,1,0:T(8,128)S(1)} all-to-all(f32[8,8,256]{2,1,0:T(8,128)S(1)} %get-tuple-element.109), channel_id=1, replica_groups=mesh['vocab'=8,'tok'=32] {'vocab'}, dimensions={0} | all-to-all | bytes 131072 | tf_op jit(solution)/shard_map/all_to_all | solution.py:210
  83.7 0.1 shard_map.75
  83.9 15.5 %all_to_all.32.stat_ref = f32[32,8,256]{2,1,0:T(8,128)S(1)} all-to-all(f32[32,8,256]{2,1,0:T(8,128)S(1)} %shard_map.75), channel_id=1, replica_groups=mesh['vocab'=8,'tok'=32] {'tok'}, dimensions={0} | all-to-all | bytes 524288 | tf_op jit(solution)/shard_map/all_to_all | solution.py:210
  99.4 1.9 %shard_map.76 = (bf16[512,1024]{1,0:T(8,128)(2,1)S(1)}, bf16[512,512]{1,0:T(8,128)(2,1)S(1)}, bf16[512,512]{1,0:T(8,128)(2,1)S(1)}, f32[1,1]{1,0:T(1,128)S(1)}) custom-call(s32[3]{0:T(128)S(1)} %pad_add_fusion.place_ref, f32[32,8,256]{2,1,0:T(8,128)S(1)} %all_to_all.32.stat_ref, f32[512,512]{1,0:T(8,128)S(1)} %get-tuple-element.110.s_ref, ...), custom_call_target="tpu_custom_call" | custom-call | flops 536870912 | tf_op jit(solution)/shard_map/pallas_call | solution.py:51
  101.2 1.3 shard_map.79
  102.6 0.5 collective-permute-start.17
  103.1 2.1 %collective-permute-done.24.in_ref = bf16[512,1024]{1,0:T(8,128)(2,1)S(1)} collective-permute-done((bf16[512,1024]{1,0:T(8,128)(2,1)S(1)}, bf16[512,1024]{1,0:T(8,128)(2,1)S(1)}, u32[]{:S(2)}, u32[]{:S(2)}) %collective-permute-start.24) | collective-permute-done | bytes 1048608 | tf_op jit(solution)/shard_map/ppermute | solution.py:304
  105.3 1.3 shard_map.80
  106.6 1.2 collective-permute-start.25
  107.8 0.9 collective-permute-start.26
  108.7 1.6 %collective-permute-start.27 = (bf16[128,1024]{1,0:T(8,128)(2,1)S(1)}, bf16[128,1024]{1,0:T(8,128)(2,1)S(1)}, u32[]{:S(2)}, u32[]{:S(2)}) collective-permute-start(bf16[128,1024]{1,0:T(8,128)(2,1)S(1)} %get-tuple-element.127), channel_id=1, source_target_pairs={{0,16},{1,17},{2,18},{3,19},{4,20},{5,21},{6,22},{7,23},{8,24},{9,... | collective-permute-start | bytes 786440 | tf_op jit(solution)/shard_map/ppermute | solution.py:300
  110.3 1.3 shard_map.77
  111.6 0.5 collective-permute-start.18
  112.1 2.8 %collective-permute-start.19 = (bf16[512,256]{1,0:T(8,128)(2,1)S(1)}, bf16[512,256]{1,0:T(8,128)(2,1)S(1)}, u32[]{:S(2)}, u32[]{:S(2)}) collective-permute-start(bf16[512,256]{1,0:T(8,128)(2,1)S(1)} %get-tuple-element.117), channel_id=1, source_target_pairs={{0,64},{32,96},{64,128},{96,160},{128,192},{160,224},{192,0},{224,... | collective-permute-start | bytes 786440 | tf_op jit(solution)/shard_map/ppermute | solution.py:295
  114.9 0.9 collective-permute-done.25.refs_1_
  115.8 2.1 %collective-permute-start.20 = (bf16[512,256]{1,0:T(8,128)(2,1)S(1)}, bf16[512,256]{1,0:T(8,128)(2,1)S(1)}, u32[]{:S(2)}, u32[]{:S(2)}) collective-permute-start(bf16[512,256]{1,0:T(8,128)(2,1)S(1)} %get-tuple-element.118), channel_id=1, source_target_pairs={{0,128},{32,160},{64,192},{96,224},{128,0},{160,32},{192,64},{224,... | collective-permute-start | bytes 786440 | tf_op jit(solution)/shard_map/ppermute | solution.py:295
  117.9 4.8 %collective-permute-done.26.refs_2_ = bf16[128,1024]{1,0:T(8,128)(2,1)S(1)} collective-permute-done((bf16[128,1024]{1,0:T(8,128)(2,1)S(1)}, bf16[128,1024]{1,0:T(8,128)(2,1)S(1)}, u32[]{:S(2)}, u32[]{:S(2)}) %collective-permute-start.26) | collective-permute-done | bytes 262176 | tf_op jit(solution)/shard_map/ppermute | solution.py:300
  122.7 0.1 shard_map.81
  122.8 0.5 collective-permute-start.28
  123.3 2.8 %collective-permute-start.29 = (bf16[128,256]{1,0:T(8,128)(2,1)S(1)}, bf16[128,256]{1,0:T(8,128)(2,1)S(1)}, u32[]{:S(2)}, u32[]{:S(2)}) collective-permute-start(bf16[128,256]{1,0:T(8,128)(2,1)S(1)} %get-tuple-element.130), channel_id=1, source_target_pairs={{0,64},{32,96},{64,128},{96,160},{128,192},{160,224},{192,0},{224,... | collective-permute-start | bytes 196616 | tf_op jit(solution)/shard_map/ppermute | solution.py:295
  126.1 0.9 collective-permute-start.30
  127.0 0.8 shard_map.78
  127.8 1.8 %collective-permute-start.21 = (bf16[128,256]{1,0:T(8,128)(2,1)S(1)}, bf16[128,256]{1,0:T(8,128)(2,1)S(1)}, u32[]{:S(2)}, u32[]{:S(2)}) collective-permute-start(bf16[128,256]{1,0:T(8,128)(2,1)S(1)} %get-tuple-element.120), channel_id=1, source_target_pairs={{0,24},{1,25},{2,26},{3,27},{4,28},{5,29},{6,30},{7,31},{8,0},{9,1... | collective-permute-start | bytes 196616 | tf_op jit(solution)/shard_map/ppermute | solution.py:300
  129.6 0.6 collective-permute-start.22
  130.2 2.0 %collective-permute-start.23 = (bf16[128,256]{1,0:T(8,128)(2,1)S(1)}, bf16[128,256]{1,0:T(8,128)(2,1)S(1)}, u32[]{:S(2)}, u32[]{:S(2)}) collective-permute-start(bf16[128,256]{1,0:T(8,128)(2,1)S(1)} %get-tuple-element.122), channel_id=1, source_target_pairs={{0,16},{1,17},{2,18},{3,19},{4,20},{5,21},{6,22},{7,23},{8,24},{9,... | collective-permute-start | bytes 196616 | tf_op jit(solution)/shard_map/ppermute | solution.py:300
  132.2 0.7 collective-permute-done.21.refs_1_
  132.9 2.2 %collective-permute-done.22.refs_2_ = bf16[128,256]{1,0:T(8,128)(2,1)S(1)} collective-permute-done((bf16[128,256]{1,0:T(8,128)(2,1)S(1)}, bf16[128,256]{1,0:T(8,128)(2,1)S(1)}, u32[]{:S(2)}, u32[]{:S(2)}) %collective-permute-start.22) | collective-permute-done | bytes 65568 | tf_op jit(solution)/shard_map/ppermute | solution.py:300
  135.0 0.9 collective-permute-done.23.refs_3_
  136.0 0.7 shard_map.82
  136.7 5.2 %all-to-all-start.3 = ((bf16[8,16,512]{2,1,0:T(8,128)(2,1)}), bf16[8,16,512]{2,1,0:T(8,128)(2,1)S(1)}, u32[]{:S(2)}, u32[]{:S(2)}) async-start(bf16[8,16,512]{2,1,0:T(8,128)(2,1)} %bitcast.5), calls=%async_computation.3 | async-start | bytes 262144 | tf_op jit(solution)/shard_map/all_to_all | solution.py:210
  141.9 9.0 %all-to-all-done.3.in_ref = bf16[8,16,512]{2,1,0:T(8,128)(2,1)S(1)} async-done(((bf16[8,16,512]{2,1,0:T(8,128)(2,1)}), bf16[8,16,512]{2,1,0:T(8,128)(2,1)S(1)}, u32[]{:S(2)}, u32[]{:S(2)}) %all-to-all-start.3) | async-done | bytes 131104 | tf_op jit(solution)/shard_map/all_to_all | solution.py:210
  151.0 0.6 copy.8
  (27 shorter events, 0.5 us)
Async XLA Ops:
  0.6 23.8 %collective-permute-start = (bf16[4096,512]{1,0:T(8,128)(2,1)}, bf16[4096,512]{1,0:T(8,128)(2,1)}, u32[]{:S(2)}, u32[]{:S(2)}) collective-permute-start(bf16[4096,512]{1,0:T(8,128)(2,1)} %sw_ref.1), channel_id=1, source_target_pairs={{0,32},{32,0},{64,96},{96,64},{128,160},{160,128},{192,224},{224,1... | collective-permute-start | bytes 12582920 | tf_op jit(solution)/shard_map/ppermute | solution.py:304
  0.7 23.7 %collective-permute-start.1 = (bf16[4096,512]{1,0:T(8,128)(2,1)}, bf16[4096,512]{1,0:T(8,128)(2,1)}, u32[]{:S(2)}, u32[]{:S(2)}) collective-permute-start(bf16[4096,512]{1,0:T(8,128)(2,1)} %tw_ref.1), channel_id=1, source_target_pairs={{0,32},{32,0},{64,96},{96,64},{128,160},{160,128},{192,224},{224,1... | collective-permute-start | bytes 12582920 | tf_op jit(solution)/shard_map/ppermute | solution.py:304
  1.3 0.7 copy-start
  24.4 7.3 %collective-permute-start.2 = (bf16[128,512]{1,0:T(8,128)(2,1)S(1)}, bf16[128,512]{1,0:T(8,128)(2,1)S(1)}, u32[]{:S(2)}, u32[]{:S(2)}) collective-permute-start(bf16[128,512]{1,0:T(8,128)(2,1)S(1)} %get-tuple-element.70.s0), channel_id=1, source_target_pairs={{0,8},{1,9},{2,10},{3,11},{4,12},{5,13},{6,14},{7,15},{8,16},{9,17... | collective-permute-start | bytes 393224 | tf_op jit(solution)/shard_map/ppermute | solution.py:300
  26.1 7.1 %collective-permute-start.3 = (bf16[128,512]{1,0:T(8,128)(2,1)S(1)}, bf16[128,512]{1,0:T(8,128)(2,1)S(1)}, u32[]{:S(2)}, u32[]{:S(2)}) collective-permute-start(bf16[128,512]{1,0:T(8,128)(2,1)S(1)} %get-tuple-element.70.s0), channel_id=1, source_target_pairs={{0,24},{1,25},{2,26},{3,27},{4,28},{5,29},{6,30},{7,31},{8,0},{9,1... | collective-permute-start | bytes 393224 | tf_op jit(solution)/shard_map/ppermute | solution.py:300
  27.7 7.0 %collective-permute-start.4 = (bf16[128,512]{1,0:T(8,128)(2,1)S(1)}, bf16[128,512]{1,0:T(8,128)(2,1)S(1)}, u32[]{:S(2)}, u32[]{:S(2)}) collective-permute-start(bf16[128,512]{1,0:T(8,128)(2,1)S(1)} %get-tuple-element.70.s0), channel_id=1, source_target_pairs={{0,16},{1,17},{2,18},{3,19},{4,20},{5,21},{6,22},{7,23},{8,24},{9,... | collective-permute-start | bytes 393224 | tf_op jit(solution)/shard_map/ppermute | solution.py:300
  29.7 5.6 %collective-permute-start.5 = (bf16[128,512]{1,0:T(8,128)(2,1)S(1)}, bf16[128,512]{1,0:T(8,128)(2,1)S(1)}, u32[]{:S(2)}, u32[]{:S(2)}) collective-permute-start(bf16[128,512]{1,0:T(8,128)(2,1)S(1)} %get-tuple-element.74.t0), channel_id=1, source_target_pairs={{0,64},{32,96},{64,128},{96,160},{128,192},{160,224},{192,0},{224,... | collective-permute-start | bytes 393224 | tf_op jit(solution)/shard_map/ppermute | solution.py:295
  30.2 6.2 %collective-permute-start.6 = (bf16[128,512]{1,0:T(8,128)(2,1)S(1)}, bf16[128,512]{1,0:T(8,128)(2,1)S(1)}, u32[]{:S(2)}, u32[]{:S(2)}) collective-permute-start(bf16[128,512]{1,0:T(8,128)(2,1)S(1)} %get-tuple-element.74.t0), channel_id=1, source_target_pairs={{0,192},{32,224},{64,0},{96,32},{128,64},{160,96},{192,128},{224,1... | collective-permute-start | bytes 393224 | tf_op jit(solution)/shard_map/ppermute | solution.py:295
  31.8 6.5 %collective-permute-start.7 = (bf16[128,512]{1,0:T(8,128)(2,1)S(1)}, bf16[128,512]{1,0:T(8,128)(2,1)S(1)}, u32[]{:S(2)}, u32[]{:S(2)}) collective-permute-start(bf16[128,512]{1,0:T(8,128)(2,1)S(1)} %get-tuple-element.74.t0), channel_id=1, source_target_pairs={{0,128},{32,160},{64,192},{96,224},{128,0},{160,32},{192,64},{224,... | collective-permute-start | bytes 393224 | tf_op jit(solution)/shard_map/ppermute | solution.py:295
  38.9 16.4 %collective-permute-start.10 = (bf16[128,2176]{1,0:T(8,128)(2,1)S(1)}, bf16[128,2176]{1,0:T(8,128)(2,1)S(1)}, u32[]{:S(2)}, u32[]{:S(2)}) collective-permute-start(bf16[128,2176]{1,0:T(8,128)(2,1)S(1)} %get-tuple-element.98.t0), channel_id=1, source_target_pairs={{0,8},{1,9},{2,10},{3,11},{4,12},{5,13},{6,14},{7,15},{8,16},{9,17... | collective-permute-start | bytes 1671176 | tf_op jit(solution)/shard_map/ppermute | solution.py:300
  39.6 15.6 %collective-permute-start.11 = (bf16[128,2176]{1,0:T(8,128)(2,1)S(1)}, bf16[128,2176]{1,0:T(8,128)(2,1)S(1)}, u32[]{:S(2)}, u32[]{:S(2)}) collective-permute-start(bf16[128,2176]{1,0:T(8,128)(2,1)S(1)} %get-tuple-element.98.t0), channel_id=1, source_target_pairs={{0,24},{1,25},{2,26},{3,27},{4,28},{5,29},{6,30},{7,31},{8,0},{9,1... | collective-permute-start | bytes 1671176 | tf_op jit(solution)/shard_map/ppermute | solution.py:300
  42.2 10.0 %collective-permute-start.8 = (bf16[512,512]{1,0:T(8,128)(2,1)S(1)}, bf16[512,512]{1,0:T(8,128)(2,1)S(1)}, u32[]{:S(2)}, u32[]{:S(2)}) collective-permute-start(bf16[512,512]{1,0:T(8,128)(2,1)S(1)} %get-tuple-element.93.s0), channel_id=1, source_target_pairs={{0,64},{32,96},{64,128},{96,160},{128,192},{160,224},{192,0},{224,... | collective-permute-start | bytes 1572872 | tf_op jit(solution)/shard_map/ppermute | solution.py:295
  43.9 11.4 %collective-permute-start.9 = (bf16[512,512]{1,0:T(8,128)(2,1)S(1)}, bf16[512,512]{1,0:T(8,128)(2,1)S(1)}, u32[]{:S(2)}, u32[]{:S(2)}) collective-permute-start(bf16[512,512]{1,0:T(8,128)(2,1)S(1)} %get-tuple-element.93.s0), channel_id=1, source_target_pairs={{0,192},{32,224},{64,0},{96,32},{128,64},{160,96},{192,128},{224,1... | collective-permute-start | bytes 1572872 | tf_op jit(solution)/shard_map/ppermute | solution.py:295
  55.3 11.7 %collective-permute-start.14 = (bf16[64,2176]{1,0:T(8,128)(2,1)S(1)}, bf16[64,2176]{1,0:T(8,128)(2,1)S(1)}, u32[]{:S(2)}, u32[]{:S(2)}) collective-permute-start(bf16[64,2176]{1,0:T(8,128)(2,1)S(1)} %slice.14), channel_id=1, source_target_pairs={{0,8},{1,9},{2,10},{3,11},{4,12},{5,13},{6,14},{7,15},{8,16},{9,17... | collective-permute-start | bytes 835592 | tf_op jit(solution)/shard_map/ppermute | solution.py:300
  55.4 11.6 %collective-permute-start.15 = (bf16[64,2176]{1,0:T(8,128)(2,1)S(1)}, bf16[64,2176]{1,0:T(8,128)(2,1)S(1)}, u32[]{:S(2)}, u32[]{:S(2)}) collective-permute-start(bf16[64,2176]{1,0:T(8,128)(2,1)S(1)} %slice.15), channel_id=1, source_target_pairs={{0,24},{1,25},{2,26},{3,27},{4,28},{5,29},{6,30},{7,31},{8,0},{9,1... | collective-permute-start | bytes 835592 | tf_op jit(solution)/shard_map/ppermute | solution.py:300
  58.7 6.4 %collective-permute-start.12 = (bf16[256,512]{1,0:T(8,128)(2,1)S(1)}, bf16[256,512]{1,0:T(8,128)(2,1)S(1)}, u32[]{:S(2)}, u32[]{:S(2)}) collective-permute-start(bf16[256,512]{1,0:T(8,128)(2,1)S(1)} %slice.12), channel_id=1, source_target_pairs={{0,64},{32,96},{64,128},{96,160},{128,192},{160,224},{192,0},{224,... | collective-permute-start | bytes 786440 | tf_op jit(solution)/shard_map/ppermute | solution.py:295
  59.1 7.8 %collective-permute-start.13 = (bf16[256,512]{1,0:T(8,128)(2,1)S(1)}, bf16[256,512]{1,0:T(8,128)(2,1)S(1)}, u32[]{:S(2)}, u32[]{:S(2)}) collective-permute-start(bf16[256,512]{1,0:T(8,128)(2,1)S(1)} %slice.13), channel_id=1, source_target_pairs={{0,192},{32,224},{64,0},{96,32},{128,64},{160,96},{192,128},{224,1... | collective-permute-start | bytes 786440 | tf_op jit(solution)/shard_map/ppermute | solution.py:295
  69.9 4.2 %collective-permute-start.16 = (f32[2,512,512]{2,1,0:T(8,128)S(1)}, f32[2,512,512]{2,1,0:T(8,128)S(1)}, u32[]{:S(2)}, u32[]{:S(2)}) collective-permute-start(f32[2,512,512]{2,1,0:T(8,128)S(1)} %get-tuple-element.103), channel_id=1, source_target_pairs={{0,32},{32,0},{64,96},{96,64},{128,160},{160,128},{192,224},{224,1... | collective-permute-start | bytes 6291464 | tf_op jit(solution)/shard_map/ppermute | solution.py:304
  102.5 2.7 %collective-permute-start.24 = (bf16[512,1024]{1,0:T(8,128)(2,1)S(1)}, bf16[512,1024]{1,0:T(8,128)(2,1)S(1)}, u32[]{:S(2)}, u32[]{:S(2)}) collective-permute-start(bf16[512,1024]{1,0:T(8,128)(2,1)S(1)} %shard_map.79), channel_id=1, source_target_pairs={{0,32},{32,0},{64,96},{96,64},{128,160},{160,128},{192,224},{224,1... | collective-permute-start | bytes 3145736 | tf_op jit(solution)/shard_map/ppermute | solution.py:304
  102.6 7.6 %collective-permute-start.17 = (bf16[512,1024]{1,0:T(8,128)(2,1)S(1)}, bf16[512,1024]{1,0:T(8,128)(2,1)S(1)}, u32[]{:S(2)}, u32[]{:S(2)}) collective-permute-start(bf16[512,1024]{1,0:T(8,128)(2,1)S(1)} %get-tuple-element.114), channel_id=1, source_target_pairs={{0,32},{32,0},{64,96},{96,64},{128,160},{160,128},{192,224},{224,1... | collective-permute-start | bytes 3145736 | tf_op jit(solution)/shard_map/ppermute | solution.py:304
  106.6 9.2 %collective-permute-start.25 = (bf16[128,1024]{1,0:T(8,128)(2,1)S(1)}, bf16[128,1024]{1,0:T(8,128)(2,1)S(1)}, u32[]{:S(2)}, u32[]{:S(2)}) collective-permute-start(bf16[128,1024]{1,0:T(8,128)(2,1)S(1)} %get-tuple-element.125), channel_id=1, source_target_pairs={{0,24},{1,25},{2,26},{3,27},{4,28},{5,29},{6,30},{7,31},{8,0},{9,1... | collective-permute-start | bytes 786440 | tf_op jit(solution)/shard_map/ppermute | solution.py:300
  107.8 14.9 %collective-permute-start.26 = (bf16[128,1024]{1,0:T(8,128)(2,1)S(1)}, bf16[128,1024]{1,0:T(8,128)(2,1)S(1)}, u32[]{:S(2)}, u32[]{:S(2)}) collective-permute-start(bf16[128,1024]{1,0:T(8,128)(2,1)S(1)} %get-tuple-element.126), channel_id=1, source_target_pairs={{0,8},{1,9},{2,10},{3,11},{4,12},{5,13},{6,14},{7,15},{8,16},{9,17... | collective-permute-start | bytes 786440 | tf_op jit(solution)/shard_map/ppermute | solution.py:300
  108.7 14.0 %collective-permute-start.27 = (bf16[128,1024]{1,0:T(8,128)(2,1)S(1)}, bf16[128,1024]{1,0:T(8,128)(2,1)S(1)}, u32[]{:S(2)}, u32[]{:S(2)}) collective-permute-start(bf16[128,1024]{1,0:T(8,128)(2,1)S(1)} %get-tuple-element.127), channel_id=1, source_target_pairs={{0,16},{1,17},{2,18},{3,19},{4,20},{5,21},{6,22},{7,23},{8,24},{9,... | collective-permute-start | bytes 786440 | tf_op jit(solution)/shard_map/ppermute | solution.py:300
  111.6 14.5 %collective-permute-start.18 = (bf16[512,256]{1,0:T(8,128)(2,1)S(1)}, bf16[512,256]{1,0:T(8,128)(2,1)S(1)}, u32[]{:S(2)}, u32[]{:S(2)}) collective-permute-start(bf16[512,256]{1,0:T(8,128)(2,1)S(1)} %get-tuple-element.116), channel_id=1, source_target_pairs={{0,192},{32,224},{64,0},{96,32},{128,64},{160,96},{192,128},{224,1... | collective-permute-start | bytes 786440 | tf_op jit(solution)/shard_map/ppermute | solution.py:295
  112.1 14.9 %collective-permute-start.19 = (bf16[512,256]{1,0:T(8,128)(2,1)S(1)}, bf16[512,256]{1,0:T(8,128)(2,1)S(1)}, u32[]{:S(2)}, u32[]{:S(2)}) collective-permute-start(bf16[512,256]{1,0:T(8,128)(2,1)S(1)} %get-tuple-element.117), channel_id=1, source_target_pairs={{0,64},{32,96},{64,128},{96,160},{128,192},{160,224},{192,0},{224,... | collective-permute-start | bytes 786440 | tf_op jit(solution)/shard_map/ppermute | solution.py:295
  115.8 11.2 %collective-permute-start.20 = (bf16[512,256]{1,0:T(8,128)(2,1)S(1)}, bf16[512,256]{1,0:T(8,128)(2,1)S(1)}, u32[]{:S(2)}, u32[]{:S(2)}) collective-permute-start(bf16[512,256]{1,0:T(8,128)(2,1)S(1)} %get-tuple-element.118), channel_id=1, source_target_pairs={{0,128},{32,160},{64,192},{96,224},{128,0},{160,32},{192,64},{224,... | collective-permute-start | bytes 786440 | tf_op jit(solution)/shard_map/ppermute | solution.py:295
  122.8 7.4 %collective-permute-start.28 = (bf16[128,256]{1,0:T(8,128)(2,1)S(1)}, bf16[128,256]{1,0:T(8,128)(2,1)S(1)}, u32[]{:S(2)}, u32[]{:S(2)}) collective-permute-start(bf16[128,256]{1,0:T(8,128)(2,1)S(1)} %get-tuple-element.129), channel_id=1, source_target_pairs={{0,192},{32,224},{64,0},{96,32},{128,64},{160,96},{192,128},{224,1... | collective-permute-start | bytes 196616 | tf_op jit(solution)/shard_map/ppermute | solution.py:295
  123.3 8.9 %collective-permute-start.29 = (bf16[128,256]{1,0:T(8,128)(2,1)S(1)}, bf16[128,256]{1,0:T(8,128)(2,1)S(1)}, u32[]{:S(2)}, u32[]{:S(2)}) collective-permute-start(bf16[128,256]{1,0:T(8,128)(2,1)S(1)} %get-tuple-element.130), channel_id=1, source_target_pairs={{0,64},{32,96},{64,128},{96,160},{128,192},{160,224},{192,0},{224,... | collective-permute-start | bytes 196616 | tf_op jit(solution)/shard_map/ppermute | solution.py:295
  126.1 6.0 %collective-permute-start.30 = (bf16[128,256]{1,0:T(8,128)(2,1)S(1)}, bf16[128,256]{1,0:T(8,128)(2,1)S(1)}, u32[]{:S(2)}, u32[]{:S(2)}) collective-permute-start(bf16[128,256]{1,0:T(8,128)(2,1)S(1)} %get-tuple-element.131), channel_id=1, source_target_pairs={{0,128},{32,160},{64,192},{96,224},{128,0},{160,32},{192,64},{224,... | collective-permute-start | bytes 196616 | tf_op jit(solution)/shard_map/ppermute | solution.py:295
  127.8 5.1 %collective-permute-start.21 = (bf16[128,256]{1,0:T(8,128)(2,1)S(1)}, bf16[128,256]{1,0:T(8,128)(2,1)S(1)}, u32[]{:S(2)}, u32[]{:S(2)}) collective-permute-start(bf16[128,256]{1,0:T(8,128)(2,1)S(1)} %get-tuple-element.120), channel_id=1, source_target_pairs={{0,24},{1,25},{2,26},{3,27},{4,28},{5,29},{6,30},{7,31},{8,0},{9,1... | collective-permute-start | bytes 196616 | tf_op jit(solution)/shard_map/ppermute | solution.py:300
  129.6 5.5 %collective-permute-start.22 = (bf16[128,256]{1,0:T(8,128)(2,1)S(1)}, bf16[128,256]{1,0:T(8,128)(2,1)S(1)}, u32[]{:S(2)}, u32[]{:S(2)}) collective-permute-start(bf16[128,256]{1,0:T(8,128)(2,1)S(1)} %get-tuple-element.121), channel_id=1, source_target_pairs={{0,8},{1,9},{2,10},{3,11},{4,12},{5,13},{6,14},{7,15},{8,16},{9,17... | collective-permute-start | bytes 196616 | tf_op jit(solution)/shard_map/ppermute | solution.py:300
  130.2 5.8 %collective-permute-start.23 = (bf16[128,256]{1,0:T(8,128)(2,1)S(1)}, bf16[128,256]{1,0:T(8,128)(2,1)S(1)}, u32[]{:S(2)}, u32[]{:S(2)}) collective-permute-start(bf16[128,256]{1,0:T(8,128)(2,1)S(1)} %get-tuple-element.122), channel_id=1, source_target_pairs={{0,16},{1,17},{2,18},{3,19},{4,20},{5,21},{6,22},{7,23},{8,24},{9,... | collective-permute-start | bytes 196616 | tf_op jit(solution)/shard_map/ppermute | solution.py:300
  136.7 14.3 %all-to-all-start.3 = ((bf16[8,16,512]{2,1,0:T(8,128)(2,1)}), bf16[8,16,512]{2,1,0:T(8,128)(2,1)S(1)}, u32[]{:S(2)}, u32[]{:S(2)}) async-start(bf16[8,16,512]{2,1,0:T(8,128)(2,1)} %bitcast.5), calls=%async_computation.3 | async-start | bytes 262144 | tf_op jit(solution)/shard_map/all_to_all | solution.py:210

commit v5 on v4

--- a/solution.py
+++ b/solution.py
@@ -20,8 +20,6 @@
 HALF = NX * W
 MIB = 1 << 20
 STEPS = (0, -1, 1, 2)
-
-X_GROUPS = [[2 * x + core for x in range(NX)] for core in range(2)]
 Z_GROUPS = [[y * NZ + z for z in range(NZ)] for y in range(NY)]
 
 
@@ -69,8 +67,9 @@
     return copy
 
 
-def pack_kernel(place_ref, source_ref, s_ref, t_ref, out_ref, s_buf, t_buf, sem):
-    columns = at_block(place_ref[1] * NX + place_ref[0], W)
+def pack_kernel(source_ref, s_ref, t_ref, out_ref, s_buf, t_buf, sem):
+    v = lax.axis_index("vocab")
+    columns = at_block(v % 2 * NX + v // 2, W)
     copies = [
         started(s_ref.at[:, columns], s_buf, sem.at[0]),
         started(t_ref.at[:, columns], t_buf, sem.at[1]),
@@ -95,12 +94,15 @@
     digits_ref[...] = in_ref[:, 2 * W :]
 
 
-def join_kernel(place_ref, s0, s1, s2, s3, t0, t1, t2, t3, digits_ref, s_out, t_out):
-    for step, ref in zip(STEPS, (s0, s1, s2, s3)):
-        s_out[at_block((place_ref[2] + step) % NY, NEAR)] = ref[...]
-    for k, ref in enumerate((t0, t1, t2, t3)):
-        t_out[:, k * W : (k + 1) * W] = ref[...]
-    t_out[:, HALF:] = digits_ref[...]
+def join_student_kernel(place_ref, far_ref, own_ref, left_ref, right_ref, out_ref):
+    for step, ref in zip(STEPS, (own_ref, left_ref, right_ref, far_ref)):
+        out_ref[at_block((place_ref[2] + step) % NY, NEAR)] = ref[...]
+
+
+def join_teacher_kernel(far_ref, own_ref, left_ref, right_ref, digits_ref, out_ref):
+    for k, ref in enumerate((own_ref, left_ref, right_ref, far_ref)):
+        out_ref[:, k * W : (k + 1) * W] = ref[...]
+    out_ref[:, HALF:] = digits_ref[...]
 
 
 def hold_kernel(place_ref, sw_ref, tw_ref, sw2_ref, tw2_ref, sw_out, tw_out, sw2_out, tw2_out, sem):
@@ -115,34 +117,59 @@
         copy.wait()
 
 
-def partial_logits(place_ref, sw_ref, tw_ref, s_refs, t_ref, out_ref, first):
-    s0, s1, s2, s3, s4 = s_refs
-    blocks = [s0[...], s1[...], s2[...], jnp.concatenate([s3[...], s4[...]], axis=0)]
+def near_kernel(own, place_ref, sw_ref, tw_ref, s0, s1, s2, t0, t1, t2, out_ref):
+    x, y = place_ref[0], place_ref[2]
+    first = place_ref[1] * NX if own else 0
     s_total = t_total = None
-    for k, (step, block) in enumerate(zip(STEPS, blocks)):
-        at = (place_ref[0] + step) % NX
-        s_part = dot(block, sw_ref[at_block(first + at, W)])
-        t_part = dot(t_ref[:, k * W : (k + 1) * W], tw_ref[at_block(at, W)])
+    for step, ref in zip(STEPS, (s0, s1, s2)):
+        s_part = dot(ref[...], sw_ref[at_block(first + (x + step) % NX, W)])
         s_total = s_part if s_total is None else s_total + s_part
+    for k, step in enumerate(STEPS):
+        columns = slice(k * W, (k + 1) * W)
+        rows = jnp.concatenate([ref[:, columns] for ref in (t0, t1, t2)], axis=0)
+        t_part = dot(rows, tw_ref[at_block((x + step) % NX, W)])
         t_total = t_part if t_total is None else t_total + t_part
     out_ref[0] = s_total
-    out_ref[1] = t_total
-
-
-def other_kernel(
-    place_ref, sw_ref, tw_ref, s0, s1, s2, s3, s4, t0, t1, t2, t3, t4, out_ref, t_all
+    for k, step in enumerate(STEPS[:3]):
+        out_ref[1, at_block((y + step) % NY, NEAR)] = t_total[k * NEAR : (k + 1) * NEAR]
+    out_ref[1, at_block((y + 2) % NY, NEAR)] = jnp.zeros((NEAR, C), F32)
+
+
+def far_terms(place_ref, sw_ref, tw_ref, s3, s4, t3, t4, first):
+    x = place_ref[0]
+    s_rows = jnp.concatenate([s3[...], s4[...]], axis=0)
+    s_part = dot(s_rows, sw_ref[at_block(first + (x + 2) % NX, W)])
+    t_total = None
+    for k, step in enumerate(STEPS):
+        columns = slice(k * W, (k + 1) * W)
+        rows = jnp.concatenate([t3[:, columns], t4[:, columns]], axis=0)
+        t_part = dot(rows, tw_ref[at_block((x + step) % NX, W)])
+        t_total = t_part if t_total is None else t_total + t_part
+    return s_part, t_total
+
+
+def far_other_kernel(place_ref, sw_ref, tw_ref, s3, s4, t3, t4, near_ref, out_ref):
+    s_part, t_part = far_terms(place_ref, sw_ref, tw_ref, s3, s4, t3, t4, 0)
+    out_ref[0] = near_ref[0] + s_part
+    out_ref[1] = near_ref[1]
+    out_ref[1, at_block((place_ref[2] + 2) % NY, NEAR)] = t_part
+
+
+def far_own_kernel(
+    place_ref, sw_ref, tw_ref, s3, s4, t3, t4, t0, t1, t2, near_ref, out_ref, digits_ref
 ):
+    y = place_ref[2]
+    s_part, t_part = far_terms(
+        place_ref, sw_ref, tw_ref, s3, s4, t3, t4, place_ref[1] * NX
+    )
+    far = at_block((y + 2) % NY, NEAR)
+    out_ref[0] = near_ref[0] + s_part
+    out_ref[1] = near_ref[1]
+    out_ref[1, far] = t_part
     for step, ref in zip(STEPS, (t0, t1, t2)):
-        t_all[at_block((place_ref[2] + step) % NY, NEAR)] = ref[...]
-    far = (place_ref[2] + STEPS[3]) % NY * 2
+        digits_ref[at_block((y + step) % NY, NEAR)] = ref[:, HALF:]
     for k, ref in enumerate((t3, t4)):
-        t_all[at_block(far + k, NEAR // 2)] = ref[...]
-    partial_logits(place_ref, sw_ref, tw_ref, (s0, s1, s2, s3, s4), t_all, out_ref, 0)
-
-
-def own_kernel(place_ref, sw_ref, tw_ref, s0, s1, s2, s3, s4, t_all, out_ref):
-    first = place_ref[1] * NX
-    partial_logits(place_ref, sw_ref, tw_ref, (s0, s1, s2, s3, s4), t_all, out_ref, first)
+        digits_ref[at_block((y + 2) % NY * 2 + k, NEAR // 2)] = ref[:, HALF:]
 
 
 def pack_stats(lse_s, mean, lse_t):
@@ -169,8 +196,10 @@
     return lse_s, mean, lse(each_t)
 
 
-def logits_kernel(own_ref, other_ref, digits_ref, s_ref, diff_ref, stat_ref):
-    digits = digits_ref[:, HALF:].astype(F32)
+def logits_kernel(
+    own_ref, other_ref, digits_ref, s_ref, diff_ref, stat_ref
+):
+    digits = digits_ref[...].astype(F32)
     index = (digits[:, 0:1] * 32.0 + digits[:, 1:2]).astype(jnp.int32)
     column = lax.broadcasted_iota(jnp.int32, (N, N), 1)
     select = (index == column).astype(F32).astype(BF)
@@ -242,18 +271,21 @@
         out_ref[:, k * H : (k + 1) * H] = part.astype(BF)
 
 
-def first_own_kernel(place_ref, g_ref, in_ref, sw_ref, *out_refs):
-    for k, part in enumerate(terms(place_ref, g_ref[...], sw_ref, place_ref[1], 0)):
-        received = in_ref[:, k * H : (k + 1) * H].astype(F32)
-        out_refs[k][...] = (part + received).astype(BF)
-
-
-def second_own_kernel(place_ref, g_ref, in_ref, sw_ref, *out_refs):
-    for k, part in enumerate(terms(place_ref, g_ref[...], sw_ref, place_ref[1], 1)):
+def own_terms_kernel(second, place_ref, g_ref, sw_ref, out_ref):
+    for k, part in enumerate(terms(place_ref, g_ref[...], sw_ref, place_ref[1], second)):
+        out_ref[:, k * H : (k + 1) * H] = part
+
+
+def first_add_kernel(own_ref, in_ref, *out_refs):
+    for k, ref in enumerate(out_refs):
         columns = slice(k * H, (k + 1) * H)
-        total = (part + in_ref[:, columns].astype(F32)).astype(BF)
-        for j, ref in enumerate(out_refs):
-            ref[:, columns] = total[j * NEAR : (j + 1) * NEAR]
+        ref[...] = (own_ref[:, columns] + in_ref[:, columns].astype(F32)).astype(BF)
+
+
+def second_add_kernel(own_ref, in_ref, *out_refs):
+    for k, ref in enumerate(out_refs):
+        rows = slice(k * NEAR, (k + 1) * NEAR)
+        ref[...] = (own_ref[rows] + in_ref[rows].astype(F32)).astype(BF)
 
 
 def total_of(refs):
@@ -305,11 +337,12 @@
 
 
 def ring(a, along):
-    return [a] + [along(a, -step) for step in STEPS[1:3]] + [along(a, 2)]
+    return along(a, 2), a, along(a, 1), along(a, -1)
 
 
 def to_ring(blocks, along):
-    return [along(a, step) if step else a for step, a in zip(STEPS, blocks)]
+    own, left, right, far = blocks
+    return along(far, 2), along(left, -1), along(right, 1), own
 
 
 def per_device(student_hidden, teacher_hidden, student_weight, teacher_weight, source_rows):
@@ -318,9 +351,9 @@
     place = jnp.stack([v // 2, v % 2, y])
     packed = call(
         pack_kernel,
-        [SM, SM, HBM, HBM],
+        [SM, HBM, HBM],
         [((NZ, ROWS, 2 * W + 128), BF)],
-        place, source_rows, in_hbm(student_hidden), in_hbm(teacher_hidden),
+        source_rows, in_hbm(student_hidden), in_hbm(teacher_hidden),
         scratch=[pltpu.VMEM((ROWS, W), BF)] * 2 + [pltpu.SemaphoreType.DMA((2,))],
     )[0]
     sw2, tw2 = to_other_core(student_weight), to_other_core(teacher_weight)
@@ -329,14 +362,15 @@
     s_near, t_near, digits = call(
         split_kernel, [VM], [((NEAR, W), BF), ((NEAR, W), BF), ((NEAR, 128), BF)], near
     )
-    s_near, t_near = ring(s_near, along_y), ring(t_near, along_x)
-    s_near, t_near = lax.optimization_barrier((s_near, t_near))
-    s_mine, t_mine = call(
-        join_kernel,
-        [SM] + [VM] * 9,
-        [((N, W), BF), ((NEAR, HALF + 128), BF)],
-        place, *s_near, *t_near, digits,
-    )
+    s_mine = call(
+        join_student_kernel, [SM] + [VM] * 4, [((N, W), BF)], place, *ring(s_near, along_y)
+    )[0]
+    t_mine = call(
+        join_teacher_kernel,
+        [VM] * 5,
+        [((NEAR, HALF + 128), BF)],
+        *ring(t_near, along_x), digits,
+    )[0]
     s_left, s_right = along_x(s_mine, 1), along_x(s_mine, -1)
     t_left, t_right = along_y(t_mine, 1), along_y(t_mine, -1)
     held = call(
@@ -346,40 +380,40 @@
         place, *(in_hbm(x) for x in (student_weight, teacher_weight, sw2, tw2)),
         scratch=[pltpu.SemaphoreType.DMA((4,))],
     )
-    s_left, s_right, t_left, t_right, held = lax.optimization_barrier(
-        (s_left, s_right, t_left, t_right, held)
-    )
+    t_left, t_right, held = lax.optimization_barrier((t_left, t_right, held))
     sw, tw, sw2, tw2 = held
-    s_rows = (
-        s_mine, s_left, s_right,
+    s_near, t_near = (s_mine, s_left, s_right), (t_mine, t_left, t_right)
+    far = (
         along_x(s_left[: N // 2], 1), along_x(s_right[N // 2 :], -1),
-    )
-    t_rows = (
-        t_mine, t_left, t_right,
         along_y(t_left[: NEAR // 2], 1), along_y(t_right[NEAR // 2 :], -1),
     )
-    s_rows, t_rows = lax.optimization_barrier((s_rows, t_rows))
-    flops = 4 * N * HALF * C
-    for_other, t_all = call(
-        other_kernel,
-        [SM] + [VM] * 12,
-        [((2, N, C), F32), ((N, HALF + 128), BF)],
-        place, sw2, tw2, *s_rows, *t_rows,
+    flops = 3 * N * HALF * C
+    part = [((2, N, C), F32)]
+
+    def near(mine, *args):
+        kernel = functools.partial(near_kernel, mine)
+        return call(kernel, [SM] + [VM] * 8, part, place, *args, flops=flops)[0]
+
+    for_other = near(False, sw2, tw2, *s_near, *t_near)
+    own = near(True, sw, tw, *s_near, *t_near)
+    far, for_other, own = lax.optimization_barrier((far, for_other, own))
+    flops = N * HALF * C
+    for_other = call(
+        far_other_kernel, [SM] + [VM] * 7, part, place, sw2, tw2, *far, for_other, flops=flops
+    )[0]
+    own, digits = call(
+        far_own_kernel,
+        [SM] + [VM] * 10,
+        part + [((N, 128), BF)],
+        place, sw, tw, *far, *t_near, own,
         flops=flops,
     )
-    own = call(
-        own_kernel,
-        [SM] + [VM] * 8,
-        [((2, N, C), F32)],
-        place, sw, tw, *s_rows, t_all,
-        flops=flops,
-    )[0]
     other, own = lax.optimization_barrier((to_other_core(for_other), own))
     s, d, stats = call(
         logits_kernel,
         [VM] * 3,
         [((N, C), F32), ((N, C), F32), ((VOC, 8, N // 2), F32)],
-        own, other, t_all,
+        own, other, digits,
         flops=6 * N * N * C,
     )
     stats = exchange(stats, "vocab")
@@ -397,21 +431,19 @@
     second = call(
         second_for_other_kernel, [SM, VM, VM], [half], place, turned, sw, flops=flops
     )[0]
-    first = call(
-        first_own_kernel,
-        [SM] + [VM] * 3,
-        [((N, H), BF)] * 4,
-        place, g, to_other_core(first), sw,
-        flops=flops,
-    )
+    first, second = to_other_core(first), to_other_core(second)
+
+    def own_terms(number, rows):
+        kernel = functools.partial(own_terms_kernel, number)
+        return call(
+            kernel, [SM, VM, VM], [((N, NX * H), F32)], place, rows, sw, flops=flops
+        )[0]
+
+    first, mine = lax.optimization_barrier((first, own_terms(0, g)))
+    first = call(first_add_kernel, [VM] * 2, [((N, H), BF)] * 4, mine, first)
     first = to_ring(first, along_x)
-    second = call(
-        second_own_kernel,
-        [SM] + [VM] * 3,
-        [((NEAR, NX * H), BF)] * 4,
-        place, turned, to_other_core(second), sw,
-        flops=flops,
-    )
+    second, mine = lax.optimization_barrier((second, own_terms(1, turned)))
+    second = call(second_add_kernel, [VM] * 2, [((NEAR, NX * H), BF)] * 4, mine, second)
     second = to_ring(second, along_y)
     blocks = [((NEAR, H), BF)] * 4
     first = call(

time: 154 us -> 150 us (0.974)
  waiting for transfers between devices: 39.3 us -> 28.1 us
  starting transfers between devices: 44 us -> 47.1 us
  blocking collectives: 44.5 us -> 47.2 us
  Pallas kernels: 21.6 us -> 23.4 us
    ppermute x13, waiting for transfers between devices: 15.8 us -> 3.89 us  [along_x(): return lax.ppermute(a, 'vocab', pairs)]
    ppermute x13, starting transfers between devices: 17.4 us -> 21.3 us  [along_x(): return lax.ppermute(a, 'vocab', pairs)]
    all_to_all x3, blocking collectives: 44.5 us -> 47.2 us  [exchange(): out = lax.all_to_all(flat, axis, 0, 0, axis_index_groups=groups, tiled=True)]
    all_to_all x1, starting transfers between devices: 5.23 us -> 3.37 us  [exchange(): out = lax.all_to_all(flat, axis, 0, 0, axis_index_groups=groups, tiled=True)]
    pallas_call x16 -> x21, Pallas kernels: 21.6 us -> 23.4 us  [call(): pl.pallas_call(kernel, in_specs=in_specs, out_specs=[VM] * len(outs), out...]
  transfers between devices with their start and end apart: 32 -> 32, of which waited for: 16 -> 13; matrix products, arithmetic and copies ran while one was open for 0% -> 0% of each run, Pallas kernels for 8% -> 11%
where the time goes in v5:
time: 150 us; the launch traced here: 149 us
  blocking collectives  47.2 us (31%)
  starting transfers between devices  47.1 us (31%)
  waiting for transfers between devices  28.1 us (19%)
  Pallas kernels  23.4 us (16%)
  between operations  2.06 us (1%)
    all_to_all x3, blocking collectives, exchange(): out = lax.all_to_all(flat, axis, 0, 0, axis_index_groups=groups, tiled=True)  47.2 us
    pallas_call x21, Pallas kernels, call(): pl.pallas_call(kernel, in_specs=in_specs, out_specs=[VM] * len(outs), out...  23.4 us
    ppermute x13, starting transfers between devices, along_x(): return lax.ppermute(a, 'vocab', pairs)  21.3 us
    ppermute x13, starting transfers between devices, along_y(): return lax.ppermute(a, 'tok', pairs)  21.2 us
    ppermute x13, waiting for transfers between devices, along_y(): return lax.ppermute(a, 'tok', pairs)  11.6 us
    all_to_all x1, waiting for transfers between devices, exchange(): out = lax.all_to_all(flat, axis, 0, 0, axis_index_groups=groups, tiled=True)  8.96 us
    ppermute x13, waiting for transfers between devices, along_x(): return lax.ppermute(a, 'vocab', pairs)  3.89 us
    ppermute x5, waiting for transfers between devices, to_other_core(): return lax.ppermute(a, 'vocab', [(k, k ^ 1) for k in range(VOC)])  3.74 us
  transfers between devices with their start and end apart: 32, of which 13 were waited for; matrix products, arithmetic and copies ran while one was open for 0% of the time, Pallas kernels for 11%

profile of v5, /device:TPU:6, one launch (start us, length us, event | category | flops | bytes accessed | tf_op | source)
XLA Modules:
  0.0 149.3 jit_solution(9338901727214613860)
XLA Ops:
  0.6 0.1 collective-permute-start
  0.7 0.5 collective-permute-start.1
  1.2 0.7 copy-done
  1.9 1.3 shard_map.68
  3.2 21.1 %all_to_all.30 = bf16[8,16,1152]{2,1,0:T(8,128)(2,1)S(1)} all-to-all(bf16[8,16,1152]{2,1,0:T(8,128)(2,1)S(1)} %shard_map.68), channel_id=1, replica_groups={{0,1,2,3,4,5,6,7},{8,9,10,11,12,13,14,15},{16,17,18,19,20,21,22,23},{24..., dimensions={0} | all-to-all | bytes 589824 | tf_op jit(solution)/shard_map/all_to_all | solution.py:239
  24.4 1.5 collective-permute-start.2
  25.9 2.1 %collective-permute-start.3 = (bf16[128,512]{1,0:T(8,128)(2,1)S(1)}, bf16[128,512]{1,0:T(8,128)(2,1)S(1)}, u32[]{:S(2)}, u32[]{:S(2)}) collective-permute-start(bf16[128,512]{1,0:T(8,128)(2,1)S(1)} %get-tuple-element.56.own_ref), channel_id=1, source_target_pairs={{0,64},{32,96},{64,128},{96,160},{128,192},{160,224},{192,0},{224,... | collective-permute-start | bytes 393224 | tf_op jit(solution)/shard_map/ppermute | solution.py:327
  28.0 3.2 %collective-permute-start.7 = (bf16[128,512]{1,0:T(8,128)(2,1)S(1)}, bf16[128,512]{1,0:T(8,128)(2,1)S(1)}, u32[]{:S(2)}, u32[]{:S(2)}) collective-permute-start(bf16[128,512]{1,0:T(8,128)(2,1)S(1)} %get-tuple-element.66.own_ref), channel_id=1, source_target_pairs={{0,16},{1,17},{2,18},{3,19},{4,20},{5,21},{6,22},{7,23},{8,24},{9,... | collective-permute-start | bytes 393224 | tf_op jit(solution)/shard_map/ppermute | solution.py:332
  31.2 0.7 collective-permute-start.8
  31.8 0.1 collective-permute-done.2.far_ref
  32.0 3.0 %collective-permute-start.9 = (bf16[128,512]{1,0:T(8,128)(2,1)S(1)}, bf16[128,512]{1,0:T(8,128)(2,1)S(1)}, u32[]{:S(2)}, u32[]{:S(2)}) collective-permute-start(bf16[128,512]{1,0:T(8,128)(2,1)S(1)} %get-tuple-element.66.own_ref), channel_id=1, source_target_pairs={{0,24},{1,25},{2,26},{3,27},{4,28},{5,29},{6,30},{7,31},{8,0},{9,1... | collective-permute-start | bytes 393224 | tf_op jit(solution)/shard_map/ppermute | solution.py:332
  35.1 0.8 collective-permute-start.5
  35.8 2.5 %collective-permute-start.6 = (bf16[128,2176]{1,0:T(8,128)(2,1)S(1)}, bf16[128,2176]{1,0:T(8,128)(2,1)S(1)}, u32[]{:S(2)}, u32[]{:S(2)}) collective-permute-start(bf16[128,2176]{1,0:T(8,128)(2,1)S(1)} %shard_map.70.t0), channel_id=1, source_target_pairs={{0,24},{1,25},{2,26},{3,27},{4,28},{5,29},{6,30},{7,31},{8,0},{9,1... | collective-permute-start | bytes 1671176 | tf_op jit(solution)/shard_map/ppermute | solution.py:332
  38.5 0.4 collective-permute-done.9.right_ref
  38.9 0.6 shard_map.72.s0
  39.5 3.2 %collective-permute-start.10 = (bf16[512,512]{1,0:T(8,128)(2,1)S(1)}, bf16[512,512]{1,0:T(8,128)(2,1)S(1)}, u32[]{:S(2)}, u32[]{:S(2)}) collective-permute-start(bf16[512,512]{1,0:T(8,128)(2,1)S(1)} %shard_map.72.s0), channel_id=1, source_target_pairs={{0,64},{32,96},{64,128},{96,160},{128,192},{160,224},{192,0},{224,... | collective-permute-start | bytes 1572872 | tf_op jit(solution)/shard_map/ppermute | solution.py:327
  42.7 4.6 %shard_map.71 = (bf16[4096,512]{1,0:T(8,128)(2,1)S(1)}, bf16[2048,512]{1,0:T(8,128)(2,1)S(1)}, bf16[2048,512]{1,0:T(8,128)(2,1)S(1)}, bf16[2048,512]{1,0:T(8,128)(2,1)S(1)}) custom-call(s32[3]{0:T(128)S(1)} %pad_add_fusion.place_ref, bf16[4096,512]{1,0:T(8,128)(2,1)} %sw_ref.1, bf16[4096,512]{1,0:T(8,128)(2,1)} %tw_ref.1, bf16[4096,512]{1,0:T(8,128)(2,1)} %copy-done.1, ...), custom_call_target="tpu_custom_call" | custom-call | tf_op jit(solution)/shard_map/pallas_call | solution.py:49
  47.3 3.7 %collective-permute-done.10.s1 = bf16[512,512]{1,0:T(8,128)(2,1)S(1)} collective-permute-done((bf16[512,512]{1,0:T(8,128)(2,1)S(1)}, bf16[512,512]{1,0:T(8,128)(2,1)S(1)}, u32[]{:S(2)}, u32[]{:S(2)}) %collective-permute-start.10) | collective-permute-done | bytes 524320 | tf_op jit(solution)/shard_map/ppermute | solution.py:327
  51.0 3.7 %collective-permute-start.11 = (bf16[256,512]{1,0:T(8,128)(2,1)S(1)}, bf16[256,512]{1,0:T(8,128)(2,1)S(1)}, u32[]{:S(2)}, u32[]{:S(2)}) collective-permute-start(bf16[256,512]{1,0:T(8,128)(2,1)S(1)} %slice.16), channel_id=1, source_target_pairs={{0,64},{32,96},{64,128},{96,160},{128,192},{160,224},{192,0},{224,... | collective-permute-start | bytes 786440 | tf_op jit(solution)/shard_map/ppermute | solution.py:327
  54.9 2.8 %collective-permute-start.14 = (bf16[64,2176]{1,0:T(8,128)(2,1)S(1)}, bf16[64,2176]{1,0:T(8,128)(2,1)S(1)}, u32[]{:S(2)}, u32[]{:S(2)}) collective-permute-start(bf16[64,2176]{1,0:T(8,128)(2,1)S(1)} %slice.14), channel_id=1, source_target_pairs={{0,8},{1,9},{2,10},{3,11},{4,12},{5,13},{6,14},{7,15},{8,16},{9,17... | collective-permute-start | bytes 835592 | tf_op jit(solution)/shard_map/ppermute | solution.py:332
  57.8 0.7 collective-permute-start.15
  58.5 2.4 %shard_map.74.near_ref = f32[2,512,512]{2,1,0:T(8,128)S(1)} custom-call(s32[3]{0:T(128)S(1)} %pad_add_fusion.place_ref, bf16[4096,512]{1,0:T(8,128)(2,1)S(1)} %get-tuple-element.69.sw_ref, bf16[2048,512]{1,0:T(8,128)(2,1)S(1)} %get-tuple-element.70.tw_ref, bf16[512,512]{1,0:T(8,128)(2,1)S(1)} %shard_map.72.s0, ...), custom_call_target="tpu_custom_call" | custom-call | flops 1610612736 | tf_op jit(solution)/shard_map/pallas_call | solution.py:49
  60.9 2.4 %shard_map.73.near_ref = f32[2,512,512]{2,1,0:T(8,128)S(1)} custom-call(s32[3]{0:T(128)S(1)} %pad_add_fusion.place_ref, bf16[2048,512]{1,0:T(8,128)(2,1)S(1)} %get-tuple-element.64.sw_ref, bf16[2048,512]{1,0:T(8,128)(2,1)S(1)} %get-tuple-element.65.tw_ref, bf16[512,512]{1,0:T(8,128)(2,1)S(1)} %shard_map.72.s0, ...), custom_call_target="tpu_custom_call" | custom-call | flops 1610612736 | tf_op jit(solution)/shard_map/pallas_call | solution.py:49
  63.3 1.3 collective-permute-done.15.t4
  64.6 1.3 shard_map.75
  65.9 1.3 shard_map.76
  67.2 2.9 %collective-permute-done.16.other_ref = f32[2,512,512]{2,1,0:T(8,128)S(1)} collective-permute-done((f32[2,512,512]{2,1,0:T(8,128)S(1)}, f32[2,512,512]{2,1,0:T(8,128)S(1)}, u32[]{:S(2)}, u32[]{:S(2)}) %collective-permute-start.16) | collective-permute-done | bytes 2097184 | tf_op jit(solution)/shard_map/ppermute | solution.py:336
  70.1 1.7 %shard_map.77 = (f32[512,512]{1,0:T(8,128)S(1)}, f32[512,512]{1,0:T(8,128)S(1)}, f32[8,8,256]{2,1,0:T(8,128)S(1)}) custom-call(f32[2,512,512]{2,1,0:T(8,128)S(1)} %get-tuple-element.78.own_ref, f32[2,512,512]{2,1,0:T(8,128)S(1)} %collective-permute-done.16.other_ref, bf16[512,128]{1,0:T(8,128)(2,1)S(1)} %get-tuple-element.80.digits_ref), custom_call_target="tpu_custom_call" | custom-call | flops 805306368 | tf_op jit(solution)/shard_map/pallas_call | solution.py:49
  71.8 9.1 %all_to_all.31.in_ref = f32[8,8,256]{2,1,0:T(8,128)S(1)} all-to-all(f32[8,8,256]{2,1,0:T(8,128)S(1)} %get-tuple-element.81), channel_id=1, replica_groups=mesh['vocab'=8,'tok'=32] {'vocab'}, dimensions={0} | all-to-all | bytes 131072 | tf_op jit(solution)/shard_map/all_to_all | solution.py:239
  80.9 0.1 shard_map.78
  81.1 17.0 %all_to_all.32.stat_ref = f32[32,8,256]{2,1,0:T(8,128)S(1)} all-to-all(f32[32,8,256]{2,1,0:T(8,128)S(1)} %shard_map.78), channel_id=1, replica_groups=mesh['vocab'=8,'tok'=32] {'tok'}, dimensions={0} | all-to-all | bytes 524288 | tf_op jit(solution)/shard_map/all_to_all | solution.py:239
  98.0 1.9 %shard_map.79 = (bf16[512,1024]{1,0:T(8,128)(2,1)S(1)}, bf16[512,512]{1,0:T(8,128)(2,1)S(1)}, bf16[512,512]{1,0:T(8,128)(2,1)S(1)}, f32[1,1]{1,0:T(1,128)S(1)}) custom-call(s32[3]{0:T(128)S(1)} %pad_add_fusion.place_ref, f32[32,8,256]{2,1,0:T(8,128)S(1)} %all_to_all.32.stat_ref, f32[512,512]{1,0:T(8,128)S(1)} %get-tuple-element.82.s_ref, ...), custom_call_target="tpu_custom_call" | custom-call | flops 536870912 | tf_op jit(solution)/shard_map/pallas_call | solution.py:49
  99.9 1.3 shard_map.83
  101.2 0.1 collective-permute-start.24
  101.3 0.5 collective-permute-start.17
  101.8 1.3 shard_map.84.own_ref
  103.1 0.9 collective-permute-done.24.in_ref
  103.9 0.2 shard_map.85
  104.1 1.6 %collective-permute-start.25 = (bf16[128,1024]{1,0:T(8,128)(2,1)S(1)}, bf16[128,1024]{1,0:T(8,128)(2,1)S(1)}, u32[]{:S(2)}, u32[]{:S(2)}) collective-permute-start(bf16[128,1024]{1,0:T(8,128)(2,1)S(1)} %get-tuple-element.100), channel_id=1, source_target_pairs={{0,16},{1,17},{2,18},{3,19},{4,20},{5,21},{6,22},{7,23},{8,24},{9,... | collective-permute-start | bytes 786440 | tf_op jit(solution)/shard_map/ppermute | solution.py:332
  105.7 1.8 %collective-permute-start.26 = (bf16[128,1024]{1,0:T(8,128)(2,1)S(1)}, bf16[128,1024]{1,0:T(8,128)(2,1)S(1)}, u32[]{:S(2)}, u32[]{:S(2)}) collective-permute-start(bf16[128,1024]{1,0:T(8,128)(2,1)S(1)} %get-tuple-element.101), channel_id=1, source_target_pairs={{0,24},{1,25},{2,26},{3,27},{4,28},{5,29},{6,30},{7,31},{8,0},{9,1... | collective-permute-start | bytes 786440 | tf_op jit(solution)/shard_map/ppermute | solution.py:332
  107.5 0.3 collective-permute-start.27
  107.7 1.3 shard_map.80.own_ref
  109.1 0.2 shard_map.81
  109.3 2.4 %collective-permute-start.18 = (bf16[512,256]{1,0:T(8,128)(2,1)S(1)}, bf16[512,256]{1,0:T(8,128)(2,1)S(1)}, u32[]{:S(2)}, u32[]{:S(2)}) collective-permute-start(bf16[512,256]{1,0:T(8,128)(2,1)S(1)} %get-tuple-element.89), channel_id=1, source_target_pairs={{0,128},{32,160},{64,192},{96,224},{128,0},{160,32},{192,64},{224,... | collective-permute-start | bytes 786440 | tf_op jit(solution)/shard_map/ppermute | solution.py:327
  111.7 0.8 collective-permute-start.19
  112.5 2.4 %collective-permute-done.25.refs_0_ = bf16[128,1024]{1,0:T(8,128)(2,1)S(1)} collective-permute-done((bf16[128,1024]{1,0:T(8,128)(2,1)S(1)}, bf16[128,1024]{1,0:T(8,128)(2,1)S(1)}, u32[]{:S(2)}, u32[]{:S(2)}) %collective-permute-start.25) | collective-permute-done | bytes 262176 | tf_op jit(solution)/shard_map/ppermute | solution.py:332
  114.9 2.1 %collective-permute-start.20 = (bf16[512,256]{1,0:T(8,128)(2,1)S(1)}, bf16[512,256]{1,0:T(8,128)(2,1)S(1)}, u32[]{:S(2)}, u32[]{:S(2)}) collective-permute-start(bf16[512,256]{1,0:T(8,128)(2,1)S(1)} %get-tuple-element.91), channel_id=1, source_target_pairs={{0,64},{32,96},{64,128},{96,160},{128,192},{160,224},{192,0},{224,... | collective-permute-start | bytes 786440 | tf_op jit(solution)/shard_map/ppermute | solution.py:327
  117.0 1.2 collective-permute-done.26.refs_1_
  118.2 1.5 collective-permute-done.27.refs_2_
  119.7 0.1 shard_map.86
  119.8 2.2 %collective-permute-start.28 = (bf16[128,256]{1,0:T(8,128)(2,1)S(1)}, bf16[128,256]{1,0:T(8,128)(2,1)S(1)}, u32[]{:S(2)}, u32[]{:S(2)}) collective-permute-start(bf16[128,256]{1,0:T(8,128)(2,1)S(1)} %get-tuple-element.104), channel_id=1, source_target_pairs={{0,128},{32,160},{64,192},{96,224},{128,0},{160,32},{192,64},{224,... | collective-permute-start | bytes 196616 | tf_op jit(solution)/shard_map/ppermute | solution.py:327
  122.0 0.9 collective-permute-start.29
  122.8 2.4 %collective-permute-start.30 = (bf16[128,256]{1,0:T(8,128)(2,1)S(1)}, bf16[128,256]{1,0:T(8,128)(2,1)S(1)}, u32[]{:S(2)}, u32[]{:S(2)}) collective-permute-start(bf16[128,256]{1,0:T(8,128)(2,1)S(1)} %get-tuple-element.106), channel_id=1, source_target_pairs={{0,64},{32,96},{64,128},{96,160},{128,192},{160,224},{192,0},{224,... | collective-permute-start | bytes 196616 | tf_op jit(solution)/shard_map/ppermute | solution.py:327
  125.2 0.8 shard_map.82
  126.0 1.7 %collective-permute-start.21 = (bf16[128,256]{1,0:T(8,128)(2,1)S(1)}, bf16[128,256]{1,0:T(8,128)(2,1)S(1)}, u32[]{:S(2)}, u32[]{:S(2)}) collective-permute-start(bf16[128,256]{1,0:T(8,128)(2,1)S(1)} %get-tuple-element.93), channel_id=1, source_target_pairs={{0,16},{1,17},{2,18},{3,19},{4,20},{5,21},{6,22},{7,23},{8,24},{9,... | collective-permute-start | bytes 196616 | tf_op jit(solution)/shard_map/ppermute | solution.py:332
  127.7 1.3 collective-permute-start.22
  129.0 0.8 collective-permute-start.23
  129.8 2.1 %collective-permute-done.21.refs_0_ = bf16[128,256]{1,0:T(8,128)(2,1)S(1)} collective-permute-done((bf16[128,256]{1,0:T(8,128)(2,1)S(1)}, bf16[128,256]{1,0:T(8,128)(2,1)S(1)}, u32[]{:S(2)}, u32[]{:S(2)}) %collective-permute-start.21) | collective-permute-done | bytes 65568 | tf_op jit(solution)/shard_map/ppermute | solution.py:332
  131.8 1.2 collective-permute-done.22.refs_1_
  133.0 1.5 collective-permute-done.23.refs_2_
  134.5 0.7 shard_map.87
  135.2 3.4 %all-to-all-start.3 = ((bf16[8,16,512]{2,1,0:T(8,128)(2,1)}), bf16[8,16,512]{2,1,0:T(8,128)(2,1)S(1)}, u32[]{:S(2)}, u32[]{:S(2)}) async-start(bf16[8,16,512]{2,1,0:T(8,128)(2,1)} %bitcast.5), calls=%async_computation.3 | async-start | bytes 262144 | tf_op jit(solution)/shard_map/all_to_all | solution.py:239
  138.6 9.0 %all-to-all-done.3.in_ref = bf16[8,16,512]{2,1,0:T(8,128)(2,1)S(1)} async-done(((bf16[8,16,512]{2,1,0:T(8,128)(2,1)}), bf16[8,16,512]{2,1,0:T(8,128)(2,1)S(1)}, u32[]{:S(2)}, u32[]{:S(2)}) %all-to-all-start.3) | async-done | bytes 131104 | tf_op jit(solution)/shard_map/all_to_all | solution.py:239
  147.6 0.6 copy.8
  (36 shorter events, 0.5 us)
Async XLA Ops:
  0.6 23.7 %collective-permute-start = (bf16[4096,512]{1,0:T(8,128)(2,1)}, bf16[4096,512]{1,0:T(8,128)(2,1)S(1)}, u32[]{:S(2)}, u32[]{:S(2)}) collective-permute-start(bf16[4096,512]{1,0:T(8,128)(2,1)} %sw_ref.1), channel_id=1, source_target_pairs={{0,32},{32,0},{64,96},{96,64},{128,160},{160,128},{192,224},{224,1... | collective-permute-start | bytes 12582920 | tf_op jit(solution)/shard_map/ppermute | solution.py:336
  0.7 23.6 %collective-permute-start.1 = (bf16[4096,512]{1,0:T(8,128)(2,1)}, bf16[4096,512]{1,0:T(8,128)(2,1)S(1)}, u32[]{:S(2)}, u32[]{:S(2)}) collective-permute-start(bf16[4096,512]{1,0:T(8,128)(2,1)} %tw_ref.1), channel_id=1, source_target_pairs={{0,32},{32,0},{64,96},{96,64},{128,160},{160,128},{192,224},{224,1... | collective-permute-start | bytes 12582920 | tf_op jit(solution)/shard_map/ppermute | solution.py:336
  1.2 0.7 copy-start
  24.3 7.7 %copy-start.1 = (bf16[4096,512]{1,0:T(8,128)(2,1)}, bf16[4096,512]{1,0:T(8,128)(2,1)S(1)}, u32[]{:S(2)}) copy-start(bf16[4096,512]{1,0:T(8,128)(2,1)S(1)} %collective-permute-done.sw2_ref) | copy-start | bytes 12582916
  24.3 10.7 %copy-start.2 = (bf16[4096,512]{1,0:T(8,128)(2,1)}, bf16[4096,512]{1,0:T(8,128)(2,1)S(1)}, u32[]{:S(2)}) copy-start(bf16[4096,512]{1,0:T(8,128)(2,1)S(1)} %collective-permute-done.1.tw2_ref) | copy-start | bytes 12582916
  24.4 7.6 %collective-permute-start.2 = (bf16[128,512]{1,0:T(8,128)(2,1)S(1)}, bf16[128,512]{1,0:T(8,128)(2,1)S(1)}, u32[]{:S(2)}, u32[]{:S(2)}) collective-permute-start(bf16[128,512]{1,0:T(8,128)(2,1)S(1)} %get-tuple-element.56.own_ref), channel_id=1, source_target_pairs={{0,128},{32,160},{64,192},{96,224},{128,0},{160,32},{192,64},{224,... | collective-permute-start | bytes 393224 | tf_op jit(solution)/shard_map/ppermute | solution.py:327
  25.9 9.1 %collective-permute-start.3 = (bf16[128,512]{1,0:T(8,128)(2,1)S(1)}, bf16[128,512]{1,0:T(8,128)(2,1)S(1)}, u32[]{:S(2)}, u32[]{:S(2)}) collective-permute-start(bf16[128,512]{1,0:T(8,128)(2,1)S(1)} %get-tuple-element.56.own_ref), channel_id=1, source_target_pairs={{0,64},{32,96},{64,128},{96,160},{128,192},{160,224},{192,0},{224,... | collective-permute-start | bytes 393224 | tf_op jit(solution)/shard_map/ppermute | solution.py:327
  28.0 7.1 %collective-permute-start.4 = (bf16[128,512]{1,0:T(8,128)(2,1)S(1)}, bf16[128,512]{1,0:T(8,128)(2,1)S(1)}, u32[]{:S(2)}, u32[]{:S(2)}) collective-permute-start(bf16[128,512]{1,0:T(8,128)(2,1)S(1)} %get-tuple-element.56.own_ref), channel_id=1, source_target_pairs={{0,192},{32,224},{64,0},{96,32},{128,64},{160,96},{192,128},{224,1... | collective-permute-start | bytes 393224 | tf_op jit(solution)/shard_map/ppermute | solution.py:327
  28.0 10.5 %collective-permute-start.7 = (bf16[128,512]{1,0:T(8,128)(2,1)S(1)}, bf16[128,512]{1,0:T(8,128)(2,1)S(1)}, u32[]{:S(2)}, u32[]{:S(2)}) collective-permute-start(bf16[128,512]{1,0:T(8,128)(2,1)S(1)} %get-tuple-element.66.own_ref), channel_id=1, source_target_pairs={{0,16},{1,17},{2,18},{3,19},{4,20},{5,21},{6,22},{7,23},{8,24},{9,... | collective-permute-start | bytes 393224 | tf_op jit(solution)/shard_map/ppermute | solution.py:332
  31.2 7.3 %collective-permute-start.8 = (bf16[128,512]{1,0:T(8,128)(2,1)S(1)}, bf16[128,512]{1,0:T(8,128)(2,1)S(1)}, u32[]{:S(2)}, u32[]{:S(2)}) collective-permute-start(bf16[128,512]{1,0:T(8,128)(2,1)S(1)} %get-tuple-element.66.own_ref), channel_id=1, source_target_pairs={{0,8},{1,9},{2,10},{3,11},{4,12},{5,13},{6,14},{7,15},{8,16},{9,17... | collective-permute-start | bytes 393224 | tf_op jit(solution)/shard_map/ppermute | solution.py:332
  32.0 6.9 %collective-permute-start.9 = (bf16[128,512]{1,0:T(8,128)(2,1)S(1)}, bf16[128,512]{1,0:T(8,128)(2,1)S(1)}, u32[]{:S(2)}, u32[]{:S(2)}) collective-permute-start(bf16[128,512]{1,0:T(8,128)(2,1)S(1)} %get-tuple-element.66.own_ref), channel_id=1, source_target_pairs={{0,24},{1,25},{2,26},{3,27},{4,28},{5,29},{6,30},{7,31},{8,0},{9,1... | collective-permute-start | bytes 393224 | tf_op jit(solution)/shard_map/ppermute | solution.py:332
  35.1 19.8 %collective-permute-start.5 = (bf16[128,2176]{1,0:T(8,128)(2,1)S(1)}, bf16[128,2176]{1,0:T(8,128)(2,1)S(1)}, u32[]{:S(2)}, u32[]{:S(2)}) collective-permute-start(bf16[128,2176]{1,0:T(8,128)(2,1)S(1)} %shard_map.70.t0), channel_id=1, source_target_pairs={{0,8},{1,9},{2,10},{3,11},{4,12},{5,13},{6,14},{7,15},{8,16},{9,17... | collective-permute-start | bytes 1671176 | tf_op jit(solution)/shard_map/ppermute | solution.py:332
  35.8 19.0 %collective-permute-start.6 = (bf16[128,2176]{1,0:T(8,128)(2,1)S(1)}, bf16[128,2176]{1,0:T(8,128)(2,1)S(1)}, u32[]{:S(2)}, u32[]{:S(2)}) collective-permute-start(bf16[128,2176]{1,0:T(8,128)(2,1)S(1)} %shard_map.70.t0), channel_id=1, source_target_pairs={{0,24},{1,25},{2,26},{3,27},{4,28},{5,29},{6,30},{7,31},{8,0},{9,1... | collective-permute-start | bytes 1671176 | tf_op jit(solution)/shard_map/ppermute | solution.py:332
  39.5 11.5 %collective-permute-start.10 = (bf16[512,512]{1,0:T(8,128)(2,1)S(1)}, bf16[512,512]{1,0:T(8,128)(2,1)S(1)}, u32[]{:S(2)}, u32[]{:S(2)}) collective-permute-start(bf16[512,512]{1,0:T(8,128)(2,1)S(1)} %shard_map.72.s0), channel_id=1, source_target_pairs={{0,64},{32,96},{64,128},{96,160},{128,192},{160,224},{192,0},{224,... | collective-permute-start | bytes 1572872 | tf_op jit(solution)/shard_map/ppermute | solution.py:327
  42.6 12.1 %collective-permute-start.12 = (bf16[512,512]{1,0:T(8,128)(2,1)S(1)}, bf16[512,512]{1,0:T(8,128)(2,1)S(1)}, u32[]{:S(2)}, u32[]{:S(2)}) collective-permute-start(bf16[512,512]{1,0:T(8,128)(2,1)S(1)} %shard_map.72.s0), channel_id=1, source_target_pairs={{0,192},{32,224},{64,0},{96,32},{128,64},{160,96},{192,128},{224,1... | collective-permute-start | bytes 1572872 | tf_op jit(solution)/shard_map/ppermute | solution.py:327
  51.0 12.2 %collective-permute-start.11 = (bf16[256,512]{1,0:T(8,128)(2,1)S(1)}, bf16[256,512]{1,0:T(8,128)(2,1)S(1)}, u32[]{:S(2)}, u32[]{:S(2)}) collective-permute-start(bf16[256,512]{1,0:T(8,128)(2,1)S(1)} %slice.16), channel_id=1, source_target_pairs={{0,64},{32,96},{64,128},{96,160},{128,192},{160,224},{192,0},{224,... | collective-permute-start | bytes 786440 | tf_op jit(solution)/shard_map/ppermute | solution.py:327
  54.8 8.5 %collective-permute-start.13 = (bf16[256,512]{1,0:T(8,128)(2,1)S(1)}, bf16[256,512]{1,0:T(8,128)(2,1)S(1)}, u32[]{:S(2)}, u32[]{:S(2)}) collective-permute-start(bf16[256,512]{1,0:T(8,128)(2,1)S(1)} %slice.17), channel_id=1, source_target_pairs={{0,192},{32,224},{64,0},{96,32},{128,64},{160,96},{192,128},{224,1... | collective-permute-start | bytes 786440 | tf_op jit(solution)/shard_map/ppermute | solution.py:327
  54.9 8.3 %collective-permute-start.14 = (bf16[64,2176]{1,0:T(8,128)(2,1)S(1)}, bf16[64,2176]{1,0:T(8,128)(2,1)S(1)}, u32[]{:S(2)}, u32[]{:S(2)}) collective-permute-start(bf16[64,2176]{1,0:T(8,128)(2,1)S(1)} %slice.14), channel_id=1, source_target_pairs={{0,8},{1,9},{2,10},{3,11},{4,12},{5,13},{6,14},{7,15},{8,16},{9,17... | collective-permute-start | bytes 835592 | tf_op jit(solution)/shard_map/ppermute | solution.py:332
  57.8 6.8 %collective-permute-start.15 = (bf16[64,2176]{1,0:T(8,128)(2,1)S(1)}, bf16[64,2176]{1,0:T(8,128)(2,1)S(1)}, u32[]{:S(2)}, u32[]{:S(2)}) collective-permute-start(bf16[64,2176]{1,0:T(8,128)(2,1)S(1)} %slice.15), channel_id=1, source_target_pairs={{0,24},{1,25},{2,26},{3,27},{4,28},{5,29},{6,30},{7,31},{8,0},{9,1... | collective-permute-start | bytes 835592 | tf_op jit(solution)/shard_map/ppermute | solution.py:332
  65.8 4.2 %collective-permute-start.16 = (f32[2,512,512]{2,1,0:T(8,128)S(1)}, f32[2,512,512]{2,1,0:T(8,128)S(1)}, u32[]{:S(2)}, u32[]{:S(2)}) collective-permute-start(f32[2,512,512]{2,1,0:T(8,128)S(1)} %shard_map.75), channel_id=1, source_target_pairs={{0,32},{32,0},{64,96},{96,64},{128,160},{160,128},{192,224},{224,1... | collective-permute-start | bytes 6291464 | tf_op jit(solution)/shard_map/ppermute | solution.py:336
  101.2 2.7 %collective-permute-start.24 = (bf16[512,1024]{1,0:T(8,128)(2,1)S(1)}, bf16[512,1024]{1,0:T(8,128)(2,1)S(1)}, u32[]{:S(2)}, u32[]{:S(2)}) collective-permute-start(bf16[512,1024]{1,0:T(8,128)(2,1)S(1)} %shard_map.83), channel_id=1, source_target_pairs={{0,32},{32,0},{64,96},{96,64},{128,160},{160,128},{192,224},{224,1... | collective-permute-start | bytes 3145736 | tf_op jit(solution)/shard_map/ppermute | solution.py:336
  101.3 7.8 %collective-permute-start.17 = (bf16[512,1024]{1,0:T(8,128)(2,1)S(1)}, bf16[512,1024]{1,0:T(8,128)(2,1)S(1)}, u32[]{:S(2)}, u32[]{:S(2)}) collective-permute-start(bf16[512,1024]{1,0:T(8,128)(2,1)S(1)} %get-tuple-element.85), channel_id=1, source_target_pairs={{0,32},{32,0},{64,96},{96,64},{128,160},{160,128},{192,224},{224,1... | collective-permute-start | bytes 3145736 | tf_op jit(solution)/shard_map/ppermute | solution.py:336
  104.1 10.8 %collective-permute-start.25 = (bf16[128,1024]{1,0:T(8,128)(2,1)S(1)}, bf16[128,1024]{1,0:T(8,128)(2,1)S(1)}, u32[]{:S(2)}, u32[]{:S(2)}) collective-permute-start(bf16[128,1024]{1,0:T(8,128)(2,1)S(1)} %get-tuple-element.100), channel_id=1, source_target_pairs={{0,16},{1,17},{2,18},{3,19},{4,20},{5,21},{6,22},{7,23},{8,24},{9,... | collective-permute-start | bytes 786440 | tf_op jit(solution)/shard_map/ppermute | solution.py:332
  105.7 12.5 %collective-permute-start.26 = (bf16[128,1024]{1,0:T(8,128)(2,1)S(1)}, bf16[128,1024]{1,0:T(8,128)(2,1)S(1)}, u32[]{:S(2)}, u32[]{:S(2)}) collective-permute-start(bf16[128,1024]{1,0:T(8,128)(2,1)S(1)} %get-tuple-element.101), channel_id=1, source_target_pairs={{0,24},{1,25},{2,26},{3,27},{4,28},{5,29},{6,30},{7,31},{8,0},{9,1... | collective-permute-start | bytes 786440 | tf_op jit(solution)/shard_map/ppermute | solution.py:332
  107.5 12.2 %collective-permute-start.27 = (bf16[128,1024]{1,0:T(8,128)(2,1)S(1)}, bf16[128,1024]{1,0:T(8,128)(2,1)S(1)}, u32[]{:S(2)}, u32[]{:S(2)}) collective-permute-start(bf16[128,1024]{1,0:T(8,128)(2,1)S(1)} %get-tuple-element.102), channel_id=1, source_target_pairs={{0,8},{1,9},{2,10},{3,11},{4,12},{5,13},{6,14},{7,15},{8,16},{9,17... | collective-permute-start | bytes 786440 | tf_op jit(solution)/shard_map/ppermute | solution.py:332
  109.3 13.6 %collective-permute-start.18 = (bf16[512,256]{1,0:T(8,128)(2,1)S(1)}, bf16[512,256]{1,0:T(8,128)(2,1)S(1)}, u32[]{:S(2)}, u32[]{:S(2)}) collective-permute-start(bf16[512,256]{1,0:T(8,128)(2,1)S(1)} %get-tuple-element.89), channel_id=1, source_target_pairs={{0,128},{32,160},{64,192},{96,224},{128,0},{160,32},{192,64},{224,... | collective-permute-start | bytes 786440 | tf_op jit(solution)/shard_map/ppermute | solution.py:327
  111.7 13.6 %collective-permute-start.19 = (bf16[512,256]{1,0:T(8,128)(2,1)S(1)}, bf16[512,256]{1,0:T(8,128)(2,1)S(1)}, u32[]{:S(2)}, u32[]{:S(2)}) collective-permute-start(bf16[512,256]{1,0:T(8,128)(2,1)S(1)} %get-tuple-element.90), channel_id=1, source_target_pairs={{0,192},{32,224},{64,0},{96,32},{128,64},{160,96},{192,128},{224,1... | collective-permute-start | bytes 786440 | tf_op jit(solution)/shard_map/ppermute | solution.py:327
  114.9 10.3 %collective-permute-start.20 = (bf16[512,256]{1,0:T(8,128)(2,1)S(1)}, bf16[512,256]{1,0:T(8,128)(2,1)S(1)}, u32[]{:S(2)}, u32[]{:S(2)}) collective-permute-start(bf16[512,256]{1,0:T(8,128)(2,1)S(1)} %get-tuple-element.91), channel_id=1, source_target_pairs={{0,64},{32,96},{64,128},{96,160},{128,192},{160,224},{192,0},{224,... | collective-permute-start | bytes 786440 | tf_op jit(solution)/shard_map/ppermute | solution.py:327
  119.8 9.2 %collective-permute-start.28 = (bf16[128,256]{1,0:T(8,128)(2,1)S(1)}, bf16[128,256]{1,0:T(8,128)(2,1)S(1)}, u32[]{:S(2)}, u32[]{:S(2)}) collective-permute-start(bf16[128,256]{1,0:T(8,128)(2,1)S(1)} %get-tuple-element.104), channel_id=1, source_target_pairs={{0,128},{32,160},{64,192},{96,224},{128,0},{160,32},{192,64},{224,... | collective-permute-start | bytes 196616 | tf_op jit(solution)/shard_map/ppermute | solution.py:327
  122.0 7.8 %collective-permute-start.29 = (bf16[128,256]{1,0:T(8,128)(2,1)S(1)}, bf16[128,256]{1,0:T(8,128)(2,1)S(1)}, u32[]{:S(2)}, u32[]{:S(2)}) collective-permute-start(bf16[128,256]{1,0:T(8,128)(2,1)S(1)} %get-tuple-element.105), channel_id=1, source_target_pairs={{0,192},{32,224},{64,0},{96,32},{128,64},{160,96},{192,128},{224,1... | collective-permute-start | bytes 196616 | tf_op jit(solution)/shard_map/ppermute | solution.py:327
  122.8 6.9 %collective-permute-start.30 = (bf16[128,256]{1,0:T(8,128)(2,1)S(1)}, bf16[128,256]{1,0:T(8,128)(2,1)S(1)}, u32[]{:S(2)}, u32[]{:S(2)}) collective-permute-start(bf16[128,256]{1,0:T(8,128)(2,1)S(1)} %get-tuple-element.106), channel_id=1, source_target_pairs={{0,64},{32,96},{64,128},{96,160},{128,192},{160,224},{192,0},{224,... | collective-permute-start | bytes 196616 | tf_op jit(solution)/shard_map/ppermute | solution.py:327
  126.0 5.9 %collective-permute-start.21 = (bf16[128,256]{1,0:T(8,128)(2,1)S(1)}, bf16[128,256]{1,0:T(8,128)(2,1)S(1)}, u32[]{:S(2)}, u32[]{:S(2)}) collective-permute-start(bf16[128,256]{1,0:T(8,128)(2,1)S(1)} %get-tuple-element.93), channel_id=1, source_target_pairs={{0,16},{1,17},{2,18},{3,19},{4,20},{5,21},{6,22},{7,23},{8,24},{9,... | collective-permute-start | bytes 196616 | tf_op jit(solution)/shard_map/ppermute | solution.py:332
  127.7 5.3 %collective-permute-start.22 = (bf16[128,256]{1,0:T(8,128)(2,1)S(1)}, bf16[128,256]{1,0:T(8,128)(2,1)S(1)}, u32[]{:S(2)}, u32[]{:S(2)}) collective-permute-start(bf16[128,256]{1,0:T(8,128)(2,1)S(1)} %get-tuple-element.94), channel_id=1, source_target_pairs={{0,24},{1,25},{2,26},{3,27},{4,28},{5,29},{6,30},{7,31},{8,0},{9,1... | collective-permute-start | bytes 196616 | tf_op jit(solution)/shard_map/ppermute | solution.py:332
  129.0 5.5 %collective-permute-start.23 = (bf16[128,256]{1,0:T(8,128)(2,1)S(1)}, bf16[128,256]{1,0:T(8,128)(2,1)S(1)}, u32[]{:S(2)}, u32[]{:S(2)}) collective-permute-start(bf16[128,256]{1,0:T(8,128)(2,1)S(1)} %get-tuple-element.95), channel_id=1, source_target_pairs={{0,8},{1,9},{2,10},{3,11},{4,12},{5,13},{6,14},{7,15},{8,16},{9,17... | collective-permute-start | bytes 196616 | tf_op jit(solution)/shard_map/ppermute | solution.py:332
  135.2 12.4 %all-to-all-start.3 = ((bf16[8,16,512]{2,1,0:T(8,128)(2,1)}), bf16[8,16,512]{2,1,0:T(8,128)(2,1)S(1)}, u32[]{:S(2)}, u32[]{:S(2)}) async-start(bf16[8,16,512]{2,1,0:T(8,128)(2,1)} %bitcast.5), calls=%async_computation.3 | async-start | bytes 262144 | tf_op jit(solution)/shard_map/all_to_all | solution.py:239

commit v6 on v3

v6 whole, which is shorter than its diff:
```python
import functools

import jax
import jax.numpy as jnp
from jax import lax
from jax.experimental import pallas as pl
from jax.experimental.pallas import tpu as pltpu
from jax.sharding import PartitionSpec as P

BF = jnp.bfloat16
F32 = jnp.float32
TOK, VOC = 32, 8
NX, NY, NZ = 4, 4, 8
N = 512
D = 4096
C = 512
W = 512
ROWS = N // TOK
NEAR = N // NY
HALF = NX * W
MIB = 1 << 20
STEPS = (0, -1, 1, 2)
Z_GROUPS = [[y * NZ + z for z in range(NZ)] for y in range(NY)]


def dot(a, b, dims=((1,), (0,))):
    return lax.dot_general(a, b, (dims, ((), ())), preferred_element_type=F32)


PARAMS = pltpu.CompilerParams(vmem_limit_bytes=20 * MIB)
VM = pl.BlockSpec(memory_space=pltpu.VMEM)
SM = pl.BlockSpec(memory_space=pltpu.SMEM)
HBM = pl.BlockSpec(memory_space=pltpu.HBM)


def out(shape, dtype):
    return pltpu.VMEM(shape, dtype)


def in_hbm(x):
    return pltpu.with_memory_space_constraint(x, pltpu.HBM)


def cost(flops, mib=0):
    return pl.CostEstimate(flops=flops, bytes_accessed=mib * MIB, transcendentals=0)


def call(kernel, in_specs, outs, *args, scratch=(), flops=0):
    return pl.pallas_call(
        kernel,
        in_specs=in_specs,
        out_specs=[VM] * len(outs),
        out_shape=[out(*o) for o in outs],
        scratch_shapes=list(scratch),
        compiler_params=PARAMS,
        cost_estimate=cost(flops),
    )(*args)


def at_block(index, size):
    return pl.ds(pl.multiple_of(index * size, size), size)


def started(src, dst, sem):
    copy = pltpu.make_async_copy(src, dst, sem)
    copy.start()
    return copy


def pack_kernel(source_ref, s_ref, t_ref, out_ref, s_buf, t_buf, sem):
    v = lax.axis_index("vocab")
    columns = at_block(v % 2 * NX + v // 2, W)
    copies = [
        started(s_ref.at[:, columns], s_buf, sem.at[0]),
        started(t_ref.at[:, columns], t_buf, sem.at[1]),
    ]
    row = lax.broadcasted_iota(jnp.int32, (ROWS, 128), 0)
    lane = lax.broadcasted_iota(jnp.int32, (ROWS, 128), 1)
    digits = jnp.zeros((ROWS, 128), jnp.int32)
    for r in range(ROWS):
        source = source_ref[r]
        value = jnp.where(lane == 0, source >> 5, jnp.where(lane == 1, source & 31, 0))
        digits = jnp.where(row == r, value, digits)
    digits = digits.astype(F32).astype(BF)
    out_ref[:, :, 2 * W :] = jnp.broadcast_to(digits[None], (NZ, ROWS, 128))
    for k, (copy, buf) in enumerate(zip(copies, (s_buf, t_buf))):
        copy.wait()
        out_ref[:, :, k * W : (k + 1) * W] = jnp.broadcast_to(buf[...][None], (NZ, ROWS, W))


def join_kernel(place_ref, far_ref, own_ref, left_ref, right_ref, out_ref, digits_ref):
    for k, (step, ref) in enumerate(zip(STEPS, (own_ref, left_ref, right_ref, far_ref))):
        out_ref[k * NEAR : (k + 1) * NEAR] = ref[:, : 2 * W]
        digits_ref[at_block((place_ref[2] + step) % NY, NEAR)] = ref[:, 2 * W :]


def hold_kernel(place_ref, sw_ref, tw_ref, sw2_ref, tw2_ref, sw_out, tw_out, sw2_out, tw2_out, sem):
    half = at_block(place_ref[1], HALF)
    copies = [
        started(sw_ref, sw_out, sem.at[0]),
        started(tw_ref.at[half], tw_out, sem.at[1]),
        started(sw2_ref.at[half], sw2_out, sem.at[2]),
        started(tw2_ref.at[half], tw2_out, sem.at[3]),
    ]
    for copy in copies:
        copy.wait()


def weights(place_ref, own, refs, step):
    at = (place_ref[0] + step) % NX
    first = place_ref[1] * NX if own else 0
    return refs[0][at_block(first + at, W)], refs[1][at_block(at, W)]


def near_kernel(own, place_ref, sw_ref, tw_ref, p0, p1, p2, out_ref):
    pieces = (p0, p1, p2)
    y = place_ref[2]

    @pl.when(place_ref[1] == 0)
    def _():
        for n in range(2):
            columns = slice(n * W, (n + 1) * W)
            total = None
            for step, ref in zip(STEPS, pieces):
                weight = weights(place_ref, own, (sw_ref, tw_ref), step)[n]
                part = dot(ref[:, columns], weight)
                total = part if total is None else total + part
            for k, step in enumerate(STEPS):
                out_ref[n, at_block((y + step) % NY, NEAR)] = total[k * NEAR : (k + 1) * NEAR]

    @pl.when(place_ref[1] == 1)
    def _():
        for n in range(2):
            columns = slice(n * W, (n + 1) * W)
            total = None
            for k, step in enumerate(STEPS):
                rows = slice(k * NEAR, (k + 1) * NEAR)
                block = jnp.concatenate([ref[rows, columns] for ref in pieces], axis=0)
                part = dot(block, weights(place_ref, own, (sw_ref, tw_ref), step)[n])
                total = part if total is None else total + part
            for k, step in enumerate(STEPS[:3]):
                out_ref[n, at_block((y + step) % NY, NEAR)] = total[k * NEAR : (k + 1) * NEAR]


def far_kernel(own, place_ref, sw_ref, tw_ref, p3, p4, near_ref, *refs):
    y = place_ref[2]
    outs = refs[:2]

    @pl.when(place_ref[1] == 0)
    def _():
        for n, out_ref in enumerate(outs):
            columns = slice(n * W, (n + 1) * W)
            block = jnp.concatenate([p3[:, columns], p4[:, columns]], axis=0)
            part = dot(block, weights(place_ref, own, (sw_ref, tw_ref), STEPS[3])[n])
            for k, step in enumerate(STEPS):
                rows = at_block((y + step) % NY, NEAR)
                out_ref[rows] = near_ref[n, rows] + part[k * NEAR : (k + 1) * NEAR]

    @pl.when(place_ref[1] == 1)
    def _():
        for n, out_ref in enumerate(outs):
            columns = slice(n * W, (n + 1) * W)
            for step in STEPS[:3]:
                rows = at_block((y + step) % NY, NEAR)
                out_ref[rows] = near_ref[n, rows]
            total = None
            for k, step in enumerate(STEPS):
                rows = slice(k % 2 * NEAR, (k % 2 + 1) * NEAR)
                block = (p3, p4)[k // 2][rows, columns]
                part = dot(block, weights(place_ref, own, (sw_ref, tw_ref), step)[n])
                total = part if total is None else total + part
            out_ref[at_block((y + STEPS[3]) % NY, NEAR)] = total


def choose_kernel(place_ref, own_ref, other_ref, out_ref):
    digits = jnp.where(
        place_ref[1] == 0, own_ref[...].astype(F32), other_ref[...].astype(F32)
    )
    index = (digits[:, 0:1] * 32.0 + digits[:, 1:2]).astype(jnp.int32)
    column = lax.broadcasted_iota(jnp.int32, (N, N), 1)
    out_ref[...] = (index == column).astype(F32).astype(BF)


def pack_stats(lse_s, mean, lse_t):
    half = N // 2
    row = lax.broadcasted_iota(jnp.int32, (8, half), 0)
    out = jnp.zeros((8, half), F32)
    for k, value in enumerate((lse_s, mean, lse_t)):
        out = jnp.where(row == k, value[:, :half], out)
        out = jnp.where(row == k + 4, value[:, half:], out)
    return out


def merge(stats):
    def rows(k):
        return jnp.concatenate([stats[:, k : k + 1], stats[:, k + 4 : k + 5]], axis=2)

    def lse(x):
        top = jnp.max(x, axis=0)
        return top + jnp.log(jnp.sum(jnp.exp(x - top[None]), axis=0))

    each_s, each_mean, each_t = rows(0), rows(1), rows(2)
    lse_s = lse(each_s)
    mean = jnp.sum(jnp.exp(each_s - lse_s[None]) * each_mean, axis=0)
    return lse_s, mean, lse(each_t)


def table_of(pairs, table):
    lane = lax.broadcasted_iota(jnp.int32, (N, 128), 1)
    for k, value in pairs:
        table = jnp.where(lane == k, value, table)
    return table


def teacher_logits_kernel(own_ref, other_ref, select_ref, t_ref, table_ref):
    t = own_ref[...] + other_ref[...]
    select = select_ref[...]
    high = t.astype(BF)
    rest = t - high.astype(F32)
    middle = rest.astype(BF)
    low = (rest - middle.astype(F32)).astype(BF)
    t = dot(select, high) + dot(select, middle) + dot(select, low)
    t_ref[...] = t
    top = jnp.max(t, axis=1, keepdims=True)
    total = jnp.sum(jnp.exp(t - top), axis=1, keepdims=True)
    table_ref[...] = table_of(((3, top), (4, total)), jnp.zeros((N, 128), F32))


def student_logits_kernel(own_ref, other_ref, t_ref, table_ref, s_ref, diff_ref, stat_ref):
    s = own_ref[...] + other_ref[...]
    s_ref[...] = s
    diff = s - t_ref[...]
    diff_ref[...] = diff
    top = jnp.max(s, axis=1, keepdims=True)
    e = jnp.exp(s - top)
    total = jnp.sum(e, axis=1, keepdims=True)
    mix = jnp.sum(e * diff, axis=1, keepdims=True)
    table = table_of(((0, top), (1, total), (2, mix)), table_ref[...])
    table = jnp.transpose(table)
    s_top, s_sum, mix, t_top, t_sum = (table[k : k + 1] for k in range(5))
    stat = pack_stats(s_top + jnp.log(s_sum), mix / s_sum, t_top + jnp.log(t_sum))
    stat_ref[...] = jnp.broadcast_to(stat[None], stat_ref.shape)


def merge_kernel(in_ref, out_ref):
    out_ref[...] = jnp.broadcast_to(pack_stats(*merge(in_ref[...]))[None], out_ref.shape)


def exchange(x, axis, groups=None):
    n = x.shape[0]
    flat = x.reshape((n * x.shape[1],) + x.shape[2:])
    out = lax.all_to_all(flat, axis, 0, 0, axis_index_groups=groups, tiled=True)
    return out.reshape(x.shape)


def terms(place_ref, g, sw_ref, core, numbers):
    for k in numbers:
        block = (place_ref[0] + STEPS[k]) % NX * 2 + core
        yield dot(g, sw_ref[at_block(block, W)], ((1,), (1,)))


def first_for_other_kernel(
    place_ref, stat_ref, s_ref, d_ref, sw_ref, out_ref, turned_ref, loss_ref, g_ref
):
    lse_s, mean, lse_t = merge(stat_ref[...])
    loss_ref[...] = jnp.sum(mean - lse_s + lse_t, axis=1, keepdims=True) / N
    row = lax.broadcasted_iota(jnp.int32, (128, N), 0)
    table = jnp.where(row == 0, lse_s, jnp.where(row == 1, mean, 0.0))
    table = jnp.transpose(table)
    prob = jnp.exp(s_ref[...] - table[:, 0:1])
    g_ref[...] = prob * (d_ref[...] - table[:, 1:2])
    for k, step in enumerate(STEPS):
        rows = g_ref[at_block((place_ref[2] + step) % NY, NEAR)]
        turned_ref[k * NEAR : (k + 1) * NEAR] = rows.astype(BF)
    for k, part in enumerate(terms(place_ref, turned_ref[...], sw_ref, 1 - place_ref[1], (0, 1))):
        out_ref[k] = part.astype(BF)


def second_for_other_kernel(place_ref, g_ref, sw_ref, out_ref):
    for k, part in enumerate(terms(place_ref, g_ref[...], sw_ref, 1 - place_ref[1], (2, 3))):
        out_ref[k] = part.astype(BF)


def own_terms_kernel(place_ref, g_ref, sw_ref, out_ref):
    for k, part in enumerate(terms(place_ref, g_ref[...], sw_ref, place_ref[1], range(NX))):
        out_ref[k] = part


def add_kernel(place_ref, own_ref, first_ref, second_ref, *out_refs):
    core = place_ref[1]
    for k in range(NX):
        received = (first_ref, second_ref)[k // 2][k % 2]
        total = (own_ref[k] + received.astype(F32)).astype(BF)

        @pl.when(core == 0)
        def _():
            out_refs[k][...] = total

        @pl.when(core == 1)
        def _():
            for j, ref in enumerate(out_refs):
                ref[k * NEAR : (k + 1) * NEAR] = total[j * NEAR : (j + 1) * NEAR]


def total_of(refs):
    total = refs[0][...].astype(F32)
    for ref in refs[1:]:
        total = total + ref[...].astype(F32)
    return total.astype(BF)


def sum_first_kernel(*refs):
    total = total_of(refs[:4])
    for k, ref in enumerate(refs[4:]):
        ref[...] = total[k * NEAR : (k + 1) * NEAR]


def sum_second_kernel(*refs):
    refs[-1][...] = total_of(refs[:4])


def sum_kernel(in_ref, out_ref):
    out_ref[...] = jnp.sum(in_ref[...].astype(F32), axis=0).astype(BF)


def summed(x):
    return call(sum_kernel, [VM], [(x.shape[1:], BF)], x)[0]


def to_other_core(a):
    return lax.ppermute(a, "vocab", [(k, k ^ 1) for k in range(VOC)])


def along_rings(a, step, x_core):
    pairs = []
    for v in range(VOC):
        for t in range(TOK):
            if v % 2 == x_core:
                to = (v // 2 + step) % NX * 2 + v % 2, t
            else:
                to = v, (t // NZ + step) % NY * NZ + t % NZ
            pairs.append((v * TOK + t, to[0] * TOK + to[1]))
    return lax.ppermute(a, ("vocab", "tok"), pairs)


def along_first(a, step):
    return along_rings(a, step, 0)


def along_second(a, step):
    return along_rings(a, step, 1)


def ring(a, along):
    return along(a, 2), a, along(a, 1), along(a, -1)


def to_ring(blocks, along):
    own, left, right, far = blocks
    return along(far, 2), along(left, -1), along(right, 1), own


def per_device(student_hidden, teacher_hidden, student_weight, teacher_weight, source_rows):
    v = lax.axis_index("vocab").astype(jnp.int32)
    y = lax.axis_index("tok").astype(jnp.int32) // NZ
    place = jnp.stack([v // 2, v % 2, y])
    packed = call(
        pack_kernel,
        [SM, HBM, HBM],
        [((NZ, ROWS, 2 * W + 128), BF)],
        source_rows, in_hbm(student_hidden), in_hbm(teacher_hidden),
        scratch=[pltpu.VMEM((ROWS, W), BF)] * 2 + [pltpu.SemaphoreType.DMA((2,))],
    )[0]
    sw2, tw2 = to_other_core(student_weight), to_other_core(teacher_weight)
    near = exchange(packed, "tok", Z_GROUPS).reshape(NEAR, 2 * W + 128)
    near, sw2, tw2 = lax.optimization_barrier((near, sw2, tw2))
    mine, digits = call(
        join_kernel,
        [SM] + [VM] * 4,
        [((N, 2 * W), BF), ((N, 128), BF)],
        place, *ring(near, along_second),
    )
    left, right = along_first(mine, 1), along_first(mine, -1)
    held = call(
        hold_kernel,
        [SM] + [HBM] * 4,
        [((D, C), BF)] + [((HALF, C), BF)] * 3,
        place, *(in_hbm(x) for x in (student_weight, teacher_weight, sw2, tw2)),
        scratch=[pltpu.SemaphoreType.DMA((4,))],
    )
    left, right, held = lax.optimization_barrier((left, right, held))
    sw, tw, sw2, tw2 = held
    far = along_first(left[: N // 2], 1), along_first(right[N // 2 :], -1)
    digits2 = to_other_core(digits)
    part = [((2, N, C), F32)]

    def near_part(own, *held):
        kernel = functools.partial(near_kernel, own)
        flops = 3 * N * HALF * C
        return call(kernel, [SM] + [VM] * 5, part, place, *held, mine, left, right, flops=flops)[0]

    logits = [((N, C), F32)]

    def far_part(own, *held_and_near):
        kernel = functools.partial(far_kernel, own)
        sw, tw, near = held_and_near
        return call(kernel, [SM] + [VM] * 5, logits * 2, place, sw, tw, *far, near)

    for_other, own = near_part(False, sw2, tw2), near_part(True, sw, tw)
    select = call(choose_kernel, [SM, VM, VM], [((N, N), BF)], place, digits, digits2)[0]
    far, for_other, own, select = lax.optimization_barrier((far, for_other, own, select))
    s_other, t_other = far_part(False, sw2, tw2, for_other)
    t_other, s_other = to_other_core(t_other), to_other_core(s_other)
    s_own, t_own = far_part(True, sw, tw, own)
    t_own, t_other = lax.optimization_barrier((t_own, t_other))
    t, table = call(
        teacher_logits_kernel,
        [VM] * 3,
        logits + [((N, 128), F32)],
        t_own, t_other, select,
    )
    s_other, t, table = lax.optimization_barrier((s_other, t, table))
    s, d, stats = call(
        student_logits_kernel,
        [VM] * 4,
        logits * 2 + [((VOC, 8, N // 2), F32)],
        s_own, s_other, t, table,
    )
    stats = exchange(stats, "vocab")
    stats = call(merge_kernel, [VM], [((TOK, 8, N // 2), F32)], stats)[0]
    stats = exchange(stats, "tok")
    half = ((NX // 2, N, W), BF)
    first, g, loss = call(
        first_for_other_kernel,
        [SM] + [VM] * 4,
        [half, ((N, C), BF), ((1, 1), F32)],
        place, stats, s, d, sw,
        scratch=[pltpu.VMEM((N, C), F32)],
    )
    second = call(second_for_other_kernel, [SM, VM, VM], [half], place, g, sw)[0]
    own = call(
        own_terms_kernel, [SM, VM, VM], [((NX, N, W), F32)], place, g, sw
    )[0]
    first, second, own = lax.optimization_barrier(
        (to_other_core(first), to_other_core(second), own)
    )
    blocks = call(
        add_kernel, [SM] + [VM] * 3, [((N, W), BF)] * 4, place, own, first, second
    )
    blocks = call(
        sum_first_kernel, [VM] * 4, [((NEAR, W), BF)] * 4, *to_ring(blocks, along_first)
    )
    partial = call(
        sum_second_kernel, [VM] * 4, [((NEAR, W), BF)], *to_ring(blocks, along_second)
    )[0]
    hidden_grad = summed(exchange(partial.reshape(NZ, ROWS, W), "tok", Z_GROUPS))
    return loss[0, 0], hidden_grad


def solution(mesh):
    in_specs = (
        P("tok", None),
        P("tok", None),
        P(None, ("vocab", "tok")),
        P(None, ("vocab", "tok")),
        P("tok"),
    )
    out_specs = (P(), P("tok", "vocab"))
    return jax.shard_map(
        per_device, mesh=mesh, in_specs=in_specs, out_specs=out_specs, check_vma=False
    )
```

time: 164 us -> 146 us (0.89); the launches traced: 161 us -> 145 us
  blocking collectives: 73.9 us -> 45.7 us
  waiting for transfers between devices: 39.5 us -> 47 us
  Pallas kernels: 19.6 us -> 24 us
    all_to_all x4 -> x3, blocking collectives: 73.9 us -> 45.7 us  [exchange(): out = lax.all_to_all(flat, axis, 0, 0, axis_index_groups=groups, tiled=True)]
    ppermute x14 -> x13, waiting for transfers between devices: 17.3 us -> 33.8 us  [along_rings(): return lax.ppermute(a, ('vocab', 'tok'), pairs)]
    all_to_all x1, waiting for transfers between devices: 16.8 us -> 8.96 us  [exchange(): out = lax.all_to_all(flat, axis, 0, 0, axis_index_groups=groups, tiled=True)]
    pallas_call x12 -> x18, Pallas kernels: 19.6 us -> 24 us  [call(): pl.pallas_call(kernel, in_specs=in_specs, out_specs=[VM] * len(outs), out...]
    ppermute x4 -> x7, waiting for transfers between devices: 5.42 us -> 4.29 us  [to_other_core(): return lax.ppermute(a, 'vocab', [(k, k ^ 1) for k in range(VOC)])]
    ppermute x14 -> x13, starting transfers between devices: 19.8 us -> 19.8 us  [along_rings(): return lax.ppermute(a, ('vocab', 'tok'), pairs)]
  transfers between devices with their start and end apart: 19 -> 21, of which waited for: 11 -> 17; matrix products, arithmetic and copies ran while one was open for 0% -> 0% of each run, Pallas kernels for 5% -> 11%
where the time goes in v6:
time: 146 us; the launch traced here: 145 us
  waiting for transfers between devices  47 us (32%)
  blocking collectives  45.7 us (31%)
  starting transfers between devices  25 us (17%)
  Pallas kernels  24 us (16%)
  between operations  1.98 us (1%)
    all_to_all x3, blocking collectives, exchange(): out = lax.all_to_all(flat, axis, 0, 0, axis_index_groups=groups, tiled=True)  45.7 us
    ppermute x13, waiting for transfers between devices, along_rings(): return lax.ppermute(a, ('vocab', 'tok'), pairs)  33.8 us
    pallas_call x18, Pallas kernels, call(): pl.pallas_call(kernel, in_specs=in_specs, out_specs=[VM] * len(outs), out...  24 us
    ppermute x13, starting transfers between devices, along_rings(): return lax.ppermute(a, ('vocab', 'tok'), pairs)  19.8 us
    all_to_all x1, waiting for transfers between devices, exchange(): out = lax.all_to_all(flat, axis, 0, 0, axis_index_groups=groups, tiled=True)  8.96 us
    ppermute x7, waiting for transfers between devices, to_other_core(): return lax.ppermute(a, 'vocab', [(k, k ^ 1) for k in range(VOC)])  4.29 us
    all_to_all x1, starting transfers between devices, exchange(): out = lax.all_to_all(flat, axis, 0, 0, axis_index_groups=groups, tiled=True)  3.37 us
  transfers between devices with their start and end apart: 21, of which 17 were waited for; matrix products, arithmetic and copies ran while one was open for 0% of the time, Pallas kernels for 11%

profile of v6, /device:TPU:6, one launch (start us, length us, event | category | flops | bytes accessed | tf_op | source)
XLA Modules:
  0.0 145.1 jit_solution(10373573203743105694)
XLA Ops:
  0.6 0.1 collective-permute-start
  0.7 0.5 collective-permute-start.1
  1.2 0.7 copy-done
  1.9 1.3 shard_map.68
  3.2 21.1 %all_to_all.30 = bf16[8,16,1152]{2,1,0:T(8,128)(2,1)S(1)} all-to-all(bf16[8,16,1152]{2,1,0:T(8,128)(2,1)S(1)} %shard_map.68), channel_id=1, replica_groups={{0,1,2,3,4,5,6,7},{8,9,10,11,12,13,14,15},{16,17,18,19,20,21,22,23},{24..., dimensions={0} | all-to-all | bytes 589824 | tf_op jit(solution)/shard_map/all_to_all | solution.py:252
  24.3 0.0 collective-permute-done.sw2_ref
  24.3 0.0 collective-permute-done.1.tw2_ref
  24.3 3.3 %collective-permute-start.2 = (bf16[128,1152]{1,0:T(8,128)(2,1)S(1)}, bf16[128,1152]{1,0:T(8,128)(2,1)S(1)}, u32[]{:S(2)}, u32[]{:S(2)}) collective-permute-start(bf16[128,1152]{1,0:T(8,128)(2,1)S(1)} %bitcast.6), channel_id=1, source_target_pairs={{0,16},{1,17},{2,18},{3,19},{4,20},{5,21},{6,22},{7,23},{8,24},{9,... | collective-permute-start | bytes 884744 | tf_op jit(solution)/shard_map/ppermute | solution.py:343
  27.6 0.7 collective-permute-start.3
  28.3 2.6 %collective-permute-start.4 = (bf16[128,1152]{1,0:T(8,128)(2,1)S(1)}, bf16[128,1152]{1,0:T(8,128)(2,1)S(1)}, u32[]{:S(2)}, u32[]{:S(2)}) collective-permute-start(bf16[128,1152]{1,0:T(8,128)(2,1)S(1)} %bitcast.8), channel_id=1, source_target_pairs={{0,24},{1,25},{2,26},{3,27},{4,28},{5,29},{6,30},{7,31},{8,0},{9,1... | collective-permute-start | bytes 884744 | tf_op jit(solution)/shard_map/ppermute | solution.py:343
  30.9 0.1 pad_add_fusion.place_ref
  30.9 1.7 %collective-permute-done.2.far_ref = bf16[128,1152]{1,0:T(8,128)(2,1)S(1)} collective-permute-done((bf16[128,1152]{1,0:T(8,128)(2,1)S(1)}, bf16[128,1152]{1,0:T(8,128)(2,1)S(1)}, u32[]{:S(2)}, u32[]{:S(2)}) %collective-permute-start.2) | collective-permute-done | bytes 294944 | tf_op jit(solution)/shard_map/ppermute | solution.py:343
  32.7 3.1 %collective-permute-done.3.left_ref = bf16[128,1152]{1,0:T(8,128)(2,1)S(1)} collective-permute-done((bf16[128,1152]{1,0:T(8,128)(2,1)S(1)}, bf16[128,1152]{1,0:T(8,128)(2,1)S(1)}, u32[]{:S(2)}, u32[]{:S(2)}) %collective-permute-start.3) | collective-permute-done | bytes 294944 | tf_op jit(solution)/shard_map/ppermute | solution.py:343
  35.8 0.3 collective-permute-done.4.right_ref
  36.2 0.6 shard_map.69
  36.8 0.6 collective-permute-start.5
  37.4 1.5 %collective-permute-start.6 = (bf16[512,1024]{1,0:T(8,128)(2,1)S(1)}, bf16[512,1024]{1,0:T(8,128)(2,1)S(1)}, u32[]{:S(2)}, u32[]{:S(2)}) collective-permute-start(bf16[512,1024]{1,0:T(8,128)(2,1)S(1)} %get-tuple-element.51.p0), channel_id=1, source_target_pairs={{0,192},{1,193},{2,194},{3,195},{4,196},{5,197},{6,198},{7,199},{8... | collective-permute-start | bytes 3145736 | tf_op jit(solution)/shard_map/ppermute | solution.py:343
  38.9 4.6 %shard_map.70 = (bf16[4096,512]{1,0:T(8,128)(2,1)S(1)}, bf16[2048,512]{1,0:T(8,128)(2,1)S(1)}, bf16[2048,512]{1,0:T(8,128)(2,1)S(1)}, bf16[2048,512]{1,0:T(8,128)(2,1)S(1)}) custom-call(s32[3]{0:T(128)S(1)} %pad_add_fusion.place_ref, bf16[4096,512]{1,0:T(8,128)(2,1)} %sw_ref.1, bf16[4096,512]{1,0:T(8,128)(2,1)} %tw_ref.1, bf16[4096,512]{1,0:T(8,128)(2,1)} %copy-done.1, ...), custom_call_target="tpu_custom_call" | custom-call | tf_op jit(solution)/shard_map/pallas_call | solution.py:49
  43.6 8.1 %collective-permute-done.5.p1 = bf16[512,1024]{1,0:T(8,128)(2,1)S(1)} collective-permute-done((bf16[512,1024]{1,0:T(8,128)(2,1)S(1)}, bf16[512,1024]{1,0:T(8,128)(2,1)S(1)}, u32[]{:S(2)}, u32[]{:S(2)}) %collective-permute-start.5) | collective-permute-done | bytes 1048608 | tf_op jit(solution)/shard_map/ppermute | solution.py:343
  51.7 1.7 %collective-permute-done.6.p2 = bf16[512,1024]{1,0:T(8,128)(2,1)S(1)} collective-permute-done((bf16[512,1024]{1,0:T(8,128)(2,1)S(1)}, bf16[512,1024]{1,0:T(8,128)(2,1)S(1)}, u32[]{:S(2)}, u32[]{:S(2)}) %collective-permute-start.6) | collective-permute-done | bytes 1048608 | tf_op jit(solution)/shard_map/ppermute | solution.py:343
  53.4 0.4 collective-permute-start.7
  53.8 1.8 %collective-permute-start.8 = (bf16[256,1024]{1,0:T(8,128)(2,1)S(1)}, bf16[256,1024]{1,0:T(8,128)(2,1)S(1)}, u32[]{:S(2)}, u32[]{:S(2)}) collective-permute-start(bf16[256,1024]{1,0:T(8,128)(2,1)S(1)} %slice.7), channel_id=1, source_target_pairs={{0,192},{1,193},{2,194},{3,195},{4,196},{5,197},{6,198},{7,199},{8... | collective-permute-start | bytes 1572872 | tf_op jit(solution)/shard_map/ppermute | solution.py:343
  55.6 0.0 collective-permute-start.9
  55.6 1.3 collective-permute-done.9.other_ref
  57.0 0.8 shard_map.73.select_ref
  57.7 2.3 %shard_map.72.near_ref = f32[2,512,512]{2,1,0:T(8,128)S(1)} custom-call(s32[3]{0:T(128)S(1)} %pad_add_fusion.place_ref, bf16[4096,512]{1,0:T(8,128)(2,1)S(1)} %get-tuple-element.58.sw_ref, bf16[2048,512]{1,0:T(8,128)(2,1)S(1)} %get-tuple-element.59.tw_ref, bf16[512,1024]{1,0:T(8,128)(2,1)S(1)} %get-tuple-element.51.p0, ...), custom_call_target="tpu_custom_call" | custom-call | flops 1610612736 | tf_op jit(solution)/shard_map/pallas_call | solution.py:49
  60.1 2.3 %shard_map.71.near_ref = f32[2,512,512]{2,1,0:T(8,128)S(1)} custom-call(s32[3]{0:T(128)S(1)} %pad_add_fusion.place_ref, bf16[2048,512]{1,0:T(8,128)(2,1)S(1)} %get-tuple-element.62.sw_ref, bf16[2048,512]{1,0:T(8,128)(2,1)S(1)} %get-tuple-element.63.tw_ref, bf16[512,1024]{1,0:T(8,128)(2,1)S(1)} %get-tuple-element.51.p0, ...), custom_call_target="tpu_custom_call" | custom-call | flops 1610612736 | tf_op jit(solution)/shard_map/pallas_call | solution.py:49
  62.4 0.2 collective-permute-done.7.p3
  62.7 1.6 %collective-permute-done.8.p4 = bf16[256,1024]{1,0:T(8,128)(2,1)S(1)} collective-permute-done((bf16[256,1024]{1,0:T(8,128)(2,1)S(1)}, bf16[256,1024]{1,0:T(8,128)(2,1)S(1)}, u32[]{:S(2)}, u32[]{:S(2)}) %collective-permute-start.8) | collective-permute-done | bytes 524320 | tf_op jit(solution)/shard_map/ppermute | solution.py:343
  64.3 1.4 shard_map.75
  65.7 0.1 collective-permute-start.11
  65.8 0.5 collective-permute-start.10
  66.3 1.3 shard_map.74
  67.6 0.9 collective-permute-done.11.other_ref
  68.5 1.2 shard_map.76
  69.7 0.3 collective-permute-done.10.other_ref
  70.0 0.5 shard_map.77
  70.5 7.9 %all_to_all.31.in_ref = f32[8,8,256]{2,1,0:T(8,128)S(1)} all-to-all(f32[8,8,256]{2,1,0:T(8,128)S(1)} %get-tuple-element.81), channel_id=1, replica_groups=mesh['vocab'=8,'tok'=32] {'vocab'}, dimensions={0} | all-to-all | bytes 131072 | tf_op jit(solution)/shard_map/all_to_all | solution.py:252
  78.4 0.1 shard_map.78
  78.5 16.7 %all_to_all.32.stat_ref = f32[32,8,256]{2,1,0:T(8,128)S(1)} all-to-all(f32[32,8,256]{2,1,0:T(8,128)S(1)} %shard_map.78), channel_id=1, replica_groups=mesh['vocab'=8,'tok'=32] {'tok'}, dimensions={0} | all-to-all | bytes 524288 | tf_op jit(solution)/shard_map/all_to_all | solution.py:252
  95.2 2.0 %shard_map.79 = (bf16[2,512,512]{2,1,0:T(8,128)(2,1)S(1)}, bf16[512,512]{1,0:T(8,128)(2,1)S(1)}, f32[1,1]{1,0:T(1,128)S(1)}) custom-call(s32[3]{0:T(128)S(1)} %pad_add_fusion.place_ref, f32[32,8,256]{2,1,0:T(8,128)S(1)} %all_to_all.32.stat_ref, f32[512,512]{1,0:T(8,128)S(1)} %get-tuple-element.82.s_ref, f32[512,512]{1,0:T(8,128)S(1)} %get-tuple-element.83.d_ref, ...), custom_call_target="tpu_custom_call" | custom-call | tf_op jit(solution)/shard_map/pallas_call | solution.py:49
  97.2 1.3 shard_map.80
  98.5 0.1 collective-permute-start.13
  98.6 0.5 collective-permute-start.12
  99.1 1.8 %shard_map.81.own_ref = f32[4,512,512]{2,1,0:T(8,128)S(1)} custom-call(s32[3]{0:T(128)S(1)} %pad_add_fusion.place_ref, bf16[512,512]{1,0:T(8,128)(2,1)S(1)} %get-tuple-element.86.g_ref, bf16[4096,512]{1,0:T(8,128)(2,1)S(1)} %get-tuple-element.58.sw_ref), custom_call_target="tpu_custom_call" | custom-call | tf_op jit(solution)/shard_map/pallas_call | solution.py:49
  100.9 0.3 collective-permute-done.13.second_ref
  101.2 1.5 %collective-permute-done.12.first_ref = bf16[2,512,512]{2,1,0:T(8,128)(2,1)S(1)} collective-permute-done((bf16[2,512,512]{2,1,0:T(8,128)(2,1)S(1)}, bf16[2,512,512]{2,1,0:T(8,128)(2,1)S(1)}, u32[]{:S(2)}, u32[]{:S(2)}) %collective-permute-start.12) | collective-permute-done | bytes 1048608 | tf_op jit(solution)/shard_map/ppermute | solution.py:331
  102.7 1.3 shard_map.82
  104.0 2.2 %collective-permute-start.14 = (bf16[512,512]{1,0:T(8,128)(2,1)S(1)}, bf16[512,512]{1,0:T(8,128)(2,1)S(1)}, u32[]{:S(2)}, u32[]{:S(2)}) collective-permute-start(bf16[512,512]{1,0:T(8,128)(2,1)S(1)} %get-tuple-element.90), channel_id=1, source_target_pairs={{0,128},{1,129},{2,130},{3,131},{4,132},{5,133},{6,134},{7,135},{8... | collective-permute-start | bytes 1572872 | tf_op jit(solution)/shard_map/ppermute | solution.py:343
  106.2 0.9 collective-permute-start.15
  107.1 2.4 %collective-permute-start.16 = (bf16[512,512]{1,0:T(8,128)(2,1)S(1)}, bf16[512,512]{1,0:T(8,128)(2,1)S(1)}, u32[]{:S(2)}, u32[]{:S(2)}) collective-permute-start(bf16[512,512]{1,0:T(8,128)(2,1)S(1)} %get-tuple-element.92), channel_id=1, source_target_pairs={{0,64},{1,65},{2,66},{3,67},{4,68},{5,69},{6,70},{7,71},{8,72},{9,... | collective-permute-start | bytes 1572872 | tf_op jit(solution)/shard_map/ppermute | solution.py:343
  109.4 5.5 %collective-permute-done.14.refs_0_ = bf16[512,512]{1,0:T(8,128)(2,1)S(1)} collective-permute-done((bf16[512,512]{1,0:T(8,128)(2,1)S(1)}, bf16[512,512]{1,0:T(8,128)(2,1)S(1)}, u32[]{:S(2)}, u32[]{:S(2)}) %collective-permute-start.14) | collective-permute-done | bytes 524320 | tf_op jit(solution)/shard_map/ppermute | solution.py:343
  114.9 5.5 %collective-permute-done.15.refs_1_ = bf16[512,512]{1,0:T(8,128)(2,1)S(1)} collective-permute-done((bf16[512,512]{1,0:T(8,128)(2,1)S(1)}, bf16[512,512]{1,0:T(8,128)(2,1)S(1)}, u32[]{:S(2)}, u32[]{:S(2)}) %collective-permute-start.15) | collective-permute-done | bytes 524320 | tf_op jit(solution)/shard_map/ppermute | solution.py:343
  120.4 0.3 shard_map.83
  120.7 1.6 %collective-permute-start.17 = (bf16[128,512]{1,0:T(8,128)(2,1)S(1)}, bf16[128,512]{1,0:T(8,128)(2,1)S(1)}, u32[]{:S(2)}, u32[]{:S(2)}) collective-permute-start(bf16[128,512]{1,0:T(8,128)(2,1)S(1)} %get-tuple-element.94), channel_id=1, source_target_pairs={{0,16},{1,17},{2,18},{3,19},{4,20},{5,21},{6,22},{7,23},{8,24},{9,... | collective-permute-start | bytes 393224 | tf_op jit(solution)/shard_map/ppermute | solution.py:343
  122.3 1.8 %collective-permute-start.18 = (bf16[128,512]{1,0:T(8,128)(2,1)S(1)}, bf16[128,512]{1,0:T(8,128)(2,1)S(1)}, u32[]{:S(2)}, u32[]{:S(2)}) collective-permute-start(bf16[128,512]{1,0:T(8,128)(2,1)S(1)} %get-tuple-element.95), channel_id=1, source_target_pairs={{0,24},{1,25},{2,26},{3,27},{4,28},{5,29},{6,30},{7,31},{8,0},{9,1... | collective-permute-start | bytes 393224 | tf_op jit(solution)/shard_map/ppermute | solution.py:343
  124.1 0.2 collective-permute-start.19
  124.3 2.9 %collective-permute-done.17.refs_0_ = bf16[128,512]{1,0:T(8,128)(2,1)S(1)} collective-permute-done((bf16[128,512]{1,0:T(8,128)(2,1)S(1)}, bf16[128,512]{1,0:T(8,128)(2,1)S(1)}, u32[]{:S(2)}, u32[]{:S(2)}) %collective-permute-start.17) | collective-permute-done | bytes 131104 | tf_op jit(solution)/shard_map/ppermute | solution.py:343
  127.3 0.0 collective-permute-done.18.refs_1_
  127.3 3.0 %collective-permute-done.19.refs_2_ = bf16[128,512]{1,0:T(8,128)(2,1)S(1)} collective-permute-done((bf16[128,512]{1,0:T(8,128)(2,1)S(1)}, bf16[128,512]{1,0:T(8,128)(2,1)S(1)}, u32[]{:S(2)}, u32[]{:S(2)}) %collective-permute-start.19) | collective-permute-done | bytes 131104 | tf_op jit(solution)/shard_map/ppermute | solution.py:343
  130.3 0.7 shard_map.84
  131.0 3.4 %all-to-all-start.3 = ((bf16[8,16,512]{2,1,0:T(8,128)(2,1)}), bf16[8,16,512]{2,1,0:T(8,128)(2,1)S(1)}, u32[]{:S(2)}, u32[]{:S(2)}) async-start(bf16[8,16,512]{2,1,0:T(8,128)(2,1)} %bitcast.5), calls=%async_computation.3 | async-start | bytes 262144 | tf_op jit(solution)/shard_map/all_to_all | solution.py:252
  134.4 9.0 %all-to-all-done.3.in_ref = bf16[8,16,512]{2,1,0:T(8,128)(2,1)S(1)} async-done(((bf16[8,16,512]{2,1,0:T(8,128)(2,1)}), bf16[8,16,512]{2,1,0:T(8,128)(2,1)S(1)}, u32[]{:S(2)}, u32[]{:S(2)}) %all-to-all-start.3) | async-done | bytes 131104 | tf_op jit(solution)/shard_map/all_to_all | solution.py:252
  143.4 0.6 copy.8
  (9 shorter events, 0.1 us)
Async XLA Ops:
  0.6 23.7 %collective-permute-start = (bf16[4096,512]{1,0:T(8,128)(2,1)}, bf16[4096,512]{1,0:T(8,128)(2,1)S(1)}, u32[]{:S(2)}, u32[]{:S(2)}) collective-permute-start(bf16[4096,512]{1,0:T(8,128)(2,1)} %sw_ref.1), channel_id=1, source_target_pairs={{0,32},{32,0},{64,96},{96,64},{128,160},{160,128},{192,224},{224,1... | collective-permute-start | bytes 12582920 | tf_op jit(solution)/shard_map/ppermute | solution.py:331
  0.7 23.6 %collective-permute-start.1 = (bf16[4096,512]{1,0:T(8,128)(2,1)}, bf16[4096,512]{1,0:T(8,128)(2,1)S(1)}, u32[]{:S(2)}, u32[]{:S(2)}) collective-permute-start(bf16[4096,512]{1,0:T(8,128)(2,1)} %tw_ref.1), channel_id=1, source_target_pairs={{0,32},{32,0},{64,96},{96,64},{128,160},{160,128},{192,224},{224,1... | collective-permute-start | bytes 12582920 | tf_op jit(solution)/shard_map/ppermute | solution.py:331
  1.2 0.7 copy-start
  24.3 3.3 %copy-start.1 = (bf16[4096,512]{1,0:T(8,128)(2,1)}, bf16[4096,512]{1,0:T(8,128)(2,1)S(1)}, u32[]{:S(2)}) copy-start(bf16[4096,512]{1,0:T(8,128)(2,1)S(1)} %collective-permute-done.sw2_ref) | copy-start | bytes 12582916
  24.3 4.0 %copy-start.2 = (bf16[4096,512]{1,0:T(8,128)(2,1)}, bf16[4096,512]{1,0:T(8,128)(2,1)S(1)}, u32[]{:S(2)}) copy-start(bf16[4096,512]{1,0:T(8,128)(2,1)S(1)} %collective-permute-done.1.tw2_ref) | copy-start | bytes 12582916
  24.3 8.3 %collective-permute-start.2 = (bf16[128,1152]{1,0:T(8,128)(2,1)S(1)}, bf16[128,1152]{1,0:T(8,128)(2,1)S(1)}, u32[]{:S(2)}, u32[]{:S(2)}) collective-permute-start(bf16[128,1152]{1,0:T(8,128)(2,1)S(1)} %bitcast.6), channel_id=1, source_target_pairs={{0,16},{1,17},{2,18},{3,19},{4,20},{5,21},{6,22},{7,23},{8,24},{9,... | collective-permute-start | bytes 884744 | tf_op jit(solution)/shard_map/ppermute | solution.py:343
  27.6 8.2 %collective-permute-start.3 = (bf16[128,1152]{1,0:T(8,128)(2,1)S(1)}, bf16[128,1152]{1,0:T(8,128)(2,1)S(1)}, u32[]{:S(2)}, u32[]{:S(2)}) collective-permute-start(bf16[128,1152]{1,0:T(8,128)(2,1)S(1)} %bitcast.7), channel_id=1, source_target_pairs={{0,8},{1,9},{2,10},{3,11},{4,12},{5,13},{6,14},{7,15},{8,16},{9,17... | collective-permute-start | bytes 884744 | tf_op jit(solution)/shard_map/ppermute | solution.py:343
  28.3 7.9 %collective-permute-start.4 = (bf16[128,1152]{1,0:T(8,128)(2,1)S(1)}, bf16[128,1152]{1,0:T(8,128)(2,1)S(1)}, u32[]{:S(2)}, u32[]{:S(2)}) collective-permute-start(bf16[128,1152]{1,0:T(8,128)(2,1)S(1)} %bitcast.8), channel_id=1, source_target_pairs={{0,24},{1,25},{2,26},{3,27},{4,28},{5,29},{6,30},{7,31},{8,0},{9,1... | collective-permute-start | bytes 884744 | tf_op jit(solution)/shard_map/ppermute | solution.py:343
  36.8 14.9 %collective-permute-start.5 = (bf16[512,1024]{1,0:T(8,128)(2,1)S(1)}, bf16[512,1024]{1,0:T(8,128)(2,1)S(1)}, u32[]{:S(2)}, u32[]{:S(2)}) collective-permute-start(bf16[512,1024]{1,0:T(8,128)(2,1)S(1)} %get-tuple-element.51.p0), channel_id=1, source_target_pairs={{0,64},{1,65},{2,66},{3,67},{4,68},{5,69},{6,70},{7,71},{8,72},{9,... | collective-permute-start | bytes 3145736 | tf_op jit(solution)/shard_map/ppermute | solution.py:343
  37.4 16.0 %collective-permute-start.6 = (bf16[512,1024]{1,0:T(8,128)(2,1)S(1)}, bf16[512,1024]{1,0:T(8,128)(2,1)S(1)}, u32[]{:S(2)}, u32[]{:S(2)}) collective-permute-start(bf16[512,1024]{1,0:T(8,128)(2,1)S(1)} %get-tuple-element.51.p0), channel_id=1, source_target_pairs={{0,192},{1,193},{2,194},{3,195},{4,196},{5,197},{6,198},{7,199},{8... | collective-permute-start | bytes 3145736 | tf_op jit(solution)/shard_map/ppermute | solution.py:343
  53.4 9.3 %collective-permute-start.7 = (bf16[256,1024]{1,0:T(8,128)(2,1)S(1)}, bf16[256,1024]{1,0:T(8,128)(2,1)S(1)}, u32[]{:S(2)}, u32[]{:S(2)}) collective-permute-start(bf16[256,1024]{1,0:T(8,128)(2,1)S(1)} %slice.6), channel_id=1, source_target_pairs={{0,64},{1,65},{2,66},{3,67},{4,68},{5,69},{6,70},{7,71},{8,72},{9,... | collective-permute-start | bytes 1572872 | tf_op jit(solution)/shard_map/ppermute | solution.py:343
  53.8 10.5 %collective-permute-start.8 = (bf16[256,1024]{1,0:T(8,128)(2,1)S(1)}, bf16[256,1024]{1,0:T(8,128)(2,1)S(1)}, u32[]{:S(2)}, u32[]{:S(2)}) collective-permute-start(bf16[256,1024]{1,0:T(8,128)(2,1)S(1)} %slice.7), channel_id=1, source_target_pairs={{0,192},{1,193},{2,194},{3,195},{4,196},{5,197},{6,198},{7,199},{8... | collective-permute-start | bytes 1572872 | tf_op jit(solution)/shard_map/ppermute | solution.py:343
  55.6 1.3 collective-permute-start.9
  65.7 2.7 %collective-permute-start.11 = (f32[512,512]{1,0:T(8,128)S(1)}, f32[512,512]{1,0:T(8,128)S(1)}, u32[]{:S(2)}, u32[]{:S(2)}) collective-permute-start(f32[512,512]{1,0:T(8,128)S(1)} %get-tuple-element.72), channel_id=1, source_target_pairs={{0,32},{32,0},{64,96},{96,64},{128,160},{160,128},{192,224},{224,1... | collective-permute-start | bytes 3145736 | tf_op jit(solution)/shard_map/ppermute | solution.py:331
  65.8 4.1 %collective-permute-start.10 = (f32[512,512]{1,0:T(8,128)S(1)}, f32[512,512]{1,0:T(8,128)S(1)}, u32[]{:S(2)}, u32[]{:S(2)}) collective-permute-start(f32[512,512]{1,0:T(8,128)S(1)} %get-tuple-element.70), channel_id=1, source_target_pairs={{0,32},{32,0},{64,96},{96,64},{128,160},{160,128},{192,224},{224,1... | collective-permute-start | bytes 3145736 | tf_op jit(solution)/shard_map/ppermute | solution.py:331
  98.5 2.7 %collective-permute-start.13 = (bf16[2,512,512]{2,1,0:T(8,128)(2,1)S(1)}, bf16[2,512,512]{2,1,0:T(8,128)(2,1)S(1)}, u32[]{:S(2)}, u32[]{:S(2)}) collective-permute-start(bf16[2,512,512]{2,1,0:T(8,128)(2,1)S(1)} %shard_map.80), channel_id=1, source_target_pairs={{0,32},{32,0},{64,96},{96,64},{128,160},{160,128},{192,224},{224,1... | collective-permute-start | bytes 3145736 | tf_op jit(solution)/shard_map/ppermute | solution.py:331
  98.6 4.1 %collective-permute-start.12 = (bf16[2,512,512]{2,1,0:T(8,128)(2,1)S(1)}, bf16[2,512,512]{2,1,0:T(8,128)(2,1)S(1)}, u32[]{:S(2)}, u32[]{:S(2)}) collective-permute-start(bf16[2,512,512]{2,1,0:T(8,128)(2,1)S(1)} %get-tuple-element.85), channel_id=1, source_target_pairs={{0,32},{32,0},{64,96},{96,64},{128,160},{160,128},{192,224},{224,1... | collective-permute-start | bytes 3145736 | tf_op jit(solution)/shard_map/ppermute | solution.py:331
  104.0 10.9 %collective-permute-start.14 = (bf16[512,512]{1,0:T(8,128)(2,1)S(1)}, bf16[512,512]{1,0:T(8,128)(2,1)S(1)}, u32[]{:S(2)}, u32[]{:S(2)}) collective-permute-start(bf16[512,512]{1,0:T(8,128)(2,1)S(1)} %get-tuple-element.90), channel_id=1, source_target_pairs={{0,128},{1,129},{2,130},{3,131},{4,132},{5,133},{6,134},{7,135},{8... | collective-permute-start | bytes 1572872 | tf_op jit(solution)/shard_map/ppermute | solution.py:343
  106.2 14.2 %collective-permute-start.15 = (bf16[512,512]{1,0:T(8,128)(2,1)S(1)}, bf16[512,512]{1,0:T(8,128)(2,1)S(1)}, u32[]{:S(2)}, u32[]{:S(2)}) collective-permute-start(bf16[512,512]{1,0:T(8,128)(2,1)S(1)} %get-tuple-element.91), channel_id=1, source_target_pairs={{0,192},{1,193},{2,194},{3,195},{4,196},{5,197},{6,198},{7,199},{8... | collective-permute-start | bytes 1572872 | tf_op jit(solution)/shard_map/ppermute | solution.py:343
  107.1 13.4 %collective-permute-start.16 = (bf16[512,512]{1,0:T(8,128)(2,1)S(1)}, bf16[512,512]{1,0:T(8,128)(2,1)S(1)}, u32[]{:S(2)}, u32[]{:S(2)}) collective-permute-start(bf16[512,512]{1,0:T(8,128)(2,1)S(1)} %get-tuple-element.92), channel_id=1, source_target_pairs={{0,64},{1,65},{2,66},{3,67},{4,68},{5,69},{6,70},{7,71},{8,72},{9,... | collective-permute-start | bytes 1572872 | tf_op jit(solution)/shard_map/ppermute | solution.py:343
  120.7 6.6 %collective-permute-start.17 = (bf16[128,512]{1,0:T(8,128)(2,1)S(1)}, bf16[128,512]{1,0:T(8,128)(2,1)S(1)}, u32[]{:S(2)}, u32[]{:S(2)}) collective-permute-start(bf16[128,512]{1,0:T(8,128)(2,1)S(1)} %get-tuple-element.94), channel_id=1, source_target_pairs={{0,16},{1,17},{2,18},{3,19},{4,20},{5,21},{6,22},{7,23},{8,24},{9,... | collective-permute-start | bytes 393224 | tf_op jit(solution)/shard_map/ppermute | solution.py:343
  122.3 5.0 %collective-permute-start.18 = (bf16[128,512]{1,0:T(8,128)(2,1)S(1)}, bf16[128,512]{1,0:T(8,128)(2,1)S(1)}, u32[]{:S(2)}, u32[]{:S(2)}) collective-permute-start(bf16[128,512]{1,0:T(8,128)(2,1)S(1)} %get-tuple-element.95), channel_id=1, source_target_pairs={{0,24},{1,25},{2,26},{3,27},{4,28},{5,29},{6,30},{7,31},{8,0},{9,1... | collective-permute-start | bytes 393224 | tf_op jit(solution)/shard_map/ppermute | solution.py:343
  124.1 6.2 %collective-permute-start.19 = (bf16[128,512]{1,0:T(8,128)(2,1)S(1)}, bf16[128,512]{1,0:T(8,128)(2,1)S(1)}, u32[]{:S(2)}, u32[]{:S(2)}) collective-permute-start(bf16[128,512]{1,0:T(8,128)(2,1)S(1)} %get-tuple-element.96), channel_id=1, source_target_pairs={{0,8},{1,9},{2,10},{3,11},{4,12},{5,13},{6,14},{7,15},{8,16},{9,17... | collective-permute-start | bytes 393224 | tf_op jit(solution)/shard_map/ppermute | solution.py:343
  131.0 12.4 %all-to-all-start.3 = ((bf16[8,16,512]{2,1,0:T(8,128)(2,1)}), bf16[8,16,512]{2,1,0:T(8,128)(2,1)S(1)}, u32[]{:S(2)}, u32[]{:S(2)}) async-start(bf16[8,16,512]{2,1,0:T(8,128)(2,1)} %bitcast.5), calls=%async_computation.3 | async-start | bytes 262144 | tf_op jit(solution)/shard_map/all_to_all | solution.py:252

commit v7 on v6

--- a/solution.py
+++ b/solution.py
@@ -69,7 +69,7 @@
 
 def pack_kernel(source_ref, s_ref, t_ref, out_ref, s_buf, t_buf, sem):
     v = lax.axis_index("vocab")
-    columns = at_block(v % 2 * NX + v // 2, W)
+    columns = at_block(v, W)
     copies = [
         started(s_ref.at[:, columns], s_buf, sem.at[0]),
         started(t_ref.at[:, columns], t_buf, sem.at[1]),
@@ -88,45 +88,44 @@
         out_ref[:, :, k * W : (k + 1) * W] = jnp.broadcast_to(buf[...][None], (NZ, ROWS, W))
 
 
-def join_kernel(place_ref, far_ref, own_ref, left_ref, right_ref, out_ref, digits_ref):
+def join_kernel(place_ref, far_ref, own_ref, left_ref, right_ref, a_ref, b_ref, digits_ref):
     for k, (step, ref) in enumerate(zip(STEPS, (own_ref, left_ref, right_ref, far_ref))):
-        out_ref[k * NEAR : (k + 1) * NEAR] = ref[:, : 2 * W]
+        (a_ref, b_ref)[k // 2][k % 2 * NEAR : (k % 2 + 1) * NEAR] = ref[:, : 2 * W]
         digits_ref[at_block((place_ref[2] + step) % NY, NEAR)] = ref[:, 2 * W :]
 
 
-def hold_kernel(place_ref, sw_ref, tw_ref, sw2_ref, tw2_ref, sw_out, tw_out, sw2_out, tw2_out, sem):
-    half = at_block(place_ref[1], HALF)
-    copies = [
-        started(sw_ref, sw_out, sem.at[0]),
-        started(tw_ref.at[half], tw_out, sem.at[1]),
-        started(sw2_ref.at[half], sw2_out, sem.at[2]),
-        started(tw2_ref.at[half], tw2_out, sem.at[3]),
-    ]
+def hold_kernel(place_ref, *refs):
+    sem = refs[-1]
+    copies = []
+    for n, (ref, out_ref) in enumerate(zip(refs[:4], refs[4:8])):
+        for x in range(NX):
+            rows = ref.at[at_block(2 * x + place_ref[1], W)]
+            copies.append(started(rows, out_ref.at[x * W : (x + 1) * W], sem.at[n, x]))
     for copy in copies:
         copy.wait()
 
 
-def weights(place_ref, own, refs, step):
-    at = (place_ref[0] + step) % NX
-    first = place_ref[1] * NX if own else 0
-    return refs[0][at_block(first + at, W)], refs[1][at_block(at, W)]
-
-
-def near_kernel(own, place_ref, sw_ref, tw_ref, p0, p1, p2, out_ref):
-    pieces = (p0, p1, p2)
+def weights(place_ref, refs, step):
+    at = at_block((place_ref[0] + step) % NX, W)
+    return [ref[at] for ref in refs]
+
+
+def near_kernel(numbers, place_ref, sw_ref, tw_ref, *refs):
+    pieces = [refs[2 * k : 2 * k + 2] for k in range(len(numbers))]
+    steps = [STEPS[k] for k in numbers]
+    before_refs, out_ref = refs[2 * len(numbers) : -1], refs[-1]
     y = place_ref[2]
 
     @pl.when(place_ref[1] == 0)
     def _():
         for n in range(2):
             columns = slice(n * W, (n + 1) * W)
-            total = None
-            for step, ref in zip(STEPS, pieces):
-                weight = weights(place_ref, own, (sw_ref, tw_ref), step)[n]
-                part = dot(ref[:, columns], weight)
+            total = before_refs[0][n] if before_refs else None
+            for step, halves in zip(steps, pieces):
+                block = jnp.concatenate([ref[:, columns] for ref in halves], axis=0)
+                part = dot(block, weights(place_ref, (sw_ref, tw_ref), step)[n])
                 total = part if total is None else total + part
-            for k, step in enumerate(STEPS):
-                out_ref[n, at_block((y + step) % NY, NEAR)] = total[k * NEAR : (k + 1) * NEAR]
+            out_ref[n] = total
 
     @pl.when(place_ref[1] == 1)
     def _():
@@ -134,15 +133,17 @@
             columns = slice(n * W, (n + 1) * W)
             total = None
             for k, step in enumerate(STEPS):
-                rows = slice(k * NEAR, (k + 1) * NEAR)
-                block = jnp.concatenate([ref[rows, columns] for ref in pieces], axis=0)
-                part = dot(block, weights(place_ref, own, (sw_ref, tw_ref), step)[n])
+                rows = slice(k % 2 * NEAR, (k % 2 + 1) * NEAR)
+                block = jnp.concatenate([halves[k // 2][rows, columns] for halves in pieces], axis=0)
+                part = dot(block, weights(place_ref, (sw_ref, tw_ref), step)[n])
                 total = part if total is None else total + part
-            for k, step in enumerate(STEPS[:3]):
-                out_ref[n, at_block((y + step) % NY, NEAR)] = total[k * NEAR : (k + 1) * NEAR]
-
-
-def far_kernel(own, place_ref, sw_ref, tw_ref, p3, p4, near_ref, *refs):
+            for k, number in enumerate(numbers):
+                out_ref[n, number * NEAR : (number + 1) * NEAR] = total[k * NEAR : (k + 1) * NEAR]
+            for before_ref in before_refs:
+                out_ref[n, :NEAR] = before_ref[n, :NEAR]
+
+
+def far_kernel(place_ref, sw_ref, tw_ref, p3, p4, near_ref, *refs):
     y = place_ref[2]
     outs = refs[:2]
 
@@ -151,23 +152,24 @@
         for n, out_ref in enumerate(outs):
             columns = slice(n * W, (n + 1) * W)
             block = jnp.concatenate([p3[:, columns], p4[:, columns]], axis=0)
-            part = dot(block, weights(place_ref, own, (sw_ref, tw_ref), STEPS[3])[n])
+            part = dot(block, weights(place_ref, (sw_ref, tw_ref), STEPS[3])[n])
             for k, step in enumerate(STEPS):
                 rows = at_block((y + step) % NY, NEAR)
-                out_ref[rows] = near_ref[n, rows] + part[k * NEAR : (k + 1) * NEAR]
+                here = slice(k * NEAR, (k + 1) * NEAR)
+                out_ref[rows] = near_ref[n, here] + part[here]
 
     @pl.when(place_ref[1] == 1)
     def _():
         for n, out_ref in enumerate(outs):
             columns = slice(n * W, (n + 1) * W)
-            for step in STEPS[:3]:
-                rows = at_block((y + step) % NY, NEAR)
-                out_ref[rows] = near_ref[n, rows]
+            for k, step in enumerate(STEPS[:3]):
+                here = slice(k * NEAR, (k + 1) * NEAR)
+                out_ref[at_block((y + step) % NY, NEAR)] = near_ref[n, here]
             total = None
             for k, step in enumerate(STEPS):
                 rows = slice(k % 2 * NEAR, (k % 2 + 1) * NEAR)
                 block = (p3, p4)[k // 2][rows, columns]
-                part = dot(block, weights(place_ref, own, (sw_ref, tw_ref), step)[n])
+                part = dot(block, weights(place_ref, (sw_ref, tw_ref), step)[n])
                 total = part if total is None else total + part
             out_ref[at_block((y + STEPS[3]) % NY, NEAR)] = total
 
@@ -253,15 +255,12 @@
     return out.reshape(x.shape)
 
 
-def terms(place_ref, g, sw_ref, core, numbers):
-    for k in numbers:
-        block = (place_ref[0] + STEPS[k]) % NX * 2 + core
-        yield dot(g, sw_ref[at_block(block, W)], ((1,), (1,)))
-
-
-def first_for_other_kernel(
-    place_ref, stat_ref, s_ref, d_ref, sw_ref, out_ref, turned_ref, loss_ref, g_ref
-):
+def terms(place_ref, g, sw_ref):
+    for step in STEPS:
+        yield dot(g, sw_ref[at_block((place_ref[0] + step) % NX, W)], ((1,), (1,)))
+
+
+def logit_grad_kernel(place_ref, stat_ref, s_ref, d_ref, turned_ref, loss_ref, g_ref):
     lse_s, mean, lse_t = merge(stat_ref[...])
     loss_ref[...] = jnp.sum(mean - lse_s + lse_t, axis=1, keepdims=True) / N
     row = lax.broadcasted_iota(jnp.int32, (128, N), 0)
@@ -272,25 +271,17 @@
     for k, step in enumerate(STEPS):
         rows = g_ref[at_block((place_ref[2] + step) % NY, NEAR)]
         turned_ref[k * NEAR : (k + 1) * NEAR] = rows.astype(BF)
-    for k, part in enumerate(terms(place_ref, turned_ref[...], sw_ref, 1 - place_ref[1], (0, 1))):
-        out_ref[k] = part.astype(BF)
-
-
-def second_for_other_kernel(place_ref, g_ref, sw_ref, out_ref):
-    for k, part in enumerate(terms(place_ref, g_ref[...], sw_ref, 1 - place_ref[1], (2, 3))):
-        out_ref[k] = part.astype(BF)
 
 
 def own_terms_kernel(place_ref, g_ref, sw_ref, out_ref):
-    for k, part in enumerate(terms(place_ref, g_ref[...], sw_ref, place_ref[1], range(NX))):
+    for k, part in enumerate(terms(place_ref, g_ref[...], sw_ref)):
         out_ref[k] = part
 
 
-def add_kernel(place_ref, own_ref, first_ref, second_ref, *out_refs):
+def add_kernel(place_ref, own_ref, g_ref, sw_ref, *out_refs):
     core = place_ref[1]
-    for k in range(NX):
-        received = (first_ref, second_ref)[k // 2][k % 2]
-        total = (own_ref[k] + received.astype(F32)).astype(BF)
+    for k, part in enumerate(terms(place_ref, g_ref[...], sw_ref)):
+        total = (own_ref[k] + part).astype(BF)
 
         @pl.when(core == 0)
         def _():
@@ -374,44 +365,51 @@
     sw2, tw2 = to_other_core(student_weight), to_other_core(teacher_weight)
     near = exchange(packed, "tok", Z_GROUPS).reshape(NEAR, 2 * W + 128)
     near, sw2, tw2 = lax.optimization_barrier((near, sw2, tw2))
-    mine, digits = call(
+    half = ((N // 2, 2 * W), BF)
+    mine_a, mine_b, digits = call(
         join_kernel,
         [SM] + [VM] * 4,
-        [((N, 2 * W), BF), ((N, 128), BF)],
+        [half, half, ((N, 128), BF)],
         place, *ring(near, along_second),
     )
-    left, right = along_first(mine, 1), along_first(mine, -1)
+    left_a, right_b = along_first(mine_a, 1), along_first(mine_b, -1)
+    left_b, right_a = along_first(mine_b, 1), along_first(mine_a, -1)
     held = call(
         hold_kernel,
         [SM] + [HBM] * 4,
-        [((D, C), BF)] + [((HALF, C), BF)] * 3,
+        [((HALF, C), BF)] * 4,
         place, *(in_hbm(x) for x in (student_weight, teacher_weight, sw2, tw2)),
-        scratch=[pltpu.SemaphoreType.DMA((4,))],
-    )
-    left, right, held = lax.optimization_barrier((left, right, held))
+        scratch=[pltpu.SemaphoreType.DMA((4, NX))],
+    )
+    left_a, right_b, held = lax.optimization_barrier((left_a, right_b, held))
+    far = along_first(left_a, 1), along_first(right_b, -1)
     sw, tw, sw2, tw2 = held
-    far = along_first(left[: N // 2], 1), along_first(right[N // 2 :], -1)
     digits2 = to_other_core(digits)
     part = [((2, N, C), F32)]
 
-    def near_part(own, *held):
-        kernel = functools.partial(near_kernel, own)
-        flops = 3 * N * HALF * C
-        return call(kernel, [SM] + [VM] * 5, part, place, *held, mine, left, right, flops=flops)[0]
-
+    def near_part(numbers, held, *pieces):
+        kernel = functools.partial(near_kernel, numbers)
+        specs = [SM] + [VM] * (2 + len(pieces))
+        flops = len(numbers) * N * HALF * C
+        return call(kernel, specs, part, place, *held, *pieces, flops=flops)[0]
+
+    weights_other, weights_own = (sw2, tw2), (sw, tw)
+    for_other = near_part((0,), weights_other, mine_a, mine_b)
+    own = near_part((0,), weights_own, mine_a, mine_b)
+    left_b, right_a, for_other, own = lax.optimization_barrier((left_b, right_a, for_other, own))
+    sides = left_a, left_b, right_a, right_b
     logits = [((N, C), F32)]
 
-    def far_part(own, *held_and_near):
-        kernel = functools.partial(far_kernel, own)
-        sw, tw, near = held_and_near
-        return call(kernel, [SM] + [VM] * 5, logits * 2, place, sw, tw, *far, near)
-
-    for_other, own = near_part(False, sw2, tw2), near_part(True, sw, tw)
+    def far_part(held, near):
+        return call(far_kernel, [SM] + [VM] * 5, logits * 2, place, *held, *far, near)
+
+    for_other = near_part((1, 2), weights_other, *sides, for_other)
+    own = near_part((1, 2), weights_own, *sides, own)
     select = call(choose_kernel, [SM, VM, VM], [((N, N), BF)], place, digits, digits2)[0]
     far, for_other, own, select = lax.optimization_barrier((far, for_other, own, select))
-    s_other, t_other = far_part(False, sw2, tw2, for_other)
+    s_other, t_other = far_part(weights_other, for_other)
     t_other, s_other = to_other_core(t_other), to_other_core(s_other)
-    s_own, t_own = far_part(True, sw, tw, own)
+    s_own, t_own = far_part(weights_own, own)
     t_own, t_other = lax.optimization_barrier((t_own, t_other))
     t, table = call(
         teacher_logits_kernel,
@@ -429,23 +427,17 @@
     stats = exchange(stats, "vocab")
     stats = call(merge_kernel, [VM], [((TOK, 8, N // 2), F32)], stats)[0]
     stats = exchange(stats, "tok")
-    half = ((NX // 2, N, W), BF)
-    first, g, loss = call(
-        first_for_other_kernel,
-        [SM] + [VM] * 4,
-        [half, ((N, C), BF), ((1, 1), F32)],
-        place, stats, s, d, sw,
+    g, loss = call(
+        logit_grad_kernel,
+        [SM] + [VM] * 3,
+        [((N, C), BF), ((1, 1), F32)],
+        place, stats, s, d,
         scratch=[pltpu.VMEM((N, C), F32)],
     )
-    second = call(second_for_other_kernel, [SM, VM, VM], [half], place, g, sw)[0]
-    own = call(
-        own_terms_kernel, [SM, VM, VM], [((NX, N, W), F32)], place, g, sw
-    )[0]
-    first, second, own = lax.optimization_barrier(
-        (to_other_core(first), to_other_core(second), own)
-    )
+    own = call(own_terms_kernel, [SM, VM, VM], [((NX, N, W), F32)], place, g, sw)[0]
+    g_other, own = lax.optimization_barrier((to_other_core(g), own))
     blocks = call(
-        add_kernel, [SM] + [VM] * 3, [((N, W), BF)] * 4, place, own, first, second
+        add_kernel, [SM] + [VM] * 3, [((N, W), BF)] * 4, place, own, g_other, sw2
     )
     blocks = call(
         sum_first_kernel, [VM] * 4, [((NEAR, W), BF)] * 4, *to_ring(blocks, along_first)

time: 146 us -> 138 us (0.945)
  waiting for transfers between devices: 47 us -> 35.8 us
  starting transfers between devices: 25 us -> 27.8 us
    ppermute x13 -> x15, waiting for transfers between devices: 33.8 us -> 24.3 us  [along_rings(): return lax.ppermute(a, ('vocab', 'tok'), pairs)]
    ppermute x13 -> x15, starting transfers between devices: 19.8 us -> 23.1 us  [along_rings(): return lax.ppermute(a, ('vocab', 'tok'), pairs)]
    ppermute x7 -> x6, waiting for transfers between devices: 4.29 us -> 2.54 us  [to_other_core(): return lax.ppermute(a, 'vocab', [(k, k ^ 1) for k in range(VOC)])]
    pallas_call x18 -> x19, Pallas kernels: 24 us -> 24.3 us  [call(): pl.pallas_call(kernel, in_specs=in_specs, out_specs=[VM] * len(outs), out...]
  transfers between devices with their start and end apart: 21 -> 22, of which waited for: 17 -> 14; matrix products, arithmetic and copies ran while one was open for 0% -> 0% of each run, Pallas kernels for 11% -> 12%
where the time goes in v7:
time: 138 us; the launch traced here: 137 us
  blocking collectives  45.7 us (33%)
  waiting for transfers between devices  35.8 us (26%)
  starting transfers between devices  27.8 us (20%)
  Pallas kernels  24.3 us (18%)
  between operations  2.02 us (1%)
    all_to_all x3, blocking collectives, exchange(): out = lax.all_to_all(flat, axis, 0, 0, axis_index_groups=groups, tiled=True)  45.7 us
    pallas_call x19, Pallas kernels, call(): pl.pallas_call(kernel, in_specs=in_specs, out_specs=[VM] * len(outs), out...  24.3 us
    ppermute x15, waiting for transfers between devices, along_rings(): return lax.ppermute(a, ('vocab', 'tok'), pairs)  24.3 us
    ppermute x15, starting transfers between devices, along_rings(): return lax.ppermute(a, ('vocab', 'tok'), pairs)  23.1 us
    all_to_all x1, waiting for transfers between devices, exchange(): out = lax.all_to_all(flat, axis, 0, 0, axis_index_groups=groups, tiled=True)  8.95 us
    all_to_all x1, starting transfers between devices, exchange(): out = lax.all_to_all(flat, axis, 0, 0, axis_index_groups=groups, tiled=True)  3.37 us
  transfers between devices with their start and end apart: 22, of which 14 were waited for; matrix products, arithmetic and copies ran while one was open for 0% of the time, Pallas kernels for 12%

profile of v7, /device:TPU:6, one launch (start us, length us, event | category | flops | bytes accessed | tf_op | source)
XLA Modules:
  0.0 137.0 jit_solution(142431575096242137)
XLA Ops:
  0.6 0.1 collective-permute-start
  0.7 0.5 collective-permute-start.1
  1.2 0.7 copy-done
  1.9 1.3 shard_map.68
  3.2 21.1 %all_to_all.30 = bf16[8,16,1152]{2,1,0:T(8,128)(2,1)S(1)} all-to-all(bf16[8,16,1152]{2,1,0:T(8,128)(2,1)S(1)} %shard_map.68), channel_id=1, replica_groups={{0,1,2,3,4,5,6,7},{8,9,10,11,12,13,14,15},{16,17,18,19,20,21,22,23},{24..., dimensions={0} | all-to-all | bytes 589824 | tf_op jit(solution)/shard_map/all_to_all | solution.py:254
  24.3 0.0 collective-permute-done.refs_2_
  24.3 3.3 %collective-permute-start.2 = (bf16[128,1152]{1,0:T(8,128)(2,1)S(1)}, bf16[128,1152]{1,0:T(8,128)(2,1)S(1)}, u32[]{:S(2)}, u32[]{:S(2)}) collective-permute-start(bf16[128,1152]{1,0:T(8,128)(2,1)S(1)} %bitcast.6), channel_id=1, source_target_pairs={{0,16},{1,17},{2,18},{3,19},{4,20},{5,21},{6,22},{7,23},{8,24},{9,... | collective-permute-start | bytes 884744 | tf_op jit(solution)/shard_map/ppermute | solution.py:334
  27.6 0.7 collective-permute-start.3
  28.3 2.6 %collective-permute-start.4 = (bf16[128,1152]{1,0:T(8,128)(2,1)S(1)}, bf16[128,1152]{1,0:T(8,128)(2,1)S(1)}, u32[]{:S(2)}, u32[]{:S(2)}) collective-permute-start(bf16[128,1152]{1,0:T(8,128)(2,1)S(1)} %bitcast.8), channel_id=1, source_target_pairs={{0,24},{1,25},{2,26},{3,27},{4,28},{5,29},{6,30},{7,31},{8,0},{9,1... | collective-permute-start | bytes 884744 | tf_op jit(solution)/shard_map/ppermute | solution.py:334
  30.9 0.1 pad_add_fusion.place_ref
  30.9 1.7 %collective-permute-done.2.far_ref = bf16[128,1152]{1,0:T(8,128)(2,1)S(1)} collective-permute-done((bf16[128,1152]{1,0:T(8,128)(2,1)S(1)}, bf16[128,1152]{1,0:T(8,128)(2,1)S(1)}, u32[]{:S(2)}, u32[]{:S(2)}) %collective-permute-start.2) | collective-permute-done | bytes 294944 | tf_op jit(solution)/shard_map/ppermute | solution.py:334
  32.7 3.1 %collective-permute-done.3.left_ref = bf16[128,1152]{1,0:T(8,128)(2,1)S(1)} collective-permute-done((bf16[128,1152]{1,0:T(8,128)(2,1)S(1)}, bf16[128,1152]{1,0:T(8,128)(2,1)S(1)}, u32[]{:S(2)}, u32[]{:S(2)}) %collective-permute-start.3) | collective-permute-done | bytes 294944 | tf_op jit(solution)/shard_map/ppermute | solution.py:334
  35.8 0.3 collective-permute-done.4.right_ref
  36.1 0.6 shard_map.69
  36.8 0.6 collective-permute-start.5
  37.3 1.5 %collective-permute-start.6 = (bf16[256,1024]{1,0:T(8,128)(2,1)S(1)}, bf16[256,1024]{1,0:T(8,128)(2,1)S(1)}, u32[]{:S(2)}, u32[]{:S(2)}) collective-permute-start(bf16[256,1024]{1,0:T(8,128)(2,1)S(1)} %get-tuple-element.55.refs_1_), channel_id=1, source_target_pairs={{0,192},{1,193},{2,194},{3,195},{4,196},{5,197},{6,198},{7,199},{8... | collective-permute-start | bytes 1572872 | tf_op jit(solution)/shard_map/ppermute | solution.py:334
  38.9 0.8 collective-permute-start.10
  39.7 2.4 %collective-permute-start.9 = (bf16[256,1024]{1,0:T(8,128)(2,1)S(1)}, bf16[256,1024]{1,0:T(8,128)(2,1)S(1)}, u32[]{:S(2)}, u32[]{:S(2)}) collective-permute-start(bf16[256,1024]{1,0:T(8,128)(2,1)S(1)} %get-tuple-element.55.refs_1_), channel_id=1, source_target_pairs={{0,64},{1,65},{2,66},{3,67},{4,68},{5,69},{6,70},{7,71},{8,72},{9,... | collective-permute-start | bytes 1572872 | tf_op jit(solution)/shard_map/ppermute | solution.py:334
  42.1 4.1 %shard_map.70 = (bf16[2048,512]{1,0:T(8,128)(2,1)S(1)}, bf16[2048,512]{1,0:T(8,128)(2,1)S(1)}, bf16[2048,512]{1,0:T(8,128)(2,1)S(1)}, bf16[2048,512]{1,0:T(8,128)(2,1)S(1)}) custom-call(s32[3]{0:T(128)S(1)} %pad_add_fusion.place_ref, bf16[4096,512]{1,0:T(8,128)(2,1)} %refs_0_.1, bf16[4096,512]{1,0:T(8,128)(2,1)} %refs_1_.1, bf16[4096,512]{1,0:T(8,128)(2,1)} %copy-done.1, ...), custom_call_target="tpu_custom_call" | custom-call | tf_op jit(solution)/shard_map/pallas_call | solution.py:49
  46.2 0.0 collective-permute-done.5.refs_0_
  46.2 1.5 %collective-permute-done.6.refs_3_ = bf16[256,1024]{1,0:T(8,128)(2,1)S(1)} collective-permute-done((bf16[256,1024]{1,0:T(8,128)(2,1)S(1)}, bf16[256,1024]{1,0:T(8,128)(2,1)S(1)}, u32[]{:S(2)}, u32[]{:S(2)}) %collective-permute-start.6) | collective-permute-done | bytes 524320 | tf_op jit(solution)/shard_map/ppermute | solution.py:334
  47.7 0.3 collective-permute-start.7
  48.0 1.7 %collective-permute-start.8 = (bf16[256,1024]{1,0:T(8,128)(2,1)S(1)}, bf16[256,1024]{1,0:T(8,128)(2,1)S(1)}, u32[]{:S(2)}, u32[]{:S(2)}) collective-permute-start(bf16[256,1024]{1,0:T(8,128)(2,1)S(1)} %collective-permute-done.6.refs_3_), channel_id=1, source_target_pairs={{0,192},{1,193},{2,194},{3,195},{4,196},{5,197},{6,198},{7,199},{8... | collective-permute-start | bytes 1572872 | tf_op jit(solution)/shard_map/ppermute | solution.py:334
  49.8 1.3 collective-permute-done.11.other_ref
  51.1 0.8 shard_map.75.select_ref
  51.9 1.3 shard_map.72.refs_4_
  53.2 1.3 shard_map.71.refs_4_
  54.4 0.0 collective-permute-done.10.refs_2_
  54.5 2.0 %shard_map.74.near_ref = f32[2,512,512]{2,1,0:T(8,128)S(1)} custom-call(s32[3]{0:T(128)S(1)} %pad_add_fusion.place_ref, bf16[2048,512]{1,0:T(8,128)(2,1)S(1)} %get-tuple-element.62.sw_ref, bf16[2048,512]{1,0:T(8,128)(2,1)S(1)} %get-tuple-element.63.tw_ref, bf16[256,1024]{1,0:T(8,128)(2,1)S(1)} %collective-permute-done.5.refs_0_, ...), custom_call_target="tpu_custom_call" | custom-call | flops 1073741824 | tf_op jit(solution)/shard_map/pallas_call | solution.py:49
  56.5 1.8 %shard_map.73.near_ref = f32[2,512,512]{2,1,0:T(8,128)S(1)} custom-call(s32[3]{0:T(128)S(1)} %pad_add_fusion.place_ref, bf16[2048,512]{1,0:T(8,128)(2,1)S(1)} %get-tuple-element.66.sw_ref, bf16[2048,512]{1,0:T(8,128)(2,1)S(1)} %get-tuple-element.67.tw_ref, bf16[256,1024]{1,0:T(8,128)(2,1)S(1)} %collective-permute-done.5.refs_0_, ...), custom_call_target="tpu_custom_call" | custom-call | flops 1073741824 | tf_op jit(solution)/shard_map/pallas_call | solution.py:49
  58.3 0.0 collective-permute-done.7.p3
  58.3 0.7 collective-permute-done.8.p4
  59.0 1.3 shard_map.77
  60.2 0.1 collective-permute-start.13
  60.4 0.5 collective-permute-start.12
  60.8 1.3 shard_map.76
  62.1 0.9 collective-permute-done.13.other_ref
  63.0 1.2 shard_map.78
  64.2 0.3 collective-permute-done.12.other_ref
  64.5 0.5 shard_map.79
  65.0 7.9 %all_to_all.31.in_ref = f32[8,8,256]{2,1,0:T(8,128)S(1)} all-to-all(f32[8,8,256]{2,1,0:T(8,128)S(1)} %get-tuple-element.89), channel_id=1, replica_groups=mesh['vocab'=8,'tok'=32] {'vocab'}, dimensions={0} | all-to-all | bytes 131072 | tf_op jit(solution)/shard_map/all_to_all | solution.py:254
  72.9 0.1 shard_map.80
  73.0 16.7 %all_to_all.32.stat_ref = f32[32,8,256]{2,1,0:T(8,128)S(1)} all-to-all(f32[32,8,256]{2,1,0:T(8,128)S(1)} %shard_map.80), channel_id=1, replica_groups=mesh['vocab'=8,'tok'=32] {'tok'}, dimensions={0} | all-to-all | bytes 524288 | tf_op jit(solution)/shard_map/all_to_all | solution.py:254
  89.8 1.3 shard_map.81
  91.1 0.1 collective-permute-start.14
  91.2 1.8 %shard_map.82.own_ref = f32[4,512,512]{2,1,0:T(8,128)S(1)} custom-call(s32[3]{0:T(128)S(1)} %pad_add_fusion.place_ref, bf16[512,512]{1,0:T(8,128)(2,1)S(1)} %get-tuple-element.93.g_ref, bf16[2048,512]{1,0:T(8,128)(2,1)S(1)} %get-tuple-element.62.sw_ref), custom_call_target="tpu_custom_call" | custom-call | tf_op jit(solution)/shard_map/pallas_call | solution.py:49
  93.0 0.1 collective-permute-done.14.g_ref
  93.1 2.6 %shard_map.83 = (bf16[512,512]{1,0:T(8,128)(2,1)S(1)}, bf16[512,512]{1,0:T(8,128)(2,1)S(1)}, bf16[512,512]{1,0:T(8,128)(2,1)S(1)}, bf16[512,512]{1,0:T(8,128)(2,1)S(1)}) custom-call(s32[3]{0:T(128)S(1)} %pad_add_fusion.place_ref, f32[4,512,512]{2,1,0:T(8,128)S(1)} %shard_map.82.own_ref, bf16[512,512]{1,0:T(8,128)(2,1)S(1)} %collective-permute-done.14.g_ref, ...), custom_call_target="tpu_custom_call" | custom-call | tf_op jit(solution)/shard_map/pallas_call | solution.py:49
  95.7 2.4 %collective-permute-start.15 = (bf16[512,512]{1,0:T(8,128)(2,1)S(1)}, bf16[512,512]{1,0:T(8,128)(2,1)S(1)}, u32[]{:S(2)}, u32[]{:S(2)}) collective-permute-start(bf16[512,512]{1,0:T(8,128)(2,1)S(1)} %get-tuple-element.96), channel_id=1, source_target_pairs={{0,128},{1,129},{2,130},{3,131},{4,132},{5,133},{6,134},{7,135},{8... | collective-permute-start | bytes 1572872 | tf_op jit(solution)/shard_map/ppermute | solution.py:334
  98.1 0.9 collective-permute-start.16
  99.0 2.4 %collective-permute-start.17 = (bf16[512,512]{1,0:T(8,128)(2,1)S(1)}, bf16[512,512]{1,0:T(8,128)(2,1)S(1)}, u32[]{:S(2)}, u32[]{:S(2)}) collective-permute-start(bf16[512,512]{1,0:T(8,128)(2,1)S(1)} %get-tuple-element.98), channel_id=1, source_target_pairs={{0,64},{1,65},{2,66},{3,67},{4,68},{5,69},{6,70},{7,71},{8,72},{9,... | collective-permute-start | bytes 1572872 | tf_op jit(solution)/shard_map/ppermute | solution.py:334
  101.4 5.5 %collective-permute-done.15.refs_0_ = bf16[512,512]{1,0:T(8,128)(2,1)S(1)} collective-permute-done((bf16[512,512]{1,0:T(8,128)(2,1)S(1)}, bf16[512,512]{1,0:T(8,128)(2,1)S(1)}, u32[]{:S(2)}, u32[]{:S(2)}) %collective-permute-start.15) | collective-permute-done | bytes 524320 | tf_op jit(solution)/shard_map/ppermute | solution.py:334
  106.8 5.5 %collective-permute-done.16.refs_1_ = bf16[512,512]{1,0:T(8,128)(2,1)S(1)} collective-permute-done((bf16[512,512]{1,0:T(8,128)(2,1)S(1)}, bf16[512,512]{1,0:T(8,128)(2,1)S(1)}, u32[]{:S(2)}, u32[]{:S(2)}) %collective-permute-start.16) | collective-permute-done | bytes 524320 | tf_op jit(solution)/shard_map/ppermute | solution.py:334
  112.4 0.3 shard_map.84
  112.6 1.6 %collective-permute-start.18 = (bf16[128,512]{1,0:T(8,128)(2,1)S(1)}, bf16[128,512]{1,0:T(8,128)(2,1)S(1)}, u32[]{:S(2)}, u32[]{:S(2)}) collective-permute-start(bf16[128,512]{1,0:T(8,128)(2,1)S(1)} %get-tuple-element.100), channel_id=1, source_target_pairs={{0,16},{1,17},{2,18},{3,19},{4,20},{5,21},{6,22},{7,23},{8,24},{9,... | collective-permute-start | bytes 393224 | tf_op jit(solution)/shard_map/ppermute | solution.py:334
  114.2 1.8 %collective-permute-start.19 = (bf16[128,512]{1,0:T(8,128)(2,1)S(1)}, bf16[128,512]{1,0:T(8,128)(2,1)S(1)}, u32[]{:S(2)}, u32[]{:S(2)}) collective-permute-start(bf16[128,512]{1,0:T(8,128)(2,1)S(1)} %get-tuple-element.101), channel_id=1, source_target_pairs={{0,24},{1,25},{2,26},{3,27},{4,28},{5,29},{6,30},{7,31},{8,0},{9,1... | collective-permute-start | bytes 393224 | tf_op jit(solution)/shard_map/ppermute | solution.py:334
  116.0 0.2 collective-permute-start.20
  116.3 2.9 %collective-permute-done.18.refs_0_ = bf16[128,512]{1,0:T(8,128)(2,1)S(1)} collective-permute-done((bf16[128,512]{1,0:T(8,128)(2,1)S(1)}, bf16[128,512]{1,0:T(8,128)(2,1)S(1)}, u32[]{:S(2)}, u32[]{:S(2)}) %collective-permute-start.18) | collective-permute-done | bytes 131104 | tf_op jit(solution)/shard_map/ppermute | solution.py:334
  119.2 0.0 collective-permute-done.19.refs_1_
  119.2 3.0 %collective-permute-done.20.refs_2_ = bf16[128,512]{1,0:T(8,128)(2,1)S(1)} collective-permute-done((bf16[128,512]{1,0:T(8,128)(2,1)S(1)}, bf16[128,512]{1,0:T(8,128)(2,1)S(1)}, u32[]{:S(2)}, u32[]{:S(2)}) %collective-permute-start.20) | collective-permute-done | bytes 131104 | tf_op jit(solution)/shard_map/ppermute | solution.py:334
  122.2 0.7 shard_map.85
  122.9 3.4 %all-to-all-start.3 = ((bf16[8,16,512]{2,1,0:T(8,128)(2,1)}), bf16[8,16,512]{2,1,0:T(8,128)(2,1)S(1)}, u32[]{:S(2)}, u32[]{:S(2)}) async-start(bf16[8,16,512]{2,1,0:T(8,128)(2,1)} %bitcast.5), calls=%async_computation.3 | async-start | bytes 262144 | tf_op jit(solution)/shard_map/all_to_all | solution.py:254
  126.3 8.9 %all-to-all-done.3.in_ref = bf16[8,16,512]{2,1,0:T(8,128)(2,1)S(1)} async-done(((bf16[8,16,512]{2,1,0:T(8,128)(2,1)}), bf16[8,16,512]{2,1,0:T(8,128)(2,1)S(1)}, u32[]{:S(2)}, u32[]{:S(2)}) %all-to-all-start.3) | async-done | bytes 131104 | tf_op jit(solution)/shard_map/all_to_all | solution.py:254
  135.3 0.6 copy.8
  (10 shorter events, 0.0 us)
Async XLA Ops:
  0.6 23.7 %collective-permute-start = (bf16[4096,512]{1,0:T(8,128)(2,1)}, bf16[4096,512]{1,0:T(8,128)(2,1)S(1)}, u32[]{:S(2)}, u32[]{:S(2)}) collective-permute-start(bf16[4096,512]{1,0:T(8,128)(2,1)} %refs_0_.1), channel_id=1, source_target_pairs={{0,32},{32,0},{64,96},{96,64},{128,160},{160,128},{192,224},{224,1... | collective-permute-start | bytes 12582920 | tf_op jit(solution)/shard_map/ppermute | solution.py:322
  0.7 23.6 %collective-permute-start.1 = (bf16[4096,512]{1,0:T(8,128)(2,1)}, bf16[4096,512]{1,0:T(8,128)(2,1)S(1)}, u32[]{:S(2)}, u32[]{:S(2)}) collective-permute-start(bf16[4096,512]{1,0:T(8,128)(2,1)} %refs_1_.1), channel_id=1, source_target_pairs={{0,32},{32,0},{64,96},{96,64},{128,160},{160,128},{192,224},{224,1... | collective-permute-start | bytes 12582920 | tf_op jit(solution)/shard_map/ppermute | solution.py:322
  1.2 0.7 copy-start
  24.3 3.3 %copy-start.1 = (bf16[4096,512]{1,0:T(8,128)(2,1)}, bf16[4096,512]{1,0:T(8,128)(2,1)S(1)}, u32[]{:S(2)}) copy-start(bf16[4096,512]{1,0:T(8,128)(2,1)S(1)} %collective-permute-done.refs_2_) | copy-start | bytes 12582916
  24.3 4.0 %copy-start.2 = (bf16[4096,512]{1,0:T(8,128)(2,1)}, bf16[4096,512]{1,0:T(8,128)(2,1)S(1)}, u32[]{:S(2)}) copy-start(bf16[4096,512]{1,0:T(8,128)(2,1)S(1)} %collective-permute-done.1.refs_3_) | copy-start | bytes 12582916
  24.3 8.3 %collective-permute-start.2 = (bf16[128,1152]{1,0:T(8,128)(2,1)S(1)}, bf16[128,1152]{1,0:T(8,128)(2,1)S(1)}, u32[]{:S(2)}, u32[]{:S(2)}) collective-permute-start(bf16[128,1152]{1,0:T(8,128)(2,1)S(1)} %bitcast.6), channel_id=1, source_target_pairs={{0,16},{1,17},{2,18},{3,19},{4,20},{5,21},{6,22},{7,23},{8,24},{9,... | collective-permute-start | bytes 884744 | tf_op jit(solution)/shard_map/ppermute | solution.py:334
  27.6 8.2 %collective-permute-start.3 = (bf16[128,1152]{1,0:T(8,128)(2,1)S(1)}, bf16[128,1152]{1,0:T(8,128)(2,1)S(1)}, u32[]{:S(2)}, u32[]{:S(2)}) collective-permute-start(bf16[128,1152]{1,0:T(8,128)(2,1)S(1)} %bitcast.7), channel_id=1, source_target_pairs={{0,8},{1,9},{2,10},{3,11},{4,12},{5,13},{6,14},{7,15},{8,16},{9,17... | collective-permute-start | bytes 884744 | tf_op jit(solution)/shard_map/ppermute | solution.py:334
  28.3 7.9 %collective-permute-start.4 = (bf16[128,1152]{1,0:T(8,128)(2,1)S(1)}, bf16[128,1152]{1,0:T(8,128)(2,1)S(1)}, u32[]{:S(2)}, u32[]{:S(2)}) collective-permute-start(bf16[128,1152]{1,0:T(8,128)(2,1)S(1)} %bitcast.8), channel_id=1, source_target_pairs={{0,24},{1,25},{2,26},{3,27},{4,28},{5,29},{6,30},{7,31},{8,0},{9,1... | collective-permute-start | bytes 884744 | tf_op jit(solution)/shard_map/ppermute | solution.py:334
  36.8 9.4 %collective-permute-start.5 = (bf16[256,1024]{1,0:T(8,128)(2,1)S(1)}, bf16[256,1024]{1,0:T(8,128)(2,1)S(1)}, u32[]{:S(2)}, u32[]{:S(2)}) collective-permute-start(bf16[256,1024]{1,0:T(8,128)(2,1)S(1)} %get-tuple-element.54.refs_0_), channel_id=1, source_target_pairs={{0,64},{1,65},{2,66},{3,67},{4,68},{5,69},{6,70},{7,71},{8,72},{9,... | collective-permute-start | bytes 1572872 | tf_op jit(solution)/shard_map/ppermute | solution.py:334
  37.3 10.4 %collective-permute-start.6 = (bf16[256,1024]{1,0:T(8,128)(2,1)S(1)}, bf16[256,1024]{1,0:T(8,128)(2,1)S(1)}, u32[]{:S(2)}, u32[]{:S(2)}) collective-permute-start(bf16[256,1024]{1,0:T(8,128)(2,1)S(1)} %get-tuple-element.55.refs_1_), channel_id=1, source_target_pairs={{0,192},{1,193},{2,194},{3,195},{4,196},{5,197},{6,198},{7,199},{8... | collective-permute-start | bytes 1572872 | tf_op jit(solution)/shard_map/ppermute | solution.py:334
  38.9 15.5 %collective-permute-start.10 = (bf16[256,1024]{1,0:T(8,128)(2,1)S(1)}, bf16[256,1024]{1,0:T(8,128)(2,1)S(1)}, u32[]{:S(2)}, u32[]{:S(2)}) collective-permute-start(bf16[256,1024]{1,0:T(8,128)(2,1)S(1)} %get-tuple-element.54.refs_0_), channel_id=1, source_target_pairs={{0,192},{1,193},{2,194},{3,195},{4,196},{5,197},{6,198},{7,199},{8... | collective-permute-start | bytes 1572872 | tf_op jit(solution)/shard_map/ppermute | solution.py:334
  39.7 14.7 %collective-permute-start.9 = (bf16[256,1024]{1,0:T(8,128)(2,1)S(1)}, bf16[256,1024]{1,0:T(8,128)(2,1)S(1)}, u32[]{:S(2)}, u32[]{:S(2)}) collective-permute-start(bf16[256,1024]{1,0:T(8,128)(2,1)S(1)} %get-tuple-element.55.refs_1_), channel_id=1, source_target_pairs={{0,64},{1,65},{2,66},{3,67},{4,68},{5,69},{6,70},{7,71},{8,72},{9,... | collective-permute-start | bytes 1572872 | tf_op jit(solution)/shard_map/ppermute | solution.py:334
  47.7 10.5 %collective-permute-start.7 = (bf16[256,1024]{1,0:T(8,128)(2,1)S(1)}, bf16[256,1024]{1,0:T(8,128)(2,1)S(1)}, u32[]{:S(2)}, u32[]{:S(2)}) collective-permute-start(bf16[256,1024]{1,0:T(8,128)(2,1)S(1)} %collective-permute-done.5.refs_0_), channel_id=1, source_target_pairs={{0,64},{1,65},{2,66},{3,67},{4,68},{5,69},{6,70},{7,71},{8,72},{9,... | collective-permute-start | bytes 1572872 | tf_op jit(solution)/shard_map/ppermute | solution.py:334
  48.0 11.0 %collective-permute-start.8 = (bf16[256,1024]{1,0:T(8,128)(2,1)S(1)}, bf16[256,1024]{1,0:T(8,128)(2,1)S(1)}, u32[]{:S(2)}, u32[]{:S(2)}) collective-permute-start(bf16[256,1024]{1,0:T(8,128)(2,1)S(1)} %collective-permute-done.6.refs_3_), channel_id=1, source_target_pairs={{0,192},{1,193},{2,194},{3,195},{4,196},{5,197},{6,198},{7,199},{8... | collective-permute-start | bytes 1572872 | tf_op jit(solution)/shard_map/ppermute | solution.py:334
  49.8 1.3 collective-permute-start.11
  60.2 2.7 %collective-permute-start.13 = (f32[512,512]{1,0:T(8,128)S(1)}, f32[512,512]{1,0:T(8,128)S(1)}, u32[]{:S(2)}, u32[]{:S(2)}) collective-permute-start(f32[512,512]{1,0:T(8,128)S(1)} %get-tuple-element.80), channel_id=1, source_target_pairs={{0,32},{32,0},{64,96},{96,64},{128,160},{160,128},{192,224},{224,1... | collective-permute-start | bytes 3145736 | tf_op jit(solution)/shard_map/ppermute | solution.py:322
  60.4 4.1 %collective-permute-start.12 = (f32[512,512]{1,0:T(8,128)S(1)}, f32[512,512]{1,0:T(8,128)S(1)}, u32[]{:S(2)}, u32[]{:S(2)}) collective-permute-start(f32[512,512]{1,0:T(8,128)S(1)} %get-tuple-element.78), channel_id=1, source_target_pairs={{0,32},{32,0},{64,96},{96,64},{128,160},{160,128},{192,224},{224,1... | collective-permute-start | bytes 3145736 | tf_op jit(solution)/shard_map/ppermute | solution.py:322
  91.1 2.0 %collective-permute-start.14 = (bf16[512,512]{1,0:T(8,128)(2,1)S(1)}, bf16[512,512]{1,0:T(8,128)(2,1)S(1)}, u32[]{:S(2)}, u32[]{:S(2)}) collective-permute-start(bf16[512,512]{1,0:T(8,128)(2,1)S(1)} %get-tuple-element.93.g_ref), channel_id=1, source_target_pairs={{0,32},{32,0},{64,96},{96,64},{128,160},{160,128},{192,224},{224,1... | collective-permute-start | bytes 1572872 | tf_op jit(solution)/shard_map/ppermute | solution.py:322
  95.7 11.1 %collective-permute-start.15 = (bf16[512,512]{1,0:T(8,128)(2,1)S(1)}, bf16[512,512]{1,0:T(8,128)(2,1)S(1)}, u32[]{:S(2)}, u32[]{:S(2)}) collective-permute-start(bf16[512,512]{1,0:T(8,128)(2,1)S(1)} %get-tuple-element.96), channel_id=1, source_target_pairs={{0,128},{1,129},{2,130},{3,131},{4,132},{5,133},{6,134},{7,135},{8... | collective-permute-start | bytes 1572872 | tf_op jit(solution)/shard_map/ppermute | solution.py:334
  98.1 14.2 %collective-permute-start.16 = (bf16[512,512]{1,0:T(8,128)(2,1)S(1)}, bf16[512,512]{1,0:T(8,128)(2,1)S(1)}, u32[]{:S(2)}, u32[]{:S(2)}) collective-permute-start(bf16[512,512]{1,0:T(8,128)(2,1)S(1)} %get-tuple-element.97), channel_id=1, source_target_pairs={{0,192},{1,193},{2,194},{3,195},{4,196},{5,197},{6,198},{7,199},{8... | collective-permute-start | bytes 1572872 | tf_op jit(solution)/shard_map/ppermute | solution.py:334
  99.0 13.4 %collective-permute-start.17 = (bf16[512,512]{1,0:T(8,128)(2,1)S(1)}, bf16[512,512]{1,0:T(8,128)(2,1)S(1)}, u32[]{:S(2)}, u32[]{:S(2)}) collective-permute-start(bf16[512,512]{1,0:T(8,128)(2,1)S(1)} %get-tuple-element.98), channel_id=1, source_target_pairs={{0,64},{1,65},{2,66},{3,67},{4,68},{5,69},{6,70},{7,71},{8,72},{9,... | collective-permute-start | bytes 1572872 | tf_op jit(solution)/shard_map/ppermute | solution.py:334
  112.6 6.6 %collective-permute-start.18 = (bf16[128,512]{1,0:T(8,128)(2,1)S(1)}, bf16[128,512]{1,0:T(8,128)(2,1)S(1)}, u32[]{:S(2)}, u32[]{:S(2)}) collective-permute-start(bf16[128,512]{1,0:T(8,128)(2,1)S(1)} %get-tuple-element.100), channel_id=1, source_target_pairs={{0,16},{1,17},{2,18},{3,19},{4,20},{5,21},{6,22},{7,23},{8,24},{9,... | collective-permute-start | bytes 393224 | tf_op jit(solution)/shard_map/ppermute | solution.py:334
  114.2 5.0 %collective-permute-start.19 = (bf16[128,512]{1,0:T(8,128)(2,1)S(1)}, bf16[128,512]{1,0:T(8,128)(2,1)S(1)}, u32[]{:S(2)}, u32[]{:S(2)}) collective-permute-start(bf16[128,512]{1,0:T(8,128)(2,1)S(1)} %get-tuple-element.101), channel_id=1, source_target_pairs={{0,24},{1,25},{2,26},{3,27},{4,28},{5,29},{6,30},{7,31},{8,0},{9,1... | collective-permute-start | bytes 393224 | tf_op jit(solution)/shard_map/ppermute | solution.py:334
  116.0 6.2 %collective-permute-start.20 = (bf16[128,512]{1,0:T(8,128)(2,1)S(1)}, bf16[128,512]{1,0:T(8,128)(2,1)S(1)}, u32[]{:S(2)}, u32[]{:S(2)}) collective-permute-start(bf16[128,512]{1,0:T(8,128)(2,1)S(1)} %get-tuple-element.102), channel_id=1, source_target_pairs={{0,8},{1,9},{2,10},{3,11},{4,12},{5,13},{6,14},{7,15},{8,16},{9,17... | collective-permute-start | bytes 393224 | tf_op jit(solution)/shard_map/ppermute | solution.py:334
  122.9 12.4 %all-to-all-start.3 = ((bf16[8,16,512]{2,1,0:T(8,128)(2,1)}), bf16[8,16,512]{2,1,0:T(8,128)(2,1)S(1)}, u32[]{:S(2)}, u32[]{:S(2)}) async-start(bf16[8,16,512]{2,1,0:T(8,128)(2,1)} %bitcast.5), calls=%async_computation.3 | async-start | bytes 262144 | tf_op jit(solution)/shard_map/all_to_all | solution.py:254

commit v8 on v7

--- a/solution.py
+++ b/solution.py
@@ -278,19 +278,41 @@
         out_ref[k] = part
 
 
-def add_kernel(place_ref, own_ref, g_ref, sw_ref, *out_refs):
-    core = place_ref[1]
-    for k, part in enumerate(terms(place_ref, g_ref[...], sw_ref)):
-        total = (own_ref[k] + part).astype(BF)
-
-        @pl.when(core == 0)
-        def _():
-            out_refs[k][...] = total
-
-        @pl.when(core == 1)
-        def _():
-            for j, ref in enumerate(out_refs):
-                ref[k * NEAR : (k + 1) * NEAR] = total[j * NEAR : (j + 1) * NEAR]
+def far_block_kernel(place_ref, own_ref, g_ref, sw_ref, a_ref, b_ref):
+    halves = a_ref, b_ref
+
+    @pl.when(place_ref[1] == 0)
+    def _():
+        weight = sw_ref[at_block((place_ref[0] + STEPS[3]) % NX, W)]
+        total = (own_ref[3] + dot(g_ref[...], weight, ((1,), (1,)))).astype(BF)
+        for k, ref in enumerate(halves):
+            ref[...] = total[k * N // 2 : (k + 1) * N // 2]
+
+    @pl.when(place_ref[1] == 1)
+    def _():
+        rows = slice(3 * NEAR, N)
+        for k, part in enumerate(terms(place_ref, g_ref[rows], sw_ref)):
+            total = (own_ref[k, rows] + part).astype(BF)
+            halves[k // 2][k % 2 * NEAR : (k % 2 + 1) * NEAR] = total
+
+
+def other_blocks_kernel(place_ref, own_ref, g_ref, sw_ref, *out_refs):
+    @pl.when(place_ref[1] == 0)
+    def _():
+        for k in range(3):
+            weight = sw_ref[at_block((place_ref[0] + STEPS[k]) % NX, W)]
+            total = (own_ref[k] + dot(g_ref[...], weight, ((1,), (1,)))).astype(BF)
+            for j in range(2):
+                out_refs[2 * k + j][...] = total[j * N // 2 : (j + 1) * N // 2]
+
+    @pl.when(place_ref[1] == 1)
+    def _():
+        rows = slice(0, 3 * NEAR)
+        for k, part in enumerate(terms(place_ref, g_ref[rows], sw_ref)):
+            total = (own_ref[k, rows] + part).astype(BF)
+            for j in range(3):
+                ref = out_refs[2 * j + k // 2]
+                ref[k % 2 * NEAR : (k % 2 + 1) * NEAR] = total[j * NEAR : (j + 1) * NEAR]
 
 
 def total_of(refs):
@@ -300,10 +322,16 @@
     return total.astype(BF)
 
 
+def pass_on_kernel(a_ref, b_ref, c_ref, d_ref, first_ref, second_ref):
+    first_ref[...] = total_of((a_ref, b_ref))
+    second_ref[...] = total_of((c_ref, d_ref))
+
+
 def sum_first_kernel(*refs):
-    total = total_of(refs[:4])
-    for k, ref in enumerate(refs[4:]):
-        ref[...] = total[k * NEAR : (k + 1) * NEAR]
+    for j in range(2):
+        total = total_of(refs[3 * j : 3 * j + 3])
+        for k in range(2):
+            refs[6 + 2 * j + k][...] = total[k * NEAR : (k + 1) * NEAR]
 
 
 def sum_second_kernel(*refs):
@@ -436,14 +464,26 @@
     )
     own = call(own_terms_kernel, [SM, VM, VM], [((NX, N, W), F32)], place, g, sw)[0]
     g_other, own = lax.optimization_barrier((to_other_core(g), own))
+    half = ((N // 2, W), BF)
+    far_a, far_b = call(
+        far_block_kernel, [SM] + [VM] * 3, [half] * 2, place, own, g_other, sw2
+    )
+    far_a, far_b = along_first(far_a, 1), along_first(far_b, -1)
+    own_a, own_b, left_a, left_b, right_a, right_b = call(
+        other_blocks_kernel, [SM] + [VM] * 3, [half] * 6, place, own, g_other, sw2
+    )
+    left_a, right_b = along_first(left_a, -1), along_first(right_b, 1)
+    right_a, left_b = call(pass_on_kernel, [VM] * 4, [half] * 2, right_a, far_a, left_b, far_b)
+    right_a, left_b = along_first(right_a, 1), along_first(left_b, -1)
     blocks = call(
-        add_kernel, [SM] + [VM] * 3, [((N, W), BF)] * 4, place, own, g_other, sw2
-    )
-    blocks = call(
-        sum_first_kernel, [VM] * 4, [((NEAR, W), BF)] * 4, *to_ring(blocks, along_first)
-    )
+        sum_first_kernel,
+        [VM] * 6,
+        [((NEAR, W), BF)] * 4,
+        *(own_a, left_a, right_a, own_b, left_b, right_b),
+    )
+    blocks = to_ring(blocks, along_second)
     partial = call(
-        sum_second_kernel, [VM] * 4, [((NEAR, W), BF)], *to_ring(blocks, along_second)
+        sum_second_kernel, [VM] * 4, [((NEAR, W), BF)], *blocks
     )[0]
     hidden_grad = summed(exchange(partial.reshape(NZ, ROWS, W), "tok", Z_GROUPS))
     return loss[0, 0], hidden_grad

time: 138 us -> 137 us (level)
  waiting for transfers between devices: 35.8 us -> 33.1 us
  starting transfers between devices: 27.8 us -> 29.8 us
    ppermute x15 -> x18, waiting for transfers between devices: 24.3 us -> 21.6 us  [along_rings(): return lax.ppermute(a, ('vocab', 'tok'), pairs)]
    ppermute x15 -> x18, starting transfers between devices: 23.1 us -> 25.2 us  [along_rings(): return lax.ppermute(a, ('vocab', 'tok'), pairs)]
    pallas_call x19 -> x21, Pallas kernels: 24.3 us -> 24.3 us  [call(): pl.pallas_call(kernel, in_specs=in_specs, out_specs=[VM] * len(outs), out...]
  transfers between devices with their start and end apart: 22 -> 25, of which waited for: 14 -> 16; matrix products, arithmetic and copies ran while one was open for 0% -> 0% of each run, Pallas kernels for 12% -> 14%
where the time goes in v8:
time: 137 us; the launch traced here: 136 us
  blocking collectives  45.7 us (33%)
  waiting for transfers between devices  33.1 us (24%)
  starting transfers between devices  29.8 us (22%)
  Pallas kernels  24.3 us (18%)
  between operations  2.04 us (1%)
    all_to_all x3, blocking collectives, exchange(): out = lax.all_to_all(flat, axis, 0, 0, axis_index_groups=groups, tiled=True)  45.7 us
    ppermute x18, starting transfers between devices, along_rings(): return lax.ppermute(a, ('vocab', 'tok'), pairs)  25.2 us
    pallas_call x21, Pallas kernels, call(): pl.pallas_call(kernel, in_specs=in_specs, out_specs=[VM] * len(outs), out...  24.3 us
    ppermute x18, waiting for transfers between devices, along_rings(): return lax.ppermute(a, ('vocab', 'tok'), pairs)  21.6 us
    all_to_all x1, waiting for transfers between devices, exchange(): out = lax.all_to_all(flat, axis, 0, 0, axis_index_groups=groups, tiled=True)  8.96 us
    all_to_all x1, starting transfers between devices, exchange(): out = lax.all_to_all(flat, axis, 0, 0, axis_index_groups=groups, tiled=True)  3.37 us
  transfers between devices with their start and end apart: 25, of which 16 were waited for; matrix products, arithmetic and copies ran while one was open for 0% of the time, Pallas kernels for 14%

profile of v8, /device:TPU:6, one launch (start us, length us, event | category | flops | bytes accessed | tf_op | source)
XLA Modules:
  0.0 136.3 jit_solution(16616414264175659097)
XLA Ops:
  0.6 0.1 collective-permute-start
  0.7 0.5 collective-permute-start.1
  1.2 0.7 copy-done
  1.9 1.3 shard_map.68
  3.2 21.1 %all_to_all.30 = bf16[8,16,1152]{2,1,0:T(8,128)(2,1)S(1)} all-to-all(bf16[8,16,1152]{2,1,0:T(8,128)(2,1)S(1)} %shard_map.68), channel_id=1, replica_groups={{0,1,2,3,4,5,6,7},{8,9,10,11,12,13,14,15},{16,17,18,19,20,21,22,23},{24..., dimensions={0} | all-to-all | bytes 589824 | tf_op jit(solution)/shard_map/all_to_all | solution.py:254
  24.3 3.3 %collective-permute-start.2 = (bf16[128,1152]{1,0:T(8,128)(2,1)S(1)}, bf16[128,1152]{1,0:T(8,128)(2,1)S(1)}, u32[]{:S(2)}, u32[]{:S(2)}) collective-permute-start(bf16[128,1152]{1,0:T(8,128)(2,1)S(1)} %bitcast.6), channel_id=1, source_target_pairs={{0,16},{1,17},{2,18},{3,19},{4,20},{5,21},{6,22},{7,23},{8,24},{9,... | collective-permute-start | bytes 884744 | tf_op jit(solution)/shard_map/ppermute | solution.py:362
  27.6 0.7 collective-permute-start.3
  28.3 2.6 %collective-permute-start.4 = (bf16[128,1152]{1,0:T(8,128)(2,1)S(1)}, bf16[128,1152]{1,0:T(8,128)(2,1)S(1)}, u32[]{:S(2)}, u32[]{:S(2)}) collective-permute-start(bf16[128,1152]{1,0:T(8,128)(2,1)S(1)} %bitcast.8), channel_id=1, source_target_pairs={{0,24},{1,25},{2,26},{3,27},{4,28},{5,29},{6,30},{7,31},{8,0},{9,1... | collective-permute-start | bytes 884744 | tf_op jit(solution)/shard_map/ppermute | solution.py:362
  30.9 0.1 pad_add_fusion.place_ref
  30.9 1.7 %collective-permute-done.2.far_ref = bf16[128,1152]{1,0:T(8,128)(2,1)S(1)} collective-permute-done((bf16[128,1152]{1,0:T(8,128)(2,1)S(1)}, bf16[128,1152]{1,0:T(8,128)(2,1)S(1)}, u32[]{:S(2)}, u32[]{:S(2)}) %collective-permute-start.2) | collective-permute-done | bytes 294944 | tf_op jit(solution)/shard_map/ppermute | solution.py:362
  32.7 3.1 %collective-permute-done.3.left_ref = bf16[128,1152]{1,0:T(8,128)(2,1)S(1)} collective-permute-done((bf16[128,1152]{1,0:T(8,128)(2,1)S(1)}, bf16[128,1152]{1,0:T(8,128)(2,1)S(1)}, u32[]{:S(2)}, u32[]{:S(2)}) %collective-permute-start.3) | collective-permute-done | bytes 294944 | tf_op jit(solution)/shard_map/ppermute | solution.py:362
  35.8 0.3 collective-permute-done.4.right_ref
  36.1 0.6 shard_map.69
  36.8 0.6 collective-permute-start.5
  37.3 1.5 %collective-permute-start.6 = (bf16[256,1024]{1,0:T(8,128)(2,1)S(1)}, bf16[256,1024]{1,0:T(8,128)(2,1)S(1)}, u32[]{:S(2)}, u32[]{:S(2)}) collective-permute-start(bf16[256,1024]{1,0:T(8,128)(2,1)S(1)} %get-tuple-element.61.refs_1_), channel_id=1, source_target_pairs={{0,192},{1,193},{2,194},{3,195},{4,196},{5,197},{6,198},{7,199},{8... | collective-permute-start | bytes 1572872 | tf_op jit(solution)/shard_map/ppermute | solution.py:362
  38.9 0.8 collective-permute-start.10
  39.7 2.4 %collective-permute-start.9 = (bf16[256,1024]{1,0:T(8,128)(2,1)S(1)}, bf16[256,1024]{1,0:T(8,128)(2,1)S(1)}, u32[]{:S(2)}, u32[]{:S(2)}) collective-permute-start(bf16[256,1024]{1,0:T(8,128)(2,1)S(1)} %get-tuple-element.61.refs_1_), channel_id=1, source_target_pairs={{0,64},{1,65},{2,66},{3,67},{4,68},{5,69},{6,70},{7,71},{8,72},{9,... | collective-permute-start | bytes 1572872 | tf_op jit(solution)/shard_map/ppermute | solution.py:362
  42.1 4.1 %shard_map.70 = (bf16[2048,512]{1,0:T(8,128)(2,1)S(1)}, bf16[2048,512]{1,0:T(8,128)(2,1)S(1)}, bf16[2048,512]{1,0:T(8,128)(2,1)S(1)}, bf16[2048,512]{1,0:T(8,128)(2,1)S(1)}) custom-call(s32[3]{0:T(128)S(1)} %pad_add_fusion.place_ref, bf16[4096,512]{1,0:T(8,128)(2,1)} %refs_0_.1, bf16[4096,512]{1,0:T(8,128)(2,1)} %refs_1_.1, bf16[4096,512]{1,0:T(8,128)(2,1)} %copy-done.1, ...), custom_call_target="tpu_custom_call" | custom-call | tf_op jit(solution)/shard_map/pallas_call | solution.py:49
  46.2 1.5 %collective-permute-done.6.refs_3_ = bf16[256,1024]{1,0:T(8,128)(2,1)S(1)} collective-permute-done((bf16[256,1024]{1,0:T(8,128)(2,1)S(1)}, bf16[256,1024]{1,0:T(8,128)(2,1)S(1)}, u32[]{:S(2)}, u32[]{:S(2)}) %collective-permute-start.6) | collective-permute-done | bytes 524320 | tf_op jit(solution)/shard_map/ppermute | solution.py:362
  47.7 0.3 collective-permute-start.7
  48.0 1.7 %collective-permute-start.8 = (bf16[256,1024]{1,0:T(8,128)(2,1)S(1)}, bf16[256,1024]{1,0:T(8,128)(2,1)S(1)}, u32[]{:S(2)}, u32[]{:S(2)}) collective-permute-start(bf16[256,1024]{1,0:T(8,128)(2,1)S(1)} %collective-permute-done.6.refs_3_), channel_id=1, source_target_pairs={{0,192},{1,193},{2,194},{3,195},{4,196},{5,197},{6,198},{7,199},{8... | collective-permute-start | bytes 1572872 | tf_op jit(solution)/shard_map/ppermute | solution.py:362
  49.8 1.3 collective-permute-done.11.other_ref
  51.1 0.8 shard_map.75.select_ref
  51.9 1.3 shard_map.72.refs_4_
  53.2 1.3 shard_map.71.refs_4_
  54.5 2.0 %shard_map.74.near_ref = f32[2,512,512]{2,1,0:T(8,128)S(1)} custom-call(s32[3]{0:T(128)S(1)} %pad_add_fusion.place_ref, bf16[2048,512]{1,0:T(8,128)(2,1)S(1)} %get-tuple-element.68.sw_ref, bf16[2048,512]{1,0:T(8,128)(2,1)S(1)} %get-tuple-element.69.tw_ref, bf16[256,1024]{1,0:T(8,128)(2,1)S(1)} %collective-permute-done.5.refs_0_, ...), custom_call_target="tpu_custom_call" | custom-call | flops 1073741824 | tf_op jit(solution)/shard_map/pallas_call | solution.py:49
  56.5 1.8 %shard_map.73.near_ref = f32[2,512,512]{2,1,0:T(8,128)S(1)} custom-call(s32[3]{0:T(128)S(1)} %pad_add_fusion.place_ref, bf16[2048,512]{1,0:T(8,128)(2,1)S(1)} %get-tuple-element.72.sw_ref, bf16[2048,512]{1,0:T(8,128)(2,1)S(1)} %get-tuple-element.73.tw_ref, bf16[256,1024]{1,0:T(8,128)(2,1)S(1)} %collective-permute-done.5.refs_0_, ...), custom_call_target="tpu_custom_call" | custom-call | flops 1073741824 | tf_op jit(solution)/shard_map/pallas_call | solution.py:49
  58.3 0.7 collective-permute-done.8.p4
  59.0 1.3 shard_map.77
  60.2 0.1 collective-permute-start.13
  60.4 0.5 collective-permute-start.12
  60.8 1.3 shard_map.76
  62.1 0.9 collective-permute-done.13.other_ref
  63.0 1.2 shard_map.78
  64.2 0.3 collective-permute-done.12.other_ref
  64.5 0.5 shard_map.79
  65.0 7.9 %all_to_all.31.in_ref = f32[8,8,256]{2,1,0:T(8,128)S(1)} all-to-all(f32[8,8,256]{2,1,0:T(8,128)S(1)} %get-tuple-element.95), channel_id=1, replica_groups=mesh['vocab'=8,'tok'=32] {'vocab'}, dimensions={0} | all-to-all | bytes 131072 | tf_op jit(solution)/shard_map/all_to_all | solution.py:254
  72.9 0.1 shard_map.80
  73.0 16.7 %all_to_all.32.stat_ref = f32[32,8,256]{2,1,0:T(8,128)S(1)} all-to-all(f32[32,8,256]{2,1,0:T(8,128)S(1)} %shard_map.80), channel_id=1, replica_groups=mesh['vocab'=8,'tok'=32] {'tok'}, dimensions={0} | all-to-all | bytes 524288 | tf_op jit(solution)/shard_map/all_to_all | solution.py:254
  89.8 1.3 shard_map.81
  91.1 0.1 collective-permute-start.14
  91.2 1.8 %shard_map.82.own_ref = f32[4,512,512]{2,1,0:T(8,128)S(1)} custom-call(s32[3]{0:T(128)S(1)} %pad_add_fusion.place_ref, bf16[512,512]{1,0:T(8,128)(2,1)S(1)} %get-tuple-element.99.g_ref, bf16[2048,512]{1,0:T(8,128)(2,1)S(1)} %get-tuple-element.68.sw_ref), custom_call_target="tpu_custom_call" | custom-call | tf_op jit(solution)/shard_map/pallas_call | solution.py:49
  93.1 1.0 shard_map.84
  94.1 2.1 %collective-permute-start.16 = (bf16[256,512]{1,0:T(8,128)(2,1)S(1)}, bf16[256,512]{1,0:T(8,128)(2,1)S(1)}, u32[]{:S(2)}, u32[]{:S(2)}) collective-permute-start(bf16[256,512]{1,0:T(8,128)(2,1)S(1)} %get-tuple-element.105), channel_id=1, source_target_pairs={{0,64},{1,65},{2,66},{3,67},{4,68},{5,69},{6,70},{7,71},{8,72},{9,... | collective-permute-start | bytes 786440 | tf_op jit(solution)/shard_map/ppermute | solution.py:362
  96.3 1.6 %shard_map.83 = (bf16[256,512]{1,0:T(8,128)(2,1)S(1)}, bf16[256,512]{1,0:T(8,128)(2,1)S(1)}, bf16[256,512]{1,0:T(8,128)(2,1)S(1)}, bf16[256,512]{1,0:T(8,128)(2,...) custom-call(s32[3]{0:T(128)S(1)} %pad_add_fusion.place_ref, f32[4,512,512]{2,1,0:T(8,128)S(1)} %shard_map.82.own_ref, ...), custom_call_target="tpu_custom_call" | custom-call | tf_op jit(solution)/shard_map/pallas_call | solution.py:49
  97.9 0.4 collective-permute-start.15
  98.3 3.0 %collective-permute-start.20 = (bf16[256,512]{1,0:T(8,128)(2,1)S(1)}, bf16[256,512]{1,0:T(8,128)(2,1)S(1)}, u32[]{:S(2)}, u32[]{:S(2)}) collective-permute-start(bf16[256,512]{1,0:T(8,128)(2,1)S(1)} %get-tuple-element.111), channel_id=1, source_target_pairs={{0,64},{1,65},{2,66},{3,67},{4,68},{5,69},{6,70},{7,71},{8,72},{9,... | collective-permute-start | bytes 786440 | tf_op jit(solution)/shard_map/ppermute | solution.py:362
  101.3 2.6 %collective-permute-done.17.d_ref = bf16[256,512]{1,0:T(8,128)(2,1)S(1)} collective-permute-done((bf16[256,512]{1,0:T(8,128)(2,1)S(1)}, bf16[256,512]{1,0:T(8,128)(2,1)S(1)}, u32[]{:S(2)}, u32[]{:S(2)}) %collective-permute-start.17) | collective-permute-done | bytes 262176 | tf_op jit(solution)/shard_map/ppermute | solution.py:362
  103.9 0.1 shard_map.85
  104.0 0.1 collective-permute-start.18
  104.1 2.0 %collective-permute-start.19 = (bf16[256,512]{1,0:T(8,128)(2,1)S(1)}, bf16[256,512]{1,0:T(8,128)(2,1)S(1)}, u32[]{:S(2)}, u32[]{:S(2)}) collective-permute-start(bf16[256,512]{1,0:T(8,128)(2,1)S(1)} %get-tuple-element.110), channel_id=1, source_target_pairs={{0,192},{1,193},{2,194},{3,195},{4,196},{5,197},{6,198},{7,199},{8... | collective-permute-start | bytes 786440 | tf_op jit(solution)/shard_map/ppermute | solution.py:362
  106.1 0.6 collective-permute-done.15.refs_1_
  106.7 3.8 %collective-permute-done.18.refs_2_ = bf16[256,512]{1,0:T(8,128)(2,1)S(1)} collective-permute-done((bf16[256,512]{1,0:T(8,128)(2,1)S(1)}, bf16[256,512]{1,0:T(8,128)(2,1)S(1)}, u32[]{:S(2)}, u32[]{:S(2)}) %collective-permute-start.18) | collective-permute-done | bytes 262176 | tf_op jit(solution)/shard_map/ppermute | solution.py:362
  110.4 1.3 collective-permute-done.19.refs_4_
  111.7 0.2 shard_map.86
  111.9 1.6 %collective-permute-start.21 = (bf16[128,512]{1,0:T(8,128)(2,1)S(1)}, bf16[128,512]{1,0:T(8,128)(2,1)S(1)}, u32[]{:S(2)}, u32[]{:S(2)}) collective-permute-start(bf16[128,512]{1,0:T(8,128)(2,1)S(1)} %get-tuple-element.112), channel_id=1, source_target_pairs={{0,16},{1,17},{2,18},{3,19},{4,20},{5,21},{6,22},{7,23},{8,24},{9,... | collective-permute-start | bytes 393224 | tf_op jit(solution)/shard_map/ppermute | solution.py:362
  113.5 1.8 %collective-permute-start.22 = (bf16[128,512]{1,0:T(8,128)(2,1)S(1)}, bf16[128,512]{1,0:T(8,128)(2,1)S(1)}, u32[]{:S(2)}, u32[]{:S(2)}) collective-permute-start(bf16[128,512]{1,0:T(8,128)(2,1)S(1)} %get-tuple-element.113), channel_id=1, source_target_pairs={{0,24},{1,25},{2,26},{3,27},{4,28},{5,29},{6,30},{7,31},{8,0},{9,1... | collective-permute-start | bytes 393224 | tf_op jit(solution)/shard_map/ppermute | solution.py:362
  115.3 0.2 collective-permute-start.23
  115.6 2.9 %collective-permute-done.21.refs_0_ = bf16[128,512]{1,0:T(8,128)(2,1)S(1)} collective-permute-done((bf16[128,512]{1,0:T(8,128)(2,1)S(1)}, bf16[128,512]{1,0:T(8,128)(2,1)S(1)}, u32[]{:S(2)}, u32[]{:S(2)}) %collective-permute-start.21) | collective-permute-done | bytes 131104 | tf_op jit(solution)/shard_map/ppermute | solution.py:362
  118.5 3.0 %collective-permute-done.23.refs_2_ = bf16[128,512]{1,0:T(8,128)(2,1)S(1)} collective-permute-done((bf16[128,512]{1,0:T(8,128)(2,1)S(1)}, bf16[128,512]{1,0:T(8,128)(2,1)S(1)}, u32[]{:S(2)}, u32[]{:S(2)}) %collective-permute-start.23) | collective-permute-done | bytes 131104 | tf_op jit(solution)/shard_map/ppermute | solution.py:362
  121.5 0.7 shard_map.87
  122.2 3.4 %all-to-all-start.3 = ((bf16[8,16,512]{2,1,0:T(8,128)(2,1)}), bf16[8,16,512]{2,1,0:T(8,128)(2,1)S(1)}, u32[]{:S(2)}, u32[]{:S(2)}) async-start(bf16[8,16,512]{2,1,0:T(8,128)(2,1)} %bitcast.5), calls=%async_computation.3 | async-start | bytes 262144 | tf_op jit(solution)/shard_map/all_to_all | solution.py:254
  125.6 9.0 %all-to-all-done.3.in_ref = bf16[8,16,512]{2,1,0:T(8,128)(2,1)S(1)} async-done(((bf16[8,16,512]{2,1,0:T(8,128)(2,1)}), bf16[8,16,512]{2,1,0:T(8,128)(2,1)S(1)}, u32[]{:S(2)}, u32[]{:S(2)}) %all-to-all-start.3) | async-done | bytes 131104 | tf_op jit(solution)/shard_map/all_to_all | solution.py:254
  134.6 0.6 copy.8
  (18 shorter events, 0.1 us)
Async XLA Ops:
  0.6 23.7 %collective-permute-start = (bf16[4096,512]{1,0:T(8,128)(2,1)}, bf16[4096,512]{1,0:T(8,128)(2,1)S(1)}, u32[]{:S(2)}, u32[]{:S(2)}) collective-permute-start(bf16[4096,512]{1,0:T(8,128)(2,1)} %refs_0_.1), channel_id=1, source_target_pairs={{0,32},{32,0},{64,96},{96,64},{128,160},{160,128},{192,224},{224,1... | collective-permute-start | bytes 12582920 | tf_op jit(solution)/shard_map/ppermute | solution.py:350
  0.7 23.6 %collective-permute-start.1 = (bf16[4096,512]{1,0:T(8,128)(2,1)}, bf16[4096,512]{1,0:T(8,128)(2,1)S(1)}, u32[]{:S(2)}, u32[]{:S(2)}) collective-permute-start(bf16[4096,512]{1,0:T(8,128)(2,1)} %refs_1_.1), channel_id=1, source_target_pairs={{0,32},{32,0},{64,96},{96,64},{128,160},{160,128},{192,224},{224,1... | collective-permute-start | bytes 12582920 | tf_op jit(solution)/shard_map/ppermute | solution.py:350
  1.2 0.7 copy-start
  24.3 3.3 %copy-start.1 = (bf16[4096,512]{1,0:T(8,128)(2,1)}, bf16[4096,512]{1,0:T(8,128)(2,1)S(1)}, u32[]{:S(2)}) copy-start(bf16[4096,512]{1,0:T(8,128)(2,1)S(1)} %collective-permute-done.refs_2_) | copy-start | bytes 12582916
  24.3 4.0 %copy-start.2 = (bf16[4096,512]{1,0:T(8,128)(2,1)}, bf16[4096,512]{1,0:T(8,128)(2,1)S(1)}, u32[]{:S(2)}) copy-start(bf16[4096,512]{1,0:T(8,128)(2,1)S(1)} %collective-permute-done.1.refs_3_) | copy-start | bytes 12582916
  24.3 8.3 %collective-permute-start.2 = (bf16[128,1152]{1,0:T(8,128)(2,1)S(1)}, bf16[128,1152]{1,0:T(8,128)(2,1)S(1)}, u32[]{:S(2)}, u32[]{:S(2)}) collective-permute-start(bf16[128,1152]{1,0:T(8,128)(2,1)S(1)} %bitcast.6), channel_id=1, source_target_pairs={{0,16},{1,17},{2,18},{3,19},{4,20},{5,21},{6,22},{7,23},{8,24},{9,... | collective-permute-start | bytes 884744 | tf_op jit(solution)/shard_map/ppermute | solution.py:362
  27.6 8.2 %collective-permute-start.3 = (bf16[128,1152]{1,0:T(8,128)(2,1)S(1)}, bf16[128,1152]{1,0:T(8,128)(2,1)S(1)}, u32[]{:S(2)}, u32[]{:S(2)}) collective-permute-start(bf16[128,1152]{1,0:T(8,128)(2,1)S(1)} %bitcast.7), channel_id=1, source_target_pairs={{0,8},{1,9},{2,10},{3,11},{4,12},{5,13},{6,14},{7,15},{8,16},{9,17... | collective-permute-start | bytes 884744 | tf_op jit(solution)/shard_map/ppermute | solution.py:362
  28.3 7.9 %collective-permute-start.4 = (bf16[128,1152]{1,0:T(8,128)(2,1)S(1)}, bf16[128,1152]{1,0:T(8,128)(2,1)S(1)}, u32[]{:S(2)}, u32[]{:S(2)}) collective-permute-start(bf16[128,1152]{1,0:T(8,128)(2,1)S(1)} %bitcast.8), channel_id=1, source_target_pairs={{0,24},{1,25},{2,26},{3,27},{4,28},{5,29},{6,30},{7,31},{8,0},{9,1... | collective-permute-start | bytes 884744 | tf_op jit(solution)/shard_map/ppermute | solution.py:362
  36.8 9.4 %collective-permute-start.5 = (bf16[256,1024]{1,0:T(8,128)(2,1)S(1)}, bf16[256,1024]{1,0:T(8,128)(2,1)S(1)}, u32[]{:S(2)}, u32[]{:S(2)}) collective-permute-start(bf16[256,1024]{1,0:T(8,128)(2,1)S(1)} %get-tuple-element.60.refs_0_), channel_id=1, source_target_pairs={{0,64},{1,65},{2,66},{3,67},{4,68},{5,69},{6,70},{7,71},{8,72},{9,... | collective-permute-start | bytes 1572872 | tf_op jit(solution)/shard_map/ppermute | solution.py:362
  37.3 10.4 %collective-permute-start.6 = (bf16[256,1024]{1,0:T(8,128)(2,1)S(1)}, bf16[256,1024]{1,0:T(8,128)(2,1)S(1)}, u32[]{:S(2)}, u32[]{:S(2)}) collective-permute-start(bf16[256,1024]{1,0:T(8,128)(2,1)S(1)} %get-tuple-element.61.refs_1_), channel_id=1, source_target_pairs={{0,192},{1,193},{2,194},{3,195},{4,196},{5,197},{6,198},{7,199},{8... | collective-permute-start | bytes 1572872 | tf_op jit(solution)/shard_map/ppermute | solution.py:362
  38.9 15.5 %collective-permute-start.10 = (bf16[256,1024]{1,0:T(8,128)(2,1)S(1)}, bf16[256,1024]{1,0:T(8,128)(2,1)S(1)}, u32[]{:S(2)}, u32[]{:S(2)}) collective-permute-start(bf16[256,1024]{1,0:T(8,128)(2,1)S(1)} %get-tuple-element.60.refs_0_), channel_id=1, source_target_pairs={{0,192},{1,193},{2,194},{3,195},{4,196},{5,197},{6,198},{7,199},{8... | collective-permute-start | bytes 1572872 | tf_op jit(solution)/shard_map/ppermute | solution.py:362
  39.7 14.7 %collective-permute-start.9 = (bf16[256,1024]{1,0:T(8,128)(2,1)S(1)}, bf16[256,1024]{1,0:T(8,128)(2,1)S(1)}, u32[]{:S(2)}, u32[]{:S(2)}) collective-permute-start(bf16[256,1024]{1,0:T(8,128)(2,1)S(1)} %get-tuple-element.61.refs_1_), channel_id=1, source_target_pairs={{0,64},{1,65},{2,66},{3,67},{4,68},{5,69},{6,70},{7,71},{8,72},{9,... | collective-permute-start | bytes 1572872 | tf_op jit(solution)/shard_map/ppermute | solution.py:362
  47.7 10.5 %collective-permute-start.7 = (bf16[256,1024]{1,0:T(8,128)(2,1)S(1)}, bf16[256,1024]{1,0:T(8,128)(2,1)S(1)}, u32[]{:S(2)}, u32[]{:S(2)}) collective-permute-start(bf16[256,1024]{1,0:T(8,128)(2,1)S(1)} %collective-permute-done.5.refs_0_), channel_id=1, source_target_pairs={{0,64},{1,65},{2,66},{3,67},{4,68},{5,69},{6,70},{7,71},{8,72},{9,... | collective-permute-start | bytes 1572872 | tf_op jit(solution)/shard_map/ppermute | solution.py:362
  48.0 11.0 %collective-permute-start.8 = (bf16[256,1024]{1,0:T(8,128)(2,1)S(1)}, bf16[256,1024]{1,0:T(8,128)(2,1)S(1)}, u32[]{:S(2)}, u32[]{:S(2)}) collective-permute-start(bf16[256,1024]{1,0:T(8,128)(2,1)S(1)} %collective-permute-done.6.refs_3_), channel_id=1, source_target_pairs={{0,192},{1,193},{2,194},{3,195},{4,196},{5,197},{6,198},{7,199},{8... | collective-permute-start | bytes 1572872 | tf_op jit(solution)/shard_map/ppermute | solution.py:362
  49.8 1.3 collective-permute-start.11
  60.2 2.7 %collective-permute-start.13 = (f32[512,512]{1,0:T(8,128)S(1)}, f32[512,512]{1,0:T(8,128)S(1)}, u32[]{:S(2)}, u32[]{:S(2)}) collective-permute-start(f32[512,512]{1,0:T(8,128)S(1)} %get-tuple-element.86), channel_id=1, source_target_pairs={{0,32},{32,0},{64,96},{96,64},{128,160},{160,128},{192,224},{224,1... | collective-permute-start | bytes 3145736 | tf_op jit(solution)/shard_map/ppermute | solution.py:350
  60.4 4.1 %collective-permute-start.12 = (f32[512,512]{1,0:T(8,128)S(1)}, f32[512,512]{1,0:T(8,128)S(1)}, u32[]{:S(2)}, u32[]{:S(2)}) collective-permute-start(f32[512,512]{1,0:T(8,128)S(1)} %get-tuple-element.84), channel_id=1, source_target_pairs={{0,32},{32,0},{64,96},{96,64},{128,160},{160,128},{192,224},{224,1... | collective-permute-start | bytes 3145736 | tf_op jit(solution)/shard_map/ppermute | solution.py:350
  91.1 2.0 %collective-permute-start.14 = (bf16[512,512]{1,0:T(8,128)(2,1)S(1)}, bf16[512,512]{1,0:T(8,128)(2,1)S(1)}, u32[]{:S(2)}, u32[]{:S(2)}) collective-permute-start(bf16[512,512]{1,0:T(8,128)(2,1)S(1)} %get-tuple-element.99.g_ref), channel_id=1, source_target_pairs={{0,32},{32,0},{64,96},{96,64},{128,160},{160,128},{192,224},{224,1... | collective-permute-start | bytes 1572872 | tf_op jit(solution)/shard_map/ppermute | solution.py:350
  94.1 7.1 %collective-permute-start.16 = (bf16[256,512]{1,0:T(8,128)(2,1)S(1)}, bf16[256,512]{1,0:T(8,128)(2,1)S(1)}, u32[]{:S(2)}, u32[]{:S(2)}) collective-permute-start(bf16[256,512]{1,0:T(8,128)(2,1)S(1)} %get-tuple-element.105), channel_id=1, source_target_pairs={{0,64},{1,65},{2,66},{3,67},{4,68},{5,69},{6,70},{7,71},{8,72},{9,... | collective-permute-start | bytes 786440 | tf_op jit(solution)/shard_map/ppermute | solution.py:362
  96.3 7.6 %collective-permute-start.17 = (bf16[256,512]{1,0:T(8,128)(2,1)S(1)}, bf16[256,512]{1,0:T(8,128)(2,1)S(1)}, u32[]{:S(2)}, u32[]{:S(2)}) collective-permute-start(bf16[256,512]{1,0:T(8,128)(2,1)S(1)} %get-tuple-element.107), channel_id=1, source_target_pairs={{0,192},{1,193},{2,194},{3,195},{4,196},{5,197},{6,198},{7,199},{8... | collective-permute-start | bytes 786440 | tf_op jit(solution)/shard_map/ppermute | solution.py:362
  97.9 8.8 %collective-permute-start.15 = (bf16[256,512]{1,0:T(8,128)(2,1)S(1)}, bf16[256,512]{1,0:T(8,128)(2,1)S(1)}, u32[]{:S(2)}, u32[]{:S(2)}) collective-permute-start(bf16[256,512]{1,0:T(8,128)(2,1)S(1)} %get-tuple-element.103), channel_id=1, source_target_pairs={{0,192},{1,193},{2,194},{3,195},{4,196},{5,197},{6,198},{7,199},{8... | collective-permute-start | bytes 786440 | tf_op jit(solution)/shard_map/ppermute | solution.py:362
  98.3 8.4 %collective-permute-start.20 = (bf16[256,512]{1,0:T(8,128)(2,1)S(1)}, bf16[256,512]{1,0:T(8,128)(2,1)S(1)}, u32[]{:S(2)}, u32[]{:S(2)}) collective-permute-start(bf16[256,512]{1,0:T(8,128)(2,1)S(1)} %get-tuple-element.111), channel_id=1, source_target_pairs={{0,64},{1,65},{2,66},{3,67},{4,68},{5,69},{6,70},{7,71},{8,72},{9,... | collective-permute-start | bytes 786440 | tf_op jit(solution)/shard_map/ppermute | solution.py:362
  104.0 6.4 %collective-permute-start.18 = (bf16[256,512]{1,0:T(8,128)(2,1)S(1)}, bf16[256,512]{1,0:T(8,128)(2,1)S(1)}, u32[]{:S(2)}, u32[]{:S(2)}) collective-permute-start(bf16[256,512]{1,0:T(8,128)(2,1)S(1)} %get-tuple-element.108), channel_id=1, source_target_pairs={{0,64},{1,65},{2,66},{3,67},{4,68},{5,69},{6,70},{7,71},{8,72},{9,... | collective-permute-start | bytes 786440 | tf_op jit(solution)/shard_map/ppermute | solution.py:362
  104.1 7.7 %collective-permute-start.19 = (bf16[256,512]{1,0:T(8,128)(2,1)S(1)}, bf16[256,512]{1,0:T(8,128)(2,1)S(1)}, u32[]{:S(2)}, u32[]{:S(2)}) collective-permute-start(bf16[256,512]{1,0:T(8,128)(2,1)S(1)} %get-tuple-element.110), channel_id=1, source_target_pairs={{0,192},{1,193},{2,194},{3,195},{4,196},{5,197},{6,198},{7,199},{8... | collective-permute-start | bytes 786440 | tf_op jit(solution)/shard_map/ppermute | solution.py:362
  111.9 6.6 %collective-permute-start.21 = (bf16[128,512]{1,0:T(8,128)(2,1)S(1)}, bf16[128,512]{1,0:T(8,128)(2,1)S(1)}, u32[]{:S(2)}, u32[]{:S(2)}) collective-permute-start(bf16[128,512]{1,0:T(8,128)(2,1)S(1)} %get-tuple-element.112), channel_id=1, source_target_pairs={{0,16},{1,17},{2,18},{3,19},{4,20},{5,21},{6,22},{7,23},{8,24},{9,... | collective-permute-start | bytes 393224 | tf_op jit(solution)/shard_map/ppermute | solution.py:362
  113.5 5.0 %collective-permute-start.22 = (bf16[128,512]{1,0:T(8,128)(2,1)S(1)}, bf16[128,512]{1,0:T(8,128)(2,1)S(1)}, u32[]{:S(2)}, u32[]{:S(2)}) collective-permute-start(bf16[128,512]{1,0:T(8,128)(2,1)S(1)} %get-tuple-element.113), channel_id=1, source_target_pairs={{0,24},{1,25},{2,26},{3,27},{4,28},{5,29},{6,30},{7,31},{8,0},{9,1... | collective-permute-start | bytes 393224 | tf_op jit(solution)/shard_map/ppermute | solution.py:362
  115.3 6.2 %collective-permute-start.23 = (bf16[128,512]{1,0:T(8,128)(2,1)S(1)}, bf16[128,512]{1,0:T(8,128)(2,1)S(1)}, u32[]{:S(2)}, u32[]{:S(2)}) collective-permute-start(bf16[128,512]{1,0:T(8,128)(2,1)S(1)} %get-tuple-element.114), channel_id=1, source_target_pairs={{0,8},{1,9},{2,10},{3,11},{4,12},{5,13},{6,14},{7,15},{8,16},{9,17... | collective-permute-start | bytes 393224 | tf_op jit(solution)/shard_map/ppermute | solution.py:362
  122.2 12.4 %all-to-all-start.3 = ((bf16[8,16,512]{2,1,0:T(8,128)(2,1)}), bf16[8,16,512]{2,1,0:T(8,128)(2,1)S(1)}, u32[]{:S(2)}, u32[]{:S(2)}) async-start(bf16[8,16,512]{2,1,0:T(8,128)(2,1)} %bitcast.5), calls=%async_computation.3 | async-start | bytes 262144 | tf_op jit(solution)/shard_map/all_to_all | solution.py:254

commit v9 on v8

--- a/solution.py
+++ b/solution.py
@@ -20,6 +20,23 @@
 HALF = NX * W
 MIB = 1 << 20
 STEPS = (0, -1, 1, 2)
+STAT = 16
+
+
+def device(x, core, y, z):
+    return (2 * x + core) * TOK + y * NZ + z
+
+
+CORE_Z_GROUPS = [
+    [device(x, core, y, z) for core in range(2) for z in range(NZ)]
+    for x in range(NX)
+    for y in range(NY)
+]
+X_Y_GROUPS = [
+    [device(x, core, y, z) for x in range(NX) for y in range(NY)]
+    for core in range(2)
+    for z in range(NZ)
+]
 Z_GROUPS = [[y * NZ + z for z in range(NZ)] for y in range(NY)]
 
 
@@ -67,13 +84,14 @@
     return copy
 
 
-def pack_kernel(source_ref, s_ref, t_ref, out_ref, s_buf, t_buf, sem):
+def pack_kernel(source_hbm, s_ref, t_ref, out_ref, s_buf, t_buf, source_ref, sem):
     v = lax.axis_index("vocab")
     columns = at_block(v, W)
     copies = [
         started(s_ref.at[:, columns], s_buf, sem.at[0]),
         started(t_ref.at[:, columns], t_buf, sem.at[1]),
     ]
+    started(source_hbm, source_ref, sem.at[2]).wait()
     row = lax.broadcasted_iota(jnp.int32, (ROWS, 128), 0)
     lane = lax.broadcasted_iota(jnp.int32, (ROWS, 128), 1)
     digits = jnp.zeros((ROWS, 128), jnp.int32)
@@ -278,6 +296,10 @@
         out_ref[k] = part
 
 
+def to_hbm_kernel(in_ref, out_ref, sem):
+    started(in_ref, out_ref, sem).wait()
+
+
 def far_block_kernel(place_ref, own_ref, g_ref, sw_ref, a_ref, b_ref):
     halves = a_ref, b_ref
 
@@ -385,10 +407,11 @@
     place = jnp.stack([v // 2, v % 2, y])
     packed = call(
         pack_kernel,
-        [SM, HBM, HBM],
+        [HBM, HBM, HBM],
         [((NZ, ROWS, 2 * W + 128), BF)],
-        source_rows, in_hbm(student_hidden), in_hbm(teacher_hidden),
-        scratch=[pltpu.VMEM((ROWS, W), BF)] * 2 + [pltpu.SemaphoreType.DMA((2,))],
+        in_hbm(source_rows), in_hbm(student_hidden), in_hbm(teacher_hidden),
+        scratch=[pltpu.VMEM((ROWS, W), BF)] * 2
+        + [pltpu.SMEM((ROWS,), jnp.int32), pltpu.SemaphoreType.DMA((3,))],
     )[0]
     sw2, tw2 = to_other_core(student_weight), to_other_core(teacher_weight)
     near = exchange(packed, "tok", Z_GROUPS).reshape(NEAR, 2 * W + 128)
@@ -449,12 +472,12 @@
     s, d, stats = call(
         student_logits_kernel,
         [VM] * 4,
-        logits * 2 + [((VOC, 8, N // 2), F32)],
+        logits * 2 + [((STAT, 8, N // 2), F32)],
         s_own, s_other, t, table,
     )
-    stats = exchange(stats, "vocab")
-    stats = call(merge_kernel, [VM], [((TOK, 8, N // 2), F32)], stats)[0]
-    stats = exchange(stats, "tok")
+    stats = exchange(stats, ("vocab", "tok"), X_Y_GROUPS)
+    stats = call(merge_kernel, [VM], [((STAT, 8, N // 2), F32)], stats)[0]
+    stats = exchange(stats, ("vocab", "tok"), CORE_Z_GROUPS)
     g, loss = call(
         logit_grad_kernel,
         [SM] + [VM] * 3,
@@ -482,6 +505,16 @@
         *(own_a, left_a, right_a, own_b, left_b, right_b),
     )
     blocks = to_ring(blocks, along_second)
+    loss = pl.pallas_call(
+        to_hbm_kernel,
+        in_specs=[VM],
+        out_specs=HBM,
+        out_shape=pltpu.HBM((1, 1), F32),
+        scratch_shapes=[pltpu.SemaphoreType.DMA(())],
+        compiler_params=PARAMS,
+        cost_estimate=cost(0),
+    )(loss)
+    blocks, loss = lax.optimization_barrier((blocks, loss))
     partial = call(
         sum_second_kernel, [VM] * 4, [((NEAR, W), BF)], *blocks
     )[0]

time: 137 us -> 132 us (0.964)
  blocking collectives: 45.7 us -> 56.7 us
  waiting for transfers between devices: 33.1 us -> 22.6 us
  starting transfers between devices: 29.8 us -> 26.3 us
    all_to_all x3 -> x4, blocking collectives: 45.7 us -> 56.7 us  [exchange(): out = lax.all_to_all(flat, axis, 0, 0, axis_index_groups=groups, tiled=True)]
    all_to_all x1 -> x0, waiting for transfers between devices: 8.96 us -> none  [exchange(): out = lax.all_to_all(flat, axis, 0, 0, axis_index_groups=groups, tiled=True)]
    all_to_all x1 -> x0, starting transfers between devices: 3.37 us -> none  [exchange(): out = lax.all_to_all(flat, axis, 0, 0, axis_index_groups=groups, tiled=True)]
    ppermute x18, waiting for transfers between devices: 21.6 us -> 20.1 us  [along_rings(): return lax.ppermute(a, ('vocab', 'tok'), pairs)]
  transfers between devices with their start and end apart: 25 -> 24, of which waited for: 16 -> 15; matrix products, arithmetic and copies ran while one was open for 0% -> 0% of each run, Pallas kernels for 14% -> 15%
where the time goes in v9:
time: 132 us
  blocking collectives  56.7 us (43%)
  starting transfers between devices  26.3 us (20%)
  Pallas kernels  25 us (19%)
  waiting for transfers between devices  22.6 us (17%)
    all_to_all x4, blocking collectives, exchange(): out = lax.all_to_all(flat, axis, 0, 0, axis_index_groups=groups, tiled=True)  56.7 us
    ppermute x18, starting transfers between devices, along_rings(): return lax.ppermute(a, ('vocab', 'tok'), pairs)  25.2 us
    pallas_call x21, Pallas kernels, call(): pl.pallas_call(kernel, in_specs=in_specs, out_specs=[VM] * len(outs), out...  23.8 us
    ppermute x18, waiting for transfers between devices, along_rings(): return lax.ppermute(a, ('vocab', 'tok'), pairs)  20.1 us
  transfers between devices with their start and end apart: 24, of which 15 were waited for; matrix products, arithmetic and copies ran while one was open for 0% of the time, Pallas kernels for 15%

profile of v9, /device:TPU:6, one launch (start us, length us, event | category | flops | bytes accessed | tf_op | source)
XLA Modules:
  0.0 132.2 jit_solution(7661283160539480840)
XLA Ops:
  0.6 0.1 collective-permute-start
  0.7 0.5 collective-permute-start.1
  1.2 0.9 shard_map.68
  2.1 21.1 %all_to_all.30 = bf16[8,16,1152]{2,1,0:T(8,128)(2,1)S(1)} all-to-all(bf16[8,16,1152]{2,1,0:T(8,128)(2,1)S(1)} %shard_map.68), channel_id=1, replica_groups={{0,1,2,3,4,5,6,7},{8,9,10,11,12,13,14,15},{16,17,18,19,20,21,22,23},{24..., dimensions={0} | all-to-all | bytes 589824 | tf_op jit(solution)/shard_map/all_to_all | solution.py:272
  23.2 3.3 %collective-permute-start.2 = (bf16[128,1152]{1,0:T(8,128)(2,1)S(1)}, bf16[128,1152]{1,0:T(8,128)(2,1)S(1)}, u32[]{:S(2)}, u32[]{:S(2)}) collective-permute-start(bf16[128,1152]{1,0:T(8,128)(2,1)S(1)} %bitcast.6), channel_id=1, source_target_pairs={{0,16},{1,17},{2,18},{3,19},{4,20},{5,21},{6,22},{7,23},{8,24},{9,... | collective-permute-start | bytes 884744 | tf_op jit(solution)/shard_map/ppermute | solution.py:384
  26.5 0.7 collective-permute-start.3
  27.2 2.6 %collective-permute-start.4 = (bf16[128,1152]{1,0:T(8,128)(2,1)S(1)}, bf16[128,1152]{1,0:T(8,128)(2,1)S(1)}, u32[]{:S(2)}, u32[]{:S(2)}) collective-permute-start(bf16[128,1152]{1,0:T(8,128)(2,1)S(1)} %bitcast.8), channel_id=1, source_target_pairs={{0,24},{1,25},{2,26},{3,27},{4,28},{5,29},{6,30},{7,31},{8,0},{9,1... | collective-permute-start | bytes 884744 | tf_op jit(solution)/shard_map/ppermute | solution.py:384
  29.8 0.1 pad_add_fusion.place_ref
  29.8 1.7 %collective-permute-done.2.far_ref = bf16[128,1152]{1,0:T(8,128)(2,1)S(1)} collective-permute-done((bf16[128,1152]{1,0:T(8,128)(2,1)S(1)}, bf16[128,1152]{1,0:T(8,128)(2,1)S(1)}, u32[]{:S(2)}, u32[]{:S(2)}) %collective-permute-start.2) | collective-permute-done | bytes 294944 | tf_op jit(solution)/shard_map/ppermute | solution.py:384
  31.6 3.1 %collective-permute-done.3.left_ref = bf16[128,1152]{1,0:T(8,128)(2,1)S(1)} collective-permute-done((bf16[128,1152]{1,0:T(8,128)(2,1)S(1)}, bf16[128,1152]{1,0:T(8,128)(2,1)S(1)}, u32[]{:S(2)}, u32[]{:S(2)}) %collective-permute-start.3) | collective-permute-done | bytes 294944 | tf_op jit(solution)/shard_map/ppermute | solution.py:384
  34.7 0.3 collective-permute-done.4.right_ref
  35.0 0.6 shard_map.69
  35.7 0.6 collective-permute-start.5
  36.2 1.5 %collective-permute-start.6 = (bf16[256,1024]{1,0:T(8,128)(2,1)S(1)}, bf16[256,1024]{1,0:T(8,128)(2,1)S(1)}, u32[]{:S(2)}, u32[]{:S(2)}) collective-permute-start(bf16[256,1024]{1,0:T(8,128)(2,1)S(1)} %get-tuple-element.66.refs_1_), channel_id=1, source_target_pairs={{0,192},{1,193},{2,194},{3,195},{4,196},{5,197},{6,198},{7,199},{8... | collective-permute-start | bytes 1572872 | tf_op jit(solution)/shard_map/ppermute | solution.py:384
  37.8 0.8 collective-permute-start.10
  38.6 2.4 %collective-permute-start.9 = (bf16[256,1024]{1,0:T(8,128)(2,1)S(1)}, bf16[256,1024]{1,0:T(8,128)(2,1)S(1)}, u32[]{:S(2)}, u32[]{:S(2)}) collective-permute-start(bf16[256,1024]{1,0:T(8,128)(2,1)S(1)} %get-tuple-element.66.refs_1_), channel_id=1, source_target_pairs={{0,64},{1,65},{2,66},{3,67},{4,68},{5,69},{6,70},{7,71},{8,72},{9,... | collective-permute-start | bytes 1572872 | tf_op jit(solution)/shard_map/ppermute | solution.py:384
  41.0 4.1 %shard_map.70 = (bf16[2048,512]{1,0:T(8,128)(2,1)S(1)}, bf16[2048,512]{1,0:T(8,128)(2,1)S(1)}, bf16[2048,512]{1,0:T(8,128)(2,1)S(1)}, bf16[2048,512]{1,0:T(8,128)(2,1)S(1)}) custom-call(s32[3]{0:T(128)S(1)} %pad_add_fusion.place_ref, bf16[4096,512]{1,0:T(8,128)(2,1)} %refs_0_.1, bf16[4096,512]{1,0:T(8,128)(2,1)} %refs_1_.1, bf16[4096,512]{1,0:T(8,128)(2,1)} %copy-done, ...), custom_call_target="tpu_custom_call" | custom-call | tf_op jit(solution)/shard_map/pallas_call | solution.py:66
  45.1 1.5 %collective-permute-done.6.refs_3_ = bf16[256,1024]{1,0:T(8,128)(2,1)S(1)} collective-permute-done((bf16[256,1024]{1,0:T(8,128)(2,1)S(1)}, bf16[256,1024]{1,0:T(8,128)(2,1)S(1)}, u32[]{:S(2)}, u32[]{:S(2)}) %collective-permute-start.6) | collective-permute-done | bytes 524320 | tf_op jit(solution)/shard_map/ppermute | solution.py:384
  46.6 0.3 collective-permute-start.7
  46.9 1.7 %collective-permute-start.8 = (bf16[256,1024]{1,0:T(8,128)(2,1)S(1)}, bf16[256,1024]{1,0:T(8,128)(2,1)S(1)}, u32[]{:S(2)}, u32[]{:S(2)}) collective-permute-start(bf16[256,1024]{1,0:T(8,128)(2,1)S(1)} %collective-permute-done.6.refs_3_), channel_id=1, source_target_pairs={{0,192},{1,193},{2,194},{3,195},{4,196},{5,197},{6,198},{7,199},{8... | collective-permute-start | bytes 1572872 | tf_op jit(solution)/shard_map/ppermute | solution.py:384
  48.7 1.3 %collective-permute-done.11.other_ref = bf16[512,128]{1,0:T(8,128)(2,1)S(1)} collective-permute-done((bf16[512,128]{1,0:T(8,128)(2,1)S(1)}, bf16[512,128]{1,0:T(8,128)(2,1)S(1)}, u32[]{:S(2)}, u32[]{:S(2)}) %collective-permute-start.11) | collective-permute-done | bytes 131104 | tf_op jit(solution)/shard_map/ppermute | solution.py:372
  50.0 0.8 shard_map.75.select_ref
  50.8 1.3 shard_map.72.refs_4_
  52.1 1.3 shard_map.71.refs_4_
  53.3 2.0 %shard_map.74.near_ref = f32[2,512,512]{2,1,0:T(8,128)S(1)} custom-call(s32[3]{0:T(128)S(1)} %pad_add_fusion.place_ref, bf16[2048,512]{1,0:T(8,128)(2,1)S(1)} %get-tuple-element.73.sw_ref, bf16[2048,512]{1,0:T(8,128)(2,1)S(1)} %get-tuple-element.74.tw_ref, bf16[256,1024]{1,0:T(8,128)(2,1)S(1)} %collective-permute-done.5.refs_0_, ...), custom_call_target="tpu_custom_call" | custom-call | flops 1073741824 | tf_op jit(solution)/shard_map/pallas_call | solution.py:66
  55.3 1.8 %shard_map.73.near_ref = f32[2,512,512]{2,1,0:T(8,128)S(1)} custom-call(s32[3]{0:T(128)S(1)} %pad_add_fusion.place_ref, bf16[2048,512]{1,0:T(8,128)(2,1)S(1)} %get-tuple-element.77.sw_ref, bf16[2048,512]{1,0:T(8,128)(2,1)S(1)} %get-tuple-element.78.tw_ref, bf16[256,1024]{1,0:T(8,128)(2,1)S(1)} %collective-permute-done.5.refs_0_, ...), custom_call_target="tpu_custom_call" | custom-call | flops 1073741824 | tf_op jit(solution)/shard_map/pallas_call | solution.py:66
  57.2 0.7 collective-permute-done.8.p4
  57.9 1.3 shard_map.77
  59.1 0.1 collective-permute-start.13
  59.2 0.5 collective-permute-start.12
  59.7 1.3 shard_map.76
  61.0 0.9 collective-permute-done.13.other_ref
  61.9 1.2 shard_map.78
  63.1 0.3 collective-permute-done.12.other_ref
  63.4 0.5 shard_map.79
  63.9 12.5 %all_to_all.31.in_ref = f32[16,8,256]{2,1,0:T(8,128)S(1)} all-to-all(f32[16,8,256]{2,1,0:T(8,128)S(1)} %get-tuple-element.100), channel_id=1, replica_groups={{0,8,16,24,64,72,80,88,128,136,144,152,192,200,208,216},{1,9,17,25,65,7..., dimensions={0} | all-to-all | bytes 262144 | tf_op jit(solution)/shard_map/all_to_all | solution.py:272
  76.4 0.2 shard_map.80
  76.6 11.1 %all_to_all.32.stat_ref = f32[16,8,256]{2,1,0:T(8,128)S(1)} all-to-all(f32[16,8,256]{2,1,0:T(8,128)S(1)} %shard_map.80), channel_id=1, replica_groups={{0,1,2,3,4,5,6,7,32,33,34,35,36,37,38,39},{8,9,10,11,12,13,14,15,40,41,..., dimensions={0} | all-to-all | bytes 262144 | tf_op jit(solution)/shard_map/all_to_all | solution.py:272
  87.7 1.6 %shard_map.81 = (bf16[512,512]{1,0:T(8,128)(2,1)S(1)}, f32[1,1]{1,0:T(1,128)}) custom-call(s32[3]{0:T(128)S(1)} %pad_add_fusion.place_ref, f32[16,8,256]{2,1,0:T(8,128)S(1)} %all_to_all.32.stat_ref, f32[512,512]{1,0:T(8,128)S(1)} %get-tuple-element.101.s_ref, f32[512,512]{1,0:T(8,128)S(1)} %get-tuple-element.102.d_ref), custom_call_target="tpu_custom_call" | custom-call | tf_op jit(solution)/shard_map/pallas_call | solution.py:66
  89.3 1.8 %shard_map.82.own_ref = f32[4,512,512]{2,1,0:T(8,128)S(1)} custom-call(s32[3]{0:T(128)S(1)} %pad_add_fusion.place_ref, bf16[512,512]{1,0:T(8,128)(2,1)S(1)} %get-tuple-element.103.g_ref, bf16[2048,512]{1,0:T(8,128)(2,1)S(1)} %get-tuple-element.73.sw_ref), custom_call_target="tpu_custom_call" | custom-call | tf_op jit(solution)/shard_map/pallas_call | solution.py:66
  91.1 0.1 collective-permute-done.14.g_ref
  91.2 1.0 shard_map.84
  92.2 2.1 %collective-permute-start.16 = (bf16[256,512]{1,0:T(8,128)(2,1)S(1)}, bf16[256,512]{1,0:T(8,128)(2,1)S(1)}, u32[]{:S(2)}, u32[]{:S(2)}) collective-permute-start(bf16[256,512]{1,0:T(8,128)(2,1)S(1)} %get-tuple-element.109), channel_id=1, source_target_pairs={{0,64},{1,65},{2,66},{3,67},{4,68},{5,69},{6,70},{7,71},{8,72},{9,... | collective-permute-start | bytes 786440 | tf_op jit(solution)/shard_map/ppermute | solution.py:384
  94.4 1.8 %shard_map.83 = (bf16[256,512]{1,0:T(8,128)(2,1)S(1)}, bf16[256,512]{1,0:T(8,128)(2,1)S(1)}, bf16[256,512]{1,0:T(8,128)(2,1)S(1)}, bf16[256,512]{1,0:T(8,128)(2,...) custom-call(s32[3]{0:T(128)S(1)} %pad_add_fusion.place_ref, f32[4,512,512]{2,1,0:T(8,128)S(1)} %shard_map.82.own_ref, ...), custom_call_target="tpu_custom_call" | custom-call | tf_op jit(solution)/shard_map/pallas_call | solution.py:66
  96.2 0.7 collective-permute-start.15
  96.9 2.7 %collective-permute-start.20 = (bf16[256,512]{1,0:T(8,128)(2,1)S(1)}, bf16[256,512]{1,0:T(8,128)(2,1)S(1)}, u32[]{:S(2)}, u32[]{:S(2)}) collective-permute-start(bf16[256,512]{1,0:T(8,128)(2,1)S(1)} %get-tuple-element.115), channel_id=1, source_target_pairs={{0,64},{1,65},{2,66},{3,67},{4,68},{5,69},{6,70},{7,71},{8,72},{9,... | collective-permute-start | bytes 786440 | tf_op jit(solution)/shard_map/ppermute | solution.py:384
  99.6 2.4 %collective-permute-done.17.d_ref = bf16[256,512]{1,0:T(8,128)(2,1)S(1)} collective-permute-done((bf16[256,512]{1,0:T(8,128)(2,1)S(1)}, bf16[256,512]{1,0:T(8,128)(2,1)S(1)}, u32[]{:S(2)}, u32[]{:S(2)}) %collective-permute-start.17) | collective-permute-done | bytes 262176 | tf_op jit(solution)/shard_map/ppermute | solution.py:384
  102.0 0.1 shard_map.85
  102.1 0.1 collective-permute-start.18
  102.2 2.0 %collective-permute-start.19 = (bf16[256,512]{1,0:T(8,128)(2,1)S(1)}, bf16[256,512]{1,0:T(8,128)(2,1)S(1)}, u32[]{:S(2)}, u32[]{:S(2)}) collective-permute-start(bf16[256,512]{1,0:T(8,128)(2,1)S(1)} %get-tuple-element.114), channel_id=1, source_target_pairs={{0,192},{1,193},{2,194},{3,195},{4,196},{5,197},{6,198},{7,199},{8... | collective-permute-start | bytes 786440 | tf_op jit(solution)/shard_map/ppermute | solution.py:384
  104.2 0.6 collective-permute-done.15.refs_1_
  104.8 3.8 %collective-permute-done.18.refs_2_ = bf16[256,512]{1,0:T(8,128)(2,1)S(1)} collective-permute-done((bf16[256,512]{1,0:T(8,128)(2,1)S(1)}, bf16[256,512]{1,0:T(8,128)(2,1)S(1)}, u32[]{:S(2)}, u32[]{:S(2)}) %collective-permute-start.18) | collective-permute-done | bytes 262176 | tf_op jit(solution)/shard_map/ppermute | solution.py:384
  108.5 1.3 collective-permute-done.19.refs_4_
  109.8 0.2 shard_map.86
  110.0 1.6 %collective-permute-start.21 = (bf16[128,512]{1,0:T(8,128)(2,1)S(1)}, bf16[128,512]{1,0:T(8,128)(2,1)S(1)}, u32[]{:S(2)}, u32[]{:S(2)}) collective-permute-start(bf16[128,512]{1,0:T(8,128)(2,1)S(1)} %get-tuple-element.116), channel_id=1, source_target_pairs={{0,16},{1,17},{2,18},{3,19},{4,20},{5,21},{6,22},{7,23},{8,24},{9,... | collective-permute-start | bytes 393224 | tf_op jit(solution)/shard_map/ppermute | solution.py:384
  111.6 1.6 %collective-permute-start.22 = (bf16[128,512]{1,0:T(8,128)(2,1)S(1)}, bf16[128,512]{1,0:T(8,128)(2,1)S(1)}, u32[]{:S(2)}, u32[]{:S(2)}) collective-permute-start(bf16[128,512]{1,0:T(8,128)(2,1)S(1)} %get-tuple-element.117), channel_id=1, source_target_pairs={{0,24},{1,25},{2,26},{3,27},{4,28},{5,29},{6,30},{7,31},{8,0},{9,1... | collective-permute-start | bytes 393224 | tf_op jit(solution)/shard_map/ppermute | solution.py:384
  113.3 0.4 collective-permute-start.23
  113.7 1.2 shard_map.87
  114.8 1.8 %collective-permute-done.21.refs_0_ = bf16[128,512]{1,0:T(8,128)(2,1)S(1)} collective-permute-done((bf16[128,512]{1,0:T(8,128)(2,1)S(1)}, bf16[128,512]{1,0:T(8,128)(2,1)S(1)}, u32[]{:S(2)}, u32[]{:S(2)}) %collective-permute-start.21) | collective-permute-done | bytes 131104 | tf_op jit(solution)/shard_map/ppermute | solution.py:384
  116.6 0.0 collective-permute-done.22.refs_1_
  116.6 2.8 %collective-permute-done.23.refs_2_ = bf16[128,512]{1,0:T(8,128)(2,1)S(1)} collective-permute-done((bf16[128,512]{1,0:T(8,128)(2,1)S(1)}, bf16[128,512]{1,0:T(8,128)(2,1)S(1)}, u32[]{:S(2)}, u32[]{:S(2)}) %collective-permute-start.23) | collective-permute-done | bytes 131104 | tf_op jit(solution)/shard_map/ppermute | solution.py:384
  119.4 0.1 shard_map.88
  119.5 12.1 %all_to_all.33.in_ref = bf16[8,16,512]{2,1,0:T(8,128)(2,1)S(1)} all-to-all(bf16[8,16,512]{2,1,0:T(8,128)(2,1)S(1)} %bitcast.10), channel_id=1, replica_groups={{0,1,2,3,4,5,6,7},{8,9,10,11,12,13,14,15},{16,17,18,19,20,21,22,23},{24..., dimensions={0} | all-to-all | bytes 262144 | tf_op jit(solution)/shard_map/all_to_all | solution.py:272
  131.6 0.6 copy.7
  (16 shorter events, 0.1 us)
Async XLA Ops:
  0.6 22.6 %collective-permute-start = (bf16[4096,512]{1,0:T(8,128)(2,1)}, bf16[4096,512]{1,0:T(8,128)(2,1)S(1)}, u32[]{:S(2)}, u32[]{:S(2)}) collective-permute-start(bf16[4096,512]{1,0:T(8,128)(2,1)} %refs_0_.1), channel_id=1, source_target_pairs={{0,32},{32,0},{64,96},{96,64},{128,160},{160,128},{192,224},{224,1... | collective-permute-start | bytes 12582920 | tf_op jit(solution)/shard_map/ppermute | solution.py:372
  0.7 22.5 %collective-permute-start.1 = (bf16[4096,512]{1,0:T(8,128)(2,1)}, bf16[4096,512]{1,0:T(8,128)(2,1)S(1)}, u32[]{:S(2)}, u32[]{:S(2)}) collective-permute-start(bf16[4096,512]{1,0:T(8,128)(2,1)} %refs_1_.1), channel_id=1, source_target_pairs={{0,32},{32,0},{64,96},{96,64},{128,160},{160,128},{192,224},{224,1... | collective-permute-start | bytes 12582920 | tf_op jit(solution)/shard_map/ppermute | solution.py:372
  23.2 3.3 %copy-start = (bf16[4096,512]{1,0:T(8,128)(2,1)}, bf16[4096,512]{1,0:T(8,128)(2,1)S(1)}, u32[]{:S(2)}) copy-start(bf16[4096,512]{1,0:T(8,128)(2,1)S(1)} %collective-permute-done.refs_2_) | copy-start | bytes 12582916
  23.2 4.0 %copy-start.1 = (bf16[4096,512]{1,0:T(8,128)(2,1)}, bf16[4096,512]{1,0:T(8,128)(2,1)S(1)}, u32[]{:S(2)}) copy-start(bf16[4096,512]{1,0:T(8,128)(2,1)S(1)} %collective-permute-done.1.refs_3_) | copy-start | bytes 12582916
  23.2 8.3 %collective-permute-start.2 = (bf16[128,1152]{1,0:T(8,128)(2,1)S(1)}, bf16[128,1152]{1,0:T(8,128)(2,1)S(1)}, u32[]{:S(2)}, u32[]{:S(2)}) collective-permute-start(bf16[128,1152]{1,0:T(8,128)(2,1)S(1)} %bitcast.6), channel_id=1, source_target_pairs={{0,16},{1,17},{2,18},{3,19},{4,20},{5,21},{6,22},{7,23},{8,24},{9,... | collective-permute-start | bytes 884744 | tf_op jit(solution)/shard_map/ppermute | solution.py:384
  26.5 8.2 %collective-permute-start.3 = (bf16[128,1152]{1,0:T(8,128)(2,1)S(1)}, bf16[128,1152]{1,0:T(8,128)(2,1)S(1)}, u32[]{:S(2)}, u32[]{:S(2)}) collective-permute-start(bf16[128,1152]{1,0:T(8,128)(2,1)S(1)} %bitcast.7), channel_id=1, source_target_pairs={{0,8},{1,9},{2,10},{3,11},{4,12},{5,13},{6,14},{7,15},{8,16},{9,17... | collective-permute-start | bytes 884744 | tf_op jit(solution)/shard_map/ppermute | solution.py:384
  27.2 7.9 %collective-permute-start.4 = (bf16[128,1152]{1,0:T(8,128)(2,1)S(1)}, bf16[128,1152]{1,0:T(8,128)(2,1)S(1)}, u32[]{:S(2)}, u32[]{:S(2)}) collective-permute-start(bf16[128,1152]{1,0:T(8,128)(2,1)S(1)} %bitcast.8), channel_id=1, source_target_pairs={{0,24},{1,25},{2,26},{3,27},{4,28},{5,29},{6,30},{7,31},{8,0},{9,1... | collective-permute-start | bytes 884744 | tf_op jit(solution)/shard_map/ppermute | solution.py:384
  35.7 9.4 %collective-permute-start.5 = (bf16[256,1024]{1,0:T(8,128)(2,1)S(1)}, bf16[256,1024]{1,0:T(8,128)(2,1)S(1)}, u32[]{:S(2)}, u32[]{:S(2)}) collective-permute-start(bf16[256,1024]{1,0:T(8,128)(2,1)S(1)} %get-tuple-element.65.refs_0_), channel_id=1, source_target_pairs={{0,64},{1,65},{2,66},{3,67},{4,68},{5,69},{6,70},{7,71},{8,72},{9,... | collective-permute-start | bytes 1572872 | tf_op jit(solution)/shard_map/ppermute | solution.py:384
  36.2 10.4 %collective-permute-start.6 = (bf16[256,1024]{1,0:T(8,128)(2,1)S(1)}, bf16[256,1024]{1,0:T(8,128)(2,1)S(1)}, u32[]{:S(2)}, u32[]{:S(2)}) collective-permute-start(bf16[256,1024]{1,0:T(8,128)(2,1)S(1)} %get-tuple-element.66.refs_1_), channel_id=1, source_target_pairs={{0,192},{1,193},{2,194},{3,195},{4,196},{5,197},{6,198},{7,199},{8... | collective-permute-start | bytes 1572872 | tf_op jit(solution)/shard_map/ppermute | solution.py:384
  37.8 15.5 %collective-permute-start.10 = (bf16[256,1024]{1,0:T(8,128)(2,1)S(1)}, bf16[256,1024]{1,0:T(8,128)(2,1)S(1)}, u32[]{:S(2)}, u32[]{:S(2)}) collective-permute-start(bf16[256,1024]{1,0:T(8,128)(2,1)S(1)} %get-tuple-element.65.refs_0_), channel_id=1, source_target_pairs={{0,192},{1,193},{2,194},{3,195},{4,196},{5,197},{6,198},{7,199},{8... | collective-permute-start | bytes 1572872 | tf_op jit(solution)/shard_map/ppermute | solution.py:384
  38.6 14.7 %collective-permute-start.9 = (bf16[256,1024]{1,0:T(8,128)(2,1)S(1)}, bf16[256,1024]{1,0:T(8,128)(2,1)S(1)}, u32[]{:S(2)}, u32[]{:S(2)}) collective-permute-start(bf16[256,1024]{1,0:T(8,128)(2,1)S(1)} %get-tuple-element.66.refs_1_), channel_id=1, source_target_pairs={{0,64},{1,65},{2,66},{3,67},{4,68},{5,69},{6,70},{7,71},{8,72},{9,... | collective-permute-start | bytes 1572872 | tf_op jit(solution)/shard_map/ppermute | solution.py:384
  46.6 10.5 %collective-permute-start.7 = (bf16[256,1024]{1,0:T(8,128)(2,1)S(1)}, bf16[256,1024]{1,0:T(8,128)(2,1)S(1)}, u32[]{:S(2)}, u32[]{:S(2)}) collective-permute-start(bf16[256,1024]{1,0:T(8,128)(2,1)S(1)} %collective-permute-done.5.refs_0_), channel_id=1, source_target_pairs={{0,64},{1,65},{2,66},{3,67},{4,68},{5,69},{6,70},{7,71},{8,72},{9,... | collective-permute-start | bytes 1572872 | tf_op jit(solution)/shard_map/ppermute | solution.py:384
  46.9 11.0 %collective-permute-start.8 = (bf16[256,1024]{1,0:T(8,128)(2,1)S(1)}, bf16[256,1024]{1,0:T(8,128)(2,1)S(1)}, u32[]{:S(2)}, u32[]{:S(2)}) collective-permute-start(bf16[256,1024]{1,0:T(8,128)(2,1)S(1)} %collective-permute-done.6.refs_3_), channel_id=1, source_target_pairs={{0,192},{1,193},{2,194},{3,195},{4,196},{5,197},{6,198},{7,199},{8... | collective-permute-start | bytes 1572872 | tf_op jit(solution)/shard_map/ppermute | solution.py:384
  48.7 1.3 %collective-permute-start.11 = (bf16[512,128]{1,0:T(8,128)(2,1)S(1)}, bf16[512,128]{1,0:T(8,128)(2,1)S(1)}, u32[]{:S(2)}, u32[]{:S(2)}) collective-permute-start(bf16[512,128]{1,0:T(8,128)(2,1)S(1)} %get-tuple-element.83.own_ref), channel_id=1, source_target_pairs={{0,32},{32,0},{64,96},{96,64},{128,160},{160,128},{192,224},{224,1... | collective-permute-start | bytes 393224 | tf_op jit(solution)/shard_map/ppermute | solution.py:372
  59.1 2.7 %collective-permute-start.13 = (f32[512,512]{1,0:T(8,128)S(1)}, f32[512,512]{1,0:T(8,128)S(1)}, u32[]{:S(2)}, u32[]{:S(2)}) collective-permute-start(f32[512,512]{1,0:T(8,128)S(1)} %get-tuple-element.91), channel_id=1, source_target_pairs={{0,32},{32,0},{64,96},{96,64},{128,160},{160,128},{192,224},{224,1... | collective-permute-start | bytes 3145736 | tf_op jit(solution)/shard_map/ppermute | solution.py:372
  59.2 4.1 %collective-permute-start.12 = (f32[512,512]{1,0:T(8,128)S(1)}, f32[512,512]{1,0:T(8,128)S(1)}, u32[]{:S(2)}, u32[]{:S(2)}) collective-permute-start(f32[512,512]{1,0:T(8,128)S(1)} %get-tuple-element.89), channel_id=1, source_target_pairs={{0,32},{32,0},{64,96},{96,64},{128,160},{160,128},{192,224},{224,1... | collective-permute-start | bytes 3145736 | tf_op jit(solution)/shard_map/ppermute | solution.py:372
  89.3 1.9 %collective-permute-start.14 = (bf16[512,512]{1,0:T(8,128)(2,1)S(1)}, bf16[512,512]{1,0:T(8,128)(2,1)S(1)}, u32[]{:S(2)}, u32[]{:S(2)}) collective-permute-start(bf16[512,512]{1,0:T(8,128)(2,1)S(1)} %get-tuple-element.103.g_ref), channel_id=1, source_target_pairs={{0,32},{32,0},{64,96},{96,64},{128,160},{160,128},{192,224},{224,1... | collective-permute-start | bytes 1572872 | tf_op jit(solution)/shard_map/ppermute | solution.py:372
  92.2 7.4 %collective-permute-start.16 = (bf16[256,512]{1,0:T(8,128)(2,1)S(1)}, bf16[256,512]{1,0:T(8,128)(2,1)S(1)}, u32[]{:S(2)}, u32[]{:S(2)}) collective-permute-start(bf16[256,512]{1,0:T(8,128)(2,1)S(1)} %get-tuple-element.109), channel_id=1, source_target_pairs={{0,64},{1,65},{2,66},{3,67},{4,68},{5,69},{6,70},{7,71},{8,72},{9,... | collective-permute-start | bytes 786440 | tf_op jit(solution)/shard_map/ppermute | solution.py:384
  94.4 7.6 %collective-permute-start.17 = (bf16[256,512]{1,0:T(8,128)(2,1)S(1)}, bf16[256,512]{1,0:T(8,128)(2,1)S(1)}, u32[]{:S(2)}, u32[]{:S(2)}) collective-permute-start(bf16[256,512]{1,0:T(8,128)(2,1)S(1)} %get-tuple-element.111), channel_id=1, source_target_pairs={{0,192},{1,193},{2,194},{3,195},{4,196},{5,197},{6,198},{7,199},{8... | collective-permute-start | bytes 786440 | tf_op jit(solution)/shard_map/ppermute | solution.py:384
  96.2 8.6 %collective-permute-start.15 = (bf16[256,512]{1,0:T(8,128)(2,1)S(1)}, bf16[256,512]{1,0:T(8,128)(2,1)S(1)}, u32[]{:S(2)}, u32[]{:S(2)}) collective-permute-start(bf16[256,512]{1,0:T(8,128)(2,1)S(1)} %get-tuple-element.107), channel_id=1, source_target_pairs={{0,192},{1,193},{2,194},{3,195},{4,196},{5,197},{6,198},{7,199},{8... | collective-permute-start | bytes 786440 | tf_op jit(solution)/shard_map/ppermute | solution.py:384
  96.9 7.9 %collective-permute-start.20 = (bf16[256,512]{1,0:T(8,128)(2,1)S(1)}, bf16[256,512]{1,0:T(8,128)(2,1)S(1)}, u32[]{:S(2)}, u32[]{:S(2)}) collective-permute-start(bf16[256,512]{1,0:T(8,128)(2,1)S(1)} %get-tuple-element.115), channel_id=1, source_target_pairs={{0,64},{1,65},{2,66},{3,67},{4,68},{5,69},{6,70},{7,71},{8,72},{9,... | collective-permute-start | bytes 786440 | tf_op jit(solution)/shard_map/ppermute | solution.py:384
  102.1 6.4 %collective-permute-start.18 = (bf16[256,512]{1,0:T(8,128)(2,1)S(1)}, bf16[256,512]{1,0:T(8,128)(2,1)S(1)}, u32[]{:S(2)}, u32[]{:S(2)}) collective-permute-start(bf16[256,512]{1,0:T(8,128)(2,1)S(1)} %get-tuple-element.112), channel_id=1, source_target_pairs={{0,64},{1,65},{2,66},{3,67},{4,68},{5,69},{6,70},{7,71},{8,72},{9,... | collective-permute-start | bytes 786440 | tf_op jit(solution)/shard_map/ppermute | solution.py:384
  102.2 7.7 %collective-permute-start.19 = (bf16[256,512]{1,0:T(8,128)(2,1)S(1)}, bf16[256,512]{1,0:T(8,128)(2,1)S(1)}, u32[]{:S(2)}, u32[]{:S(2)}) collective-permute-start(bf16[256,512]{1,0:T(8,128)(2,1)S(1)} %get-tuple-element.114), channel_id=1, source_target_pairs={{0,192},{1,193},{2,194},{3,195},{4,196},{5,197},{6,198},{7,199},{8... | collective-permute-start | bytes 786440 | tf_op jit(solution)/shard_map/ppermute | solution.py:384
  110.0 6.6 %collective-permute-start.21 = (bf16[128,512]{1,0:T(8,128)(2,1)S(1)}, bf16[128,512]{1,0:T(8,128)(2,1)S(1)}, u32[]{:S(2)}, u32[]{:S(2)}) collective-permute-start(bf16[128,512]{1,0:T(8,128)(2,1)S(1)} %get-tuple-element.116), channel_id=1, source_target_pairs={{0,16},{1,17},{2,18},{3,19},{4,20},{5,21},{6,22},{7,23},{8,24},{9,... | collective-permute-start | bytes 393224 | tf_op jit(solution)/shard_map/ppermute | solution.py:384
  111.6 5.0 %collective-permute-start.22 = (bf16[128,512]{1,0:T(8,128)(2,1)S(1)}, bf16[128,512]{1,0:T(8,128)(2,1)S(1)}, u32[]{:S(2)}, u32[]{:S(2)}) collective-permute-start(bf16[128,512]{1,0:T(8,128)(2,1)S(1)} %get-tuple-element.117), channel_id=1, source_target_pairs={{0,24},{1,25},{2,26},{3,27},{4,28},{5,29},{6,30},{7,31},{8,0},{9,1... | collective-permute-start | bytes 393224 | tf_op jit(solution)/shard_map/ppermute | solution.py:384
  113.3 6.2 %collective-permute-start.23 = (bf16[128,512]{1,0:T(8,128)(2,1)S(1)}, bf16[128,512]{1,0:T(8,128)(2,1)S(1)}, u32[]{:S(2)}, u32[]{:S(2)}) collective-permute-start(bf16[128,512]{1,0:T(8,128)(2,1)S(1)} %get-tuple-element.118), channel_id=1, source_target_pairs={{0,8},{1,9},{2,10},{3,11},{4,12},{5,13},{6,14},{7,15},{8,16},{9,17... | collective-permute-start | bytes 393224 | tf_op jit(solution)/shard_map/ppermute | solution.py:384

commit v10 on v9

--- a/solution.py
+++ b/solution.py
@@ -161,13 +161,12 @@
                 out_ref[n, :NEAR] = before_ref[n, :NEAR]
 
 
-def far_kernel(place_ref, sw_ref, tw_ref, p3, p4, near_ref, *refs):
+def far_kernel(numbers, place_ref, sw_ref, tw_ref, p3, p4, near_ref, *outs):
     y = place_ref[2]
-    outs = refs[:2]
 
     @pl.when(place_ref[1] == 0)
     def _():
-        for n, out_ref in enumerate(outs):
+        for n, out_ref in zip(numbers, outs):
             columns = slice(n * W, (n + 1) * W)
             block = jnp.concatenate([p3[:, columns], p4[:, columns]], axis=0)
             part = dot(block, weights(place_ref, (sw_ref, tw_ref), STEPS[3])[n])
@@ -178,7 +177,7 @@
 
     @pl.when(place_ref[1] == 1)
     def _():
-        for n, out_ref in enumerate(outs):
+        for n, out_ref in zip(numbers, outs):
             columns = slice(n * W, (n + 1) * W)
             for k, step in enumerate(STEPS[:3]):
                 here = slice(k * NEAR, (k + 1) * NEAR)
@@ -278,9 +277,8 @@
         yield dot(g, sw_ref[at_block((place_ref[0] + step) % NX, W)], ((1,), (1,)))
 
 
-def logit_grad_kernel(place_ref, stat_ref, s_ref, d_ref, turned_ref, loss_ref, g_ref):
-    lse_s, mean, lse_t = merge(stat_ref[...])
-    loss_ref[...] = jnp.sum(mean - lse_s + lse_t, axis=1, keepdims=True) / N
+def logit_grad_kernel(place_ref, stat_ref, s_ref, d_ref, turned_ref, g_ref):
+    lse_s, mean, _ = merge(stat_ref[...])
     row = lax.broadcasted_iota(jnp.int32, (128, N), 0)
     table = jnp.where(row == 0, lse_s, jnp.where(row == 1, mean, 0.0))
     table = jnp.transpose(table)
@@ -296,8 +294,10 @@
         out_ref[k] = part
 
 
-def to_hbm_kernel(in_ref, out_ref, sem):
-    started(in_ref, out_ref, sem).wait()
+def loss_kernel(stat_ref, out_ref, loss_ref, sem):
+    lse_s, mean, lse_t = merge(stat_ref[...])
+    loss_ref[...] = jnp.sum(mean - lse_s + lse_t, axis=1, keepdims=True) / N
+    started(loss_ref, out_ref, sem).wait()
 
 
 def far_block_kernel(place_ref, own_ref, g_ref, sw_ref, a_ref, b_ref):
@@ -451,16 +451,18 @@
     sides = left_a, left_b, right_a, right_b
     logits = [((N, C), F32)]
 
-    def far_part(held, near):
-        return call(far_kernel, [SM] + [VM] * 5, logits * 2, place, *held, *far, near)
+    def far_part(numbers, held, near):
+        kernel = functools.partial(far_kernel, numbers)
+        outs = logits * len(numbers)
+        return call(kernel, [SM] + [VM] * 5, outs, place, *held, *far, near)
 
     for_other = near_part((1, 2), weights_other, *sides, for_other)
     own = near_part((1, 2), weights_own, *sides, own)
     select = call(choose_kernel, [SM, VM, VM], [((N, N), BF)], place, digits, digits2)[0]
     far, for_other, own, select = lax.optimization_barrier((far, for_other, own, select))
-    s_other, t_other = far_part(weights_other, for_other)
-    t_other, s_other = to_other_core(t_other), to_other_core(s_other)
-    s_own, t_own = far_part(weights_own, own)
+    t_other = to_other_core(far_part((1,), weights_other, for_other)[0])
+    s_other = to_other_core(far_part((0,), weights_other, for_other)[0])
+    s_own, t_own = far_part((0, 1), weights_own, own)
     t_own, t_other = lax.optimization_barrier((t_own, t_other))
     t, table = call(
         teacher_logits_kernel,
@@ -478,13 +480,13 @@
     stats = exchange(stats, ("vocab", "tok"), X_Y_GROUPS)
     stats = call(merge_kernel, [VM], [((STAT, 8, N // 2), F32)], stats)[0]
     stats = exchange(stats, ("vocab", "tok"), CORE_Z_GROUPS)
-    g, loss = call(
+    g = call(
         logit_grad_kernel,
         [SM] + [VM] * 3,
-        [((N, C), BF), ((1, 1), F32)],
+        [((N, C), BF)],
         place, stats, s, d,
         scratch=[pltpu.VMEM((N, C), F32)],
-    )
+    )[0]
     own = call(own_terms_kernel, [SM, VM, VM], [((NX, N, W), F32)], place, g, sw)[0]
     g_other, own = lax.optimization_barrier((to_other_core(g), own))
     half = ((N // 2, W), BF)
@@ -506,14 +508,14 @@
     )
     blocks = to_ring(blocks, along_second)
     loss = pl.pallas_call(
-        to_hbm_kernel,
+        loss_kernel,
         in_specs=[VM],
         out_specs=HBM,
         out_shape=pltpu.HBM((1, 1), F32),
-        scratch_shapes=[pltpu.SemaphoreType.DMA(())],
+        scratch_shapes=[pltpu.VMEM((1, 1), F32), pltpu.SemaphoreType.DMA(())],
         compiler_params=PARAMS,
         cost_estimate=cost(0),
-    )(loss)
+    )(stats)
     blocks, loss = lax.optimization_barrier((blocks, loss))
     partial = call(
         sum_second_kernel, [VM] * 4, [((NEAR, W), BF)], *blocks

time: 132 us -> 132 us (level)
    pallas_call x21 -> x22, Pallas kernels: 23.8 us -> 24.2 us  [call(): pl.pallas_call(kernel, in_specs=in_specs, out_specs=[VM] * len(outs), out...]
  transfers between devices with their start and end apart: 24 -> 24, of which waited for: 15 -> 13; matrix products, arithmetic and copies ran while one was open for 0% -> 0% of each run, Pallas kernels for 15% -> 15%
where the time goes in v10:
time: 132 us
  blocking collectives  56.7 us (43%)
  starting transfers between devices  26.5 us (20%)
  Pallas kernels  25 us (19%)
  waiting for transfers between devices  21.8 us (17%)
    all_to_all x4, blocking collectives, exchange(): out = lax.all_to_all(flat, axis, 0, 0, axis_index_groups=groups, tiled=True)  56.7 us
    ppermute x18, starting transfers between devices, along_rings(): return lax.ppermute(a, ('vocab', 'tok'), pairs)  25.2 us
    pallas_call x22, Pallas kernels, call(): pl.pallas_call(kernel, in_specs=in_specs, out_specs=[VM] * len(outs), out...  24.2 us
    ppermute x18, waiting for transfers between devices, along_rings(): return lax.ppermute(a, ('vocab', 'tok'), pairs)  20.4 us
  transfers between devices with their start and end apart: 24, of which 13 were waited for; matrix products, arithmetic and copies ran while one was open for 0% of the time, Pallas kernels for 15%

profile of v10, /device:TPU:6, one launch (start us, length us, event | category | flops | bytes accessed | tf_op | source)
XLA Modules:
  0.0 131.7 jit_solution(6886392237049620539)
XLA Ops:
  0.6 0.1 collective-permute-start
  0.7 0.5 collective-permute-start.1
  1.2 0.9 shard_map.68
  2.1 21.1 %all_to_all.30 = bf16[8,16,1152]{2,1,0:T(8,128)(2,1)S(1)} all-to-all(bf16[8,16,1152]{2,1,0:T(8,128)(2,1)S(1)} %shard_map.68), channel_id=1, replica_groups={{0,1,2,3,4,5,6,7},{8,9,10,11,12,13,14,15},{16,17,18,19,20,21,22,23},{24..., dimensions={0} | all-to-all | bytes 589824 | tf_op jit(solution)/shard_map/all_to_all | solution.py:271
  23.2 3.3 %collective-permute-start.2 = (bf16[128,1152]{1,0:T(8,128)(2,1)S(1)}, bf16[128,1152]{1,0:T(8,128)(2,1)S(1)}, u32[]{:S(2)}, u32[]{:S(2)}) collective-permute-start(bf16[128,1152]{1,0:T(8,128)(2,1)S(1)} %bitcast.6), channel_id=1, source_target_pairs={{0,16},{1,17},{2,18},{3,19},{4,20},{5,21},{6,22},{7,23},{8,24},{9,... | collective-permute-start | bytes 884744 | tf_op jit(solution)/shard_map/ppermute | solution.py:384
  26.5 0.7 collective-permute-start.3
  27.2 2.6 %collective-permute-start.4 = (bf16[128,1152]{1,0:T(8,128)(2,1)S(1)}, bf16[128,1152]{1,0:T(8,128)(2,1)S(1)}, u32[]{:S(2)}, u32[]{:S(2)}) collective-permute-start(bf16[128,1152]{1,0:T(8,128)(2,1)S(1)} %bitcast.8), channel_id=1, source_target_pairs={{0,24},{1,25},{2,26},{3,27},{4,28},{5,29},{6,30},{7,31},{8,0},{9,1... | collective-permute-start | bytes 884744 | tf_op jit(solution)/shard_map/ppermute | solution.py:384
  29.8 0.1 pad_add_fusion.place_ref
  29.8 1.7 %collective-permute-done.2.far_ref = bf16[128,1152]{1,0:T(8,128)(2,1)S(1)} collective-permute-done((bf16[128,1152]{1,0:T(8,128)(2,1)S(1)}, bf16[128,1152]{1,0:T(8,128)(2,1)S(1)}, u32[]{:S(2)}, u32[]{:S(2)}) %collective-permute-start.2) | collective-permute-done | bytes 294944 | tf_op jit(solution)/shard_map/ppermute | solution.py:384
  31.6 3.1 %collective-permute-done.3.left_ref = bf16[128,1152]{1,0:T(8,128)(2,1)S(1)} collective-permute-done((bf16[128,1152]{1,0:T(8,128)(2,1)S(1)}, bf16[128,1152]{1,0:T(8,128)(2,1)S(1)}, u32[]{:S(2)}, u32[]{:S(2)}) %collective-permute-start.3) | collective-permute-done | bytes 294944 | tf_op jit(solution)/shard_map/ppermute | solution.py:384
  34.7 0.3 collective-permute-done.4.right_ref
  35.0 0.6 shard_map.69
  35.7 0.6 collective-permute-start.5
  36.2 1.5 %collective-permute-start.6 = (bf16[256,1024]{1,0:T(8,128)(2,1)S(1)}, bf16[256,1024]{1,0:T(8,128)(2,1)S(1)}, u32[]{:S(2)}, u32[]{:S(2)}) collective-permute-start(bf16[256,1024]{1,0:T(8,128)(2,1)S(1)} %get-tuple-element.62.refs_1_), channel_id=1, source_target_pairs={{0,192},{1,193},{2,194},{3,195},{4,196},{5,197},{6,198},{7,199},{8... | collective-permute-start | bytes 1572872 | tf_op jit(solution)/shard_map/ppermute | solution.py:384
  37.8 0.8 collective-permute-start.10
  38.6 2.4 %collective-permute-start.9 = (bf16[256,1024]{1,0:T(8,128)(2,1)S(1)}, bf16[256,1024]{1,0:T(8,128)(2,1)S(1)}, u32[]{:S(2)}, u32[]{:S(2)}) collective-permute-start(bf16[256,1024]{1,0:T(8,128)(2,1)S(1)} %get-tuple-element.62.refs_1_), channel_id=1, source_target_pairs={{0,64},{1,65},{2,66},{3,67},{4,68},{5,69},{6,70},{7,71},{8,72},{9,... | collective-permute-start | bytes 1572872 | tf_op jit(solution)/shard_map/ppermute | solution.py:384
  41.0 4.1 %shard_map.70 = (bf16[2048,512]{1,0:T(8,128)(2,1)S(1)}, bf16[2048,512]{1,0:T(8,128)(2,1)S(1)}, bf16[2048,512]{1,0:T(8,128)(2,1)S(1)}, bf16[2048,512]{1,0:T(8,128)(2,1)S(1)}) custom-call(s32[3]{0:T(128)S(1)} %pad_add_fusion.place_ref, bf16[4096,512]{1,0:T(8,128)(2,1)} %refs_0_.1, bf16[4096,512]{1,0:T(8,128)(2,1)} %refs_1_.1, bf16[4096,512]{1,0:T(8,128)(2,1)} %copy-done, ...), custom_call_target="tpu_custom_call" | custom-call | tf_op jit(solution)/shard_map/pallas_call | solution.py:66
  45.1 1.5 %collective-permute-done.6.refs_3_ = bf16[256,1024]{1,0:T(8,128)(2,1)S(1)} collective-permute-done((bf16[256,1024]{1,0:T(8,128)(2,1)S(1)}, bf16[256,1024]{1,0:T(8,128)(2,1)S(1)}, u32[]{:S(2)}, u32[]{:S(2)}) %collective-permute-start.6) | collective-permute-done | bytes 524320 | tf_op jit(solution)/shard_map/ppermute | solution.py:384
  46.6 0.3 collective-permute-start.7
  46.9 1.7 %collective-permute-start.8 = (bf16[256,1024]{1,0:T(8,128)(2,1)S(1)}, bf16[256,1024]{1,0:T(8,128)(2,1)S(1)}, u32[]{:S(2)}, u32[]{:S(2)}) collective-permute-start(bf16[256,1024]{1,0:T(8,128)(2,1)S(1)} %collective-permute-done.6.refs_3_), channel_id=1, source_target_pairs={{0,192},{1,193},{2,194},{3,195},{4,196},{5,197},{6,198},{7,199},{8... | collective-permute-start | bytes 1572872 | tf_op jit(solution)/shard_map/ppermute | solution.py:384
  48.7 1.3 %collective-permute-done.11.other_ref = bf16[512,128]{1,0:T(8,128)(2,1)S(1)} collective-permute-done((bf16[512,128]{1,0:T(8,128)(2,1)S(1)}, bf16[512,128]{1,0:T(8,128)(2,1)S(1)}, u32[]{:S(2)}, u32[]{:S(2)}) %collective-permute-start.11) | collective-permute-done | bytes 131104 | tf_op jit(solution)/shard_map/ppermute | solution.py:372
  50.0 0.8 shard_map.75.select_ref
  50.8 1.3 shard_map.72.refs_4_
  52.1 1.3 shard_map.71.refs_4_
  53.3 2.0 %shard_map.74.near_ref = f32[2,512,512]{2,1,0:T(8,128)S(1)} custom-call(s32[3]{0:T(128)S(1)} %pad_add_fusion.place_ref, bf16[2048,512]{1,0:T(8,128)(2,1)S(1)} %get-tuple-element.69.sw_ref, bf16[2048,512]{1,0:T(8,128)(2,1)S(1)} %get-tuple-element.70.tw_ref, bf16[256,1024]{1,0:T(8,128)(2,1)S(1)} %collective-permute-done.5.refs_0_, ...), custom_call_target="tpu_custom_call" | custom-call | flops 1073741824 | tf_op jit(solution)/shard_map/pallas_call | solution.py:66
  55.3 1.8 %shard_map.73.near_ref = f32[2,512,512]{2,1,0:T(8,128)S(1)} custom-call(s32[3]{0:T(128)S(1)} %pad_add_fusion.place_ref, bf16[2048,512]{1,0:T(8,128)(2,1)S(1)} %get-tuple-element.73.sw_ref, bf16[2048,512]{1,0:T(8,128)(2,1)S(1)} %get-tuple-element.74.tw_ref, bf16[256,1024]{1,0:T(8,128)(2,1)S(1)} %collective-permute-done.5.refs_0_, ...), custom_call_target="tpu_custom_call" | custom-call | flops 1073741824 | tf_op jit(solution)/shard_map/pallas_call | solution.py:66
  57.2 0.7 collective-permute-done.8.p4
  57.9 1.0 shard_map.78
  58.9 0.1 collective-permute-start.13
  59.0 1.0 shard_map.77
  60.0 0.6 collective-permute-start.12
  60.6 1.3 shard_map.76
  61.9 1.3 shard_map.79
  63.1 0.6 shard_map.80
  63.7 12.5 %all_to_all.31.in_ref = f32[16,8,256]{2,1,0:T(8,128)S(1)} all-to-all(f32[16,8,256]{2,1,0:T(8,128)S(1)} %get-tuple-element.94), channel_id=1, replica_groups={{0,8,16,24,64,72,80,88,128,136,144,152,192,200,208,216},{1,9,17,25,65,7..., dimensions={0} | all-to-all | bytes 262144 | tf_op jit(solution)/shard_map/all_to_all | solution.py:271
  76.2 0.2 shard_map.81
  76.4 11.1 %all_to_all.32.stat_ref = f32[16,8,256]{2,1,0:T(8,128)S(1)} all-to-all(f32[16,8,256]{2,1,0:T(8,128)S(1)} %shard_map.81), channel_id=1, replica_groups={{0,1,2,3,4,5,6,7,32,33,34,35,36,37,38,39},{8,9,10,11,12,13,14,15,40,41,..., dimensions={0} | all-to-all | bytes 262144 | tf_op jit(solution)/shard_map/all_to_all | solution.py:271
  87.5 1.2 shard_map.82.g_ref
  88.6 0.1 collective-permute-start.14
  88.7 1.8 %shard_map.83.own_ref = f32[4,512,512]{2,1,0:T(8,128)S(1)} custom-call(s32[3]{0:T(128)S(1)} %pad_add_fusion.place_ref, bf16[512,512]{1,0:T(8,128)(2,1)S(1)} %shard_map.82.g_ref, bf16[2048,512]{1,0:T(8,128)(2,1)S(1)} %get-tuple-element.69.sw_ref), custom_call_target="tpu_custom_call" | custom-call | tf_op jit(solution)/shard_map/pallas_call | solution.py:66
  90.6 0.1 collective-permute-done.14.g_ref
  90.6 1.0 shard_map.85
  91.7 2.1 %collective-permute-start.16 = (bf16[256,512]{1,0:T(8,128)(2,1)S(1)}, bf16[256,512]{1,0:T(8,128)(2,1)S(1)}, u32[]{:S(2)}, u32[]{:S(2)}) collective-permute-start(bf16[256,512]{1,0:T(8,128)(2,1)S(1)} %get-tuple-element.102), channel_id=1, source_target_pairs={{0,64},{1,65},{2,66},{3,67},{4,68},{5,69},{6,70},{7,71},{8,72},{9,... | collective-permute-start | bytes 786440 | tf_op jit(solution)/shard_map/ppermute | solution.py:384
  93.8 1.8 %shard_map.84 = (bf16[256,512]{1,0:T(8,128)(2,1)S(1)}, bf16[256,512]{1,0:T(8,128)(2,1)S(1)}, bf16[256,512]{1,0:T(8,128)(2,1)S(1)}, bf16[256,512]{1,0:T(8,128)(2,...) custom-call(s32[3]{0:T(128)S(1)} %pad_add_fusion.place_ref, f32[4,512,512]{2,1,0:T(8,128)S(1)} %shard_map.83.own_ref, ...), custom_call_target="tpu_custom_call" | custom-call | tf_op jit(solution)/shard_map/pallas_call | solution.py:66
  95.6 0.7 collective-permute-start.15
  96.3 2.7 %collective-permute-start.20 = (bf16[256,512]{1,0:T(8,128)(2,1)S(1)}, bf16[256,512]{1,0:T(8,128)(2,1)S(1)}, u32[]{:S(2)}, u32[]{:S(2)}) collective-permute-start(bf16[256,512]{1,0:T(8,128)(2,1)S(1)} %get-tuple-element.108), channel_id=1, source_target_pairs={{0,64},{1,65},{2,66},{3,67},{4,68},{5,69},{6,70},{7,71},{8,72},{9,... | collective-permute-start | bytes 786440 | tf_op jit(solution)/shard_map/ppermute | solution.py:384
  99.0 2.4 %collective-permute-done.17.d_ref = bf16[256,512]{1,0:T(8,128)(2,1)S(1)} collective-permute-done((bf16[256,512]{1,0:T(8,128)(2,1)S(1)}, bf16[256,512]{1,0:T(8,128)(2,1)S(1)}, u32[]{:S(2)}, u32[]{:S(2)}) %collective-permute-start.17) | collective-permute-done | bytes 262176 | tf_op jit(solution)/shard_map/ppermute | solution.py:384
  101.4 0.1 shard_map.86
  101.5 0.1 collective-permute-start.18
  101.6 2.0 %collective-permute-start.19 = (bf16[256,512]{1,0:T(8,128)(2,1)S(1)}, bf16[256,512]{1,0:T(8,128)(2,1)S(1)}, u32[]{:S(2)}, u32[]{:S(2)}) collective-permute-start(bf16[256,512]{1,0:T(8,128)(2,1)S(1)} %get-tuple-element.107), channel_id=1, source_target_pairs={{0,192},{1,193},{2,194},{3,195},{4,196},{5,197},{6,198},{7,199},{8... | collective-permute-start | bytes 786440 | tf_op jit(solution)/shard_map/ppermute | solution.py:384
  103.6 0.6 collective-permute-done.15.refs_1_
  104.2 3.8 %collective-permute-done.18.refs_2_ = bf16[256,512]{1,0:T(8,128)(2,1)S(1)} collective-permute-done((bf16[256,512]{1,0:T(8,128)(2,1)S(1)}, bf16[256,512]{1,0:T(8,128)(2,1)S(1)}, u32[]{:S(2)}, u32[]{:S(2)}) %collective-permute-start.18) | collective-permute-done | bytes 262176 | tf_op jit(solution)/shard_map/ppermute | solution.py:384
  108.0 1.3 collective-permute-done.19.refs_4_
  109.3 0.2 shard_map.87
  109.5 1.6 %collective-permute-start.21 = (bf16[128,512]{1,0:T(8,128)(2,1)S(1)}, bf16[128,512]{1,0:T(8,128)(2,1)S(1)}, u32[]{:S(2)}, u32[]{:S(2)}) collective-permute-start(bf16[128,512]{1,0:T(8,128)(2,1)S(1)} %get-tuple-element.109), channel_id=1, source_target_pairs={{0,16},{1,17},{2,18},{3,19},{4,20},{5,21},{6,22},{7,23},{8,24},{9,... | collective-permute-start | bytes 393224 | tf_op jit(solution)/shard_map/ppermute | solution.py:384
  111.1 1.6 %collective-permute-start.22 = (bf16[128,512]{1,0:T(8,128)(2,1)S(1)}, bf16[128,512]{1,0:T(8,128)(2,1)S(1)}, u32[]{:S(2)}, u32[]{:S(2)}) collective-permute-start(bf16[128,512]{1,0:T(8,128)(2,1)S(1)} %get-tuple-element.110), channel_id=1, source_target_pairs={{0,24},{1,25},{2,26},{3,27},{4,28},{5,29},{6,30},{7,31},{8,0},{9,1... | collective-permute-start | bytes 393224 | tf_op jit(solution)/shard_map/ppermute | solution.py:384
  112.7 0.4 collective-permute-start.23
  113.1 0.8 shard_map.88
  113.9 2.1 %collective-permute-done.21.refs_0_ = bf16[128,512]{1,0:T(8,128)(2,1)S(1)} collective-permute-done((bf16[128,512]{1,0:T(8,128)(2,1)S(1)}, bf16[128,512]{1,0:T(8,128)(2,1)S(1)}, u32[]{:S(2)}, u32[]{:S(2)}) %collective-permute-start.21) | collective-permute-done | bytes 131104 | tf_op jit(solution)/shard_map/ppermute | solution.py:384
  116.0 0.0 collective-permute-done.22.refs_1_
  116.1 2.8 %collective-permute-done.23.refs_2_ = bf16[128,512]{1,0:T(8,128)(2,1)S(1)} collective-permute-done((bf16[128,512]{1,0:T(8,128)(2,1)S(1)}, bf16[128,512]{1,0:T(8,128)(2,1)S(1)}, u32[]{:S(2)}, u32[]{:S(2)}) %collective-permute-start.23) | collective-permute-done | bytes 131104 | tf_op jit(solution)/shard_map/ppermute | solution.py:384
  118.9 0.1 shard_map.89
  119.0 12.1 %all_to_all.33.in_ref = bf16[8,16,512]{2,1,0:T(8,128)(2,1)S(1)} all-to-all(bf16[8,16,512]{2,1,0:T(8,128)(2,1)S(1)} %bitcast.10), channel_id=1, replica_groups={{0,1,2,3,4,5,6,7},{8,9,10,11,12,13,14,15},{16,17,18,19,20,21,22,23},{24..., dimensions={0} | all-to-all | bytes 262144 | tf_op jit(solution)/shard_map/all_to_all | solution.py:271
  131.0 0.6 copy.7
  (17 shorter events, 0.1 us)
Async XLA Ops:
  0.6 22.6 %collective-permute-start = (bf16[4096,512]{1,0:T(8,128)(2,1)}, bf16[4096,512]{1,0:T(8,128)(2,1)S(1)}, u32[]{:S(2)}, u32[]{:S(2)}) collective-permute-start(bf16[4096,512]{1,0:T(8,128)(2,1)} %refs_0_.1), channel_id=1, source_target_pairs={{0,32},{32,0},{64,96},{96,64},{128,160},{160,128},{192,224},{224,1... | collective-permute-start | bytes 12582920 | tf_op jit(solution)/shard_map/ppermute | solution.py:372
  0.7 22.5 %collective-permute-start.1 = (bf16[4096,512]{1,0:T(8,128)(2,1)}, bf16[4096,512]{1,0:T(8,128)(2,1)S(1)}, u32[]{:S(2)}, u32[]{:S(2)}) collective-permute-start(bf16[4096,512]{1,0:T(8,128)(2,1)} %refs_1_.1), channel_id=1, source_target_pairs={{0,32},{32,0},{64,96},{96,64},{128,160},{160,128},{192,224},{224,1... | collective-permute-start | bytes 12582920 | tf_op jit(solution)/shard_map/ppermute | solution.py:372
  23.2 3.3 %copy-start = (bf16[4096,512]{1,0:T(8,128)(2,1)}, bf16[4096,512]{1,0:T(8,128)(2,1)S(1)}, u32[]{:S(2)}) copy-start(bf16[4096,512]{1,0:T(8,128)(2,1)S(1)} %collective-permute-done.refs_2_) | copy-start | bytes 12582916
  23.2 4.0 %copy-start.1 = (bf16[4096,512]{1,0:T(8,128)(2,1)}, bf16[4096,512]{1,0:T(8,128)(2,1)S(1)}, u32[]{:S(2)}) copy-start(bf16[4096,512]{1,0:T(8,128)(2,1)S(1)} %collective-permute-done.1.refs_3_) | copy-start | bytes 12582916
  23.2 8.3 %collective-permute-start.2 = (bf16[128,1152]{1,0:T(8,128)(2,1)S(1)}, bf16[128,1152]{1,0:T(8,128)(2,1)S(1)}, u32[]{:S(2)}, u32[]{:S(2)}) collective-permute-start(bf16[128,1152]{1,0:T(8,128)(2,1)S(1)} %bitcast.6), channel_id=1, source_target_pairs={{0,16},{1,17},{2,18},{3,19},{4,20},{5,21},{6,22},{7,23},{8,24},{9,... | collective-permute-start | bytes 884744 | tf_op jit(solution)/shard_map/ppermute | solution.py:384
  26.5 8.2 %collective-permute-start.3 = (bf16[128,1152]{1,0:T(8,128)(2,1)S(1)}, bf16[128,1152]{1,0:T(8,128)(2,1)S(1)}, u32[]{:S(2)}, u32[]{:S(2)}) collective-permute-start(bf16[128,1152]{1,0:T(8,128)(2,1)S(1)} %bitcast.7), channel_id=1, source_target_pairs={{0,8},{1,9},{2,10},{3,11},{4,12},{5,13},{6,14},{7,15},{8,16},{9,17... | collective-permute-start | bytes 884744 | tf_op jit(solution)/shard_map/ppermute | solution.py:384
  27.2 7.9 %collective-permute-start.4 = (bf16[128,1152]{1,0:T(8,128)(2,1)S(1)}, bf16[128,1152]{1,0:T(8,128)(2,1)S(1)}, u32[]{:S(2)}, u32[]{:S(2)}) collective-permute-start(bf16[128,1152]{1,0:T(8,128)(2,1)S(1)} %bitcast.8), channel_id=1, source_target_pairs={{0,24},{1,25},{2,26},{3,27},{4,28},{5,29},{6,30},{7,31},{8,0},{9,1... | collective-permute-start | bytes 884744 | tf_op jit(solution)/shard_map/ppermute | solution.py:384
  35.7 9.4 %collective-permute-start.5 = (bf16[256,1024]{1,0:T(8,128)(2,1)S(1)}, bf16[256,1024]{1,0:T(8,128)(2,1)S(1)}, u32[]{:S(2)}, u32[]{:S(2)}) collective-permute-start(bf16[256,1024]{1,0:T(8,128)(2,1)S(1)} %get-tuple-element.61.refs_0_), channel_id=1, source_target_pairs={{0,64},{1,65},{2,66},{3,67},{4,68},{5,69},{6,70},{7,71},{8,72},{9,... | collective-permute-start | bytes 1572872 | tf_op jit(solution)/shard_map/ppermute | solution.py:384
  36.2 10.4 %collective-permute-start.6 = (bf16[256,1024]{1,0:T(8,128)(2,1)S(1)}, bf16[256,1024]{1,0:T(8,128)(2,1)S(1)}, u32[]{:S(2)}, u32[]{:S(2)}) collective-permute-start(bf16[256,1024]{1,0:T(8,128)(2,1)S(1)} %get-tuple-element.62.refs_1_), channel_id=1, source_target_pairs={{0,192},{1,193},{2,194},{3,195},{4,196},{5,197},{6,198},{7,199},{8... | collective-permute-start | bytes 1572872 | tf_op jit(solution)/shard_map/ppermute | solution.py:384
  37.8 15.5 %collective-permute-start.10 = (bf16[256,1024]{1,0:T(8,128)(2,1)S(1)}, bf16[256,1024]{1,0:T(8,128)(2,1)S(1)}, u32[]{:S(2)}, u32[]{:S(2)}) collective-permute-start(bf16[256,1024]{1,0:T(8,128)(2,1)S(1)} %get-tuple-element.61.refs_0_), channel_id=1, source_target_pairs={{0,192},{1,193},{2,194},{3,195},{4,196},{5,197},{6,198},{7,199},{8... | collective-permute-start | bytes 1572872 | tf_op jit(solution)/shard_map/ppermute | solution.py:384
  38.6 14.7 %collective-permute-start.9 = (bf16[256,1024]{1,0:T(8,128)(2,1)S(1)}, bf16[256,1024]{1,0:T(8,128)(2,1)S(1)}, u32[]{:S(2)}, u32[]{:S(2)}) collective-permute-start(bf16[256,1024]{1,0:T(8,128)(2,1)S(1)} %get-tuple-element.62.refs_1_), channel_id=1, source_target_pairs={{0,64},{1,65},{2,66},{3,67},{4,68},{5,69},{6,70},{7,71},{8,72},{9,... | collective-permute-start | bytes 1572872 | tf_op jit(solution)/shard_map/ppermute | solution.py:384
  46.6 10.5 %collective-permute-start.7 = (bf16[256,1024]{1,0:T(8,128)(2,1)S(1)}, bf16[256,1024]{1,0:T(8,128)(2,1)S(1)}, u32[]{:S(2)}, u32[]{:S(2)}) collective-permute-start(bf16[256,1024]{1,0:T(8,128)(2,1)S(1)} %collective-permute-done.5.refs_0_), channel_id=1, source_target_pairs={{0,64},{1,65},{2,66},{3,67},{4,68},{5,69},{6,70},{7,71},{8,72},{9,... | collective-permute-start | bytes 1572872 | tf_op jit(solution)/shard_map/ppermute | solution.py:384
  46.9 11.0 %collective-permute-start.8 = (bf16[256,1024]{1,0:T(8,128)(2,1)S(1)}, bf16[256,1024]{1,0:T(8,128)(2,1)S(1)}, u32[]{:S(2)}, u32[]{:S(2)}) collective-permute-start(bf16[256,1024]{1,0:T(8,128)(2,1)S(1)} %collective-permute-done.6.refs_3_), channel_id=1, source_target_pairs={{0,192},{1,193},{2,194},{3,195},{4,196},{5,197},{6,198},{7,199},{8... | collective-permute-start | bytes 1572872 | tf_op jit(solution)/shard_map/ppermute | solution.py:384
  48.7 1.3 %collective-permute-start.11 = (bf16[512,128]{1,0:T(8,128)(2,1)S(1)}, bf16[512,128]{1,0:T(8,128)(2,1)S(1)}, u32[]{:S(2)}, u32[]{:S(2)}) collective-permute-start(bf16[512,128]{1,0:T(8,128)(2,1)S(1)} %get-tuple-element.79.own_ref), channel_id=1, source_target_pairs={{0,32},{32,0},{64,96},{96,64},{128,160},{160,128},{192,224},{224,1... | collective-permute-start | bytes 393224 | tf_op jit(solution)/shard_map/ppermute | solution.py:372
  58.9 3.0 %collective-permute-start.13 = (f32[512,512]{1,0:T(8,128)S(1)}, f32[512,512]{1,0:T(8,128)S(1)}, u32[]{:S(2)}, u32[]{:S(2)}) collective-permute-start(f32[512,512]{1,0:T(8,128)S(1)} %shard_map.78), channel_id=1, source_target_pairs={{0,32},{32,0},{64,96},{96,64},{128,160},{160,128},{192,224},{224,1... | collective-permute-start | bytes 3145736 | tf_op jit(solution)/shard_map/ppermute | solution.py:372
  60.0 3.1 %collective-permute-start.12 = (f32[512,512]{1,0:T(8,128)S(1)}, f32[512,512]{1,0:T(8,128)S(1)}, u32[]{:S(2)}, u32[]{:S(2)}) collective-permute-start(f32[512,512]{1,0:T(8,128)S(1)} %shard_map.77), channel_id=1, source_target_pairs={{0,32},{32,0},{64,96},{96,64},{128,160},{160,128},{192,224},{224,1... | collective-permute-start | bytes 3145736 | tf_op jit(solution)/shard_map/ppermute | solution.py:372
  88.6 2.0 %collective-permute-start.14 = (bf16[512,512]{1,0:T(8,128)(2,1)S(1)}, bf16[512,512]{1,0:T(8,128)(2,1)S(1)}, u32[]{:S(2)}, u32[]{:S(2)}) collective-permute-start(bf16[512,512]{1,0:T(8,128)(2,1)S(1)} %shard_map.82.g_ref), channel_id=1, source_target_pairs={{0,32},{32,0},{64,96},{96,64},{128,160},{160,128},{192,224},{224,1... | collective-permute-start | bytes 1572872 | tf_op jit(solution)/shard_map/ppermute | solution.py:372
  91.7 7.4 %collective-permute-start.16 = (bf16[256,512]{1,0:T(8,128)(2,1)S(1)}, bf16[256,512]{1,0:T(8,128)(2,1)S(1)}, u32[]{:S(2)}, u32[]{:S(2)}) collective-permute-start(bf16[256,512]{1,0:T(8,128)(2,1)S(1)} %get-tuple-element.102), channel_id=1, source_target_pairs={{0,64},{1,65},{2,66},{3,67},{4,68},{5,69},{6,70},{7,71},{8,72},{9,... | collective-permute-start | bytes 786440 | tf_op jit(solution)/shard_map/ppermute | solution.py:384
  93.8 7.6 %collective-permute-start.17 = (bf16[256,512]{1,0:T(8,128)(2,1)S(1)}, bf16[256,512]{1,0:T(8,128)(2,1)S(1)}, u32[]{:S(2)}, u32[]{:S(2)}) collective-permute-start(bf16[256,512]{1,0:T(8,128)(2,1)S(1)} %get-tuple-element.104), channel_id=1, source_target_pairs={{0,192},{1,193},{2,194},{3,195},{4,196},{5,197},{6,198},{7,199},{8... | collective-permute-start | bytes 786440 | tf_op jit(solution)/shard_map/ppermute | solution.py:384
  95.6 8.6 %collective-permute-start.15 = (bf16[256,512]{1,0:T(8,128)(2,1)S(1)}, bf16[256,512]{1,0:T(8,128)(2,1)S(1)}, u32[]{:S(2)}, u32[]{:S(2)}) collective-permute-start(bf16[256,512]{1,0:T(8,128)(2,1)S(1)} %get-tuple-element.100), channel_id=1, source_target_pairs={{0,192},{1,193},{2,194},{3,195},{4,196},{5,197},{6,198},{7,199},{8... | collective-permute-start | bytes 786440 | tf_op jit(solution)/shard_map/ppermute | solution.py:384
  96.3 7.9 %collective-permute-start.20 = (bf16[256,512]{1,0:T(8,128)(2,1)S(1)}, bf16[256,512]{1,0:T(8,128)(2,1)S(1)}, u32[]{:S(2)}, u32[]{:S(2)}) collective-permute-start(bf16[256,512]{1,0:T(8,128)(2,1)S(1)} %get-tuple-element.108), channel_id=1, source_target_pairs={{0,64},{1,65},{2,66},{3,67},{4,68},{5,69},{6,70},{7,71},{8,72},{9,... | collective-permute-start | bytes 786440 | tf_op jit(solution)/shard_map/ppermute | solution.py:384
  101.5 6.4 %collective-permute-start.18 = (bf16[256,512]{1,0:T(8,128)(2,1)S(1)}, bf16[256,512]{1,0:T(8,128)(2,1)S(1)}, u32[]{:S(2)}, u32[]{:S(2)}) collective-permute-start(bf16[256,512]{1,0:T(8,128)(2,1)S(1)} %get-tuple-element.105), channel_id=1, source_target_pairs={{0,64},{1,65},{2,66},{3,67},{4,68},{5,69},{6,70},{7,71},{8,72},{9,... | collective-permute-start | bytes 786440 | tf_op jit(solution)/shard_map/ppermute | solution.py:384
  101.6 7.7 %collective-permute-start.19 = (bf16[256,512]{1,0:T(8,128)(2,1)S(1)}, bf16[256,512]{1,0:T(8,128)(2,1)S(1)}, u32[]{:S(2)}, u32[]{:S(2)}) collective-permute-start(bf16[256,512]{1,0:T(8,128)(2,1)S(1)} %get-tuple-element.107), channel_id=1, source_target_pairs={{0,192},{1,193},{2,194},{3,195},{4,196},{5,197},{6,198},{7,199},{8... | collective-permute-start | bytes 786440 | tf_op jit(solution)/shard_map/ppermute | solution.py:384
  109.5 6.6 %collective-permute-start.21 = (bf16[128,512]{1,0:T(8,128)(2,1)S(1)}, bf16[128,512]{1,0:T(8,128)(2,1)S(1)}, u32[]{:S(2)}, u32[]{:S(2)}) collective-permute-start(bf16[128,512]{1,0:T(8,128)(2,1)S(1)} %get-tuple-element.109), channel_id=1, source_target_pairs={{0,16},{1,17},{2,18},{3,19},{4,20},{5,21},{6,22},{7,23},{8,24},{9,... | collective-permute-start | bytes 393224 | tf_op jit(solution)/shard_map/ppermute | solution.py:384
  111.1 5.0 %collective-permute-start.22 = (bf16[128,512]{1,0:T(8,128)(2,1)S(1)}, bf16[128,512]{1,0:T(8,128)(2,1)S(1)}, u32[]{:S(2)}, u32[]{:S(2)}) collective-permute-start(bf16[128,512]{1,0:T(8,128)(2,1)S(1)} %get-tuple-element.110), channel_id=1, source_target_pairs={{0,24},{1,25},{2,26},{3,27},{4,28},{5,29},{6,30},{7,31},{8,0},{9,1... | collective-permute-start | bytes 393224 | tf_op jit(solution)/shard_map/ppermute | solution.py:384
  112.7 6.2 %collective-permute-start.23 = (bf16[128,512]{1,0:T(8,128)(2,1)S(1)}, bf16[128,512]{1,0:T(8,128)(2,1)S(1)}, u32[]{:S(2)}, u32[]{:S(2)}) collective-permute-start(bf16[128,512]{1,0:T(8,128)(2,1)S(1)} %get-tuple-element.111), channel_id=1, source_target_pairs={{0,8},{1,9},{2,10},{3,11},{4,12},{5,13},{6,14},{7,15},{8,16},{9,17... | collective-permute-start | bytes 393224 | tf_op jit(solution)/shard_map/ppermute | solution.py:384

commit v11 on v10

--- a/solution.py
+++ b/solution.py
@@ -477,9 +477,9 @@
         logits * 2 + [((STAT, 8, N // 2), F32)],
         s_own, s_other, t, table,
     )
+    stats = exchange(stats, ("vocab", "tok"), CORE_Z_GROUPS)
+    stats = call(merge_kernel, [VM], [((STAT, 8, N // 2), F32)], stats)[0]
     stats = exchange(stats, ("vocab", "tok"), X_Y_GROUPS)
-    stats = call(merge_kernel, [VM], [((STAT, 8, N // 2), F32)], stats)[0]
-    stats = exchange(stats, ("vocab", "tok"), CORE_Z_GROUPS)
     g = call(
         logit_grad_kernel,
         [SM] + [VM] * 3,

time: 132 us -> 132 us (level)
  no operation moved by 1% of the time
where the time goes in v11:
time: 132 us
  blocking collectives  56.7 us (43%)
  starting transfers between devices  26.5 us (20%)
  Pallas kernels  25 us (19%)
  waiting for transfers between devices  21.8 us (17%)
    all_to_all x4, blocking collectives, exchange(): out = lax.all_to_all(flat, axis, 0, 0, axis_index_groups=groups, tiled=True)  56.7 us
    ppermute x18, starting transfers between devices, along_rings(): return lax.ppermute(a, ('vocab', 'tok'), pairs)  25.2 us
    pallas_call x22, Pallas kernels, call(): pl.pallas_call(kernel, in_specs=in_specs, out_specs=[VM] * len(outs), out...  24.2 us
    ppermute x18, waiting for transfers between devices, along_rings(): return lax.ppermute(a, ('vocab', 'tok'), pairs)  20.4 us
  transfers between devices with their start and end apart: 24, of which 13 were waited for; matrix products, arithmetic and copies ran while one was open for 0% of the time, Pallas kernels for 15%

profile of v11, /device:TPU:6, one launch (start us, length us, event | category | flops | bytes accessed | tf_op | source)
XLA Modules:
  0.0 131.7 jit_solution(12034192156847331099)
XLA Ops:
  0.6 0.1 collective-permute-start
  0.7 0.5 collective-permute-start.1
  1.2 0.9 shard_map.68
  2.1 21.1 %all_to_all.30 = bf16[8,16,1152]{2,1,0:T(8,128)(2,1)S(1)} all-to-all(bf16[8,16,1152]{2,1,0:T(8,128)(2,1)S(1)} %shard_map.68), channel_id=1, replica_groups={{0,1,2,3,4,5,6,7},{8,9,10,11,12,13,14,15},{16,17,18,19,20,21,22,23},{24..., dimensions={0} | all-to-all | bytes 589824 | tf_op jit(solution)/shard_map/all_to_all | solution.py:271
  23.2 3.3 %collective-permute-start.2 = (bf16[128,1152]{1,0:T(8,128)(2,1)S(1)}, bf16[128,1152]{1,0:T(8,128)(2,1)S(1)}, u32[]{:S(2)}, u32[]{:S(2)}) collective-permute-start(bf16[128,1152]{1,0:T(8,128)(2,1)S(1)} %bitcast.6), channel_id=1, source_target_pairs={{0,16},{1,17},{2,18},{3,19},{4,20},{5,21},{6,22},{7,23},{8,24},{9,... | collective-permute-start | bytes 884744 | tf_op jit(solution)/shard_map/ppermute | solution.py:384
  26.5 0.7 collective-permute-start.3
  27.2 2.6 %collective-permute-start.4 = (bf16[128,1152]{1,0:T(8,128)(2,1)S(1)}, bf16[128,1152]{1,0:T(8,128)(2,1)S(1)}, u32[]{:S(2)}, u32[]{:S(2)}) collective-permute-start(bf16[128,1152]{1,0:T(8,128)(2,1)S(1)} %bitcast.8), channel_id=1, source_target_pairs={{0,24},{1,25},{2,26},{3,27},{4,28},{5,29},{6,30},{7,31},{8,0},{9,1... | collective-permute-start | bytes 884744 | tf_op jit(solution)/shard_map/ppermute | solution.py:384
  29.8 0.1 pad_add_fusion.place_ref
  29.8 1.7 %collective-permute-done.2.far_ref = bf16[128,1152]{1,0:T(8,128)(2,1)S(1)} collective-permute-done((bf16[128,1152]{1,0:T(8,128)(2,1)S(1)}, bf16[128,1152]{1,0:T(8,128)(2,1)S(1)}, u32[]{:S(2)}, u32[]{:S(2)}) %collective-permute-start.2) | collective-permute-done | bytes 294944 | tf_op jit(solution)/shard_map/ppermute | solution.py:384
  31.6 3.1 %collective-permute-done.3.left_ref = bf16[128,1152]{1,0:T(8,128)(2,1)S(1)} collective-permute-done((bf16[128,1152]{1,0:T(8,128)(2,1)S(1)}, bf16[128,1152]{1,0:T(8,128)(2,1)S(1)}, u32[]{:S(2)}, u32[]{:S(2)}) %collective-permute-start.3) | collective-permute-done | bytes 294944 | tf_op jit(solution)/shard_map/ppermute | solution.py:384
  34.7 0.3 collective-permute-done.4.right_ref
  35.0 0.6 shard_map.69
  35.7 0.6 collective-permute-start.5
  36.2 1.5 %collective-permute-start.6 = (bf16[256,1024]{1,0:T(8,128)(2,1)S(1)}, bf16[256,1024]{1,0:T(8,128)(2,1)S(1)}, u32[]{:S(2)}, u32[]{:S(2)}) collective-permute-start(bf16[256,1024]{1,0:T(8,128)(2,1)S(1)} %get-tuple-element.62.refs_1_), channel_id=1, source_target_pairs={{0,192},{1,193},{2,194},{3,195},{4,196},{5,197},{6,198},{7,199},{8... | collective-permute-start | bytes 1572872 | tf_op jit(solution)/shard_map/ppermute | solution.py:384
  37.8 0.8 collective-permute-start.10
  38.6 2.4 %collective-permute-start.9 = (bf16[256,1024]{1,0:T(8,128)(2,1)S(1)}, bf16[256,1024]{1,0:T(8,128)(2,1)S(1)}, u32[]{:S(2)}, u32[]{:S(2)}) collective-permute-start(bf16[256,1024]{1,0:T(8,128)(2,1)S(1)} %get-tuple-element.62.refs_1_), channel_id=1, source_target_pairs={{0,64},{1,65},{2,66},{3,67},{4,68},{5,69},{6,70},{7,71},{8,72},{9,... | collective-permute-start | bytes 1572872 | tf_op jit(solution)/shard_map/ppermute | solution.py:384
  41.0 4.1 %shard_map.70 = (bf16[2048,512]{1,0:T(8,128)(2,1)S(1)}, bf16[2048,512]{1,0:T(8,128)(2,1)S(1)}, bf16[2048,512]{1,0:T(8,128)(2,1)S(1)}, bf16[2048,512]{1,0:T(8,128)(2,1)S(1)}) custom-call(s32[3]{0:T(128)S(1)} %pad_add_fusion.place_ref, bf16[4096,512]{1,0:T(8,128)(2,1)} %refs_0_.1, bf16[4096,512]{1,0:T(8,128)(2,1)} %refs_1_.1, bf16[4096,512]{1,0:T(8,128)(2,1)} %copy-done, ...), custom_call_target="tpu_custom_call" | custom-call | tf_op jit(solution)/shard_map/pallas_call | solution.py:66
  45.1 1.5 %collective-permute-done.6.refs_3_ = bf16[256,1024]{1,0:T(8,128)(2,1)S(1)} collective-permute-done((bf16[256,1024]{1,0:T(8,128)(2,1)S(1)}, bf16[256,1024]{1,0:T(8,128)(2,1)S(1)}, u32[]{:S(2)}, u32[]{:S(2)}) %collective-permute-start.6) | collective-permute-done | bytes 524320 | tf_op jit(solution)/shard_map/ppermute | solution.py:384
  46.6 0.3 collective-permute-start.7
  46.9 1.7 %collective-permute-start.8 = (bf16[256,1024]{1,0:T(8,128)(2,1)S(1)}, bf16[256,1024]{1,0:T(8,128)(2,1)S(1)}, u32[]{:S(2)}, u32[]{:S(2)}) collective-permute-start(bf16[256,1024]{1,0:T(8,128)(2,1)S(1)} %collective-permute-done.6.refs_3_), channel_id=1, source_target_pairs={{0,192},{1,193},{2,194},{3,195},{4,196},{5,197},{6,198},{7,199},{8... | collective-permute-start | bytes 1572872 | tf_op jit(solution)/shard_map/ppermute | solution.py:384
  48.7 1.3 %collective-permute-done.11.other_ref = bf16[512,128]{1,0:T(8,128)(2,1)S(1)} collective-permute-done((bf16[512,128]{1,0:T(8,128)(2,1)S(1)}, bf16[512,128]{1,0:T(8,128)(2,1)S(1)}, u32[]{:S(2)}, u32[]{:S(2)}) %collective-permute-start.11) | collective-permute-done | bytes 131104 | tf_op jit(solution)/shard_map/ppermute | solution.py:372
  50.0 0.8 shard_map.75.select_ref
  50.8 1.3 shard_map.72.refs_4_
  52.1 1.3 shard_map.71.refs_4_
  53.3 2.0 %shard_map.74.near_ref = f32[2,512,512]{2,1,0:T(8,128)S(1)} custom-call(s32[3]{0:T(128)S(1)} %pad_add_fusion.place_ref, bf16[2048,512]{1,0:T(8,128)(2,1)S(1)} %get-tuple-element.69.sw_ref, bf16[2048,512]{1,0:T(8,128)(2,1)S(1)} %get-tuple-element.70.tw_ref, bf16[256,1024]{1,0:T(8,128)(2,1)S(1)} %collective-permute-done.5.refs_0_, ...), custom_call_target="tpu_custom_call" | custom-call | flops 1073741824 | tf_op jit(solution)/shard_map/pallas_call | solution.py:66
  55.3 1.8 %shard_map.73.near_ref = f32[2,512,512]{2,1,0:T(8,128)S(1)} custom-call(s32[3]{0:T(128)S(1)} %pad_add_fusion.place_ref, bf16[2048,512]{1,0:T(8,128)(2,1)S(1)} %get-tuple-element.73.sw_ref, bf16[2048,512]{1,0:T(8,128)(2,1)S(1)} %get-tuple-element.74.tw_ref, bf16[256,1024]{1,0:T(8,128)(2,1)S(1)} %collective-permute-done.5.refs_0_, ...), custom_call_target="tpu_custom_call" | custom-call | flops 1073741824 | tf_op jit(solution)/shard_map/pallas_call | solution.py:66
  57.2 0.7 collective-permute-done.8.p4
  57.9 1.0 shard_map.78
  58.9 0.1 collective-permute-start.13
  59.0 1.0 shard_map.77
  60.0 0.6 collective-permute-start.12
  60.6 1.3 shard_map.76
  61.9 1.3 shard_map.79
  63.1 0.6 shard_map.80
  63.7 11.1 %all_to_all.31.in_ref = f32[16,8,256]{2,1,0:T(8,128)S(1)} all-to-all(f32[16,8,256]{2,1,0:T(8,128)S(1)} %get-tuple-element.94), channel_id=1, replica_groups={{0,1,2,3,4,5,6,7,32,33,34,35,36,37,38,39},{8,9,10,11,12,13,14,15,40,41,..., dimensions={0} | all-to-all | bytes 262144 | tf_op jit(solution)/shard_map/all_to_all | solution.py:271
  74.8 0.2 shard_map.81
  75.0 12.5 %all_to_all.32.stat_ref = f32[16,8,256]{2,1,0:T(8,128)S(1)} all-to-all(f32[16,8,256]{2,1,0:T(8,128)S(1)} %shard_map.81), channel_id=1, replica_groups={{0,8,16,24,64,72,80,88,128,136,144,152,192,200,208,216},{1,9,17,25,65,7..., dimensions={0} | all-to-all | bytes 262144 | tf_op jit(solution)/shard_map/all_to_all | solution.py:271
  87.5 1.2 shard_map.82.g_ref
  88.6 0.1 collective-permute-start.14
  88.7 1.8 %shard_map.83.own_ref = f32[4,512,512]{2,1,0:T(8,128)S(1)} custom-call(s32[3]{0:T(128)S(1)} %pad_add_fusion.place_ref, bf16[512,512]{1,0:T(8,128)(2,1)S(1)} %shard_map.82.g_ref, bf16[2048,512]{1,0:T(8,128)(2,1)S(1)} %get-tuple-element.69.sw_ref), custom_call_target="tpu_custom_call" | custom-call | tf_op jit(solution)/shard_map/pallas_call | solution.py:66
  90.6 0.1 collective-permute-done.14.g_ref
  90.6 1.0 shard_map.85
  91.7 2.1 %collective-permute-start.16 = (bf16[256,512]{1,0:T(8,128)(2,1)S(1)}, bf16[256,512]{1,0:T(8,128)(2,1)S(1)}, u32[]{:S(2)}, u32[]{:S(2)}) collective-permute-start(bf16[256,512]{1,0:T(8,128)(2,1)S(1)} %get-tuple-element.102), channel_id=1, source_target_pairs={{0,64},{1,65},{2,66},{3,67},{4,68},{5,69},{6,70},{7,71},{8,72},{9,... | collective-permute-start | bytes 786440 | tf_op jit(solution)/shard_map/ppermute | solution.py:384
  93.8 1.8 %shard_map.84 = (bf16[256,512]{1,0:T(8,128)(2,1)S(1)}, bf16[256,512]{1,0:T(8,128)(2,1)S(1)}, bf16[256,512]{1,0:T(8,128)(2,1)S(1)}, bf16[256,512]{1,0:T(8,128)(2,...) custom-call(s32[3]{0:T(128)S(1)} %pad_add_fusion.place_ref, f32[4,512,512]{2,1,0:T(8,128)S(1)} %shard_map.83.own_ref, ...), custom_call_target="tpu_custom_call" | custom-call | tf_op jit(solution)/shard_map/pallas_call | solution.py:66
  95.6 0.7 collective-permute-start.15
  96.3 2.7 %collective-permute-start.20 = (bf16[256,512]{1,0:T(8,128)(2,1)S(1)}, bf16[256,512]{1,0:T(8,128)(2,1)S(1)}, u32[]{:S(2)}, u32[]{:S(2)}) collective-permute-start(bf16[256,512]{1,0:T(8,128)(2,1)S(1)} %get-tuple-element.108), channel_id=1, source_target_pairs={{0,64},{1,65},{2,66},{3,67},{4,68},{5,69},{6,70},{7,71},{8,72},{9,... | collective-permute-start | bytes 786440 | tf_op jit(solution)/shard_map/ppermute | solution.py:384
  99.0 2.4 %collective-permute-done.17.d_ref = bf16[256,512]{1,0:T(8,128)(2,1)S(1)} collective-permute-done((bf16[256,512]{1,0:T(8,128)(2,1)S(1)}, bf16[256,512]{1,0:T(8,128)(2,1)S(1)}, u32[]{:S(2)}, u32[]{:S(2)}) %collective-permute-start.17) | collective-permute-done | bytes 262176 | tf_op jit(solution)/shard_map/ppermute | solution.py:384
  101.4 0.1 shard_map.86
  101.5 0.1 collective-permute-start.18
  101.6 2.0 %collective-permute-start.19 = (bf16[256,512]{1,0:T(8,128)(2,1)S(1)}, bf16[256,512]{1,0:T(8,128)(2,1)S(1)}, u32[]{:S(2)}, u32[]{:S(2)}) collective-permute-start(bf16[256,512]{1,0:T(8,128)(2,1)S(1)} %get-tuple-element.107), channel_id=1, source_target_pairs={{0,192},{1,193},{2,194},{3,195},{4,196},{5,197},{6,198},{7,199},{8... | collective-permute-start | bytes 786440 | tf_op jit(solution)/shard_map/ppermute | solution.py:384
  103.6 0.6 collective-permute-done.15.refs_1_
  104.2 3.8 %collective-permute-done.18.refs_2_ = bf16[256,512]{1,0:T(8,128)(2,1)S(1)} collective-permute-done((bf16[256,512]{1,0:T(8,128)(2,1)S(1)}, bf16[256,512]{1,0:T(8,128)(2,1)S(1)}, u32[]{:S(2)}, u32[]{:S(2)}) %collective-permute-start.18) | collective-permute-done | bytes 262176 | tf_op jit(solution)/shard_map/ppermute | solution.py:384
  108.0 1.3 collective-permute-done.19.refs_4_
  109.3 0.2 shard_map.87
  109.5 1.6 %collective-permute-start.21 = (bf16[128,512]{1,0:T(8,128)(2,1)S(1)}, bf16[128,512]{1,0:T(8,128)(2,1)S(1)}, u32[]{:S(2)}, u32[]{:S(2)}) collective-permute-start(bf16[128,512]{1,0:T(8,128)(2,1)S(1)} %get-tuple-element.109), channel_id=1, source_target_pairs={{0,16},{1,17},{2,18},{3,19},{4,20},{5,21},{6,22},{7,23},{8,24},{9,... | collective-permute-start | bytes 393224 | tf_op jit(solution)/shard_map/ppermute | solution.py:384
  111.1 1.6 %collective-permute-start.22 = (bf16[128,512]{1,0:T(8,128)(2,1)S(1)}, bf16[128,512]{1,0:T(8,128)(2,1)S(1)}, u32[]{:S(2)}, u32[]{:S(2)}) collective-permute-start(bf16[128,512]{1,0:T(8,128)(2,1)S(1)} %get-tuple-element.110), channel_id=1, source_target_pairs={{0,24},{1,25},{2,26},{3,27},{4,28},{5,29},{6,30},{7,31},{8,0},{9,1... | collective-permute-start | bytes 393224 | tf_op jit(solution)/shard_map/ppermute | solution.py:384
  112.7 0.4 collective-permute-start.23
  113.1 0.8 shard_map.88
  113.9 2.1 %collective-permute-done.21.refs_0_ = bf16[128,512]{1,0:T(8,128)(2,1)S(1)} collective-permute-done((bf16[128,512]{1,0:T(8,128)(2,1)S(1)}, bf16[128,512]{1,0:T(8,128)(2,1)S(1)}, u32[]{:S(2)}, u32[]{:S(2)}) %collective-permute-start.21) | collective-permute-done | bytes 131104 | tf_op jit(solution)/shard_map/ppermute | solution.py:384
  116.0 0.0 collective-permute-done.22.refs_1_
  116.1 2.8 %collective-permute-done.23.refs_2_ = bf16[128,512]{1,0:T(8,128)(2,1)S(1)} collective-permute-done((bf16[128,512]{1,0:T(8,128)(2,1)S(1)}, bf16[128,512]{1,0:T(8,128)(2,1)S(1)}, u32[]{:S(2)}, u32[]{:S(2)}) %collective-permute-start.23) | collective-permute-done | bytes 131104 | tf_op jit(solution)/shard_map/ppermute | solution.py:384
  118.9 0.1 shard_map.89
  119.0 12.1 %all_to_all.33.in_ref = bf16[8,16,512]{2,1,0:T(8,128)(2,1)S(1)} all-to-all(bf16[8,16,512]{2,1,0:T(8,128)(2,1)S(1)} %bitcast.10), channel_id=1, replica_groups={{0,1,2,3,4,5,6,7},{8,9,10,11,12,13,14,15},{16,17,18,19,20,21,22,23},{24..., dimensions={0} | all-to-all | bytes 262144 | tf_op jit(solution)/shard_map/all_to_all | solution.py:271
  131.0 0.6 copy.7
  (17 shorter events, 0.1 us)
Async XLA Ops:
  0.6 22.6 %collective-permute-start = (bf16[4096,512]{1,0:T(8,128)(2,1)}, bf16[4096,512]{1,0:T(8,128)(2,1)S(1)}, u32[]{:S(2)}, u32[]{:S(2)}) collective-permute-start(bf16[4096,512]{1,0:T(8,128)(2,1)} %refs_0_.1), channel_id=1, source_target_pairs={{0,32},{32,0},{64,96},{96,64},{128,160},{160,128},{192,224},{224,1... | collective-permute-start | bytes 12582920 | tf_op jit(solution)/shard_map/ppermute | solution.py:372
  0.7 22.5 %collective-permute-start.1 = (bf16[4096,512]{1,0:T(8,128)(2,1)}, bf16[4096,512]{1,0:T(8,128)(2,1)S(1)}, u32[]{:S(2)}, u32[]{:S(2)}) collective-permute-start(bf16[4096,512]{1,0:T(8,128)(2,1)} %refs_1_.1), channel_id=1, source_target_pairs={{0,32},{32,0},{64,96},{96,64},{128,160},{160,128},{192,224},{224,1... | collective-permute-start | bytes 12582920 | tf_op jit(solution)/shard_map/ppermute | solution.py:372
  23.2 3.3 %copy-start = (bf16[4096,512]{1,0:T(8,128)(2,1)}, bf16[4096,512]{1,0:T(8,128)(2,1)S(1)}, u32[]{:S(2)}) copy-start(bf16[4096,512]{1,0:T(8,128)(2,1)S(1)} %collective-permute-done.refs_2_) | copy-start | bytes 12582916
  23.2 4.0 %copy-start.1 = (bf16[4096,512]{1,0:T(8,128)(2,1)}, bf16[4096,512]{1,0:T(8,128)(2,1)S(1)}, u32[]{:S(2)}) copy-start(bf16[4096,512]{1,0:T(8,128)(2,1)S(1)} %collective-permute-done.1.refs_3_) | copy-start | bytes 12582916
  23.2 8.3 %collective-permute-start.2 = (bf16[128,1152]{1,0:T(8,128)(2,1)S(1)}, bf16[128,1152]{1,0:T(8,128)(2,1)S(1)}, u32[]{:S(2)}, u32[]{:S(2)}) collective-permute-start(bf16[128,1152]{1,0:T(8,128)(2,1)S(1)} %bitcast.6), channel_id=1, source_target_pairs={{0,16},{1,17},{2,18},{3,19},{4,20},{5,21},{6,22},{7,23},{8,24},{9,... | collective-permute-start | bytes 884744 | tf_op jit(solution)/shard_map/ppermute | solution.py:384
  26.5 8.2 %collective-permute-start.3 = (bf16[128,1152]{1,0:T(8,128)(2,1)S(1)}, bf16[128,1152]{1,0:T(8,128)(2,1)S(1)}, u32[]{:S(2)}, u32[]{:S(2)}) collective-permute-start(bf16[128,1152]{1,0:T(8,128)(2,1)S(1)} %bitcast.7), channel_id=1, source_target_pairs={{0,8},{1,9},{2,10},{3,11},{4,12},{5,13},{6,14},{7,15},{8,16},{9,17... | collective-permute-start | bytes 884744 | tf_op jit(solution)/shard_map/ppermute | solution.py:384
  27.2 7.9 %collective-permute-start.4 = (bf16[128,1152]{1,0:T(8,128)(2,1)S(1)}, bf16[128,1152]{1,0:T(8,128)(2,1)S(1)}, u32[]{:S(2)}, u32[]{:S(2)}) collective-permute-start(bf16[128,1152]{1,0:T(8,128)(2,1)S(1)} %bitcast.8), channel_id=1, source_target_pairs={{0,24},{1,25},{2,26},{3,27},{4,28},{5,29},{6,30},{7,31},{8,0},{9,1... | collective-permute-start | bytes 884744 | tf_op jit(solution)/shard_map/ppermute | solution.py:384
  35.7 9.4 %collective-permute-start.5 = (bf16[256,1024]{1,0:T(8,128)(2,1)S(1)}, bf16[256,1024]{1,0:T(8,128)(2,1)S(1)}, u32[]{:S(2)}, u32[]{:S(2)}) collective-permute-start(bf16[256,1024]{1,0:T(8,128)(2,1)S(1)} %get-tuple-element.61.refs_0_), channel_id=1, source_target_pairs={{0,64},{1,65},{2,66},{3,67},{4,68},{5,69},{6,70},{7,71},{8,72},{9,... | collective-permute-start | bytes 1572872 | tf_op jit(solution)/shard_map/ppermute | solution.py:384
  36.2 10.4 %collective-permute-start.6 = (bf16[256,1024]{1,0:T(8,128)(2,1)S(1)}, bf16[256,1024]{1,0:T(8,128)(2,1)S(1)}, u32[]{:S(2)}, u32[]{:S(2)}) collective-permute-start(bf16[256,1024]{1,0:T(8,128)(2,1)S(1)} %get-tuple-element.62.refs_1_), channel_id=1, source_target_pairs={{0,192},{1,193},{2,194},{3,195},{4,196},{5,197},{6,198},{7,199},{8... | collective-permute-start | bytes 1572872 | tf_op jit(solution)/shard_map/ppermute | solution.py:384
  37.8 15.5 %collective-permute-start.10 = (bf16[256,1024]{1,0:T(8,128)(2,1)S(1)}, bf16[256,1024]{1,0:T(8,128)(2,1)S(1)}, u32[]{:S(2)}, u32[]{:S(2)}) collective-permute-start(bf16[256,1024]{1,0:T(8,128)(2,1)S(1)} %get-tuple-element.61.refs_0_), channel_id=1, source_target_pairs={{0,192},{1,193},{2,194},{3,195},{4,196},{5,197},{6,198},{7,199},{8... | collective-permute-start | bytes 1572872 | tf_op jit(solution)/shard_map/ppermute | solution.py:384
  38.6 14.7 %collective-permute-start.9 = (bf16[256,1024]{1,0:T(8,128)(2,1)S(1)}, bf16[256,1024]{1,0:T(8,128)(2,1)S(1)}, u32[]{:S(2)}, u32[]{:S(2)}) collective-permute-start(bf16[256,1024]{1,0:T(8,128)(2,1)S(1)} %get-tuple-element.62.refs_1_), channel_id=1, source_target_pairs={{0,64},{1,65},{2,66},{3,67},{4,68},{5,69},{6,70},{7,71},{8,72},{9,... | collective-permute-start | bytes 1572872 | tf_op jit(solution)/shard_map/ppermute | solution.py:384
  46.6 10.5 %collective-permute-start.7 = (bf16[256,1024]{1,0:T(8,128)(2,1)S(1)}, bf16[256,1024]{1,0:T(8,128)(2,1)S(1)}, u32[]{:S(2)}, u32[]{:S(2)}) collective-permute-start(bf16[256,1024]{1,0:T(8,128)(2,1)S(1)} %collective-permute-done.5.refs_0_), channel_id=1, source_target_pairs={{0,64},{1,65},{2,66},{3,67},{4,68},{5,69},{6,70},{7,71},{8,72},{9,... | collective-permute-start | bytes 1572872 | tf_op jit(solution)/shard_map/ppermute | solution.py:384
  46.9 11.0 %collective-permute-start.8 = (bf16[256,1024]{1,0:T(8,128)(2,1)S(1)}, bf16[256,1024]{1,0:T(8,128)(2,1)S(1)}, u32[]{:S(2)}, u32[]{:S(2)}) collective-permute-start(bf16[256,1024]{1,0:T(8,128)(2,1)S(1)} %collective-permute-done.6.refs_3_), channel_id=1, source_target_pairs={{0,192},{1,193},{2,194},{3,195},{4,196},{5,197},{6,198},{7,199},{8... | collective-permute-start | bytes 1572872 | tf_op jit(solution)/shard_map/ppermute | solution.py:384
  48.7 1.3 %collective-permute-start.11 = (bf16[512,128]{1,0:T(8,128)(2,1)S(1)}, bf16[512,128]{1,0:T(8,128)(2,1)S(1)}, u32[]{:S(2)}, u32[]{:S(2)}) collective-permute-start(bf16[512,128]{1,0:T(8,128)(2,1)S(1)} %get-tuple-element.79.own_ref), channel_id=1, source_target_pairs={{0,32},{32,0},{64,96},{96,64},{128,160},{160,128},{192,224},{224,1... | collective-permute-start | bytes 393224 | tf_op jit(solution)/shard_map/ppermute | solution.py:372
  58.9 3.0 %collective-permute-start.13 = (f32[512,512]{1,0:T(8,128)S(1)}, f32[512,512]{1,0:T(8,128)S(1)}, u32[]{:S(2)}, u32[]{:S(2)}) collective-permute-start(f32[512,512]{1,0:T(8,128)S(1)} %shard_map.78), channel_id=1, source_target_pairs={{0,32},{32,0},{64,96},{96,64},{128,160},{160,128},{192,224},{224,1... | collective-permute-start | bytes 3145736 | tf_op jit(solution)/shard_map/ppermute | solution.py:372
  60.0 3.1 %collective-permute-start.12 = (f32[512,512]{1,0:T(8,128)S(1)}, f32[512,512]{1,0:T(8,128)S(1)}, u32[]{:S(2)}, u32[]{:S(2)}) collective-permute-start(f32[512,512]{1,0:T(8,128)S(1)} %shard_map.77), channel_id=1, source_target_pairs={{0,32},{32,0},{64,96},{96,64},{128,160},{160,128},{192,224},{224,1... | collective-permute-start | bytes 3145736 | tf_op jit(solution)/shard_map/ppermute | solution.py:372
  88.6 2.0 %collective-permute-start.14 = (bf16[512,512]{1,0:T(8,128)(2,1)S(1)}, bf16[512,512]{1,0:T(8,128)(2,1)S(1)}, u32[]{:S(2)}, u32[]{:S(2)}) collective-permute-start(bf16[512,512]{1,0:T(8,128)(2,1)S(1)} %shard_map.82.g_ref), channel_id=1, source_target_pairs={{0,32},{32,0},{64,96},{96,64},{128,160},{160,128},{192,224},{224,1... | collective-permute-start | bytes 1572872 | tf_op jit(solution)/shard_map/ppermute | solution.py:372
  91.7 7.4 %collective-permute-start.16 = (bf16[256,512]{1,0:T(8,128)(2,1)S(1)}, bf16[256,512]{1,0:T(8,128)(2,1)S(1)}, u32[]{:S(2)}, u32[]{:S(2)}) collective-permute-start(bf16[256,512]{1,0:T(8,128)(2,1)S(1)} %get-tuple-element.102), channel_id=1, source_target_pairs={{0,64},{1,65},{2,66},{3,67},{4,68},{5,69},{6,70},{7,71},{8,72},{9,... | collective-permute-start | bytes 786440 | tf_op jit(solution)/shard_map/ppermute | solution.py:384
  93.8 7.6 %collective-permute-start.17 = (bf16[256,512]{1,0:T(8,128)(2,1)S(1)}, bf16[256,512]{1,0:T(8,128)(2,1)S(1)}, u32[]{:S(2)}, u32[]{:S(2)}) collective-permute-start(bf16[256,512]{1,0:T(8,128)(2,1)S(1)} %get-tuple-element.104), channel_id=1, source_target_pairs={{0,192},{1,193},{2,194},{3,195},{4,196},{5,197},{6,198},{7,199},{8... | collective-permute-start | bytes 786440 | tf_op jit(solution)/shard_map/ppermute | solution.py:384
  95.6 8.6 %collective-permute-start.15 = (bf16[256,512]{1,0:T(8,128)(2,1)S(1)}, bf16[256,512]{1,0:T(8,128)(2,1)S(1)}, u32[]{:S(2)}, u32[]{:S(2)}) collective-permute-start(bf16[256,512]{1,0:T(8,128)(2,1)S(1)} %get-tuple-element.100), channel_id=1, source_target_pairs={{0,192},{1,193},{2,194},{3,195},{4,196},{5,197},{6,198},{7,199},{8... | collective-permute-start | bytes 786440 | tf_op jit(solution)/shard_map/ppermute | solution.py:384
  96.3 7.9 %collective-permute-start.20 = (bf16[256,512]{1,0:T(8,128)(2,1)S(1)}, bf16[256,512]{1,0:T(8,128)(2,1)S(1)}, u32[]{:S(2)}, u32[]{:S(2)}) collective-permute-start(bf16[256,512]{1,0:T(8,128)(2,1)S(1)} %get-tuple-element.108), channel_id=1, source_target_pairs={{0,64},{1,65},{2,66},{3,67},{4,68},{5,69},{6,70},{7,71},{8,72},{9,... | collective-permute-start | bytes 786440 | tf_op jit(solution)/shard_map/ppermute | solution.py:384
  101.5 6.4 %collective-permute-start.18 = (bf16[256,512]{1,0:T(8,128)(2,1)S(1)}, bf16[256,512]{1,0:T(8,128)(2,1)S(1)}, u32[]{:S(2)}, u32[]{:S(2)}) collective-permute-start(bf16[256,512]{1,0:T(8,128)(2,1)S(1)} %get-tuple-element.105), channel_id=1, source_target_pairs={{0,64},{1,65},{2,66},{3,67},{4,68},{5,69},{6,70},{7,71},{8,72},{9,... | collective-permute-start | bytes 786440 | tf_op jit(solution)/shard_map/ppermute | solution.py:384
  101.6 7.7 %collective-permute-start.19 = (bf16[256,512]{1,0:T(8,128)(2,1)S(1)}, bf16[256,512]{1,0:T(8,128)(2,1)S(1)}, u32[]{:S(2)}, u32[]{:S(2)}) collective-permute-start(bf16[256,512]{1,0:T(8,128)(2,1)S(1)} %get-tuple-element.107), channel_id=1, source_target_pairs={{0,192},{1,193},{2,194},{3,195},{4,196},{5,197},{6,198},{7,199},{8... | collective-permute-start | bytes 786440 | tf_op jit(solution)/shard_map/ppermute | solution.py:384
  109.5 6.6 %collective-permute-start.21 = (bf16[128,512]{1,0:T(8,128)(2,1)S(1)}, bf16[128,512]{1,0:T(8,128)(2,1)S(1)}, u32[]{:S(2)}, u32[]{:S(2)}) collective-permute-start(bf16[128,512]{1,0:T(8,128)(2,1)S(1)} %get-tuple-element.109), channel_id=1, source_target_pairs={{0,16},{1,17},{2,18},{3,19},{4,20},{5,21},{6,22},{7,23},{8,24},{9,... | collective-permute-start | bytes 393224 | tf_op jit(solution)/shard_map/ppermute | solution.py:384
  111.1 5.0 %collective-permute-start.22 = (bf16[128,512]{1,0:T(8,128)(2,1)S(1)}, bf16[128,512]{1,0:T(8,128)(2,1)S(1)}, u32[]{:S(2)}, u32[]{:S(2)}) collective-permute-start(bf16[128,512]{1,0:T(8,128)(2,1)S(1)} %get-tuple-element.110), channel_id=1, source_target_pairs={{0,24},{1,25},{2,26},{3,27},{4,28},{5,29},{6,30},{7,31},{8,0},{9,1... | collective-permute-start | bytes 393224 | tf_op jit(solution)/shard_map/ppermute | solution.py:384
  112.7 6.2 %collective-permute-start.23 = (bf16[128,512]{1,0:T(8,128)(2,1)S(1)}, bf16[128,512]{1,0:T(8,128)(2,1)S(1)}, u32[]{:S(2)}, u32[]{:S(2)}) collective-permute-start(bf16[128,512]{1,0:T(8,128)(2,1)S(1)} %get-tuple-element.111), channel_id=1, source_target_pairs={{0,8},{1,9},{2,10},{3,11},{4,12},{5,13},{6,14},{7,15},{8,16},{9,17... | collective-permute-start | bytes 393224 | tf_op jit(solution)/shard_map/ppermute | solution.py:384
